TPU v7x, 32 devices: a whole 2x2x4 slice. The times are simulated.
32 devices in a mesh: rep: 2 (over y), ep: 16 (over z, x, core).
Axes of the slice: x: 2, y: 2, z: 4, core: 2. Of those that a mesh axis runs over, the one named last changes fastest.
Arguments:
- out_grad: bfloat16 [8192, 3584], P(('rep', 'ep')), may hold values from -0.8984375 to 0.8984375
- expert_ids: int32 [8192, 8], P(('rep', 'ep')), may hold values from 0 to 127, as said below
- slots: int32 [8192, 8], P(('rep', 'ep')), may hold values from -1 to 11, as said below
- gate_weights: bfloat16 [8192, 8], P(('rep', 'ep')), may hold values from 0.049804688 to 0.59765625
- saved_gate_up: bfloat16 [2, 16, 192, 2048], P('rep', 'ep'), may hold values from -6 to 6
- master: float32 [16, 1024, 3584], P('ep', 'rep'), may hold values from -0.1875 to 0.1875
- moment1: bfloat16 [16, 1024, 3584], P('ep', 'rep'), may hold values from -0.59765625 to 0.59765625
- moment2: bfloat16 [16, 1024, 3584], P('ep', 'rep'), may hold values from 0.0009994507 to 0.0099487305
Outputs:
- grad_gate_up: bfloat16 [2, 16, 192, 2048], P('rep', 'ep')
- gate_grad: float32 [8192, 8], P(('rep', 'ep'))
- master_out: float32 [16, 1024, 3584], P('ep', 'rep')
- moment1_out: bfloat16 [16, 1024, 3584], P('ep', 'rep')
- moment2_out: bfloat16 [16, 1024, 3584], P('ep', 'rep')
Inputs may be any that keep to these rules, and one draw needn't show every extreme that they name: `expert_ids`: each row names 8 different experts of 0 to 127. Within the rows of one device, the choices naming one expert, taken in order of token then choice, have slots 0, 1, 2 and so on; those from 12 on are -1. Every device has an expert of the window with more than 12 such choices.
All inputs are finite; a program needn't handle non-finite values.
Results may differ from a plain program's by a relative error of at most 0.025.
Values may be sent and summed in bfloat16 or wider, within the bound.
No kernel may reach another device: no remote copies, remote signals or barrier semaphores. Data moves between devices by JAX's collectives and lax.ppermute only.
A program may use at most 128 MiB of HBM per device.

v0:
```python
import jax
import jax.numpy as jnp
from jax import lax
from jax.sharding import PartitionSpec as P

TOPK = 8
EXP_LOCAL = 8
SEND = 12


beta_one = 0.9
beta_two = 0.95
learn_rate = 0.002
decay_rate = 0.1
adam_eps = 1e-08
adam_step = 50


def swiglu_backward(gate_up, weights, grad_proj):
    half_width = gate_up.shape[-1] // 2
    gate_part = gate_up[..., :half_width].astype(jnp.float32)
    up_part = gate_up[..., half_width:].astype(jnp.float32)
    sigmoid_gate = jax.nn.sigmoid(gate_part)
    silu_gate = gate_part * sigmoid_gate
    hidden = lax.optimization_barrier((silu_gate * up_part).astype(jnp.bfloat16))
    scale = weights.astype(jnp.float32)[..., None]
    scaled = (scale * hidden.astype(jnp.float32)).astype(jnp.bfloat16)
    grad_hidden = scale * grad_proj
    d_gate = grad_hidden * up_part * sigmoid_gate * (1.0 + gate_part * (1.0 - sigmoid_gate))
    d_up = grad_hidden * silu_gate
    return (hidden, scaled, jnp.concatenate([d_gate, d_up], axis=-1).astype(jnp.bfloat16))


def adamw(master, moment1, moment2, grad):
    m_new = beta_one * moment1.astype(jnp.float32) + (1.0 - beta_one) * grad
    v_new = beta_two * moment2.astype(jnp.float32) + (1.0 - beta_two) * grad * grad
    corr_one = 1.0 - beta_one**adam_step
    corr_two = 1.0 - beta_two**adam_step
    update = m_new / corr_one / (jnp.sqrt(v_new / corr_two) + adam_eps)
    master_new = master - learn_rate * (update + decay_rate * master)
    return (master_new, m_new.astype(jnp.bfloat16), v_new.astype(jnp.bfloat16))


def per_device(out_grad, expert_ids, slots, gate_weights, saved_gate_up, master, moment1, moment2):
    ep_size = lax.axis_size("ep")
    tok_rows = out_grad.shape[0]
    width = out_grad.shape[1]
    filled = ep_size * SEND
    live = (expert_ids % EXP_LOCAL == 0) & (slots >= 0)
    position = jnp.where(live, expert_ids // EXP_LOCAL * SEND + slots, filled)
    flat_pos = position.reshape(-1)
    token_of = jnp.broadcast_to(
        jnp.arange(tok_rows, dtype=jnp.int32)[:, None], position.shape
    ).reshape(-1)
    source_row = jnp.full((filled + 1,), tok_rows, jnp.int32).at[flat_pos].set(token_of)[:filled]
    padded = jnp.concatenate([out_grad, jnp.zeros((1, width), out_grad.dtype)], axis=0)
    send_rows = padded[source_row].reshape(ep_size, SEND, width)
    send_weights = (
        jnp.zeros((filled + 1,), gate_weights.dtype).at[flat_pos].set(gate_weights.reshape(-1))
    )
    send_weights = send_weights[:filled].reshape(ep_size, SEND)
    recv_rows, recv_weights = (
        lax.all_to_all(send_rows, "ep", split_axis=0, concat_axis=0, tiled=True),
        lax.all_to_all(send_weights, "ep", split_axis=0, concat_axis=0, tiled=True),
    )
    dout = recv_rows.reshape(filled, width)
    slot_weight = recv_weights.reshape(filled)
    full_weight = lax.all_gather(master[0].astype(jnp.bfloat16), "rep", axis=0, tiled=True)
    grad_proj = lax.dot_general(
        dout, full_weight, (((1,), (1,)), ((), ())), preferred_element_type=jnp.float32
    )
    gate_up = saved_gate_up[0, 0]
    hidden, scaled, grad_gate_up = swiglu_backward(gate_up, slot_weight, grad_proj)
    grad = lax.psum_scatter(
        lax.dot_general(
            scaled, dout, (((0,), (0,)), ((), ())), preferred_element_type=jnp.float32
        ).astype(jnp.bfloat16),
        "rep",
        scatter_dimension=0,
        tiled=True,
    ).astype(jnp.float32)
    master_out, moment1_out, moment2_out = adamw(master, moment1, moment2, grad[None])
    expert_out = jnp.dot(hidden, full_weight, preferred_element_type=jnp.float32).astype(
        jnp.bfloat16
    )
    back_rows = lax.all_to_all(
        expert_out.reshape(ep_size, SEND, width), "ep", split_axis=0, concat_axis=0, tiled=True
    )
    back_pad = jnp.concatenate(
        [back_rows.reshape(filled, width), jnp.zeros((1, width), jnp.bfloat16)], axis=0
    )
    grad_f = out_grad.astype(jnp.float32)
    scores = [
        jnp.sum(grad_f * back_pad[position[:, which]].astype(jnp.float32), axis=-1)
        for which in range(TOPK)
    ]
    gate_grad = jnp.stack(scores, axis=1)
    gate_grad = jnp.where(live, gate_grad, jnp.zeros((), jnp.float32))
    return (
        grad_gate_up.reshape(saved_gate_up.shape),
        gate_grad,
        master_out,
        moment1_out,
        moment2_out,
    )


def solution(mesh):
    in_specs = (
        P(("rep", "ep"), None),
        P(("rep", "ep"), None),
        P(("rep", "ep"), None),
        P(("rep", "ep"), None),
        P("rep", "ep", None, None),
        P("ep", "rep", None),
        P("ep", "rep", None),
        P("ep", "rep", None),
    )
    out_specs = (
        P("rep", "ep", None, None),
        P(("rep", "ep"), None),
        P("ep", "rep", None),
        P("ep", "rep", None),
        P("ep", "rep", None),
    )
    return jax.shard_map(
        per_device, mesh=mesh, in_specs=in_specs, out_specs=out_specs, check_vma=False
    )
```

profile of v0, /device:TPU:0, one launch (start us, length us, event | category | flops | bytes accessed | tf_op | source)
XLA Modules:
  0.0 388.1 jit_solution(13796663343921003582)
XLA Ops:
  7.2 0.8 copy.16
  8.0 0.1 reshape.192
  8.1 0.7 fusion.38
  8.8 0.1 copy.15
  9.0 0.1 reshape.108
  9.1 14.6 %scatter_custom_fusion = bf16[193]{0:T(256)(128)(2,1)S(1)} fusion(s32[2048]{0:T(1024)S(1)} %bitcast.57, bf16[2048]{0:T(1024)(128)(2,1)S(1)} %reshape.192, bf16[]{:T(256)} %constant.22.clone.1), kind=kCustom, calls=%fused_computation.98 | custom fusion | bytes 388 | tf_op jit(solution)/shard_map/scatter | solution.py:59
  23.7 0.7 all_to_all.16
  24.4 7.4 %all-to-all-start = ((bf16[16,1,12]{2,1,0:T(2,128)(2,1)}), bf16[16,1,12]{2,1,0:T(2,128)(2,1)S(1)}, u32[]{:S(2)}, u32[]{:S(2)}) async-start(bf16[16,1,12]{2,1,0:T(2,128)(2,1)} %all_to_all.16), calls=%async_computation | async-start | bytes 16384 | tf_op jit(solution)/shard_map/all_to_all | solution.py:64
  31.8 0.1 reshape.200
  31.9 8.0 %scatter_custom_fusion.1 = s32[193]{0:T(256)S(1)} fusion(s32[2048]{0:T(1024)S(1)} %bitcast.58, s32[2048]{0:T(1024)S(1)} %reshape.200, s32[]{:T(128)} %constant.56.clone.1), kind=kCustom, calls=%fused_computation.96 | custom fusion | bytes 776 | tf_op jit(solution)/shard_map/scatter | solution.py:55
  39.9 1.6 concatenate.21
  41.6 1.4 gather_fusion
  43.0 1.4 reshape.111
  44.4 0.0 all-to-all-done
  44.4 6.1 %all-to-all-start.1 = ((bf16[16,12,3584]{2,1,0:T(8,128)(2,1)}), bf16[16,12,3584]{2,1,0:T(8,128)(2,1)S(1)}, u32[]{:S(2)}, u32[]{:S(2)}) async-start(bf16[16,12,3584]{2,1,0:T(8,128)(2,1)} %reshape.111), calls=%async_computation.1 | async-start | bytes 3670016 | tf_op jit(solution)/shard_map/all_to_all | solution.py:63
  50.5 0.0 reduce-scatter.2.cloned.1.call-start
  50.6 0.0 copy-done.1
  50.6 1.0 fusion.27
  51.7 0.1 reshape.115
  51.7 35.3 %all-to-all-done.1 = bf16[16,12,3584]{2,1,0:T(8,128)(2,1)S(1)} async-done(((bf16[16,12,3584]{2,1,0:T(8,128)(2,1)}), bf16[16,12,3584]{2,1,0:T(8,128)(2,1)S(1)}, u32[]{:S(2)}, u32[]{:S(2)}) %all-to-all-start.1) | async-done | bytes 1376288 | tf_op jit(solution)/shard_map/all_to_all | solution.py:63
  87.1 0.3 reshape.112
  87.4 6.2 %convolution_convert_fusion = bf16[1024,3584]{1,0:T(8,128)(2,1)} fusion(bf16[192,3584]{1,0:T(8,128)(2,1)S(1)} %reshape.112, bf16[192,1024]{1,0:T(8,128)(2,1)} %fusion.27, f32[192]{0:T(256)S(1)} %reshape.115), kind=kOutput, calls=%fused_computation.21 | convolution fusion | flops 1413545984 | bytes 9110272 | tf_op jit(solution)/shard_map/dot_general | solution.py:75
  93.7 0.0 reduce-scatter.2.cloned.1.call-update
  93.7 0.2 all-gather.3.cloned.1.call-start
  93.9 93.9 %reduce-scatter.2.cloned.1.call-done = bf16[512,3584]{1,0:T(8,128)(2,1)} async-done(((bf16[1024,3584]{1,0:T(8,128)(2,1)}), bf16[512,3584]{1,0:T(8,128)(2,1)}) %reduce-scatter.2.cloned.1.call-update) | async-done | bytes 3670032 | tf_op jit(solution)/shard_map/reduce_scatter | solution.py:74
  187.8 20.1 %fusion.8 = (bf16[1,512,3584]{2,1,0:T(8,128)(2,1)}, f32[1,512,3584]{2,1,0:T(8,128)}, bf16[1,512,3584]{2,1,0:T(8,128)(2,1)}, bf16[1,512,3584]{2,1,0:T(8,128)(2,1)}) fusion(bf16[512,3584]{1,0:T(8,128)(2,1)} %reduce-scatter.2.cloned.1.call-done, bf16[1,512,3584]{2,1,0:T(8,128)(2,1)} %param.15, f32[1,512,3584]{2,1,0:T(8,128)} %param.13, ...), kind=kLoop, calls=%fused_computation.31 | loop fusion | flops 38535168 | bytes 36700160 | tf_op jit(solution)/shard_map/convert_element_type | solution.py:41
  207.9 0.0 all-gather.3.cloned.1.call-update
  207.9 92.3 %all-gather.3.cloned.1.call-done = bf16[1,1024,3584]{2,1,0:T(8,128)(2,1)} async-done(((bf16[1,512,3584]{2,1,0:T(8,128)(2,1)}), bf16[1,1024,3584]{2,1,0:T(8,128)(2,1)}) %all-gather.3.cloned.1.call-update) | async-done | bytes 7340048 | tf_op jit(solution)/shard_map/all_gather | solution.py:68
  300.3 0.0 copy-done
  300.3 4.7 %fusion.10 = bf16[192,3584]{1,0:T(8,128)(2,1)S(1)} fusion(bf16[192,1024]{1,0:T(8,128)(2,1)S(1)} %copy-done, bf16[1,1024,3584]{2,1,0:T(8,128)(2,1)} %all-gather.3.cloned.1.call-done), kind=kOutput, calls=%fused_computation.33 | convolution fusion | flops 1409974272 | bytes 9109504 | tf_op jit(solution)/shard_map/dot_general | solution.py:83
  304.9 1.5 reshape.113
  306.4 5.6 %all-to-all-start.2 = ((bf16[16,12,3584]{2,1,0:T(8,128)(2,1)}), bf16[16,12,3584]{2,1,0:T(8,128)(2,1)S(1)}, u32[]{:S(2)}, u32[]{:S(2)}) async-start(bf16[16,12,3584]{2,1,0:T(8,128)(2,1)} %reshape.113), calls=%async_computation.2 | async-start | bytes 3670016 | tf_op jit(solution)/shard_map/all_to_all | solution.py:86
  312.2 5.9 %fusion.34 = (bf16[1,1,192,1024]{3,2,1,0:T(8,128)(2,1)S(1)}, bf16[1,1,192,1024]{3,2,1,0:T(8,128)(2,1)S(1)}) fusion(bf16[192,2048]{1,0:T(8,128)(2,1)} %bitcast.55, bf16[192,3584]{1,0:T(8,128)(2,1)S(1)} %reshape.112, bf16[1,1024,3584]{2,1,0:T(8,128)(2,1)} %all-gather.3.cloned.1.call-done, f32[192]{0:T(256)S(1)} %reshape.115), kind=kOutput, calls=%fused_computation.61 | convolution fusion | flops 1412431872 | bytes 10289920 | tf_op jit(solution)/shard_map/dot_general | solution.py:69
  318.1 0.9 pad_maximum_fusion
  319.0 29.6 %all-to-all-done.2 = bf16[16,12,3584]{2,1,0:T(8,128)(2,1)S(1)} async-done(((bf16[16,12,3584]{2,1,0:T(8,128)(2,1)}), bf16[16,12,3584]{2,1,0:T(8,128)(2,1)S(1)}, u32[]{:S(2)}, u32[]{:S(2)}) %all-to-all-start.2) | async-done | bytes 1376288 | tf_op jit(solution)/shard_map/all_to_all | solution.py:86
  348.6 1.2 reshape.114
  349.8 1.4 concatenate.25
  351.3 1.7 gather_fusion.8
  353.0 3.0 gather_fusion.7
  356.0 3.0 gather_fusion.6
  359.0 3.0 gather_fusion.5
  362.0 3.0 gather_fusion.4
  365.0 2.9 gather_fusion.3
  367.9 3.0 gather_fusion.2
  370.9 3.0 gather_fusion.1
  373.9 6.8 %fusion.20 = (f32[256]{0:T(256)S(1)}, f32[256]{0:T(256)S(1)}, f32[256]{0:T(256)S(1)}, f32[256]{0:T(256)S(1)}, f32[256]{0:T(256)S(1)}, /*index=5*/f32[256]{0:T(256)S(1)}, f32[256]{0:T(256)S(1)}, f32[256]{0:T(256)S(1)}) fusion(bf16[256,3584]{1,0:T(8,128)(2,1)} %param.8, bf16[256,3584]{1,0:T(8,128)(2,1)S(1)} %gather_fusion.8, ...), kind=kLoop, calls=%fused_computation.41 | loop fusion | flops 22935552 | bytes 16523264 | tf_op jit(solution)/shard_map/reduce_sum | solution.py:94
  380.7 0.0 copy-done.2
  380.7 0.6 broadcast_select_fusion
  (20 shorter events, 0.2 us)
Async XLA Ops:
  24.4 20.0 %all-to-all-start = ((bf16[16,1,12]{2,1,0:T(2,128)(2,1)}), bf16[16,1,12]{2,1,0:T(2,128)(2,1)S(1)}, u32[]{:S(2)}, u32[]{:S(2)}) async-start(bf16[16,1,12]{2,1,0:T(2,128)(2,1)} %all_to_all.16), calls=%async_computation | async-start | bytes 16384 | tf_op jit(solution)/shard_map/all_to_all | solution.py:64
  44.4 6.2 %copy-start.1 = (bf16[1,1,192,2048]{3,2,1,0:T(8,128)(2,1)S(1)}, bf16[1,1,192,2048]{3,2,1,0:T(8,128)(2,1)}, u32[]{:S(2)}) copy-start(bf16[1,1,192,2048]{3,2,1,0:T(8,128)(2,1)} %param.12) | copy-start | bytes 2359300
  44.4 42.7 %all-to-all-start.1 = ((bf16[16,12,3584]{2,1,0:T(8,128)(2,1)}), bf16[16,12,3584]{2,1,0:T(8,128)(2,1)S(1)}, u32[]{:S(2)}, u32[]{:S(2)}) async-start(bf16[16,12,3584]{2,1,0:T(8,128)(2,1)} %reshape.111), calls=%async_computation.1 | async-start | bytes 3670016 | tf_op jit(solution)/shard_map/all_to_all | solution.py:63
  50.5 137.3 %reduce-scatter.2.cloned.1.call-start = ((), (), s32[]{:S(2)}) async-start(), calls=%async_computation.4 | async-start | bytes 11010048 | tf_op jit(solution)/shard_map/reduce_scatter | solution.py:74
  93.7 206.5 %all-gather.3.cloned.1.call-start = ((), (), s32[]{:S(2)}) async-start(), calls=%async_computation.5 | async-start | bytes 11010048 | tf_op jit(solution)/shard_map/all_gather | solution.py:68
  207.9 92.4 %copy-start = (bf16[192,1024]{1,0:T(8,128)(2,1)S(1)}, bf16[192,1024]{1,0:T(8,128)(2,1)}, u32[]{:S(2)}) copy-start(bf16[192,1024]{1,0:T(8,128)(2,1)} %fusion.27) | copy-start | bytes 1179652
  306.4 42.2 %all-to-all-start.2 = ((bf16[16,12,3584]{2,1,0:T(8,128)(2,1)}), bf16[16,12,3584]{2,1,0:T(8,128)(2,1)S(1)}, u32[]{:S(2)}, u32[]{:S(2)}) async-start(bf16[16,12,3584]{2,1,0:T(8,128)(2,1)} %reshape.113), calls=%async_computation.2 | async-start | bytes 3670016 | tf_op jit(solution)/shard_map/all_to_all | solution.py:86
  373.9 6.8 %copy-start.2 = (s32[256,8]{0,1:T(8,128)S(1)}, s32[256,8]{0,1:T(8,128)}, u32[]{:S(2)}) copy-start(s32[256,8]{0,1:T(8,128)} %param.10) | copy-start | bytes 24580
  373.9 6.8 %copy-start.3 = (s32[256,8]{0,1:T(8,128)S(1)}, s32[256,8]{0,1:T(8,128)}, u32[]{:S(2)}) copy-start(s32[256,8]{0,1:T(8,128)} %param.9) | copy-start | bytes 24580
Sparse Core Ops, SparseCore 0:
  93.8 93.9 reduce-scatter.1
  208.0 92.1 all-gather.2
where the time goes:
time: 393 us; the launch traced here: 388 us
  waiting for transfers between devices  251 us (64%)
  local copies, waits for them, and re-layouts  56.2 us (14%)
  other arithmetic  30.3 us (8%)
  starting transfers between devices  19.4 us (5%)
  matrix products  16.8 us (4%)
  between operations  14.3 us (4%)
    reduce_scatter x1, waiting for transfers between devices, per_device(): lax.psum_scatter(lax.dot_general(scaled, dout, (((0,), (0,)), ((), ())),...  93.9 us
    all_gather x1, waiting for transfers between devices, per_device(): lax.all_gather(master[0].astype(jnp.bfloat16), 'rep', axis=0, tiled=True)  92.3 us
    all_to_all x1, waiting for transfers between devices, per_device(): lax.all_to_all(send_rows, 'ep', split_axis=0, concat_axis=0, tiled=True)  35.3 us
    all_to_all x1, waiting for transfers between devices, per_device(): lax.all_to_all(expert_out.reshape(ep_size, SEND, width), 'ep', split_axis...  29.6 us
    gather x8, local copies, waits for them, and re-layouts, per_device(): back_pad[position[:, which]].astype(jnp.float32)  22.6 us
    convert_element_type x1, other arithmetic, adamw(): return (master_new, m_new.astype(jnp.bfloat16), v_new.astype(jnp.bfloat16))  20.1 us
    scatter x1, local copies, waits for them, and re-layouts, per_device(): jnp.zeros((filled + 1,), gate_weights.dtype).at[flat_pos]  14.6 us
    scatter x1, local copies, waits for them, and re-layouts, per_device(): jnp.full((filled + 1,), tok_rows, jnp.int32).at[flat_pos].set(token_of)  8.03 us
  transfers between devices with their start and end apart: 5, of which 4 were waited for; matrix products, arithmetic and copies ran while one was open for 5% of the time, Pallas kernels for 0%

commit v1 on v0

v1 whole, which is shorter than its diff:
```python
import functools

import jax
import jax.numpy as jnp
from jax import lax
from jax.experimental import pallas as pl
from jax.experimental.pallas import tpu as pltpu
from jax.sharding import PartitionSpec as P

TOPK = 8
EXP_LOCAL = 8
SEND = 12
LANE = 128
UNIT = 512
ROWS = 16

beta_one = 0.9
beta_two = 0.95
learn_rate = 0.002
decay_rate = 0.1
adam_eps = 1e-08
adam_step = 50

f32 = jnp.float32
bf16 = jnp.bfloat16


def params(mib=48):
    return pltpu.CompilerParams(vmem_limit_bytes=mib * 1024 * 1024)


def cost(flops, nbytes, transcendentals=0):
    return pl.CostEstimate(
        flops=int(flops), bytes_accessed=int(nbytes), transcendentals=int(transcendentals)
    )


def div_send(index):
    return lax.shift_right_logical(index * 10923, 17)


def dispatch_kernel(ids_ref, slots_ref, gates_ref, grad_ref, *out_refs):
    blocks = len(out_refs)
    rows = blocks * ROWS
    me = lax.axis_index("ep")
    ids = ids_ref[...]
    slots = slots_ref[...]
    gates = gates_ref[...].astype(f32)
    tok, width = grad_ref.shape
    part = width // 4
    live = (ids % EXP_LOCAL == 0) & (slots >= 0)
    place = jnp.where(live, ((ids // EXP_LOCAL) ^ me) * ROWS + slots, -1)
    row = lax.broadcasted_iota(jnp.int32, (rows, tok), 0)

    def pick_rows(at):
        pick = jnp.zeros((rows, tok), f32)
        for k in range(TOPK):
            pick = jnp.where(row == at[k : k + 1], gates[k : k + 1], pick)
        return pick.astype(bf16)

    main = pick_rows(place)
    for j in range(3):
        inside = (slots >= 4 * j) & (slots < 4 * j + 4) & live
        tail = pick_rows(jnp.where(inside, place + SEND - 4 * j, -1))
        total = jnp.dot(
            main, grad_ref[:, j * part : (j + 1) * part], preferred_element_type=f32
        )
        total += jnp.dot(tail, grad_ref[:, 3 * part :], preferred_element_type=f32)
        total = total.astype(bf16)
        for k in range(blocks):
            out_refs[k][:, j * part : (j + 1) * part] = total[k * ROWS : (k + 1) * ROWS]


def dispatch(blocks, ids, slots, gates, out_grad):
    tok, width = out_grad.shape
    return pl.pallas_call(
        dispatch_kernel,
        out_shape=[jax.ShapeDtypeStruct((ROWS, width // 4 * 3), bf16)] * blocks,
        compiler_params=params(),
        cost_estimate=cost(2 * blocks * ROWS * tok * width, 4 * tok * width),
    )(ids, slots, gates, out_grad)


def hidden_kernel(gate_up_ref, hidden_ref, coef_gate_ref, coef_up_ref):
    shards, _, part = hidden_ref.shape
    width = shards * part
    for q in range(shards):
        gate = gate_up_ref[:, q * part : (q + 1) * part].astype(f32)
        up = gate_up_ref[:, width + q * part : width + (q + 1) * part].astype(f32)
        sig = jax.nn.sigmoid(gate)
        silu = gate * sig
        hidden_ref[q] = (silu * up).astype(bf16)
        coef_gate_ref[q] = up * sig * (1.0 + gate * (1.0 - sig))
        coef_up_ref[q] = silu


def hidden_parts(gate_up, shards):
    slots, width = gate_up.shape
    part = width // 2 // shards
    shape = (shards, slots, part)
    return pl.pallas_call(
        hidden_kernel,
        out_shape=[
            jax.ShapeDtypeStruct(shape, bf16),
            jax.ShapeDtypeStruct(shape, f32),
            jax.ShapeDtypeStruct(shape, f32),
        ],
        compiler_params=params(),
        cost_estimate=cost(8 * slots * width, 8 * slots * width, slots * width),
    )(gate_up)


def project_kernel(blocks, *refs):
    arrived, (weight_ref, hidden_ref) = refs[:blocks], refs[blocks : blocks + 2]
    rows_ref, proj_ref, send_ref, score_ref = refs[blocks + 2 :]
    me = lax.axis_index("ep")
    count = rows_ref.shape[0]
    part = arrived[0].shape[1] // 3
    stack = jnp.concatenate([ref[...] for ref in arrived], axis=0)
    slot = lax.broadcasted_iota(jnp.int32, (count, blocks * ROWS), 0)
    col = lax.broadcasted_iota(jnp.int32, (count, blocks * ROWS), 1)
    block = div_send(slot)
    inner = slot - SEND * block
    base = (block ^ me) * ROWS
    order = (col == base + inner).astype(f32).astype(bf16)
    rows_ref[:, : 3 * part] = jnp.dot(
        order, stack[:, : 3 * part], preferred_element_type=f32
    ).astype(bf16)
    tail = jnp.zeros((count, part), f32)
    for j in range(3):
        inside = (inner >= 4 * j) & (inner < 4 * j + 4)
        order = jnp.where(inside & (col == base + SEND + inner - 4 * j), 1.0, 0.0).astype(bf16)
        tail += jnp.dot(
            order, stack[:, j * part : (j + 1) * part], preferred_element_type=f32
        )
    rows_ref[:, 3 * part :] = tail.astype(bf16)
    proj = lax.dot_general(
        rows_ref[...], weight_ref[...], (((1,), (1,)), ((), ())), preferred_element_type=f32
    )
    proj_ref[...] = proj
    send_ref[...] = proj.astype(bf16)
    score = jnp.sum(proj * hidden_ref[...].astype(f32), axis=1, keepdims=True)
    slot_of = lax.broadcasted_iota(jnp.int32, (count, LANE), 0)
    lane_of = lax.broadcasted_iota(jnp.int32, (count, LANE), 1)
    spread = jnp.where(slot_of - SEND * div_send(slot_of) == lane_of, score, 0.0)
    block_of = lax.broadcasted_iota(jnp.int32, (blocks, count), 0)
    slot_at = lax.broadcasted_iota(jnp.int32, (blocks, count), 1)
    gather = (div_send(slot_at) == block_of).astype(f32)
    score_ref[...] = jnp.dot(
        gather, spread, precision=lax.Precision.HIGHEST, preferred_element_type=f32
    )


def project(arrived, weight, hidden):
    blocks = len(arrived)
    count = blocks * SEND
    part, width = weight.shape
    return pl.pallas_call(
        functools.partial(project_kernel, blocks),
        out_shape=[
            jax.ShapeDtypeStruct((count, width), bf16),
            jax.ShapeDtypeStruct((count, part), f32),
            jax.ShapeDtypeStruct((count, part), bf16),
            jax.ShapeDtypeStruct((blocks, LANE), f32),
        ],
        compiler_params=params(),
        cost_estimate=cost(4 * count * part * width, 2 * width * (part + 2 * count)),
    )(*arrived, weight, hidden)


def adamw_kernel(hidden_ref, *refs):
    rows_refs, (master_ref, one_ref, two_ref) = refs[:-6], refs[-6:-3]
    master_out, one_out, two_out = refs[-3:]
    count = rows_refs[0].shape[0]
    grad = jnp.dot(hidden_ref[:, :count], rows_refs[0][...], preferred_element_type=f32)
    for s in range(1, len(rows_refs)):
        grad += jnp.dot(
            hidden_ref[:, s * count : (s + 1) * count],
            rows_refs[s][...],
            preferred_element_type=f32,
        )
    m_new = beta_one * one_ref[0].astype(f32) + (1.0 - beta_one) * grad
    v_new = beta_two * two_ref[0].astype(f32) + (1.0 - beta_two) * grad * grad
    corr_one = 1.0 - beta_one**adam_step
    corr_two = 1.0 - beta_two**adam_step
    rate = learn_rate * corr_two**0.5 / corr_one
    root = v_new * lax.rsqrt(v_new) + adam_eps * corr_two**0.5
    keep = 1.0 - learn_rate * decay_rate
    master_out[0] = keep * master_ref[0] - rate * m_new / root
    one_out[0] = m_new.astype(bf16)
    two_out[0] = v_new.astype(bf16)


def adamw(hidden_t, rows, master, one, two):
    part, depth = hidden_t.shape
    count, width = rows[0].shape
    state = pl.BlockSpec((1, part, UNIT), lambda i: (0, 0, i))
    return pl.pallas_call(
        adamw_kernel,
        grid=(width // UNIT,),
        in_specs=[pl.BlockSpec((part, depth), lambda i: (0, 0))]
        + [pl.BlockSpec((count, UNIT), lambda i: (0, i))] * len(rows)
        + [state] * 3,
        out_specs=[state, state, state],
        out_shape=[
            jax.ShapeDtypeStruct(master.shape, f32),
            jax.ShapeDtypeStruct(one.shape, bf16),
            jax.ShapeDtypeStruct(two.shape, bf16),
        ],
        compiler_params=params(),
        cost_estimate=cost(2 * part * depth * width, 16 * part * width, part * width),
    )(hidden_t, *rows, master, one, two)


def gate_up_kernel(place_ref, coef_gate_ref, coef_up_ref, *refs):
    out_ref = refs[-1]
    shards, _, part = coef_gate_ref.shape
    for s in range(shards):
        at = place_ref[s]
        grad = refs[s][...].astype(f32)
        low = pl.multiple_of(at * part, part)
        out_ref[:, pl.ds(low, part)] = (grad * coef_gate_ref[at]).astype(bf16)
        high = pl.multiple_of(shards * part + at * part, part)
        out_ref[:, pl.ds(high, part)] = (grad * coef_up_ref[at]).astype(bf16)


def gate_up_grad(place, coef_gate, coef_up, grads):
    shards, slots, part = coef_gate.shape
    vmem = pl.BlockSpec(memory_space=pltpu.VMEM)
    return pl.pallas_call(
        gate_up_kernel,
        in_specs=[pl.BlockSpec(memory_space=pltpu.SMEM)] + [vmem] * (2 + shards),
        out_specs=vmem,
        out_shape=jax.ShapeDtypeStruct((slots, 2 * shards * part), bf16),
        compiler_params=params(),
        cost_estimate=cost(4 * shards * slots * part, 16 * shards * slots * part),
    )(place, coef_gate, coef_up, *grads)


def score_kernel(ids_ref, slots_ref, gates_ref, score_ref, out_ref):
    shards, blocks, _ = score_ref.shape
    score = score_ref[0]
    for s in range(1, shards):
        score += score_ref[s]
    ids = ids_ref[...]
    slots = slots_ref[...]
    tok = ids.shape[1]
    live = (ids % EXP_LOCAL == 0) & (slots >= 0)
    owner = ids // EXP_LOCAL
    lane = lax.broadcasted_iota(jnp.int32, (LANE, tok), 0)
    block = lax.broadcasted_iota(jnp.int32, (blocks, tok), 0)
    for k in range(TOPK):
        pick = (lane == slots[k : k + 1]).astype(f32)
        value = jnp.dot(score, pick, precision=lax.Precision.HIGHEST, preferred_element_type=f32)
        value = jnp.sum(jnp.where(block == owner[k : k + 1], value, 0.0), axis=0, keepdims=True)
        out_ref[k : k + 1] = jnp.where(
            live[k : k + 1], value / gates_ref[k : k + 1].astype(f32), 0.0
        )


def gate_scores(ids, slots, gates, score):
    return pl.pallas_call(
        score_kernel,
        out_shape=jax.ShapeDtypeStruct(ids.shape, f32),
        compiler_params=params(),
        cost_estimate=cost(1 << 24, 1 << 16),
    )(ids, slots, gates, score)


def exchange_order(blocks):
    half = blocks // 2
    order = [half]
    for k in range(1, half):
        order += [k, half + k]
    return order


def per_device(out_grad, expert_ids, slots, gate_weights, saved_gate_up, master, moment1, moment2):
    ep_size = lax.axis_size("ep")
    rep_size = lax.axis_size("rep")
    me = lax.axis_index("rep")
    ids_t, slots_t, gates_t = expert_ids.T, slots.T, gate_weights.T

    def shift(value, step):
        perm = [(i, (i + step) % rep_size) for i in range(rep_size)]
        return lax.ppermute(value, "rep", perm)

    sends = dispatch(ep_size, ids_t, slots_t, gates_t, out_grad)
    own = [sends[0]] + [None] * (ep_size - 1)
    for k in exchange_order(ep_size):
        own[k] = lax.ppermute(sends[k], "ep", [(i, i ^ k) for i in range(ep_size)])
    arrived = [own] + [[shift(block, s) for block in own] for s in range(1, rep_size)]

    hidden, coef_gate, coef_up = hidden_parts(saved_gate_up[0, 0], rep_size)
    parts = [
        lax.dynamic_index_in_dim(hidden, (me + s) % rep_size, 0, keepdims=False)
        for s in range(rep_size)
    ]
    parts = [parts[0]] + [shift(parts[s], s) for s in range(1, rep_size)]
    hidden_t = jnp.concatenate(parts, axis=0).T
    place = jnp.stack([(me + s) % rep_size for s in range(rep_size)]).astype(jnp.int32)
    weight = master[0].astype(bf16)

    outs = [project(arrived[s], weight, parts[s]) for s in range(rep_size)]
    rows, projs, halves, scores = zip(*outs)
    grads = [projs[0]] + [shift(halves[s], rep_size - s) for s in range(1, rep_size)]

    score = jnp.stack([scores[s] for s in range(rep_size)])
    order = jnp.stack([(me - i) % rep_size for i in range(rep_size)])
    score = jnp.take(score, order, axis=0).reshape(rep_size * ep_size, 1, LANE)
    score = lax.all_to_all(score, ("rep", "ep"), split_axis=0, concat_axis=0, tiled=True)

    done = adamw(hidden_t, rows, master, moment1, moment2)
    grad_gate_up = gate_up_grad(place, coef_gate, coef_up, grads)
    gate_grad = gate_scores(
        ids_t, slots_t, gates_t, score.reshape(rep_size, ep_size, LANE)
    ).T
    return (grad_gate_up.reshape(saved_gate_up.shape), gate_grad) + tuple(done)


def solution(mesh):
    in_specs = (
        P(("rep", "ep"), None),
        P(("rep", "ep"), None),
        P(("rep", "ep"), None),
        P(("rep", "ep"), None),
        P("rep", "ep", None, None),
        P("ep", "rep", None),
        P("ep", "rep", None),
        P("ep", "rep", None),
    )
    out_specs = (
        P("rep", "ep", None, None),
        P(("rep", "ep"), None),
        P("ep", "rep", None),
        P("ep", "rep", None),
        P("ep", "rep", None),
    )
    return jax.shard_map(
        per_device, mesh=mesh, in_specs=in_specs, out_specs=out_specs, check_vma=False
    )
```

time: 393 us -> 128 us (0.33)
  waiting for transfers between devices: 251 us -> 15.7 us
  local copies, waits for them, and re-layouts: 56.2 us -> 24.8 us
  Pallas kernels: 0 us -> 30 us
  starting transfers between devices: 19.4 us -> 48 us
  other arithmetic: 30.3 us -> 7.51 us
  matrix products: 16.8 us -> 0 us
  between operations: 14.3 us -> 0.84 us
    reduce_scatter x1 -> x0, waiting for transfers between devices: 93.9 us -> none  [per_device(): lax.psum_scatter(lax.dot_general(scaled, dout, (((0,), (0,)), ((), ())),...]
    all_gather x1 -> x0, waiting for transfers between devices: 92.3 us -> none  [per_device(): lax.all_gather(master[0].astype(jnp.bfloat16), 'rep', axis=0, tiled=True)]
    all_to_all x3 -> x1, waiting for transfers between devices: 64.9 us -> 0.01 us  [per_device(): lax.all_to_all(score, ('rep', 'ep'), split_axis=0, concat_axis=0, tiled=T...]
    ppermute x0 -> x33, starting transfers between devices: none -> 41.5 us  [the longest x18 21.4 us: shift(): return lax.ppermute(value, 'rep', perm)]
    pallas_call x0 -> x7, Pallas kernels: none -> 30 us  [the longest x1 15.8 us: adamw(): pl.pallas_call(adamw_kernel, grid=(width // UNIT,), in_specs=[pl.BlockSpe...]
    gather x9 -> x1, local copies, waits for them, and re-layouts: 24 us -> 0.55 us  [per_device(): score = jnp.take(score, order, axis=0).reshape(rep_size * ep_size, 1, LANE)]
    scatter x2 -> x0, local copies, waits for them, and re-layouts: 22.6 us -> none  [the longest x1 14.6 us: per_device(): jnp.zeros((filled + 1,), gate_weights.dtype).at[flat_pos]]
    unnamed x9 -> x62, local copies, waits for them, and re-layouts: 0.82 us -> 22 us
  transfers between devices with their start and end apart: 5 -> 34, of which waited for: 4 -> 6; matrix products, arithmetic and copies ran while one was open for 5% -> 7% of each run, Pallas kernels for 0% -> 17%
where the time goes in v1:
time: 128 us; the launch traced here: 127 us
  starting transfers between devices  48 us (38%)
  Pallas kernels  30 us (23%)
  local copies, waits for them, and re-layouts  24.8 us (19%)
  waiting for transfers between devices  15.7 us (12%)
  other arithmetic  7.51 us (6%)
    unnamed x62, local copies, waits for them, and re-layouts  22 us
    ppermute x18, starting transfers between devices, shift(): return lax.ppermute(value, 'rep', perm)  21.4 us
    ppermute x15, starting transfers between devices, per_device(): own[k] = lax.ppermute(sends[k], 'ep', [(i, i ^ k) for i in range(ep_size)])  20.2 us
    pallas_call x1, Pallas kernels, adamw(): pl.pallas_call(adamw_kernel, grid=(width // UNIT,), in_specs=[pl.BlockSpe...  15.8 us
    ppermute x15, waiting for transfers between devices, per_device(): own[k] = lax.ppermute(sends[k], 'ep', [(i, i ^ k) for i in range(ep_size)])  9.8 us
    pallas_call x2, Pallas kernels, project(): pl.pallas_call(functools.partial(project_kernel, blocks), out_shape=[jax....  9.49 us
    all_to_all x1, starting transfers between devices, per_device(): lax.all_to_all(score, ('rep', 'ep'), split_axis=0, concat_axis=0, tiled=T...  6.46 us
    ppermute x18, waiting for transfers between devices, shift(): return lax.ppermute(value, 'rep', perm)  5.94 us
  transfers between devices with their start and end apart: 34, of which 6 were waited for; matrix products, arithmetic and copies ran while one was open for 7% of the time, Pallas kernels for 17%

profile of v1, /device:TPU:0, one launch (start us, length us, event | category | flops | bytes accessed | tf_op | source)
XLA Modules:
  0.0 126.9 jit_solution(3374824674034707983)
XLA Ops:
  0.6 1.5 %copy-done = bf16[256,3584]{1,0:T(8,128)(2,1)S(1)} copy-done((bf16[256,3584]{1,0:T(8,128)(2,1)S(1)}, bf16[256,3584]{1,0:T(8,128)(2,1)}, u32[]{:S(2)}) %copy-start) | copy-done | bytes 1835032
  4.2 1.4 %shard_map.120 = (bf16[16,2688]{1,0:T(8,128)(2,1)S(1)}, bf16[16,2688]{1,0:T(8,128)(2,1)S(1)}, bf16[16,2688]{1,0:T(8,128)(2,1)S(1)}, bf16[16,2688]{1,0:T(8,128)(2...) custom-call(s32[8,256]{1,0:T(8,128)S(1)} %bitcast.29, ...), custom_call_target="tpu_custom_call" | custom-call | flops 469762048 | bytes 3670016 | tf_op jit(solution)/shard_map/pallas_call | solution.py:76
  6.1 2.6 %collective-permute-start.1 = (bf16[16,2688]{1,0:T(8,128)(2,1)S(1)}, bf16[16,2688]{1,0:T(8,128)(2,1)S(1)}, u32[]{:S(2)}, u32[]{:S(2)}) collective-permute-start(bf16[16,2688]{1,0:T(8,128)(2,1)S(1)} %get-tuple-element.37), channel_id=1, source_target_pairs={{0,2},{1,3},{2,0},{3,1},{4,6},{5,7},{6,4},{7,5},{8,10},{9,11},{10,... | collective-permute-start | bytes 258056 | tf_op jit(solution)/shard_map/ppermute | solution.py:291
  8.8 1.8 %collective-permute-start.3 = (bf16[16,2688]{1,0:T(8,128)(2,1)S(1)}, bf16[16,2688]{1,0:T(8,128)(2,1)S(1)}, u32[]{:S(2)}, u32[]{:S(2)}) collective-permute-start(bf16[16,2688]{1,0:T(8,128)(2,1)S(1)} %get-tuple-element.39), channel_id=1, source_target_pairs={{0,4},{1,5},{2,6},{3,7},{4,0},{5,1},{6,2},{7,3},{8,12},{9,13},{10,... | collective-permute-start | bytes 258056 | tf_op jit(solution)/shard_map/ppermute | solution.py:291
  10.6 5.4 %convert_bitcast_fusion.refs_16_ = bf16[512,3584]{1,0:T(8,128)(2,1)} fusion(f32[1,512,3584]{2,1,0:T(8,128)} %refs_2_.1), kind=kLoop, calls=%fused_computation.1 | loop fusion | flops 1835008 | bytes 11010048 | tf_op jit(solution)/shard_map/convert_element_type | solution.py:302
  16.0 2.5 %collective-permute-start.5 = (bf16[16,2688]{1,0:T(8,128)(2,1)S(1)}, bf16[16,2688]{1,0:T(8,128)(2,1)S(1)}, u32[]{:S(2)}, u32[]{:S(2)}) collective-permute-start(bf16[16,2688]{1,0:T(8,128)(2,1)S(1)} %get-tuple-element.41), channel_id=1, source_target_pairs={{0,6},{1,7},{2,4},{3,5},{4,2},{5,3},{6,0},{7,1},{8,14},{9,15},{10,... | collective-permute-start | bytes 258056 | tf_op jit(solution)/shard_map/ppermute | solution.py:291
  18.7 2.7 %collective-permute-start.7 = (bf16[16,2688]{1,0:T(8,128)(2,1)S(1)}, bf16[16,2688]{1,0:T(8,128)(2,1)S(1)}, u32[]{:S(2)}, u32[]{:S(2)}) collective-permute-start(bf16[16,2688]{1,0:T(8,128)(2,1)S(1)} %get-tuple-element.43), channel_id=1, source_target_pairs={{0,8},{1,9},{2,10},{3,11},{4,12},{5,13},{6,14},{7,15},{8,0},{9,1},... | collective-permute-start | bytes 258056 | tf_op jit(solution)/shard_map/ppermute | solution.py:291
  22.9 0.9 copy-done.4
  23.8 3.6 %collective-permute-start.9 = (bf16[16,2688]{1,0:T(8,128)(2,1)S(1)}, bf16[16,2688]{1,0:T(8,128)(2,1)S(1)}, u32[]{:S(2)}, u32[]{:S(2)}) collective-permute-start(bf16[16,2688]{1,0:T(8,128)(2,1)S(1)} %get-tuple-element.45), channel_id=1, source_target_pairs={{0,10},{1,11},{2,8},{3,9},{4,14},{5,15},{6,12},{7,13},{8,2},{9,3},... | collective-permute-start | bytes 258056 | tf_op jit(solution)/shard_map/ppermute | solution.py:291
  27.5 3.5 %collective-permute-start.11 = (bf16[16,2688]{1,0:T(8,128)(2,1)S(1)}, bf16[16,2688]{1,0:T(8,128)(2,1)S(1)}, u32[]{:S(2)}, u32[]{:S(2)}) collective-permute-start(bf16[16,2688]{1,0:T(8,128)(2,1)S(1)} %get-tuple-element.47), channel_id=1, source_target_pairs={{0,12},{1,13},{2,14},{3,15},{4,8},{5,9},{6,10},{7,11},{8,4},{9,5},... | collective-permute-start | bytes 258056 | tf_op jit(solution)/shard_map/ppermute | solution.py:291
  32.1 6.3 %collective-permute-done.8.refs_9_ = bf16[16,2688]{1,0:T(8,128)(2,1)S(1)} collective-permute-done((bf16[16,2688]{1,0:T(8,128)(2,1)S(1)}, bf16[16,2688]{1,0:T(8,128)(2,1)S(1)}, u32[]{:S(2)}, u32[]{:S(2)}) %collective-permute-start.8) | collective-permute-done | bytes 86048 | tf_op jit(solution)/shard_map/ppermute | solution.py:291
  38.4 1.5 %collective-permute-start.13 = (bf16[16,2688]{1,0:T(8,128)(2,1)S(1)}, bf16[16,2688]{1,0:T(8,128)(2,1)S(1)}, u32[]{:S(2)}, u32[]{:S(2)}) collective-permute-start(bf16[16,2688]{1,0:T(8,128)(2,1)S(1)} %get-tuple-element.49), channel_id=1, source_target_pairs={{0,14},{1,15},{2,12},{3,13},{4,10},{5,11},{6,8},{7,9},{8,6},{9,7},... | collective-permute-start | bytes 258056 | tf_op jit(solution)/shard_map/ppermute | solution.py:291
  39.9 1.9 %collective-permute-done.9.refs_10_ = bf16[16,2688]{1,0:T(8,128)(2,1)S(1)} collective-permute-done((bf16[16,2688]{1,0:T(8,128)(2,1)S(1)}, bf16[16,2688]{1,0:T(8,128)(2,1)S(1)}, u32[]{:S(2)}, u32[]{:S(2)}) %collective-permute-start.9) | collective-permute-done | bytes 86048 | tf_op jit(solution)/shard_map/ppermute | solution.py:291
  41.9 1.1 collective-permute-start.14
  43.0 1.5 %collective-permute-start.15 = (bf16[16,2688]{1,0:T(8,128)(2,1)S(1)}, bf16[16,2688]{1,0:T(8,128)(2,1)S(1)}, u32[]{:S(2)}, u32[]{:S(2)}) collective-permute-start(bf16[16,2688]{1,0:T(8,128)(2,1)S(1)} %get-tuple-element.35.refs_0_), channel_id=1, source_target_pairs={{0,16},{16,0},{1,17},{17,1},{2,18},{18,2},{3,19},{19,3},{4,20},{20... | collective-permute-start | bytes 258056 | tf_op jit(solution)/shard_map/ppermute | solution.py:286
  45.1 1.5 %collective-permute-start.17 = (bf16[16,2688]{1,0:T(8,128)(2,1)S(1)}, bf16[16,2688]{1,0:T(8,128)(2,1)S(1)}, u32[]{:S(2)}, u32[]{:S(2)}) collective-permute-start(bf16[16,2688]{1,0:T(8,128)(2,1)S(1)} %collective-permute-done.1.refs_2_), channel_id=1, source_target_pairs={{0,16},{16,0},{1,17},{17,1},{2,18},{18,2},{3,19},{19,3},{4,20},{20... | collective-permute-start | bytes 258056 | tf_op jit(solution)/shard_map/ppermute | solution.py:286
  46.7 1.0 collective-permute-start.31
  47.7 1.4 %collective-permute-done.14.refs_15_ = bf16[16,2688]{1,0:T(8,128)(2,1)S(1)} collective-permute-done((bf16[16,2688]{1,0:T(8,128)(2,1)S(1)}, bf16[16,2688]{1,0:T(8,128)(2,1)S(1)}, u32[]{:S(2)}, u32[]{:S(2)}) %collective-permute-start.14) | collective-permute-done | bytes 86048 | tf_op jit(solution)/shard_map/ppermute | solution.py:291
  49.1 1.5 %collective-permute-start.18 = (bf16[16,2688]{1,0:T(8,128)(2,1)S(1)}, bf16[16,2688]{1,0:T(8,128)(2,1)S(1)}, u32[]{:S(2)}, u32[]{:S(2)}) collective-permute-start(bf16[16,2688]{1,0:T(8,128)(2,1)S(1)} %collective-permute-done.2.refs_3_), channel_id=1, source_target_pairs={{0,16},{16,0},{1,17},{17,1},{2,18},{18,2},{3,19},{19,3},{4,20},{20... | collective-permute-start | bytes 258056 | tf_op jit(solution)/shard_map/ppermute | solution.py:286
  51.1 1.5 %collective-permute-start.20 = (bf16[16,2688]{1,0:T(8,128)(2,1)S(1)}, bf16[16,2688]{1,0:T(8,128)(2,1)S(1)}, u32[]{:S(2)}, u32[]{:S(2)}) collective-permute-start(bf16[16,2688]{1,0:T(8,128)(2,1)S(1)} %collective-permute-done.4.refs_5_), channel_id=1, source_target_pairs={{0,16},{16,0},{1,17},{17,1},{2,18},{18,2},{3,19},{19,3},{4,20},{20... | collective-permute-start | bytes 258056 | tf_op jit(solution)/shard_map/ppermute | solution.py:286
  54.0 5.3 %collective-permute-done.18.refs_3_ = bf16[16,2688]{1,0:T(8,128)(2,1)S(1)} collective-permute-done((bf16[16,2688]{1,0:T(8,128)(2,1)S(1)}, bf16[16,2688]{1,0:T(8,128)(2,1)S(1)}, u32[]{:S(2)}, u32[]{:S(2)}) %collective-permute-start.18) | collective-permute-done | bytes 86048 | tf_op jit(solution)/shard_map/ppermute | solution.py:286
  59.9 1.5 %collective-permute-start.22 = (bf16[16,2688]{1,0:T(8,128)(2,1)S(1)}, bf16[16,2688]{1,0:T(8,128)(2,1)S(1)}, u32[]{:S(2)}, u32[]{:S(2)}) collective-permute-start(bf16[16,2688]{1,0:T(8,128)(2,1)S(1)} %collective-permute-done.6.refs_7_), channel_id=1, source_target_pairs={{0,16},{16,0},{1,17},{17,1},{2,18},{18,2},{3,19},{19,3},{4,20},{20... | collective-permute-start | bytes 258056 | tf_op jit(solution)/shard_map/ppermute | solution.py:286
  62.1 1.2 collective-permute-start.23
  64.0 1.2 collective-permute-start.24
  65.8 1.2 collective-permute-start.25
  67.7 1.1 collective-permute-start.26
  69.5 1.2 collective-permute-start.27
  71.3 1.2 collective-permute-start.28
  73.2 1.2 collective-permute-start.29
  75.2 4.6 %shard_map.121 = (bf16[192,3584]{1,0:T(8,128)(2,1)S(1)}, f32[192,512]{1,0:T(8,128)S(1)}, bf16[192,512]{1,0:T(8,128)(2,1)}, f32[16,128]{1,0:T(8,128)S(1)}) custom-call(bf16[16,2688]{1,0:T(8,128)(2,1)S(1)} %get-tuple-element.35.refs_0_, bf16[16,2688]{1,0:T(8,128)(2,1)S(1)} %collective-permute-done.refs_1_, ...), custom_call_target="tpu_custom_call" | custom-call | flops 1409286144 | bytes 6422528 | tf_op jit(solution)/shard_map/pallas_call | solution.py:158
  79.8 1.1 copy.20.refs_17_
  81.5 0.9 copy-done.7
  82.4 0.9 copy-done.9
  83.3 0.9 copy-done.11
  84.2 0.9 copy-done.13
  85.1 0.9 copy-done.15
  86.0 0.9 copy-done.17
  86.9 0.9 copy-done.19
  88.7 0.9 copy-done.23
  89.5 4.9 %shard_map.122 = (bf16[192,3584]{1,0:T(8,128)(2,1)S(1)}, f32[192,512]{1,0:T(8,128)}, bf16[192,512]{1,0:T(8,128)(2,1)S(1)}, f32[16,128]{1,0:T(8,128)S(1)}) custom-call(bf16[16,2688]{1,0:T(8,128)(2,1)S(1)} %collective-permute-done.15.refs_0_, bf16[16,2688]{1,0:T(8,128)(2,1)S(1)} %collective-permute-done.16.refs_1_, bf16[16,2688]{1,0:T(8,128)(2,1)S(1)} %copy-done.7, ...), custom_call_target="tpu_custom_call" | custom-call | flops 1409286144 | bytes 6422528 | tf_op jit(solution)/shard_map/pallas_call | solution.py:158
  96.4 6.5 %all-to-all-start = ((f32[32,1,128]{2,1,0:T(1,128)}), f32[32,1,128]{2,1,0:T(1,128)S(1)}, u32[]{:S(2)}, u32[]{:S(2)}) async-start(f32[32,1,128]{2,1,0:T(1,128)} %broadcast_select_fusion), calls=%async_computation | async-start | bytes 32768 | tf_op jit(solution)/shard_map/all_to_all | solution.py:311
  102.8 1.8 %collective-permute-start.32 = (bf16[192,512]{1,0:T(8,128)(2,1)}, bf16[192,512]{1,0:T(8,128)(2,1)S(1)}, u32[]{:S(2)}, u32[]{:S(2)}) collective-permute-start(bf16[192,512]{1,0:T(8,128)(2,1)} %copy-done.30), channel_id=1, source_target_pairs={{0,16},{16,0},{1,17},{17,1},{2,18},{18,2},{3,19},{19,3},{4,20},{20... | collective-permute-start | bytes 589832 | tf_op jit(solution)/shard_map/ppermute | solution.py:286
  104.7 1.2 maximum_bitcast_fusion.hidden_ref
  105.9 15.8 %shard_map.125 = (f32[1,512,3584]{2,1,0:T(8,128)}, bf16[1,512,3584]{2,1,0:T(8,128)(2,1)}, bf16[1,512,3584]{2,1,0:T(8,128)(2,1)}) custom-call(bf16[512,384]{1,0:T(8,128)(2,1)S(1)} %maximum_bitcast_fusion.hidden_ref, bf16[192,3584]{1,0:T(8,128)(2,1)S(1)} %get-tuple-element.56.refs_0_, bf16[192,3584]{1,0:T(8,128)(2,1)S(1)} %get-tuple-element.57.refs_1_, ...), custom_call_target="tpu_custom_call" | custom-call | flops 1409286144 | bytes 29360128 | tf_op jit(solution)/shard_map/pallas_call | solution.py:198
  121.7 1.3 %shard_map.124 = f32[8,256]{1,0:T(8,128)} custom-call(s32[8,256]{1,0:T(8,128)S(1)} %bitcast.30, s32[8,256]{1,0:T(8,128)S(1)} %bitcast.32, bf16[8,256]{1,0:T(8,128)(2,1)S(1)} %bitcast.36, f32[2,16,128]{2,1,0:T(8,128)S(1)} %bitcast.28), custom_call_target="tpu_custom_call" | custom-call | flops 16777216 | bytes 65536 | tf_op jit(solution)/shard_map/pallas_call | solution.py:262
  123.1 1.1 copy-done.3
  124.2 1.1 copy-done.5
  125.3 1.6 %shard_map.123 = bf16[192,2048]{1,0:T(8,128)(2,1)} custom-call(s32[2]{0:T(128)S(1)} %pad_add_fusion.place_ref, f32[2,192,512]{2,1,0:T(8,128)S(1)} %copy-done.3, f32[2,192,512]{2,1,0:T(8,128)S(1)} %copy-done.5, f32[192,512]{1,0:T(8,128)S(1)} %get-tuple-element.52.refs_0_, bf16[192,512]{1,0:T(8,128)(2,1)S(1)} %collective-permute-done.32.refs_1_), custom_call_target="tpu_custom_call" | custom-call | flops 786432 | bytes 3145728 | tf_op jit(solution)/shard_map/pallas_call | solution.py:230
  (104 shorter events, 17.4 us)
Async XLA Ops:
  0.6 1.5 %copy-start = (bf16[256,3584]{1,0:T(8,128)(2,1)S(1)}, bf16[256,3584]{1,0:T(8,128)(2,1)}, u32[]{:S(2)}) copy-start(bf16[256,3584]{1,0:T(8,128)(2,1)} %grad_ref.1) | copy-start | bytes 5505028
  5.6 10.4 %collective-permute-start = (bf16[16,2688]{1,0:T(8,128)(2,1)S(1)}, bf16[16,2688]{1,0:T(8,128)(2,1)S(1)}, u32[]{:S(2)}, u32[]{:S(2)}) collective-permute-start(bf16[16,2688]{1,0:T(8,128)(2,1)S(1)} %get-tuple-element.36), channel_id=1, source_target_pairs={{0,1},{1,0},{2,3},{3,2},{4,5},{5,4},{6,7},{7,6},{8,9},{9,8},{10,11... | collective-permute-start | bytes 258056 | tf_op jit(solution)/shard_map/ppermute | solution.py:291
  6.1 12.4 %collective-permute-start.1 = (bf16[16,2688]{1,0:T(8,128)(2,1)S(1)}, bf16[16,2688]{1,0:T(8,128)(2,1)S(1)}, u32[]{:S(2)}, u32[]{:S(2)}) collective-permute-start(bf16[16,2688]{1,0:T(8,128)(2,1)S(1)} %get-tuple-element.37), channel_id=1, source_target_pairs={{0,2},{1,3},{2,0},{3,1},{4,6},{5,7},{6,4},{7,5},{8,10},{9,11},{10,... | collective-permute-start | bytes 258056 | tf_op jit(solution)/shard_map/ppermute | solution.py:291
  8.7 10.0 %collective-permute-start.2 = (bf16[16,2688]{1,0:T(8,128)(2,1)S(1)}, bf16[16,2688]{1,0:T(8,128)(2,1)S(1)}, u32[]{:S(2)}, u32[]{:S(2)}) collective-permute-start(bf16[16,2688]{1,0:T(8,128)(2,1)S(1)} %get-tuple-element.38), channel_id=1, source_target_pairs={{0,3},{1,2},{2,1},{3,0},{4,7},{5,6},{6,5},{7,4},{8,11},{9,10},{10,... | collective-permute-start | bytes 258056 | tf_op jit(solution)/shard_map/ppermute | solution.py:291
  8.8 15.0 %collective-permute-start.3 = (bf16[16,2688]{1,0:T(8,128)(2,1)S(1)}, bf16[16,2688]{1,0:T(8,128)(2,1)S(1)}, u32[]{:S(2)}, u32[]{:S(2)}) collective-permute-start(bf16[16,2688]{1,0:T(8,128)(2,1)S(1)} %get-tuple-element.39), channel_id=1, source_target_pairs={{0,4},{1,5},{2,6},{3,7},{4,0},{5,1},{6,2},{7,3},{8,12},{9,13},{10,... | collective-permute-start | bytes 258056 | tf_op jit(solution)/shard_map/ppermute | solution.py:291
  10.6 11.0 %copy-start.1 = (bf16[1,1,192,2048]{3,2,1,0:T(8,128)(2,1)S(1)}, bf16[1,1,192,2048]{3,2,1,0:T(8,128)(2,1)}, u32[]{:S(2)}) copy-start(bf16[1,1,192,2048]{3,2,1,0:T(8,128)(2,1)} %param.12) | copy-start | bytes 2359300
  10.6 13.2 %collective-permute-start.4 = (bf16[16,2688]{1,0:T(8,128)(2,1)S(1)}, bf16[16,2688]{1,0:T(8,128)(2,1)S(1)}, u32[]{:S(2)}, u32[]{:S(2)}) collective-permute-start(bf16[16,2688]{1,0:T(8,128)(2,1)S(1)} %get-tuple-element.40), channel_id=1, source_target_pairs={{0,5},{1,4},{2,7},{3,6},{4,1},{5,0},{6,3},{7,2},{8,13},{9,12},{10,... | collective-permute-start | bytes 258056 | tf_op jit(solution)/shard_map/ppermute | solution.py:291
  16.0 11.4 %collective-permute-start.5 = (bf16[16,2688]{1,0:T(8,128)(2,1)S(1)}, bf16[16,2688]{1,0:T(8,128)(2,1)S(1)}, u32[]{:S(2)}, u32[]{:S(2)}) collective-permute-start(bf16[16,2688]{1,0:T(8,128)(2,1)S(1)} %get-tuple-element.41), channel_id=1, source_target_pairs={{0,6},{1,7},{2,4},{3,5},{4,2},{5,3},{6,0},{7,1},{8,14},{9,15},{10,... | collective-permute-start | bytes 258056 | tf_op jit(solution)/shard_map/ppermute | solution.py:291
  18.5 8.9 %collective-permute-start.6 = (bf16[16,2688]{1,0:T(8,128)(2,1)S(1)}, bf16[16,2688]{1,0:T(8,128)(2,1)S(1)}, u32[]{:S(2)}, u32[]{:S(2)}) collective-permute-start(bf16[16,2688]{1,0:T(8,128)(2,1)S(1)} %get-tuple-element.42), channel_id=1, source_target_pairs={{0,7},{1,6},{2,5},{3,4},{4,3},{5,2},{6,1},{7,0},{8,15},{9,14},{10,... | collective-permute-start | bytes 258056 | tf_op jit(solution)/shard_map/ppermute | solution.py:291
  18.7 12.3 %collective-permute-start.7 = (bf16[16,2688]{1,0:T(8,128)(2,1)S(1)}, bf16[16,2688]{1,0:T(8,128)(2,1)S(1)}, u32[]{:S(2)}, u32[]{:S(2)}) collective-permute-start(bf16[16,2688]{1,0:T(8,128)(2,1)S(1)} %get-tuple-element.43), channel_id=1, source_target_pairs={{0,8},{1,9},{2,10},{3,11},{4,12},{5,13},{6,14},{7,15},{8,0},{9,1},... | collective-permute-start | bytes 258056 | tf_op jit(solution)/shard_map/ppermute | solution.py:291
  22.9 0.9 copy-start.4
  23.8 14.6 %collective-permute-start.8 = (bf16[16,2688]{1,0:T(8,128)(2,1)S(1)}, bf16[16,2688]{1,0:T(8,128)(2,1)S(1)}, u32[]{:S(2)}, u32[]{:S(2)}) collective-permute-start(bf16[16,2688]{1,0:T(8,128)(2,1)S(1)} %get-tuple-element.44), channel_id=1, source_target_pairs={{0,9},{1,8},{2,11},{3,10},{4,13},{5,12},{6,15},{7,14},{8,1},{9,0},... | collective-permute-start | bytes 258056 | tf_op jit(solution)/shard_map/ppermute | solution.py:291
  23.8 18.0 %collective-permute-start.9 = (bf16[16,2688]{1,0:T(8,128)(2,1)S(1)}, bf16[16,2688]{1,0:T(8,128)(2,1)S(1)}, u32[]{:S(2)}, u32[]{:S(2)}) collective-permute-start(bf16[16,2688]{1,0:T(8,128)(2,1)S(1)} %get-tuple-element.45), channel_id=1, source_target_pairs={{0,10},{1,11},{2,8},{3,9},{4,14},{5,15},{6,12},{7,13},{8,2},{9,3},... | collective-permute-start | bytes 258056 | tf_op jit(solution)/shard_map/ppermute | solution.py:291
  27.4 15.6 %collective-permute-start.10 = (bf16[16,2688]{1,0:T(8,128)(2,1)S(1)}, bf16[16,2688]{1,0:T(8,128)(2,1)S(1)}, u32[]{:S(2)}, u32[]{:S(2)}) collective-permute-start(bf16[16,2688]{1,0:T(8,128)(2,1)S(1)} %get-tuple-element.46), channel_id=1, source_target_pairs={{0,11},{1,10},{2,9},{3,8},{4,15},{5,14},{6,13},{7,12},{8,3},{9,2},... | collective-permute-start | bytes 258056 | tf_op jit(solution)/shard_map/ppermute | solution.py:291
  27.5 17.1 %collective-permute-start.11 = (bf16[16,2688]{1,0:T(8,128)(2,1)S(1)}, bf16[16,2688]{1,0:T(8,128)(2,1)S(1)}, u32[]{:S(2)}, u32[]{:S(2)}) collective-permute-start(bf16[16,2688]{1,0:T(8,128)(2,1)S(1)} %get-tuple-element.47), channel_id=1, source_target_pairs={{0,12},{1,13},{2,14},{3,15},{4,8},{5,9},{6,10},{7,11},{8,4},{9,5},... | collective-permute-start | bytes 258056 | tf_op jit(solution)/shard_map/ppermute | solution.py:291
  31.0 14.0 %collective-permute-start.12 = (bf16[16,2688]{1,0:T(8,128)(2,1)S(1)}, bf16[16,2688]{1,0:T(8,128)(2,1)S(1)}, u32[]{:S(2)}, u32[]{:S(2)}) collective-permute-start(bf16[16,2688]{1,0:T(8,128)(2,1)S(1)} %get-tuple-element.48), channel_id=1, source_target_pairs={{0,13},{1,12},{2,15},{3,14},{4,9},{5,8},{6,11},{7,10},{8,5},{9,4},... | collective-permute-start | bytes 258056 | tf_op jit(solution)/shard_map/ppermute | solution.py:291
  38.4 8.3 %collective-permute-start.13 = (bf16[16,2688]{1,0:T(8,128)(2,1)S(1)}, bf16[16,2688]{1,0:T(8,128)(2,1)S(1)}, u32[]{:S(2)}, u32[]{:S(2)}) collective-permute-start(bf16[16,2688]{1,0:T(8,128)(2,1)S(1)} %get-tuple-element.49), channel_id=1, source_target_pairs={{0,14},{1,15},{2,12},{3,13},{4,10},{5,11},{6,8},{7,9},{8,6},{9,7},... | collective-permute-start | bytes 258056 | tf_op jit(solution)/shard_map/ppermute | solution.py:291
  41.9 7.2 %collective-permute-start.14 = (bf16[16,2688]{1,0:T(8,128)(2,1)S(1)}, bf16[16,2688]{1,0:T(8,128)(2,1)S(1)}, u32[]{:S(2)}, u32[]{:S(2)}) collective-permute-start(bf16[16,2688]{1,0:T(8,128)(2,1)S(1)} %get-tuple-element.50), channel_id=1, source_target_pairs={{0,15},{1,14},{2,13},{3,12},{4,11},{5,10},{6,9},{7,8},{8,7},{9,6},... | collective-permute-start | bytes 258056 | tf_op jit(solution)/shard_map/ppermute | solution.py:291
  43.0 7.6 %collective-permute-start.15 = (bf16[16,2688]{1,0:T(8,128)(2,1)S(1)}, bf16[16,2688]{1,0:T(8,128)(2,1)S(1)}, u32[]{:S(2)}, u32[]{:S(2)}) collective-permute-start(bf16[16,2688]{1,0:T(8,128)(2,1)S(1)} %get-tuple-element.35.refs_0_), channel_id=1, source_target_pairs={{0,16},{16,0},{1,17},{17,1},{2,18},{18,2},{3,19},{19,3},{4,20},{20... | collective-permute-start | bytes 258056 | tf_op jit(solution)/shard_map/ppermute | solution.py:286
  44.5 6.6 %collective-permute-start.16 = (bf16[16,2688]{1,0:T(8,128)(2,1)S(1)}, bf16[16,2688]{1,0:T(8,128)(2,1)S(1)}, u32[]{:S(2)}, u32[]{:S(2)}) collective-permute-start(bf16[16,2688]{1,0:T(8,128)(2,1)S(1)} %collective-permute-done.refs_1_), channel_id=1, source_target_pairs={{0,16},{16,0},{1,17},{17,1},{2,18},{18,2},{3,19},{19,3},{4,20},{20... | collective-permute-start | bytes 258056 | tf_op jit(solution)/shard_map/ppermute | solution.py:286
  45.1 7.6 %collective-permute-start.17 = (bf16[16,2688]{1,0:T(8,128)(2,1)S(1)}, bf16[16,2688]{1,0:T(8,128)(2,1)S(1)}, u32[]{:S(2)}, u32[]{:S(2)}) collective-permute-start(bf16[16,2688]{1,0:T(8,128)(2,1)S(1)} %collective-permute-done.1.refs_2_), channel_id=1, source_target_pairs={{0,16},{16,0},{1,17},{17,1},{2,18},{18,2},{3,19},{19,3},{4,20},{20... | collective-permute-start | bytes 258056 | tf_op jit(solution)/shard_map/ppermute | solution.py:286
  46.7 27.7 %collective-permute-start.31 = (bf16[192,512]{0,1:T(8,128)(2,1)S(1)}, bf16[192,512]{0,1:T(8,128)(2,1)}, u32[]{:S(2)}, u32[]{:S(2)}) collective-permute-start(bf16[192,512]{0,1:T(8,128)(2,1)S(1)} %bitcast.39), channel_id=1, source_target_pairs={{0,16},{16,0},{1,17},{17,1},{2,18},{18,2},{3,19},{19,3},{4,20},{20... | collective-permute-start | bytes 589832 | tf_op jit(solution)/shard_map/ppermute | solution.py:286
  49.1 10.2 %collective-permute-start.18 = (bf16[16,2688]{1,0:T(8,128)(2,1)S(1)}, bf16[16,2688]{1,0:T(8,128)(2,1)S(1)}, u32[]{:S(2)}, u32[]{:S(2)}) collective-permute-start(bf16[16,2688]{1,0:T(8,128)(2,1)S(1)} %collective-permute-done.2.refs_3_), channel_id=1, source_target_pairs={{0,16},{16,0},{1,17},{17,1},{2,18},{18,2},{3,19},{19,3},{4,20},{20... | collective-permute-start | bytes 258056 | tf_op jit(solution)/shard_map/ppermute | solution.py:286
  50.6 10.8 %collective-permute-start.19 = (bf16[16,2688]{1,0:T(8,128)(2,1)S(1)}, bf16[16,2688]{1,0:T(8,128)(2,1)S(1)}, u32[]{:S(2)}, u32[]{:S(2)}) collective-permute-start(bf16[16,2688]{1,0:T(8,128)(2,1)S(1)} %collective-permute-done.3.refs_4_), channel_id=1, source_target_pairs={{0,16},{16,0},{1,17},{17,1},{2,18},{18,2},{3,19},{19,3},{4,20},{20... | collective-permute-start | bytes 258056 | tf_op jit(solution)/shard_map/ppermute | solution.py:286
  51.1 12.2 %collective-permute-start.20 = (bf16[16,2688]{1,0:T(8,128)(2,1)S(1)}, bf16[16,2688]{1,0:T(8,128)(2,1)S(1)}, u32[]{:S(2)}, u32[]{:S(2)}) collective-permute-start(bf16[16,2688]{1,0:T(8,128)(2,1)S(1)} %collective-permute-done.4.refs_5_), channel_id=1, source_target_pairs={{0,16},{16,0},{1,17},{17,1},{2,18},{18,2},{3,19},{19,3},{4,20},{20... | collective-permute-start | bytes 258056 | tf_op jit(solution)/shard_map/ppermute | solution.py:286
  53.3 11.8 %collective-permute-start.21 = (bf16[16,2688]{1,0:T(8,128)(2,1)S(1)}, bf16[16,2688]{1,0:T(8,128)(2,1)S(1)}, u32[]{:S(2)}, u32[]{:S(2)}) collective-permute-start(bf16[16,2688]{1,0:T(8,128)(2,1)S(1)} %collective-permute-done.5.refs_6_), channel_id=1, source_target_pairs={{0,16},{16,0},{1,17},{17,1},{2,18},{18,2},{3,19},{19,3},{4,20},{20... | collective-permute-start | bytes 258056 | tf_op jit(solution)/shard_map/ppermute | solution.py:286
  59.9 7.1 %collective-permute-start.22 = (bf16[16,2688]{1,0:T(8,128)(2,1)S(1)}, bf16[16,2688]{1,0:T(8,128)(2,1)S(1)}, u32[]{:S(2)}, u32[]{:S(2)}) collective-permute-start(bf16[16,2688]{1,0:T(8,128)(2,1)S(1)} %collective-permute-done.6.refs_7_), channel_id=1, source_target_pairs={{0,16},{16,0},{1,17},{17,1},{2,18},{18,2},{3,19},{19,3},{4,20},{20... | collective-permute-start | bytes 258056 | tf_op jit(solution)/shard_map/ppermute | solution.py:286
  62.1 6.7 %collective-permute-start.23 = (bf16[16,2688]{1,0:T(8,128)(2,1)S(1)}, bf16[16,2688]{1,0:T(8,128)(2,1)S(1)}, u32[]{:S(2)}, u32[]{:S(2)}) collective-permute-start(bf16[16,2688]{1,0:T(8,128)(2,1)S(1)} %collective-permute-done.7.refs_8_), channel_id=1, source_target_pairs={{0,16},{16,0},{1,17},{17,1},{2,18},{18,2},{3,19},{19,3},{4,20},{20... | collective-permute-start | bytes 258056 | tf_op jit(solution)/shard_map/ppermute | solution.py:286
  64.0 6.7 %collective-permute-start.24 = (bf16[16,2688]{1,0:T(8,128)(2,1)S(1)}, bf16[16,2688]{1,0:T(8,128)(2,1)S(1)}, u32[]{:S(2)}, u32[]{:S(2)}) collective-permute-start(bf16[16,2688]{1,0:T(8,128)(2,1)S(1)} %collective-permute-done.8.refs_9_), channel_id=1, source_target_pairs={{0,16},{16,0},{1,17},{17,1},{2,18},{18,2},{3,19},{19,3},{4,20},{20... | collective-permute-start | bytes 258056 | tf_op jit(solution)/shard_map/ppermute | solution.py:286
  65.8 6.8 %collective-permute-start.25 = (bf16[16,2688]{1,0:T(8,128)(2,1)S(1)}, bf16[16,2688]{1,0:T(8,128)(2,1)S(1)}, u32[]{:S(2)}, u32[]{:S(2)}) collective-permute-start(bf16[16,2688]{1,0:T(8,128)(2,1)S(1)} %collective-permute-done.9.refs_10_), channel_id=1, source_target_pairs={{0,16},{16,0},{1,17},{17,1},{2,18},{18,2},{3,19},{19,3},{4,20},{20... | collective-permute-start | bytes 258056 | tf_op jit(solution)/shard_map/ppermute | solution.py:286
  67.7 13.2 %collective-permute-start.26 = (bf16[16,2688]{1,0:T(8,128)(2,1)S(1)}, bf16[16,2688]{1,0:T(8,128)(2,1)}, u32[]{:S(2)}, u32[]{:S(2)}) collective-permute-start(bf16[16,2688]{1,0:T(8,128)(2,1)S(1)} %collective-permute-done.10.refs_11_), channel_id=1, source_target_pairs={{0,16},{16,0},{1,17},{17,1},{2,18},{18,2},{3,19},{19,3},{4,20},{20... | collective-permute-start | bytes 258056 | tf_op jit(solution)/shard_map/ppermute | solution.py:286
  69.5 11.4 %collective-permute-start.27 = (bf16[16,2688]{1,0:T(8,128)(2,1)S(1)}, bf16[16,2688]{1,0:T(8,128)(2,1)}, u32[]{:S(2)}, u32[]{:S(2)}) collective-permute-start(bf16[16,2688]{1,0:T(8,128)(2,1)S(1)} %collective-permute-done.11.refs_12_), channel_id=1, source_target_pairs={{0,16},{16,0},{1,17},{17,1},{2,18},{18,2},{3,19},{19,3},{4,20},{20... | collective-permute-start | bytes 258056 | tf_op jit(solution)/shard_map/ppermute | solution.py:286
  71.3 9.6 %collective-permute-start.28 = (bf16[16,2688]{1,0:T(8,128)(2,1)S(1)}, bf16[16,2688]{1,0:T(8,128)(2,1)}, u32[]{:S(2)}, u32[]{:S(2)}) collective-permute-start(bf16[16,2688]{1,0:T(8,128)(2,1)S(1)} %collective-permute-done.12.refs_13_), channel_id=1, source_target_pairs={{0,16},{16,0},{1,17},{17,1},{2,18},{18,2},{3,19},{19,3},{4,20},{20... | collective-permute-start | bytes 258056 | tf_op jit(solution)/shard_map/ppermute | solution.py:286
  73.2 7.7 %collective-permute-start.29 = (bf16[16,2688]{1,0:T(8,128)(2,1)S(1)}, bf16[16,2688]{1,0:T(8,128)(2,1)}, u32[]{:S(2)}, u32[]{:S(2)}) collective-permute-start(bf16[16,2688]{1,0:T(8,128)(2,1)S(1)} %collective-permute-done.13.refs_14_), channel_id=1, source_target_pairs={{0,16},{16,0},{1,17},{17,1},{2,18},{18,2},{3,19},{19,3},{4,20},{20... | collective-permute-start | bytes 258056 | tf_op jit(solution)/shard_map/ppermute | solution.py:286
  74.4 7.2 %collective-permute-start.30 = (bf16[16,2688]{1,0:T(8,128)(2,1)S(1)}, bf16[16,2688]{1,0:T(8,128)(2,1)}, u32[]{:S(2)}, u32[]{:S(2)}) collective-permute-start(bf16[16,2688]{1,0:T(8,128)(2,1)S(1)} %collective-permute-done.14.refs_15_), channel_id=1, source_target_pairs={{0,16},{16,0},{1,17},{17,1},{2,18},{18,2},{3,19},{19,3},{4,20},{20... | collective-permute-start | bytes 258056 | tf_op jit(solution)/shard_map/ppermute | solution.py:286
  81.5 0.9 copy-start.7
  82.4 0.9 copy-start.9
  83.3 0.9 copy-start.11
  84.2 0.9 copy-start.13
  85.1 0.9 copy-start.15
  86.0 0.9 copy-start.17
  96.4 25.3 %all-to-all-start = ((f32[32,1,128]{2,1,0:T(1,128)}), f32[32,1,128]{2,1,0:T(1,128)S(1)}, u32[]{:S(2)}, u32[]{:S(2)}) async-start(f32[32,1,128]{2,1,0:T(1,128)} %broadcast_select_fusion), calls=%async_computation | async-start | bytes 32768 | tf_op jit(solution)/shard_map/all_to_all | solution.py:311
  102.8 20.2 %collective-permute-start.32 = (bf16[192,512]{1,0:T(8,128)(2,1)}, bf16[192,512]{1,0:T(8,128)(2,1)S(1)}, u32[]{:S(2)}, u32[]{:S(2)}) collective-permute-start(bf16[192,512]{1,0:T(8,128)(2,1)} %copy-done.30), channel_id=1, source_target_pairs={{0,16},{16,0},{1,17},{17,1},{2,18},{18,2},{3,19},{19,3},{4,20},{20... | collective-permute-start | bytes 589832 | tf_op jit(solution)/shard_map/ppermute | solution.py:286
  105.9 15.8 %copy-start.25 = (s32[256,8]{0,1:T(8,128)S(1)}, s32[256,8]{0,1:T(8,128)}, u32[]{:S(2)}) copy-start(s32[256,8]{0,1:T(8,128)} %param.9) | copy-start | bytes 24580
  105.9 15.8 %copy-start.27 = (s32[256,8]{0,1:T(8,128)S(1)}, s32[256,8]{0,1:T(8,128)}, u32[]{:S(2)}) copy-start(s32[256,8]{0,1:T(8,128)} %param.10) | copy-start | bytes 24580
  105.9 15.8 %copy-start.29 = (bf16[256,8]{0,1:T(8,128)(2,1)S(1)}, bf16[256,8]{0,1:T(8,128)(2,1)}, u32[]{:S(2)}) copy-start(bf16[256,8]{0,1:T(8,128)(2,1)} %param.11) | copy-start | bytes 12292
  123.0 1.1 copy-start.3
  124.2 1.1 copy-start.5
  (17 other events, 12.0 us)

commit v2 on v1

v2 whole, which is shorter than its diff:
```python
import functools

import jax
import jax.numpy as jnp
from jax import lax
from jax.experimental import pallas as pl
from jax.experimental.pallas import tpu as pltpu
from jax.sharding import PartitionSpec as P

TOPK = 8
EXP_LOCAL = 8
SEND = 12
LANE = 128
UNIT = 512
ROWS = 16

beta_one = 0.9
beta_two = 0.95
learn_rate = 0.002
decay_rate = 0.1
adam_eps = 1e-08
adam_step = 50

f32 = jnp.float32
bf16 = jnp.bfloat16
VMEM = pl.BlockSpec(memory_space=pltpu.VMEM)
HBM = pl.BlockSpec(memory_space=pltpu.HBM)


def in_hbm(*arrays):
    return [pltpu.with_memory_space_constraint(array, pltpu.HBM) for array in arrays]


def shape_of(dims, dtype):
    return jax.ShapeDtypeStruct(tuple(dims), dtype)


def params(nbytes):
    mib = min(56, max(12, 4 + 2 * int(nbytes) // 2**20))
    return pltpu.CompilerParams(vmem_limit_bytes=mib * 2**20)


def cost(flops, nbytes, transcendentals=0):
    return pl.CostEstimate(
        flops=int(flops), bytes_accessed=int(nbytes), transcendentals=int(transcendentals)
    )


def div_send(index):
    return lax.shift_right_logical(index * 10923, 17)


def split_width(width):
    units = width // UNIT
    return (units - max(1, round(units * 2 / 7))) * UNIT


def dispatch_kernel(first, ids_hbm, slots_hbm, gates_hbm, grad_hbm, *refs):
    outs, (ids_ref, slots_ref, gates_ref, grad_ref, sems) = refs[:2], refs[2:]
    copies = [
        pltpu.make_async_copy(source, target, sems.at[i])
        for i, (source, target) in enumerate(
            [
                (ids_hbm, ids_ref),
                (slots_hbm, slots_ref),
                (gates_hbm, gates_ref),
                (grad_hbm, grad_ref),
            ]
        )
    ]
    for copy in copies:
        copy.start()
    for copy in copies[:3]:
        copy.wait()
    rows = outs[0].shape[0]
    ids = ids_ref[...]
    slots = slots_ref[...]
    gates = gates_ref[...].astype(f32)
    tok, width = grad_ref.shape
    live = (ids % EXP_LOCAL == 0) & (slots >= 0)
    place = jnp.where(live, (ids // EXP_LOCAL) * ROWS + slots, -1)
    row = lax.broadcasted_iota(jnp.int32, (rows, tok), 0)

    def pick_rows(at):
        pick = jnp.zeros((rows, tok), f32)
        for k in range(TOPK):
            pick = jnp.where(row == at[k : k + 1], gates[k : k + 1], pick)
        return pick.astype(bf16)

    main = pick_rows(place)
    tails = []
    for j in range(3):
        inside = (slots >= 4 * j) & (slots < 4 * j + 4) & live
        tails.append(pick_rows(jnp.where(inside, place + SEND - 4 * j, -1)))
    copies[3].wait()
    for out_ref, low, high in ((outs[1], first, width), (outs[0], 0, first)):
        part = (high - low) // 4
        for j in range(3):
            total = jnp.dot(
                main,
                grad_ref[:, low + j * part : low + (j + 1) * part],
                preferred_element_type=f32,
            )
            total += jnp.dot(
                tails[j], grad_ref[:, low + 3 * part : high], preferred_element_type=f32
            )
            out_ref[:, j * part : (j + 1) * part] = total.astype(bf16)


def dispatch(blocks, first, ids, slots, gates, out_grad):
    tok, width = out_grad.shape
    rows = blocks * ROWS
    return pl.pallas_call(
        functools.partial(dispatch_kernel, first),
        in_specs=[HBM] * 4,
        out_specs=[VMEM] * 2,
        out_shape=[
            shape_of((rows, first // 4 * 3), bf16),
            shape_of((rows, (width - first) // 4 * 3), bf16),
        ],
        scratch_shapes=[
            pltpu.VMEM(ids.shape, jnp.int32),
            pltpu.VMEM(slots.shape, jnp.int32),
            pltpu.VMEM(gates.shape, bf16),
            pltpu.VMEM(out_grad.shape, bf16),
            pltpu.SemaphoreType.DMA((4,)),
        ],
        compiler_params=params(4 * rows * width + 2 * tok * width),
        cost_estimate=cost(2 * rows * tok * width, 4 * tok * width),
    )(*in_hbm(ids, slots, gates, out_grad))


def hidden_kernel(gate_up_ref, after_ref, hidden_ref, coef_gate_ref, coef_up_ref):
    del after_ref
    shards, _, part = hidden_ref.shape
    width = shards * part
    for q in range(shards):
        gate = gate_up_ref[:, q * part : (q + 1) * part].astype(f32)
        up = gate_up_ref[:, width + q * part : width + (q + 1) * part].astype(f32)
        sig = jax.nn.sigmoid(gate)
        silu = gate * sig
        hidden_ref[q] = (silu * up).astype(bf16)
        coef_gate_ref[q] = up * sig * (1.0 + gate * (1.0 - sig))
        coef_up_ref[q] = silu


def hidden_parts(gate_up, shards, after):
    slots, width = gate_up.shape
    shape = (shards, slots, width // 2 // shards)
    return pl.pallas_call(
        hidden_kernel,
        in_specs=[VMEM, pl.BlockSpec(memory_space=pl.ANY)],
        out_shape=[shape_of(shape, bf16), shape_of(shape, f32), shape_of(shape, f32)],
        compiler_params=params(8 * slots * width),
        cost_estimate=cost(8 * slots * width, 8 * slots * width, slots * width),
    )(gate_up, after)


def load_kernel(first, after_ref, master_hbm, one_hbm, two_hbm, *refs):
    del after_ref
    master_ref, one_ref, two_ref, weight_a, weight_b, sems = refs
    part = master_ref.shape[0]
    step = part // 4
    copies = []
    for i in range(4):
        own = pl.ds(i * step, step)
        copies.append(
            pltpu.make_async_copy(master_hbm.at[0, own], master_ref.at[own], sems.at[i])
        )
    copies.append(pltpu.make_async_copy(one_hbm.at[0], one_ref, sems.at[4]))
    copies.append(pltpu.make_async_copy(two_hbm.at[0], two_ref, sems.at[5]))
    for copy in copies:
        copy.start()
    for i in range(4):
        copies[i].wait()
        own = pl.ds(i * step, step)
        weight_a[own, :] = master_ref[own, :first].astype(bf16)
        weight_b[own, :] = master_ref[own, first:].astype(bf16)
    copies[4].wait()
    copies[5].wait()


def load_state(first, master, one, two, after):
    _, part, width = master.shape
    return pl.pallas_call(
        functools.partial(load_kernel, first),
        in_specs=[pl.BlockSpec(memory_space=pl.ANY)] + [HBM] * 3,
        out_specs=[VMEM] * 5,
        out_shape=[
            pltpu.VMEM((part, width), f32),
            pltpu.VMEM((part, width), bf16),
            pltpu.VMEM((part, width), bf16),
            pltpu.VMEM((part, first), bf16),
            pltpu.VMEM((part, width - first), bf16),
        ],
        scratch_shapes=[pltpu.SemaphoreType.DMA((6,))],
        compiler_params=params(0),
        cost_estimate=cost(part * width, 14 * part * width),
    )(after, *in_hbm(master, one, two))


def reorder(arrived, rows_ref):
    count, width = rows_ref.shape
    part = width // 4
    total = arrived.shape[0]
    slot = lax.broadcasted_iota(jnp.int32, (count, total), 0)
    col = lax.broadcasted_iota(jnp.int32, (count, total), 1)
    block = div_send(slot)
    inner = slot - SEND * block
    base = block * ROWS
    order = jnp.where(col == base + inner, 1.0, 0.0).astype(bf16)
    rows_ref[:, : 3 * part] = jnp.dot(order, arrived, preferred_element_type=f32).astype(bf16)
    tail = jnp.zeros((count, part), f32)
    for j in range(3):
        inside = (inner >= 4 * j) & (inner < 4 * j + 4)
        order = jnp.where(inside & (col == base + SEND + inner - 4 * j), 1.0, 0.0).astype(bf16)
        tail += jnp.dot(
            order, arrived[:, j * part : (j + 1) * part], preferred_element_type=f32
        )
    rows_ref[:, 3 * part :] = tail.astype(bf16)


def times_weight(rows_ref, weight_ref):
    return lax.dot_general(
        rows_ref[...], weight_ref[...], (((1,), (1,)), ((), ())), preferred_element_type=f32
    )


def begin_kernel(arrived_ref, weight_ref, *refs):
    hidden_refs, (rows_ref, proj_ref, hidden_t_ref) = refs[:-3], refs[-3:]
    reorder(arrived_ref[...], rows_ref)
    proj_ref[...] = times_weight(rows_ref, weight_ref)
    count = rows_ref.shape[0]
    for s, hidden_ref in enumerate(hidden_refs):
        hidden_t_ref[:, s * count : (s + 1) * count] = (
            hidden_ref[...].astype(f32).T.astype(bf16)
        )


def begin(blocks, arrived, weight, hidden):
    count = blocks * SEND
    part, width = weight.shape
    return pl.pallas_call(
        begin_kernel,
        out_shape=[
            shape_of((count, width), bf16),
            shape_of((count, part), f32),
            shape_of((part, len(hidden) * count), bf16),
        ],
        compiler_params=params(
            2 * (arrived.size + weight.size + count * width) + 6 * count * part * len(hidden)
        ),
        cost_estimate=cost(4 * count * part * width, 2 * width * (part + 2 * count)),
    )(arrived, weight, *hidden)


def finish_kernel(group, blocks, shards, weight_a, weight_b, *refs):
    refs = list(refs)
    own = group[0] == 0
    proj_in = refs.pop(0) if own else None
    peers = [s for s in group if s > 0]
    arrived_a = {s: refs.pop(0) for s in peers}
    arrived_b = {s: refs.pop(0) for s in group}
    hidden = {s: refs.pop(0) for s in group}
    score_ref = refs.pop(0)
    rows_a = {s: refs.pop(0) for s in peers}
    rows_b = {s: refs.pop(0) for s in group}
    proj_out = {s: refs.pop(0) for s in group}
    me = lax.axis_index("rep")
    if len(group) < shards:
        score_ref[...] = jnp.zeros(score_ref.shape, f32)
    count = blocks * SEND
    slot_of = lax.broadcasted_iota(jnp.int32, (count, LANE), 0)
    lane_of = lax.broadcasted_iota(jnp.int32, (count, LANE), 1)
    block_of = lax.broadcasted_iota(jnp.int32, (blocks, count), 0)
    slot_at = lax.broadcasted_iota(jnp.int32, (blocks, count), 1)
    gather = (div_send(slot_at) == block_of).astype(f32)
    for s in reversed(group):
        arrived = arrived_b[s][...]
        reorder(arrived.reshape(blocks * ROWS, arrived.shape[-1]), rows_b[s])
        proj = times_weight(rows_b[s], weight_b)
        if s == 0:
            proj += proj_in[...]
        else:
            reorder(arrived_a[s][...], rows_a[s])
            proj += times_weight(rows_a[s], weight_a)
        proj_out[s][...] = proj.astype(proj_out[s].dtype)
        score = jnp.sum(proj * hidden[s][...].astype(f32), axis=1, keepdims=True)
        spread = jnp.where(slot_of - SEND * div_send(slot_of) == lane_of, score, 0.0)
        score = jnp.dot(
            gather, spread, precision=lax.Precision.HIGHEST, preferred_element_type=f32
        )
        at = lax.rem(me + shards - s, shards)
        score_ref[pl.ds(at * blocks, blocks)] = score.reshape(blocks, 1, LANE)


def finish(group, weight_a, weight_b, proj, arrived_a, arrived_b, hidden):
    blocks, shards, _, packed = arrived_b.shape
    count = blocks * SEND
    part, first = weight_a.shape
    rest = weight_b.shape[1]
    peers = [s for s in group if s > 0]
    args = [weight_a, weight_b] + ([proj] if group[0] == 0 else [])
    args += [arrived_a[s] for s in peers]
    specs = [pl.BlockSpec(arg.shape, lambda i: (0, 0)) for arg in args]
    for s in group:
        args.append(arrived_b)
        specs.append(
            pl.BlockSpec((blocks, 1, ROWS, packed), lambda i, s=s: (0, s, 0, 0))
        )
    for s in group:
        args.append(hidden[s])
        specs.append(pl.BlockSpec(hidden[s].shape, lambda i: (0, 0)))
    out = [shape_of((shards * blocks, 1, LANE), f32)]
    out += [shape_of((count, first), bf16) for s in peers]
    out += [shape_of((count, rest), bf16) for s in group]
    out += [shape_of((count, part), bf16 if s else f32) for s in group]
    nbytes = sum(a.size * a.dtype.itemsize for a in args if a is not arrived_b)
    nbytes += sum(a.size * a.dtype.itemsize for a in out)
    nbytes += len(group) * blocks * ROWS * packed * 2
    outs = list(
        pl.pallas_call(
            functools.partial(finish_kernel, tuple(group), blocks, shards),
            grid=(1,),
            in_specs=specs,
            out_specs=[
                pl.BlockSpec(o.shape, lambda i, n=len(o.shape): (0,) * n) for o in out
            ],
            out_shape=out,
            compiler_params=params(nbytes),
            cost_estimate=cost(
                4 * len(group) * count * part * (first + rest), nbytes
            ),
        )(*args)
    )
    score = outs.pop(0)
    rows_a = {s: outs.pop(0) for s in peers}
    rows_b = {s: outs.pop(0) for s in group}
    projs = {s: outs.pop(0) for s in group}
    return score, rows_a, rows_b, projs


def adamw_kernel(shards, hidden_ref, *refs):
    rows_a, rows_b = refs[:shards], refs[shards : 2 * shards]
    master_ref, one_ref, two_ref = refs[2 * shards : 2 * shards + 3]
    outs, news, sems = refs[-7:-4], refs[-4:-1], refs[-1]
    count, first = rows_a[0].shape
    width = master_ref.shape[1]
    corr_one = 1.0 - beta_one**adam_step
    corr_two = 1.0 - beta_two**adam_step
    rate = learn_rate * corr_two**0.5 / corr_one
    keep = 1.0 - learn_rate * decay_rate

    def write(col, index):
        return [
            pltpu.make_async_copy(
                new.at[:, pl.ds(col, UNIT)], out.at[0, :, pl.ds(col, UNIT)], sems.at[j, index]
            )
            for j, (new, out) in enumerate(zip(news, outs))
        ]

    def update(rows, base, i):
        at = pl.multiple_of(i * UNIT, UNIT)
        grad = jnp.dot(
            hidden_ref[:, :count], rows[0][:, pl.ds(at, UNIT)], preferred_element_type=f32
        )
        for s in range(1, shards):
            grad += jnp.dot(
                hidden_ref[:, s * count : (s + 1) * count],
                rows[s][:, pl.ds(at, UNIT)],
                preferred_element_type=f32,
            )
        cols = pl.ds(pl.multiple_of(base + at, UNIT), UNIT)
        m_new = beta_one * one_ref[:, cols].astype(f32) + (1.0 - beta_one) * grad
        v_new = beta_two * two_ref[:, cols].astype(f32) + (1.0 - beta_two) * (grad * grad)
        root = v_new * lax.rsqrt(v_new) + adam_eps * corr_two**0.5
        news[0][:, cols] = keep * master_ref[:, cols] - rate * m_new / root
        news[1][:, cols] = m_new.astype(bf16)
        news[2][:, cols] = v_new.astype(bf16)
        for copy in write(pl.multiple_of(base + at, UNIT), base // UNIT + i):
            copy.start()

    @pl.loop(0, first // UNIT)
    def _(i):
        update(rows_a, 0, i)

    @pl.loop(0, (width - first) // UNIT)
    def _(i):
        update(rows_b, first, i)

    for index in range(width // UNIT):
        for copy in write(index * UNIT, index):
            copy.wait()


def adamw(hidden_t, rows_a, rows_b, master, one, two):
    part, depth = hidden_t.shape
    width = master.shape[1]
    shards = len(rows_a)
    shape = (1, part, width)
    return pl.pallas_call(
        functools.partial(adamw_kernel, shards),
        in_specs=[VMEM] * (4 + 2 * shards),
        out_specs=[HBM] * 3,
        out_shape=[shape_of(shape, f32), shape_of(shape, bf16), shape_of(shape, bf16)],
        scratch_shapes=[
            pltpu.VMEM((part, width), f32),
            pltpu.VMEM((part, width), bf16),
            pltpu.VMEM((part, width), bf16),
            pltpu.SemaphoreType.DMA((3, width // UNIT)),
        ],
        compiler_params=params(6 * part * width + 2 * depth * width),
        cost_estimate=cost(2 * part * depth * width, 16 * part * width, part * width),
    )(hidden_t, *rows_a, *rows_b, master, one, two)


def gate_up_kernel(place_ref, coef_gate_ref, coef_up_ref, *refs):
    out_ref = refs[-1]
    shards, _, part = coef_gate_ref.shape
    for s in range(shards):
        at = place_ref[s]
        grad = refs[s][...].astype(f32)
        low = pl.multiple_of(at * part, part)
        out_ref[:, pl.ds(low, part)] = (grad * coef_gate_ref[at]).astype(bf16)
        high = pl.multiple_of(shards * part + at * part, part)
        out_ref[:, pl.ds(high, part)] = (grad * coef_up_ref[at]).astype(bf16)


def gate_up_grad(place, coef_gate, coef_up, grads):
    shards, slots, part = coef_gate.shape
    return pl.pallas_call(
        gate_up_kernel,
        in_specs=[pl.BlockSpec(memory_space=pltpu.SMEM)] + [VMEM] * (2 + shards),
        out_specs=VMEM,
        out_shape=shape_of((slots, 2 * shards * part), bf16),
        compiler_params=params(16 * shards * slots * part),
        cost_estimate=cost(4 * shards * slots * part, 16 * shards * slots * part),
    )(place, coef_gate, coef_up, *grads)


def score_kernel(ids_ref, slots_ref, gates_ref, score_ref, out_ref):
    shards, blocks = score_ref.shape[:2]
    score = score_ref[0].reshape(blocks, LANE)
    for s in range(1, shards):
        score += score_ref[s].reshape(blocks, LANE)
    ids = ids_ref[...]
    slots = slots_ref[...]
    tok = ids.shape[1]
    live = (ids % EXP_LOCAL == 0) & (slots >= 0)
    owner = ids // EXP_LOCAL
    lane = lax.broadcasted_iota(jnp.int32, (LANE, tok), 0)
    block = lax.broadcasted_iota(jnp.int32, (blocks, tok), 0)
    for k in range(TOPK):
        pick = (lane == slots[k : k + 1]).astype(f32)
        value = jnp.dot(score, pick, precision=lax.Precision.HIGHEST, preferred_element_type=f32)
        value = jnp.sum(jnp.where(block == owner[k : k + 1], value, 0.0), axis=0, keepdims=True)
        out_ref[k : k + 1] = jnp.where(
            live[k : k + 1], value / gates_ref[k : k + 1].astype(f32), 0.0
        )


def gate_scores(ids, slots, gates, score):
    return pl.pallas_call(
        score_kernel,
        out_shape=shape_of(ids.shape, f32),
        compiler_params=params(0),
        cost_estimate=cost(1 << 24, 1 << 16),
    )(ids, slots, gates, score)


def per_device(out_grad, expert_ids, slots, gate_weights, saved_gate_up, master, moment1, moment2):
    ep_size = lax.axis_size("ep")
    rep_size = lax.axis_size("rep")
    me = lax.axis_index("rep")
    ids_t, slots_t, gates_t = expert_ids.T, slots.T, gate_weights.T
    first = split_width(out_grad.shape[1])
    steps = range(1, rep_size)

    def shift(value, step):
        perm = [(i, (i + step) % rep_size) for i in range(rep_size)]
        return lax.ppermute(value, "rep", perm)

    def exchange(value):
        return lax.all_to_all(value, "ep", split_axis=0, concat_axis=0, tiled=True)

    send_a, send_b = dispatch(ep_size, first, ids_t, slots_t, gates_t, out_grad)
    mixed = [send_b] + [shift(send_b, s) for s in steps]
    arrived_a = exchange(send_a.reshape(ep_size, ROWS, -1)).reshape(send_a.shape)
    arrived_a = [arrived_a] + [shift(arrived_a, s) for s in steps]
    mixed = jnp.stack([part.reshape(ep_size, ROWS, -1) for part in mixed], axis=1)
    arrived_b = exchange(mixed.reshape(ep_size, rep_size * ROWS, -1)).reshape(mixed.shape)

    hidden, coef_gate, coef_up = hidden_parts(saved_gate_up[0, 0], rep_size, send_b)
    parts = [
        lax.dynamic_index_in_dim(hidden, (me + s) % rep_size, 0, keepdims=False)
        for s in range(rep_size)
    ]
    parts = [parts[0]] + [shift(parts[s], s) for s in steps]
    place = jnp.stack([(me + s) % rep_size for s in range(rep_size)]).astype(jnp.int32)
    master_v, one_v, two_v, weight_a, weight_b = load_state(
        first, master, moment1, moment2, send_b
    )

    rows_own, proj, hidden_t = begin(ep_size, arrived_a[0], weight_a, parts)
    score, rows_a, rows_b, projs = None, {0: rows_own}, {}, {}
    for low in range(0, rep_size, 2):
        group = list(range(low, min(low + 2, rep_size)))
        partial, more_a, more_b, more = finish(
            group, weight_a, weight_b, proj, arrived_a, arrived_b, parts
        )
        score = partial if score is None else score + partial
        rows_a.update(more_a)
        rows_b.update(more_b)
        projs.update(more)
    grads = [projs[0]] + [shift(projs[s], rep_size - s) for s in steps]
    score = lax.all_to_all(score, ("rep", "ep"), split_axis=0, concat_axis=0, tiled=True)

    every = range(rep_size)
    done = adamw(
        hidden_t, [rows_a[s] for s in every], [rows_b[s] for s in every], master_v, one_v, two_v
    )
    grad_gate_up = gate_up_grad(place, coef_gate, coef_up, grads)
    gate_grad = gate_scores(
        ids_t, slots_t, gates_t, score.reshape(rep_size, ep_size, 1, LANE)
    ).T
    return (grad_gate_up.reshape(saved_gate_up.shape), gate_grad) + tuple(done)


def solution(mesh):
    in_specs = (
        P(("rep", "ep"), None),
        P(("rep", "ep"), None),
        P(("rep", "ep"), None),
        P(("rep", "ep"), None),
        P("rep", "ep", None, None),
        P("ep", "rep", None),
        P("ep", "rep", None),
        P("ep", "rep", None),
    )
    out_specs = (
        P("rep", "ep", None, None),
        P(("rep", "ep"), None),
        P("ep", "rep", None),
        P("ep", "rep", None),
        P("ep", "rep", None),
    )
    return jax.shard_map(
        per_device, mesh=mesh, in_specs=in_specs, out_specs=out_specs, check_vma=False
    )
```

time: 128 us -> 116 us (0.906)
  starting transfers between devices: 48 us -> 24 us
  waiting for transfers between devices: 15.7 us -> 30.2 us
  local copies, waits for them, and re-layouts: 24.8 us -> 31.8 us
  other arithmetic: 7.51 us -> 0.69 us
  Pallas kernels: 30 us -> 27.5 us
    ppermute x15 -> x0, starting transfers between devices: 20.2 us -> none  [per_device(): own[k] = lax.ppermute(sends[k], 'ep', [(i, i ^ k) for i in range(ep_size)])]
    ppermute x18 -> x4, starting transfers between devices: 21.4 us -> 5.22 us  [shift(): return lax.ppermute(value, 'rep', perm)]
    ppermute x18 -> x4, waiting for transfers between devices: 5.94 us -> 20.8 us  [shift(): return lax.ppermute(value, 'rep', perm)]
    all_to_all x0 -> x2, starting transfers between devices: none -> 14 us  [exchange(): return lax.all_to_all(value, 'ep', split_axis=0, concat_axis=0, tiled=True)]
    ppermute x15 -> x0, waiting for transfers between devices: 9.8 us -> none  [per_device(): own[k] = lax.ppermute(sends[k], 'ep', [(i, i ^ k) for i in range(ep_size)])]
    all_to_all x0 -> x2, waiting for transfers between devices: none -> 9.38 us  [exchange(): return lax.all_to_all(value, 'ep', split_axis=0, concat_axis=0, tiled=True)]
    unnamed x62 -> x54, local copies, waits for them, and re-layouts: 22 us -> 30.7 us
    convert_element_type x1 -> x0, other arithmetic: 5.39 us -> none  [per_device(): weight = master[0].astype(bf16)]
  transfers between devices with their start and end apart: 34 -> 7, of which waited for: 6 -> 3; matrix products, arithmetic and copies ran while one was open for 7% -> 1% of each run, Pallas kernels for 17% -> 14%
where the time goes in v2:
time: 116 us; the launch traced here: 115 us
  local copies, waits for them, and re-layouts  31.8 us (27%)
  waiting for transfers between devices  30.2 us (26%)
  Pallas kernels  27.5 us (24%)
  starting transfers between devices  24 us (21%)
    unnamed x54, local copies, waits for them, and re-layouts  30.7 us
    ppermute x4, waiting for transfers between devices, shift(): return lax.ppermute(value, 'rep', perm)  20.8 us
    all_to_all x2, starting transfers between devices, exchange(): return lax.all_to_all(value, 'ep', split_axis=0, concat_axis=0, tiled=True)  14 us
    all_to_all x2, waiting for transfers between devices, exchange(): return lax.all_to_all(value, 'ep', split_axis=0, concat_axis=0, tiled=True)  9.38 us
    pallas_call x1, Pallas kernels, adamw(): pl.pallas_call(functools.partial(adamw_kernel, shards), in_specs=[VMEM] *...  8.1 us
    pallas_call x1, Pallas kernels, load_state(): pl.pallas_call(functools.partial(load_kernel, first), in_specs=[pl.BlockS...  5.31 us
    ppermute x4, starting transfers between devices, shift(): return lax.ppermute(value, 'rep', perm)  5.22 us
    all_to_all x1, starting transfers between devices, per_device(): lax.all_to_all(score, ('rep', 'ep'), split_axis=0, concat_axis=0, tiled=T...  4.71 us
  transfers between devices with their start and end apart: 7, of which 3 were waited for; matrix products, arithmetic and copies ran while one was open for 1% of the time, Pallas kernels for 14%

profile of v2, /device:TPU:0, one launch (start us, length us, event | category | flops | bytes accessed | tf_op | source)
XLA Modules:
  0.0 114.9 jit_solution(66527975404475353)
XLA Ops:
  0.6 4.2 %shard_map.119 = (bf16[256,1920]{1,0:T(8,128)(2,1)}, bf16[256,768]{1,0:T(8,128)(2,1)S(1)}) custom-call(s32[8,256]{1,0:T(8,128)} %bitcast.26, s32[8,256]{1,0:T(8,128)} %bitcast.28, bf16[8,256]{1,0:T(8,128)(2,1)} %bitcast.30, bf16[256,3584]{1,0:T(8,128)(2,1)} %grad_hbm.1), custom_call_target="tpu_custom_call" | custom-call | flops 469762048 | bytes 3670016 | tf_op jit(solution)/shard_map/pallas_call | solution.py:113
  4.9 0.0 copy-start.8
  4.9 7.5 %all-to-all-start = ((bf16[16,16,1920]{2,1,0:T(8,128)(2,1)}), bf16[16,16,1920]{2,1,0:T(8,128)(2,1)S(1)}, u32[]{:S(2)}, u32[]{:S(2)}) async-start(bf16[16,16,1920]{2,1,0:T(8,128)(2,1)} %bitcast.6), calls=%async_computation | async-start | bytes 1966080 | tf_op jit(solution)/shard_map/all_to_all | solution.py:484
  12.4 1.6 %collective-permute-start.2 = (bf16[256,768]{1,0:T(8,128)(2,1)S(1)}, bf16[256,768]{1,0:T(8,128)(2,1)S(1)}, u32[]{:S(2)}, u32[]{:S(2)}) collective-permute-start(bf16[256,768]{1,0:T(8,128)(2,1)S(1)} %get-tuple-element.27.after_ref), channel_id=1, source_target_pairs={{0,16},{16,0},{1,17},{17,1},{2,18},{18,2},{3,19},{19,3},{4,20},{20... | collective-permute-start | bytes 1179656 | tf_op jit(solution)/shard_map/ppermute | solution.py:481
  14.0 9.8 %collective-permute-done.2 = bf16[256,768]{1,0:T(8,128)(2,1)S(1)} collective-permute-done((bf16[256,768]{1,0:T(8,128)(2,1)S(1)}, bf16[256,768]{1,0:T(8,128)(2,1)S(1)}, u32[]{:S(2)}, u32[]{:S(2)}) %collective-permute-start.2) | collective-permute-done | bytes 393248 | tf_op jit(solution)/shard_map/ppermute | solution.py:481
  23.8 0.1 pad_maximum_fusion
  23.9 1.0 copy.13
  24.9 9.4 %all-to-all-done = bf16[16,16,1920]{2,1,0:T(8,128)(2,1)S(1)} async-done(((bf16[16,16,1920]{2,1,0:T(8,128)(2,1)}), bf16[16,16,1920]{2,1,0:T(8,128)(2,1)S(1)}, u32[]{:S(2)}, u32[]{:S(2)}) %all-to-all-start) | async-done | bytes 983072 | tf_op jit(solution)/shard_map/all_to_all | solution.py:484
  34.3 6.5 %all-to-all-start.1 = ((bf16[16,32,768]{2,1,0:T(8,128)(2,1)}), bf16[16,32,768]{2,1,0:T(8,128)(2,1)S(1)}, u32[]{:S(2)}, u32[]{:S(2)}) async-start(bf16[16,32,768]{2,1,0:T(8,128)(2,1)} %bitcast.32), calls=%async_computation.1 | async-start | bytes 1572864 | tf_op jit(solution)/shard_map/all_to_all | solution.py:484
  40.8 1.6 %collective-permute-start.1 = (bf16[256,1920]{1,0:T(8,128)(2,1)S(1)}, bf16[256,1920]{1,0:T(8,128)(2,1)}, u32[]{:S(2)}, u32[]{:S(2)}) collective-permute-start(bf16[256,1920]{1,0:T(8,128)(2,1)S(1)} %bitcast.19), channel_id=1, source_target_pairs={{0,16},{16,0},{1,17},{17,1},{2,18},{18,2},{3,19},{19,3},{4,20},{20... | collective-permute-start | bytes 2949128 | tf_op jit(solution)/shard_map/ppermute | solution.py:481
  42.4 0.4 shard_map.120
  42.8 0.9 copy-done.11
  43.7 0.8 copy-done.9
  44.6 0.5 collective-permute-start
  45.1 5.3 %shard_map.121 = (f32[512,3584]{1,0:T(8,128)S(1)}, bf16[512,3584]{1,0:T(8,128)(2,1)S(1)}, bf16[512,3584]{1,0:T(8,128)(2,1)S(1)}, bf16[512,2560]{1,0:T(8,128)(2,1)S(1)}, bf16[512,1024]{1,0:T(8,128)(2,1)S(1)}) custom-call(bf16[256,768]{1,0:T(8,128)(2,1)S(1)} %get-tuple-element.27.after_ref, f32[1,512,3584]{2,1,0:T(8,128)} %master_hbm.1, ...), custom_call_target="tpu_custom_call" | custom-call | flops 1835008 | bytes 25690112 | tf_op jit(solution)/shard_map/pallas_call | solution.py:185
  50.4 0.0 copy-start
  50.4 3.0 %copy-done = f32[512,3584]{1,0:T(8,128)} copy-done((f32[512,3584]{1,0:T(8,128)}, f32[512,3584]{1,0:T(8,128)S(1)}, u32[]{:S(2)}) %copy-start) | copy-done | bytes 7340056
  53.5 1.8 %copy-done.2 = bf16[512,3584]{1,0:T(8,128)(2,1)} copy-done((bf16[512,3584]{1,0:T(8,128)(2,1)}, bf16[512,3584]{1,0:T(8,128)(2,1)S(1)}, u32[]{:S(2)}) %copy-start.2) | copy-done | bytes 3670040
  55.3 1.8 %copy-done.4 = bf16[512,3584]{1,0:T(8,128)(2,1)} copy-done((bf16[512,3584]{1,0:T(8,128)(2,1)}, bf16[512,3584]{1,0:T(8,128)(2,1)S(1)}, u32[]{:S(2)}) %copy-start.4) | copy-done | bytes 3670040
  57.1 1.0 copy-done.25
  58.1 10.9 %collective-permute-done.refs_1_.refs_5_ = bf16[192,512]{1,0:T(8,128)(2,1)S(1)} collective-permute-done((bf16[192,512]{1,0:T(8,128)(2,1)S(1)}, bf16[192,512]{1,0:T(8,128)(2,1)S(1)}, u32[]{:S(2)}, u32[]{:S(2)}) %collective-permute-start) | collective-permute-done | bytes 196640 | tf_op jit(solution)/shard_map/ppermute | solution.py:481
  69.1 1.5 %shard_map.122 = (bf16[192,2560]{1,0:T(8,128)(2,1)S(1)}, f32[192,512]{1,0:T(8,128)S(1)}, bf16[512,384]{1,0:T(8,128)(2,1)S(1)}) custom-call(bf16[256,1920]{1,0:T(8,128)(2,1)S(1)} %bitcast.20, bf16[512,2560]{1,0:T(8,128)(2,1)S(1)} %get-tuple-element.30.weight_ref.weight_a, bf16[192,512]{1,0:T(8,128)(2,1)S(1)} %get-tuple-element.50.refs_0_.refs_4_, ...), custom_call_target="tpu_custom_call" | custom-call | flops 1006632960 | bytes 4587520 | tf_op jit(solution)/shard_map/pallas_call | solution.py:243
  70.6 1.5 %copy-done.6 = bf16[512,2560]{1,0:T(8,128)(2,1)} copy-done((bf16[512,2560]{1,0:T(8,128)(2,1)}, bf16[512,2560]{1,0:T(8,128)(2,1)S(1)}, u32[]{:S(2)}) %copy-start.6) | copy-done | bytes 2621464
  72.0 0.8 copy-done.15
  72.8 1.7 %copy-done.7 = bf16[512,2560]{1,0:T(8,128)(2,1)S(1)} copy-done((bf16[512,2560]{1,0:T(8,128)(2,1)S(1)}, bf16[512,2560]{1,0:T(8,128)(2,1)}, u32[]{:S(2)}) %copy-start.7) | copy-done | bytes 2621464
  74.5 1.2 %copy-done.26 = bf16[512,1024]{1,0:T(8,128)(2,1)S(1)} copy-done((bf16[512,1024]{1,0:T(8,128)(2,1)S(1)}, bf16[512,1024]{1,0:T(8,128)(2,1)}, u32[]{:S(2)}) %copy-start.26) | copy-done | bytes 1048600
  75.8 4.7 %shard_map.123 = (f32[32,1,128]{2,1,0:T(1,128)}, bf16[192,2560]{1,0:T(8,128)(2,1)S(1)}, bf16[192,1024]{1,0:T(8,128)(2,1)S(1)}, bf16[192,1024]{1,0:T(8,128)(2,1)S...) custom-call(bf16[512,2560]{1,0:T(8,128)(2,1)S(1)} %copy-done.7, bf16[512,1024]{1,0:T(8,128)(2,1)S(1)} %copy-done.26, ...), custom_call_target="tpu_custom_call" | custom-call | flops 2818572288 | bytes 8601600 | tf_op jit(solution)/shard_map/pallas_call | solution.py:322
  80.5 0.7 copy-done.13
  81.2 0.8 copy-done.17
  82.0 0.7 copy-done.19
  82.7 1.5 %collective-permute-start.3 = (bf16[192,512]{1,0:T(8,128)(2,1)}, bf16[192,512]{1,0:T(8,128)(2,1)}, u32[]{:S(2)}, u32[]{:S(2)}) collective-permute-start(bf16[192,512]{1,0:T(8,128)(2,1)} %get-tuple-element.36), channel_id=1, source_target_pairs={{0,16},{16,0},{1,17},{17,1},{2,18},{18,2},{3,19},{19,3},{4,20},{20... | collective-permute-start | bytes 589832 | tf_op jit(solution)/shard_map/ppermute | solution.py:481
  84.2 0.6 pad_add_fusion.place_ref
  84.9 4.7 %all-to-all-start.2 = ((f32[32,1,128]{2,1,0:T(1,128)}), f32[32,1,128]{2,1,0:T(1,128)S(1)}, u32[]{:S(2)}, u32[]{:S(2)}) async-start(f32[32,1,128]{2,1,0:T(1,128)} %get-tuple-element.37), calls=%async_computation.2 | async-start | bytes 32768 | tf_op jit(solution)/shard_map/all_to_all | solution.py:516
  89.6 0.0 copy-start.1
  89.6 3.1 %copy-done.1 = f32[512,3584]{1,0:T(8,128)S(1)} copy-done((f32[512,3584]{1,0:T(8,128)S(1)}, f32[512,3584]{1,0:T(8,128)}, u32[]{:S(2)}) %copy-start.1) | copy-done | bytes 7340056
  92.7 2.0 %copy-done.3 = bf16[512,3584]{1,0:T(8,128)(2,1)S(1)} copy-done((bf16[512,3584]{1,0:T(8,128)(2,1)S(1)}, bf16[512,3584]{1,0:T(8,128)(2,1)}, u32[]{:S(2)}) %copy-start.3) | copy-done | bytes 3670040
  94.7 2.0 %copy-done.5 = bf16[512,3584]{1,0:T(8,128)(2,1)S(1)} copy-done((bf16[512,3584]{1,0:T(8,128)(2,1)S(1)}, bf16[512,3584]{1,0:T(8,128)(2,1)}, u32[]{:S(2)}) %copy-start.5) | copy-done | bytes 3670040
  96.8 1.0 copy-done.16
  97.7 1.0 copy-done.18
  98.7 1.0 copy-done.20
  99.7 8.1 %shard_map.126 = (f32[1,512,3584]{2,1,0:T(8,128)}, bf16[1,512,3584]{2,1,0:T(8,128)(2,1)}, bf16[1,512,3584]{2,1,0:T(8,128)(2,1)}) custom-call(bf16[512,384]{1,0:T(8,128)(2,1)S(1)} %copy-done.16, bf16[192,2560]{1,0:T(8,128)(2,1)S(1)} %get-tuple-element.39.refs_0_, bf16[192,2560]{1,0:T(8,128)(2,1)S(1)} %get-tuple-element.40.refs_1_, ...), custom_call_target="tpu_custom_call" | custom-call | flops 1409286144 | bytes 29360128 | tf_op jit(solution)/shard_map/pallas_call | solution.py:401
  107.9 0.7 copy-done.21
  108.6 0.7 copy-done.22
  109.3 0.7 copy-done.23
  109.9 1.3 %shard_map.125 = f32[8,256]{1,0:T(8,128)} custom-call(s32[8,256]{1,0:T(8,128)S(1)} %bitcast.27, s32[8,256]{1,0:T(8,128)S(1)} %bitcast.29, bf16[8,256]{1,0:T(8,128)(2,1)S(1)} %bitcast.31, f32[2,16,1,128]{3,2,1,0:T(1,128)S(1)} %bitcast.25), custom_call_target="tpu_custom_call" | custom-call | flops 16777216 | bytes 65536 | tf_op jit(solution)/shard_map/pallas_call | solution.py:463
  111.3 1.0 copy-done.14
  112.3 0.6 copy-done.24
  112.9 1.9 %shard_map.124 = bf16[192,2048]{1,0:T(8,128)(2,1)} custom-call(s32[2]{0:T(128)S(1)} %copy-done.24, f32[2,192,512]{2,1,0:T(8,128)S(1)} %copy-done.10, f32[2,192,512]{2,1,0:T(8,128)S(1)} %copy-done.12, f32[192,512]{1,0:T(8,128)S(1)} %copy-done.14, bf16[192,512]{1,0:T(8,128)(2,1)} %collective-permute-done.3.refs_1_), custom_call_target="tpu_custom_call" | custom-call | flops 786432 | bytes 3145728 | tf_op jit(solution)/shard_map/pallas_call | solution.py:431
  (32 shorter events, 0.1 us)
Async XLA Ops:
  4.9 37.5 %copy-start.8 = (bf16[1,1,192,2048]{3,2,1,0:T(8,128)(2,1)S(1)}, bf16[1,1,192,2048]{3,2,1,0:T(8,128)(2,1)}, u32[]{:S(2)}) copy-start(bf16[1,1,192,2048]{3,2,1,0:T(8,128)(2,1)} %param.12) | copy-start | bytes 2359300
  4.9 29.4 %all-to-all-start = ((bf16[16,16,1920]{2,1,0:T(8,128)(2,1)}), bf16[16,16,1920]{2,1,0:T(8,128)(2,1)S(1)}, u32[]{:S(2)}, u32[]{:S(2)}) async-start(bf16[16,16,1920]{2,1,0:T(8,128)(2,1)} %bitcast.6), calls=%async_computation | async-start | bytes 1966080 | tf_op jit(solution)/shard_map/all_to_all | solution.py:484
  12.4 11.4 %collective-permute-start.2 = (bf16[256,768]{1,0:T(8,128)(2,1)S(1)}, bf16[256,768]{1,0:T(8,128)(2,1)S(1)}, u32[]{:S(2)}, u32[]{:S(2)}) collective-permute-start(bf16[256,768]{1,0:T(8,128)(2,1)S(1)} %get-tuple-element.27.after_ref), channel_id=1, source_target_pairs={{0,16},{16,0},{1,17},{17,1},{2,18},{18,2},{3,19},{19,3},{4,20},{20... | collective-permute-start | bytes 1179656 | tf_op jit(solution)/shard_map/ppermute | solution.py:481
  34.3 38.5 %all-to-all-start.1 = ((bf16[16,32,768]{2,1,0:T(8,128)(2,1)}), bf16[16,32,768]{2,1,0:T(8,128)(2,1)S(1)}, u32[]{:S(2)}, u32[]{:S(2)}) async-start(bf16[16,32,768]{2,1,0:T(8,128)(2,1)} %bitcast.32), calls=%async_computation.1 | async-start | bytes 1572864 | tf_op jit(solution)/shard_map/all_to_all | solution.py:484
  40.8 32.0 %collective-permute-start.1 = (bf16[256,1920]{1,0:T(8,128)(2,1)S(1)}, bf16[256,1920]{1,0:T(8,128)(2,1)}, u32[]{:S(2)}, u32[]{:S(2)}) collective-permute-start(bf16[256,1920]{1,0:T(8,128)(2,1)S(1)} %bitcast.19), channel_id=1, source_target_pairs={{0,16},{16,0},{1,17},{17,1},{2,18},{18,2},{3,19},{19,3},{4,20},{20... | collective-permute-start | bytes 2949128 | tf_op jit(solution)/shard_map/ppermute | solution.py:481
  42.8 0.9 copy-start.11
  43.7 0.9 copy-start.9
  44.6 24.5 %collective-permute-start = (bf16[192,512]{1,0:T(8,128)(2,1)S(1)}, bf16[192,512]{1,0:T(8,128)(2,1)S(1)}, u32[]{:S(2)}, u32[]{:S(2)}) collective-permute-start(bf16[192,512]{1,0:T(8,128)(2,1)S(1)} %get-tuple-element.49), channel_id=1, source_target_pairs={{0,16},{16,0},{1,17},{17,1},{2,18},{18,2},{3,19},{19,3},{4,20},{20... | collective-permute-start | bytes 589832 | tf_op jit(solution)/shard_map/ppermute | solution.py:481
  50.4 3.1 %copy-start = (f32[512,3584]{1,0:T(8,128)}, f32[512,3584]{1,0:T(8,128)S(1)}, u32[]{:S(2)}) copy-start(f32[512,3584]{1,0:T(8,128)S(1)} %get-tuple-element.43.refs_4_) | copy-start | bytes 22020100
  53.5 1.8 %copy-start.2 = (bf16[512,3584]{1,0:T(8,128)(2,1)}, bf16[512,3584]{1,0:T(8,128)(2,1)S(1)}, u32[]{:S(2)}) copy-start(bf16[512,3584]{1,0:T(8,128)(2,1)S(1)} %get-tuple-element.44.refs_5_) | copy-start | bytes 11010052
  55.3 1.8 %copy-start.4 = (bf16[512,3584]{1,0:T(8,128)(2,1)}, bf16[512,3584]{1,0:T(8,128)(2,1)S(1)}, u32[]{:S(2)}) copy-start(bf16[512,3584]{1,0:T(8,128)(2,1)S(1)} %get-tuple-element.45.refs_6_) | copy-start | bytes 11010052
  57.1 1.0 copy-start.25
  70.5 1.5 %copy-start.6 = (bf16[512,2560]{1,0:T(8,128)(2,1)}, bf16[512,2560]{1,0:T(8,128)(2,1)S(1)}, u32[]{:S(2)}) copy-start(bf16[512,2560]{1,0:T(8,128)(2,1)S(1)} %get-tuple-element.30.weight_ref.weight_a) | copy-start | bytes 7864324
  72.0 0.8 copy-start.15
  72.8 1.7 %copy-start.7 = (bf16[512,2560]{1,0:T(8,128)(2,1)S(1)}, bf16[512,2560]{1,0:T(8,128)(2,1)}, u32[]{:S(2)}) copy-start(bf16[512,2560]{1,0:T(8,128)(2,1)} %copy-done.6) | copy-start | bytes 7864324
  74.5 1.2 %copy-start.26 = (bf16[512,1024]{1,0:T(8,128)(2,1)S(1)}, bf16[512,1024]{1,0:T(8,128)(2,1)}, u32[]{:S(2)}) copy-start(bf16[512,1024]{1,0:T(8,128)(2,1)} %copy-done.25) | copy-start | bytes 3145732
  80.5 0.7 copy-start.13
  81.2 0.8 copy-start.17
  82.0 0.7 copy-start.19
  82.7 28.6 %collective-permute-start.3 = (bf16[192,512]{1,0:T(8,128)(2,1)}, bf16[192,512]{1,0:T(8,128)(2,1)}, u32[]{:S(2)}, u32[]{:S(2)}) collective-permute-start(bf16[192,512]{1,0:T(8,128)(2,1)} %get-tuple-element.36), channel_id=1, source_target_pairs={{0,16},{16,0},{1,17},{17,1},{2,18},{18,2},{3,19},{19,3},{4,20},{20... | collective-permute-start | bytes 589832 | tf_op jit(solution)/shard_map/ppermute | solution.py:481
  84.9 23.0 %all-to-all-start.2 = ((f32[32,1,128]{2,1,0:T(1,128)}), f32[32,1,128]{2,1,0:T(1,128)S(1)}, u32[]{:S(2)}, u32[]{:S(2)}) async-start(f32[32,1,128]{2,1,0:T(1,128)} %get-tuple-element.37), calls=%async_computation.2 | async-start | bytes 32768 | tf_op jit(solution)/shard_map/all_to_all | solution.py:516
  89.6 3.1 %copy-start.1 = (f32[512,3584]{1,0:T(8,128)S(1)}, f32[512,3584]{1,0:T(8,128)}, u32[]{:S(2)}) copy-start(f32[512,3584]{1,0:T(8,128)} %copy-done) | copy-start | bytes 22020100
  92.7 2.0 %copy-start.3 = (bf16[512,3584]{1,0:T(8,128)(2,1)S(1)}, bf16[512,3584]{1,0:T(8,128)(2,1)}, u32[]{:S(2)}) copy-start(bf16[512,3584]{1,0:T(8,128)(2,1)} %copy-done.2) | copy-start | bytes 11010052
  94.7 2.0 %copy-start.5 = (bf16[512,3584]{1,0:T(8,128)(2,1)S(1)}, bf16[512,3584]{1,0:T(8,128)(2,1)}, u32[]{:S(2)}) copy-start(bf16[512,3584]{1,0:T(8,128)(2,1)} %copy-done.4) | copy-start | bytes 11010052
  96.7 1.0 copy-start.16
  97.7 1.0 copy-start.18
  98.7 1.0 copy-start.20
  99.7 11.5 %copy-start.10 = (f32[2,192,512]{2,1,0:T(8,128)S(1)}, f32[2,192,512]{2,1,0:T(8,128)}, u32[]{:S(2)}) copy-start(f32[2,192,512]{2,1,0:T(8,128)} %copy-done.9) | copy-start | bytes 2359300
  99.7 11.5 %copy-start.12 = (f32[2,192,512]{2,1,0:T(8,128)S(1)}, f32[2,192,512]{2,1,0:T(8,128)}, u32[]{:S(2)}) copy-start(f32[2,192,512]{2,1,0:T(8,128)} %copy-done.11) | copy-start | bytes 2359300
  107.9 0.7 copy-start.21
  108.6 0.7 copy-start.22
  109.3 0.7 copy-start.23
  111.3 1.0 copy-start.14
  112.3 0.6 copy-start.24

commit v3 on v0

v3 whole, which is shorter than its diff:
```python
import functools

import jax
import jax.numpy as jnp
from jax import lax
from jax.experimental import pallas as pl
from jax.experimental.pallas import tpu as pltpu
from jax.sharding import PartitionSpec as P

TOPK = 8
EXP_LOCAL = 8
SEND = 12
LANE = 128
UNIT = 512
ROWS = 16

beta_one = 0.9
beta_two = 0.95
learn_rate = 0.002
decay_rate = 0.1
adam_eps = 1e-08
adam_step = 50

f32 = jnp.float32
bf16 = jnp.bfloat16
HBM = pl.BlockSpec(memory_space=pltpu.HBM)
ANY = pl.BlockSpec(memory_space=pl.ANY)


def in_hbm(*arrays):
    return [pltpu.with_memory_space_constraint(array, pltpu.HBM) for array in arrays]


def out_hbm(dims, dtype):
    return pltpu.HBM(tuple(dims), dtype)


def block(dims, at=None):
    at = at or (0,) * len(dims)
    return pl.BlockSpec(tuple(dims), lambda i: at)


def params(nbytes):
    mib = min(60, max(16, 8 + 3 * int(nbytes) // 2**20))
    return pltpu.CompilerParams(vmem_limit_bytes=mib * 2**20)


def cost(flops, nbytes, transcendentals=0):
    return pl.CostEstimate(
        flops=int(flops), bytes_accessed=int(nbytes), transcendentals=int(transcendentals)
    )


def div_send(index):
    return lax.shift_right_logical(index * 10923, 17)


def pack(cols):
    return cols // 4 * 3


def chunk_edges(width):
    units = width // UNIT
    last = units - max(1, round(units * 2 / 7))
    return (0, last * 2 // 5 * UNIT, last * UNIT, width)


def tail_order(count, total, j, slots_first):
    a = lax.broadcasted_iota(jnp.int32, (count, total), 0)
    b = lax.broadcasted_iota(jnp.int32, (count, total), 1)
    if slots_first:
        block_of = div_send(a)
        inner = a - SEND * block_of
        hit = b == block_of * ROWS + SEND + inner - 4 * j
    else:
        inner = (a & (ROWS - 1)) - SEND + 4 * j
        hit = (b == a - SEND + 4 * j) & ((a & (ROWS - 1)) >= SEND)
    return jnp.where(hit & (inner >= 4 * j) & (inner < 4 * j + 4), 1.0, 0.0).astype(bf16)


def dispatch_kernel(edges, ids_hbm, slots_hbm, gates_hbm, grad_hbm, *refs):
    outs, (ids_ref, slots_ref, gates_ref, grad_ref, sems) = refs[:2], refs[2:]
    pairs = [
        (ids_hbm, ids_ref),
        (slots_hbm, slots_ref),
        (gates_hbm, gates_ref),
        (grad_hbm, grad_ref),
    ]
    copies = [
        pltpu.make_async_copy(source, target, sems.at[i])
        for i, (source, target) in enumerate(pairs)
    ]
    for copy in copies:
        copy.start()
    for copy in copies[:3]:
        copy.wait()
    rows = outs[0].shape[0]
    ids = ids_ref[...]
    slots = slots_ref[...]
    gates = gates_ref[...].astype(f32)
    tok = ids.shape[1]
    live = ((ids & (EXP_LOCAL - 1)) == 0) & (slots >= 0)
    place = jnp.where(live, ids // EXP_LOCAL * ROWS + slots, -1)
    row = lax.broadcasted_iota(jnp.int32, (rows, tok), 0)
    main = jnp.zeros((rows, tok), f32)
    for k in range(TOPK):
        main = jnp.where(row == place[k : k + 1], gates[k : k + 1], main)
    main = main.astype(bf16)
    tails = [
        jnp.dot(
            tail_order(rows, rows, j, False), main, preferred_element_type=f32
        ).astype(bf16)
        for j in range(3)
    ]
    copies[3].wait()
    chunks = list(zip(edges[:-1], edges[1:]))
    base = 0
    for index, (low, high) in enumerate(chunks):
        out_ref = outs[int(index == len(chunks) - 1)]
        base = 0 if index == len(chunks) - 1 else base
        part = (high - low) // 4
        for j in range(3):
            total = jnp.dot(
                main,
                grad_ref[:, low + j * part : low + (j + 1) * part],
                preferred_element_type=f32,
            )
            total += jnp.dot(
                tails[j], grad_ref[:, low + 3 * part : high], preferred_element_type=f32
            )
            out_ref[:, base : base + part] = total.astype(bf16)
            base += part


def dispatch(blocks, edges, ids, slots, gates, out_grad):
    tok, width = out_grad.shape
    rows = blocks * ROWS
    shapes = [(rows, pack(edges[-2])), (rows, pack(width - edges[-2]))]
    return pl.pallas_call(
        functools.partial(dispatch_kernel, edges),
        grid=(1,),
        in_specs=[HBM] * 4,
        out_specs=[block(shape) for shape in shapes],
        out_shape=[out_hbm(shape, bf16) for shape in shapes],
        scratch_shapes=[
            pltpu.VMEM(ids.shape, jnp.int32),
            pltpu.VMEM(slots.shape, jnp.int32),
            pltpu.VMEM(gates.shape, bf16),
            pltpu.VMEM(out_grad.shape, bf16),
            pltpu.SemaphoreType.DMA((4,)),
        ],
        compiler_params=params(2 * rows * width + 2 * tok * width),
        cost_estimate=cost(2 * rows * tok * width, 4 * tok * width),
    )(*in_hbm(ids, slots, gates, out_grad))


def swiglu_part(gate_up_ref, shards, step, part):
    at = lax.rem(lax.axis_index("rep") + step, shards)
    low = pl.multiple_of(at * part, part)
    high = pl.multiple_of((shards + at) * part, part)
    gate = gate_up_ref[:, pl.ds(low, part)].astype(f32)
    up = gate_up_ref[:, pl.ds(high, part)].astype(f32)
    return low, high, gate, up, jax.nn.sigmoid(gate)


def hidden_kernel(gate_up_ref, after_ref, *out_refs):
    del after_ref
    for s, out_ref in enumerate(out_refs):
        _, _, gate, up, sig = swiglu_part(gate_up_ref, len(out_refs), s, out_ref.shape[1])
        out_ref[...] = (gate * sig * up).astype(bf16)


def hidden_parts(gate_up, shards, after):
    slots, width = gate_up.shape
    shape = (slots, width // 2 // shards)
    return pl.pallas_call(
        hidden_kernel,
        grid=(1,),
        in_specs=[block(gate_up.shape), HBM],
        out_specs=[block(shape)] * shards,
        out_shape=[out_hbm(shape, bf16)] * shards,
        compiler_params=params(3 * slots * width),
        cost_estimate=cost(8 * slots * width, 3 * slots * width, slots * width),
    )(*in_hbm(gate_up, after))


def cast_kernel(master_ref, after_ref, weight_ref):
    del after_ref
    weight_ref[...] = master_ref[0].astype(bf16)


def cast_weight(master, after):
    _, part, width = master.shape
    rows = part // 4
    return pl.pallas_call(
        cast_kernel,
        grid=(4,),
        in_specs=[pl.BlockSpec((1, rows, width), lambda i: (0, i, 0)), HBM],
        out_specs=pl.BlockSpec((rows, width), lambda i: (i, 0)),
        out_shape=out_hbm((part, width), bf16),
        compiler_params=params(6 * rows * width),
        cost_estimate=cost(part * width, 6 * part * width),
    )(*in_hbm(master, after))


def mix_kernel(count, *refs):
    out_ref = refs[-1]
    for s in range(count):
        value = refs[s][...]
        out_ref[:, s * ROWS : (s + 1) * ROWS, :] = value


def mix(parts, blocks, weight, after):
    packed = parts[0].shape[1]
    parts = [part.reshape(blocks, ROWS, packed) for part in parts]
    shape = (blocks, len(parts) * ROWS, packed)
    return pl.pallas_call(
        functools.partial(mix_kernel, len(parts)),
        grid=(1,),
        in_specs=[block(part.shape) for part in parts] + [HBM] + [ANY] * len(after),
        out_specs=block(shape),
        out_shape=out_hbm(shape, bf16),
        compiler_params=params(4 * parts[0].size * len(parts)),
        cost_estimate=cost(0, 4 * parts[0].size * len(parts)),
    )(*in_hbm(parts[0]), *parts[1:], *in_hbm(weight), *after)


def reorder(arrived, rows_ref):
    count, width = rows_ref.shape
    part = width // 4
    total = arrived.shape[0]
    slot = lax.broadcasted_iota(jnp.int32, (count, total), 0)
    col = lax.broadcasted_iota(jnp.int32, (count, total), 1)
    order = jnp.where(col == slot + (ROWS - SEND) * div_send(slot), 1.0, 0.0).astype(bf16)
    rows_ref[:, : 3 * part] = jnp.dot(order, arrived, preferred_element_type=f32).astype(bf16)
    tail = jnp.zeros((count, part), f32)
    for j in range(3):
        tail += jnp.dot(
            tail_order(count, total, j, True),
            arrived[:, j * part : (j + 1) * part],
            preferred_element_type=f32,
        )
    rows_ref[:, 3 * part :] = tail.astype(bf16)


def times_weight(rows_ref, weight_ref):
    return lax.dot_general(
        rows_ref[...], weight_ref[...], (((1,), (1,)), ((), ())), preferred_element_type=f32
    )


def score_block(blocks, proj, hidden):
    count = blocks * SEND
    score = jnp.sum(proj * hidden.astype(f32), axis=1, keepdims=True)
    slot_of = lax.broadcasted_iota(jnp.int32, (count, LANE), 0)
    lane_of = lax.broadcasted_iota(jnp.int32, (count, LANE), 1)
    spread = jnp.where(slot_of - SEND * div_send(slot_of) == lane_of, score, 0.0)
    block_of = lax.broadcasted_iota(jnp.int32, (blocks, count), 0)
    slot_at = lax.broadcasted_iota(jnp.int32, (blocks, count), 1)
    gather = (div_send(slot_at) == block_of).astype(f32)
    score = jnp.dot(
        gather, spread, precision=lax.Precision.HIGHEST, preferred_element_type=f32
    )
    return score.reshape(blocks, 1, LANE)


def absorb_kernel(chunks, more, *refs):
    refs = list(refs)
    arrived = [refs.pop(0) for _ in range(chunks)]
    weights = [refs.pop(0) for _ in range(chunks)]
    before_ref = refs.pop(0) if more else None
    rows_refs, proj_ref = refs[:-1], refs[-1]
    proj = before_ref[...] if more else 0.0
    for arrived_ref, weight_ref, rows_ref in zip(arrived, weights, rows_refs):
        reorder(arrived_ref[...], rows_ref)
        proj += times_weight(rows_ref, weight_ref)
    proj_ref[...] = proj


def absorb(blocks, edges, chunks, arrived, weight, before):
    count = blocks * SEND
    part = weight.shape[0]
    base, specs, weight_specs, out = 0, [], [], []
    for c in chunks:
        width = edges[c + 1] - edges[c]
        specs.append(pl.BlockSpec((pl.Element(arrived.shape[0]), pl.Element(pack(width))),
                                  lambda i, base=base: (0, base)))
        weight_specs.append(pl.BlockSpec((pl.Element(part), pl.Element(width)),
                                         lambda i, low=edges[c]: (0, low)))
        out.append(((count, width), bf16))
        base += pack(width)
    out.append(((count, part), f32))
    args = [arrived] * len(chunks) + in_hbm(*[weight] * len(chunks))
    specs += weight_specs
    if before is not None:
        args += in_hbm(before)
        specs.append(block(before.shape))
    cols = sum(edges[c + 1] - edges[c] for c in chunks)
    nbytes = 4 * count * cols + 2 * part * cols + 8 * count * part
    return pl.pallas_call(
        functools.partial(absorb_kernel, len(chunks), before is not None),
        grid=(1,),
        in_specs=specs,
        out_specs=[block(shape) for shape, _ in out],
        out_shape=[out_hbm(shape, dtype) for shape, dtype in out],
        compiler_params=params(nbytes),
        cost_estimate=cost(4 * count * part * cols, nbytes),
    )(*args)


def finish_kernel(group, blocks, shards, weight_ref, *refs):
    refs, size = list(refs), len(group)
    arrived, before, hidden = refs[:size], refs[size : 2 * size], refs[2 * size : 3 * size]
    outs = refs[3 * size + 1 :]
    score_ref, rows_refs, proj_refs = outs[0], outs[1 : size + 1], outs[size + 1 :]
    me = lax.axis_index("rep")
    if size < shards:
        score_ref[...] = jnp.zeros(score_ref.shape, f32)
    for i, s in enumerate(group):
        value = arrived[i][...]
        reorder(value.reshape(blocks * ROWS, value.shape[-1]), rows_refs[i])
        proj = before[i][...] + times_weight(rows_refs[i], weight_ref)
        proj_refs[i][...] = proj.astype(bf16)
        at = lax.rem(me + shards - s, shards)
        score_ref[pl.ds(at * blocks, blocks)] = score_block(blocks, proj, hidden[i][...])


def finish(group, edges, weight, before, arrived, hidden, after):
    blocks, shards, _, packed = arrived.shape
    count = blocks * SEND
    part = weight.shape[0]
    low, high = edges[-2:]
    args = in_hbm(weight) + [arrived] * len(group)
    specs = [
        pl.BlockSpec((pl.Element(part), pl.Element(high - low)), lambda i: (0, low))
    ]
    specs += [block((blocks, 1, ROWS, packed), (0, s, 0, 0)) for s in group]
    for s in group:
        args += in_hbm(before[s])
        specs.append(block((count, part)))
    for s in group:
        args.append(hidden[s])
        specs.append(block((count, part)))
    args += in_hbm(after)
    specs.append(HBM)
    out = [((shards * blocks, 1, LANE), f32)]
    out += [((count, high - low), bf16)] * len(group)
    out += [((count, part), bf16)] * len(group)
    nbytes = 2 * part * (high - low) + 4 * len(group) * count * (high - low + 3 * part)
    outs = pl.pallas_call(
        functools.partial(finish_kernel, tuple(group), blocks, shards),
        grid=(1,),
        in_specs=specs,
        out_specs=[block(shape) for shape, _ in out],
        out_shape=[jax.ShapeDtypeStruct(*out[0])]
        + [out_hbm(shape, dtype) for shape, dtype in out[1:]],
        compiler_params=params(nbytes),
        cost_estimate=cost(4 * len(group) * count * part * (high - low), nbytes),
    )(*args)
    size = len(group)
    return outs[0], outs[1 : size + 1], outs[size + 1 :]


def adamw_kernel(shards, *refs):
    hidden_refs, rows_refs = refs[:shards], refs[shards : 2 * shards]
    master_ref, one_ref, two_ref = refs[2 * shards : 2 * shards + 3]
    master_out, one_out, two_out = refs[-3:]
    corr_one = 1.0 - beta_one**adam_step
    corr_two = 1.0 - beta_two**adam_step
    rate = learn_rate * corr_two**0.5 / corr_one
    keep = 1.0 - learn_rate * decay_rate
    grad = 0.0
    for hidden_ref, rows_ref in zip(hidden_refs, rows_refs):
        grad += lax.dot_general(
            hidden_ref[...], rows_ref[...], (((0,), (0,)), ((), ())),
            preferred_element_type=f32,
        )
    m_new = beta_one * one_ref[0].astype(f32) + (1.0 - beta_one) * grad
    v_new = beta_two * two_ref[0].astype(f32) + (1.0 - beta_two) * (grad * grad)
    root = v_new * lax.rsqrt(v_new) + adam_eps * corr_two**0.5
    master_out[0] = keep * master_ref[0] - rate * m_new / root
    one_out[0] = m_new.astype(bf16)
    two_out[0] = v_new.astype(bf16)


def adamw(low, high, hidden, rows, state, done):
    part = hidden[0].shape[1]
    count = rows[0].shape[0]
    shards = len(rows)
    base = low // UNIT
    spec = pl.BlockSpec((1, part, UNIT), lambda i: (0, 0, base + i))
    args = list(hidden) + in_hbm(*rows, *state, *done)
    depth = count * shards
    cols = high - low
    return pl.pallas_call(
        functools.partial(adamw_kernel, shards),
        grid=(cols // UNIT,),
        in_specs=[block((count, part))] * shards
        + [pl.BlockSpec((count, UNIT), lambda i: (0, i))] * shards
        + [spec] * 3
        + [HBM] * len(done),
        out_specs=[spec] * 3,
        out_shape=[out_hbm(array.shape, array.dtype) for array in state],
        input_output_aliases={2 * shards + 3 + i: i for i in range(len(done))},
        compiler_params=params(16 * part * UNIT + 2 * depth * (part + UNIT)),
        cost_estimate=cost(2 * part * depth * cols, 16 * part * cols, part * cols),
    )(*args)


def gate_up_kernel(gate_up_ref, *refs):
    grad_refs, out_ref = refs[:-1], refs[-1]
    shards, part = len(grad_refs), grad_refs[0].shape[1]
    for s, grad_ref in enumerate(grad_refs):
        low, high, gate, up, sig = swiglu_part(gate_up_ref, shards, s, part)
        grad = grad_ref[...].astype(f32)
        out_ref[:, pl.ds(low, part)] = (
            grad * up * sig * (1.0 + gate * (1.0 - sig))
        ).astype(bf16)
        out_ref[:, pl.ds(high, part)] = (grad * (gate * sig)).astype(bf16)


def gate_up_grad(gate_up, grads):
    size = gate_up.size
    return pl.pallas_call(
        gate_up_kernel,
        grid=(1,),
        in_specs=[block(gate_up.shape)] + [block(grad.shape) for grad in grads],
        out_specs=block(gate_up.shape),
        out_shape=out_hbm(gate_up.shape, bf16),
        compiler_params=params(8 * size),
        cost_estimate=cost(12 * size, 5 * size, size),
    )(*in_hbm(gate_up, grads[0]), *grads[1:])


def score_kernel(ids_ref, slots_ref, gates_ref, score_ref, out_ref):
    shards, blocks = score_ref.shape[:2]
    score = score_ref[0].reshape(blocks, LANE)
    for s in range(1, shards):
        score += score_ref[s].reshape(blocks, LANE)
    ids = ids_ref[...]
    slots = slots_ref[...]
    tok = ids.shape[1]
    live = ((ids & (EXP_LOCAL - 1)) == 0) & (slots >= 0)
    owner = ids // EXP_LOCAL
    lane = lax.broadcasted_iota(jnp.int32, (LANE, tok), 0)
    block_of = lax.broadcasted_iota(jnp.int32, (blocks, tok), 0)
    for k in range(TOPK):
        pick = (lane == slots[k : k + 1]).astype(f32)
        value = jnp.dot(score, pick, precision=lax.Precision.HIGHEST, preferred_element_type=f32)
        value = jnp.where(block_of == owner[k : k + 1], value, 0.0)
        value = jnp.sum(value, axis=0, keepdims=True)
        out_ref[k : k + 1] = jnp.where(
            live[k : k + 1], value / gates_ref[k : k + 1].astype(f32), 0.0
        )


def gate_scores(ids, slots, gates, score):
    return pl.pallas_call(
        score_kernel,
        grid=(1,),
        in_specs=[block(array.shape) for array in (ids, slots, gates, score)],
        out_specs=block(ids.shape),
        out_shape=out_hbm(ids.shape, f32),
        compiler_params=params(0),
        cost_estimate=cost(1 << 24, 1 << 16),
    )(*in_hbm(ids, slots, gates), score)


def per_device(out_grad, expert_ids, slots, gate_weights, saved_gate_up, master, moment1, moment2):
    ep_size = lax.axis_size("ep")
    rep_size = lax.axis_size("rep")
    ids_t, slots_t, gates_t = expert_ids.T, slots.T, gate_weights.T
    gate_up = saved_gate_up[0, 0]
    state = (master, moment1, moment2)
    edges = chunk_edges(out_grad.shape[1])
    steps = range(1, rep_size)
    every = range(rep_size)

    def shift(value, step):
        perm = [(i, (i + step) % rep_size) for i in every]
        return lax.ppermute(value, "rep", perm)

    def exchange(value):
        return lax.all_to_all(value, "ep", split_axis=0, concat_axis=0, tiled=True)

    send_a, send_b = dispatch(ep_size, edges, ids_t, slots_t, gates_t, out_grad)
    mixed = [send_b] + [shift(send_b, s) for s in steps]
    parts = hidden_parts(gate_up, rep_size, send_b)
    hidden = [parts[0]] + [shift(parts[s], s) for s in steps]
    weight = cast_weight(master, send_b)
    arrived = exchange(send_a.reshape(ep_size, ROWS, -1)).reshape(send_a.shape)
    mixed = mix(mixed, ep_size, weight, hidden[1:])
    arrived_b = exchange(mixed).reshape(ep_size, rep_size, ROWS, -1)

    half = pack(edges[1])
    peers = [[shift(arrived[:, :half], s), shift(arrived[:, half:], s)] for s in steps]

    rows_0, rows_1, proj = absorb(ep_size, edges, (0, 1), arrived, weight, None)
    rows, before = [[rows_0], [rows_1], []], [proj]
    for s in steps:
        more, proj = absorb(ep_size, edges, (0,), peers[s - 1][0], weight, None)
        rows[0].append(more)
        before.append(proj)
    done = adamw(edges[0], edges[1], hidden, rows[0], state, ())
    for s in steps:
        more, before[s] = absorb(ep_size, edges, (1,), peers[s - 1][1], weight, before[s])
        rows[1].append(more)

    score, projs = None, []
    for low in range(0, rep_size, 2):
        group = list(range(low, min(low + 2, rep_size)))
        partial, more, final = finish(
            group, edges, weight, before, arrived_b, hidden, done[2]
        )
        score = partial if score is None else score + partial
        rows[2] += more
        projs += final
    grads = [projs[0]] + [shift(projs[s], rep_size - s) for s in steps]
    score = lax.all_to_all(score, ("rep", "ep"), split_axis=0, concat_axis=0, tiled=True)

    for c in (1, 2):
        done = adamw(edges[c], edges[c + 1], hidden, rows[c], state, done)
    grad_gate_up = gate_up_grad(gate_up, grads)
    gate_grad = gate_scores(
        ids_t, slots_t, gates_t, score.reshape(rep_size, ep_size, 1, LANE)
    ).T
    return (grad_gate_up.reshape(saved_gate_up.shape), gate_grad) + tuple(done)


def solution(mesh):
    in_specs = (
        P(("rep", "ep"), None),
        P(("rep", "ep"), None),
        P(("rep", "ep"), None),
        P(("rep", "ep"), None),
        P("rep", "ep", None, None),
        P("ep", "rep", None),
        P("ep", "rep", None),
        P("ep", "rep", None),
    )
    out_specs = (
        P("rep", "ep", None, None),
        P(("rep", "ep"), None),
        P("ep", "rep", None),
        P("ep", "rep", None),
        P("ep", "rep", None),
    )
    return jax.shard_map(
        per_device, mesh=mesh, in_specs=in_specs, out_specs=out_specs, check_vma=False
    )
```

time: 393 us -> 103 us (0.26); the launches traced: 388 us -> 102 us
  waiting for transfers between devices: 251 us -> 28.5 us
  local copies, waits for them, and re-layouts: 56.2 us -> 0.08 us
  Pallas kernels: 0 us -> 48.9 us
  other arithmetic: 30.3 us -> 0 us
  matrix products: 16.8 us -> 0 us
  between operations: 14.3 us -> 0.69 us
  starting transfers between devices: 19.4 us -> 24.4 us
    reduce_scatter x1 -> x0, waiting for transfers between devices: 93.9 us -> none  [per_device(): lax.psum_scatter(lax.dot_general(scaled, dout, (((0,), (0,)), ((), ())),...]
    all_gather x1 -> x0, waiting for transfers between devices: 92.3 us -> none  [per_device(): lax.all_gather(master[0].astype(jnp.bfloat16), 'rep', axis=0, tiled=True)]
    all_to_all x3, waiting for transfers between devices: 64.9 us -> 4.09 us  [the longest x2 4.09 us: exchange(): return lax.all_to_all(value, 'ep', split_axis=0, concat_axis=0, tiled=True)]
    pallas_call x0 -> x13, Pallas kernels: none -> 48.9 us  [the longest x3 18 us: adamw(): pl.pallas_call(functools.partial(adamw_kernel, shards), grid=(cols // UNI...]
    ppermute x0 -> x5, waiting for transfers between devices: none -> 24.4 us  [shift(): return lax.ppermute(value, 'rep', perm)]
    gather x9 -> x0, local copies, waits for them, and re-layouts: 24 us -> none  [the longest x8 22.6 us: per_device(): back_pad[position[:, which]].astype(jnp.float32)]
    scatter x2 -> x0, local copies, waits for them, and re-layouts: 22.6 us -> none  [the longest x1 14.6 us: per_device(): jnp.zeros((filled + 1,), gate_weights.dtype).at[flat_pos]]
    convert_element_type x3 -> x0, other arithmetic: 21.1 us -> none  [the longest x1 20.1 us: adamw(): return (master_new, m_new.astype(jnp.bfloat16), v_new.astype(jnp.bfloat16))]
  transfers between devices with their start and end apart: 5 -> 8, of which waited for: 4 -> 3; matrix products, arithmetic and copies ran while one was open for 5% -> 0% of each run, Pallas kernels for 0% -> 38%
where the time goes in v3:
time: 103 us; the launch traced here: 102 us
  Pallas kernels  48.9 us (47%)
  waiting for transfers between devices  28.5 us (28%)
  starting transfers between devices  24.4 us (24%)
    ppermute x5, waiting for transfers between devices, shift(): return lax.ppermute(value, 'rep', perm)  24.4 us
    pallas_call x3, Pallas kernels, adamw(): pl.pallas_call(functools.partial(adamw_kernel, shards), grid=(cols // UNI...  18 us
    all_to_all x2, starting transfers between devices, exchange(): return lax.all_to_all(value, 'ep', split_axis=0, concat_axis=0, tiled=True)  13.9 us
    pallas_call x3, Pallas kernels, absorb(): pl.pallas_call(functools.partial(absorb_kernel, len(chunks), before is no...  9.85 us
    ppermute x5, starting transfers between devices, shift(): return lax.ppermute(value, 'rep', perm)  5.77 us
    pallas_call x1, Pallas kernels, cast_weight(): pl.pallas_call(cast_kernel, grid=(4,), in_specs=[pl.BlockSpec((1, rows, w...  5.38 us
    all_to_all x1, starting transfers between devices, per_device(): lax.all_to_all(score, ('rep', 'ep'), split_axis=0, concat_axis=0, tiled=T...  4.71 us
    all_to_all x2, waiting for transfers between devices, exchange(): return lax.all_to_all(value, 'ep', split_axis=0, concat_axis=0, tiled=True)  4.09 us
  transfers between devices with their start and end apart: 8, of which 3 were waited for; matrix products, arithmetic and copies ran while one was open for 0% of the time, Pallas kernels for 38%

profile of v3, /device:TPU:0, one launch (start us, length us, event | category | flops | bytes accessed | tf_op | source)
XLA Modules:
  0.0 102.5 jit_solution(15692045203774500698)
XLA Ops:
  0.6 3.4 %shard_map.119 = (bf16[256,1920]{1,0:T(8,128)(2,1)}, bf16[256,768]{1,0:T(8,128)(2,1)}) custom-call(s32[8,256]{1,0:T(8,128)} %bitcast.25, s32[8,256]{1,0:T(8,128)} %bitcast.27, bf16[8,256]{1,0:T(8,128)(2,1)} %bitcast.29, bf16[256,3584]{1,0:T(8,128)(2,1)} %grad_hbm.1), custom_call_target="tpu_custom_call" | custom-call | flops 469762048 | bytes 3670016 | tf_op jit(solution)/shard_map/pallas_call | solution.py:139
  4.1 7.4 %all-to-all-start.1 = ((bf16[16,16,1920]{2,1,0:T(8,128)(2,1)}), bf16[16,16,1920]{2,1,0:T(8,128)(2,1)S(1)}, u32[]{:S(2)}, u32[]{:S(2)}) async-start(bf16[16,16,1920]{2,1,0:T(8,128)(2,1)} %bitcast.23), calls=%async_computation.1 | async-start | bytes 1966080 | tf_op jit(solution)/shard_map/all_to_all | solution.py:484
  11.5 1.6 %collective-permute-start = (bf16[256,768]{1,0:T(8,128)(2,1)}, bf16[256,768]{1,0:T(8,128)(2,1)S(1)}, u32[]{:S(2)}, u32[]{:S(2)}) collective-permute-start(bf16[256,768]{1,0:T(8,128)(2,1)} %get-tuple-element.30.after_ref), channel_id=1, source_target_pairs={{0,16},{16,0},{1,17},{17,1},{2,18},{18,2},{3,19},{19,3},{4,20},{20... | collective-permute-start | bytes 1179656 | tf_op jit(solution)/shard_map/ppermute | solution.py:481
  13.0 2.0 %shard_map.121 = (bf16[192,512]{1,0:T(8,128)(2,1)}, bf16[192,512]{1,0:T(8,128)(2,1)}) custom-call(bf16[192,2048]{1,0:T(8,128)(2,1)} %bitcast.21, bf16[256,768]{1,0:T(8,128)(2,1)} %get-tuple-element.30.after_ref), custom_call_target="tpu_custom_call" | custom-call | flops 3145728 | bytes 1179648 | tf_op jit(solution)/shard_map/pallas_call | solution.py:176
  15.0 0.5 collective-permute-start.1
  15.5 5.4 %shard_map.120.refs_2_.refs_3_.refs_1_.weight_ref = bf16[512,3584]{1,0:T(8,128)(2,1)} custom-call(f32[1,512,3584]{2,1,0:T(8,128)} %refs_4_.5, bf16[256,768]{1,0:T(8,128)(2,1)} %get-tuple-element.30.after_ref), custom_call_target="tpu_custom_call" | custom-call | flops 1835008 | bytes 11010048 | tf_op jit(solution)/shard_map/pallas_call | solution.py:195
  20.9 6.4 %collective-permute-done.1.refs_3_.refs_1_.refs_5_ = bf16[192,512]{1,0:T(8,128)(2,1)S(1)} collective-permute-done((bf16[192,512]{1,0:T(8,128)(2,1)}, bf16[192,512]{1,0:T(8,128)(2,1)S(1)}, u32[]{:S(2)}, u32[]{:S(2)}) %collective-permute-start.1) | collective-permute-done | bytes 196640 | tf_op jit(solution)/shard_map/ppermute | solution.py:481
  27.3 0.0 collective-permute-done
  27.3 1.9 %shard_map.122 = bf16[16,32,768]{2,1,0:T(8,128)(2,1)} custom-call(bf16[16,16,768]{2,1,0:T(8,128)(2,1)} %bitcast.20, bf16[16,16,768]{2,1,0:T(8,128)(2,1)S(1)} %bitcast.18, bf16[512,3584]{1,0:T(8,128)(2,1)} %shard_map.120.refs_2_.refs_3_.refs_1_.weight_ref, bf16[192,512]{1,0:T(8,128)(2,1)S(1)} %collective-permute-done.1.refs_3_.refs_1_.refs_5_), custom_call_target="tpu_custom_call" | custom-call | bytes 1572864 | tf_op jit(solution)/shard_map/pallas_call | solution.py:217
  29.2 4.1 %all-to-all-done.1 = bf16[16,16,1920]{2,1,0:T(8,128)(2,1)S(1)} async-done(((bf16[16,16,1920]{2,1,0:T(8,128)(2,1)}), bf16[16,16,1920]{2,1,0:T(8,128)(2,1)S(1)}, u32[]{:S(2)}, u32[]{:S(2)}) %all-to-all-start.1) | async-done | bytes 983072 | tf_op jit(solution)/shard_map/all_to_all | solution.py:484
  33.3 6.5 %all-to-all-start = ((bf16[16,32,768]{2,1,0:T(8,128)(2,1)}), bf16[16,32,768]{2,1,0:T(8,128)(2,1)S(1)}, u32[]{:S(2)}, u32[]{:S(2)}) async-start(bf16[16,32,768]{2,1,0:T(8,128)(2,1)} %shard_map.122), calls=%async_computation | async-start | bytes 1572864 | tf_op jit(solution)/shard_map/all_to_all | solution.py:484
  39.9 1.6 %collective-permute-start.2 = (bf16[256,1152]{1,0:T(8,128)(2,1)S(1)}, bf16[256,1152]{1,0:T(8,128)(2,1)S(1)}, u32[]{:S(2)}, u32[]{:S(2)}) collective-permute-start(bf16[256,1152]{1,0:T(8,128)(2,1)S(1)} %slice.8), channel_id=1, source_target_pairs={{0,16},{16,0},{1,17},{17,1},{2,18},{18,2},{3,19},{19,3},{4,20},{20... | collective-permute-start | bytes 1769480 | tf_op jit(solution)/shard_map/ppermute | solution.py:481
  41.5 0.6 collective-permute-start.3
  42.1 4.0 %shard_map.123 = (bf16[192,1024]{1,0:T(8,128)(2,1)}, bf16[192,1536]{1,0:T(8,128)(2,1)}, f32[192,512]{1,0:T(8,128)}) custom-call(bf16[256,1920]{1,0:T(8,128)(2,1)S(1)} %bitcast.14, bf16[256,1920]{1,0:T(8,128)(2,1)S(1)} %bitcast.15, bf16[512,3584]{1,0:T(8,128)(2,1)} %shard_map.120.refs_2_.refs_3_.refs_1_.weight_ref, ...), custom_call_target="tpu_custom_call" | custom-call | flops 1006632960 | bytes 5373952 | tf_op jit(solution)/shard_map/pallas_call | solution.py:300
  46.1 0.0 copy-start
  46.1 18.0 %collective-permute-done.3.refs_0_ = bf16[256,768]{1,0:T(8,128)(2,1)S(1)} collective-permute-done((bf16[256,768]{1,0:T(8,128)(2,1)S(1)}, bf16[256,768]{1,0:T(8,128)(2,1)S(1)}, u32[]{:S(2)}, u32[]{:S(2)}) %collective-permute-start.3) | collective-permute-done | bytes 393248 | tf_op jit(solution)/shard_map/ppermute | solution.py:481
  64.1 2.6 %shard_map.124 = (bf16[192,1024]{1,0:T(8,128)(2,1)}, f32[192,512]{1,0:T(8,128)}) custom-call(bf16[256,768]{1,0:T(8,128)(2,1)S(1)} %collective-permute-done.3.refs_0_, bf16[512,3584]{1,0:T(8,128)(2,1)} %shard_map.120.refs_2_.refs_3_.refs_1_.weight_ref), custom_call_target="tpu_custom_call" | custom-call | flops 402653184 | bytes 2621440 | tf_op jit(solution)/shard_map/pallas_call | solution.py:300
  66.7 0.0 copy-done
  66.7 4.9 %shard_map.126 = (f32[1,512,3584]{2,1,0:T(8,128)}, bf16[1,512,3584]{2,1,0:T(8,128)(2,1)}, bf16[1,512,3584]{2,1,0:T(8,128)(2,1)}) custom-call(bf16[192,512]{1,0:T(8,128)(2,1)S(1)} %copy-done, bf16[192,512]{1,0:T(8,128)(2,1)S(1)} %collective-permute-done.1.refs_3_.refs_1_.refs_5_, bf16[192,1024]{1,0:T(8,128)(2,1)} %get-tuple-element.37.refs_2_, ...), custom_call_target="tpu_custom_call" | custom-call | flops 402653184 | bytes 8388608 | tf_op jit(solution)/shard_map/pallas_call | solution.py:395
  71.6 0.0 collective-permute-done.2.refs_0_
  71.7 3.2 %shard_map.125 = (bf16[192,1536]{1,0:T(8,128)(2,1)}, f32[192,512]{1,0:T(8,128)}) custom-call(bf16[256,1152]{1,0:T(8,128)(2,1)S(1)} %collective-permute-done.2.refs_0_, bf16[512,3584]{1,0:T(8,128)(2,1)} %shard_map.120.refs_2_.refs_3_.refs_1_.weight_ref, f32[192,512]{1,0:T(8,128)} %get-tuple-element.34.refs_2_), custom_call_target="tpu_custom_call" | custom-call | flops 603979776 | bytes 3538944 | tf_op jit(solution)/shard_map/pallas_call | solution.py:300
  74.9 0.0 all-to-all-done
  74.9 3.8 %shard_map.127 = (f32[32,1,128]{2,1,0:T(1,128)}, bf16[192,1024]{1,0:T(8,128)(2,1)}, bf16[192,1024]{1,0:T(8,128)(2,1)}, bf16[192,512]{1,0:T(8,128)(2,1)}, bf16[192,512]{1,0:T(8,128)(2,1)}) custom-call(bf16[512,3584]{1,0:T(8,128)(2,1)} %shard_map.120.refs_2_.refs_3_.refs_1_.weight_ref, bf16[16,2,16,768]{3,2,1,0:T(8,128)(2,1)S(1)} %bitcast.16, ...), custom_call_target="tpu_custom_call" | custom-call | flops 805306368 | bytes 4980736 | tf_op jit(solution)/shard_map/pallas_call | solution.py:350
  78.7 1.5 %collective-permute-start.4 = (bf16[192,512]{1,0:T(8,128)(2,1)}, bf16[192,512]{1,0:T(8,128)(2,1)S(1)}, u32[]{:S(2)}, u32[]{:S(2)}) collective-permute-start(bf16[192,512]{1,0:T(8,128)(2,1)} %get-tuple-element.41), channel_id=1, source_target_pairs={{0,16},{16,0},{1,17},{17,1},{2,18},{18,2},{3,19},{19,3},{4,20},{20... | collective-permute-start | bytes 589832 | tf_op jit(solution)/shard_map/ppermute | solution.py:481
  80.2 4.7 %all-to-all-start.2 = ((f32[32,1,128]{2,1,0:T(1,128)}), f32[32,1,128]{2,1,0:T(1,128)S(1)}, u32[]{:S(2)}, u32[]{:S(2)}) async-start(f32[32,1,128]{2,1,0:T(1,128)} %get-tuple-element.42), calls=%async_computation.2 | async-start | bytes 32768 | tf_op jit(solution)/shard_map/all_to_all | solution.py:519
  84.9 8.1 %shard_map.130 = (f32[1,512,3584]{2,1,0:T(8,128)}, bf16[1,512,3584]{2,1,0:T(8,128)(2,1)}, bf16[1,512,3584]{2,1,0:T(8,128)(2,1)}) custom-call(bf16[192,512]{1,0:T(8,128)(2,1)S(1)} %copy-done, bf16[192,512]{1,0:T(8,128)(2,1)S(1)} %collective-permute-done.1.refs_3_.refs_1_.refs_5_, ...), custom_call_target="tpu_custom_call", output_to_operand_aliasing={{0}: (7, {}), {1}: (8, {}), {2}: (9, {})} | custom-call | flops 603979776 | bytes 12582912 | tf_op jit(solution)/shard_map/pallas_call | solution.py:395
  93.0 5.0 %shard_map.131 = (f32[1,512,3584]{2,1,0:T(8,128)}, bf16[1,512,3584]{2,1,0:T(8,128)(2,1)}, bf16[1,512,3584]{2,1,0:T(8,128)(2,1)}) custom-call(bf16[192,512]{1,0:T(8,128)(2,1)S(1)} %copy-done, bf16[192,512]{1,0:T(8,128)(2,1)S(1)} %collective-permute-done.1.refs_3_.refs_1_.refs_5_, ...), custom_call_target="tpu_custom_call", output_to_operand_aliasing={{0}: (7, {}), {1}: (8, {}), {2}: (9, {})} | custom-call | flops 402653184 | bytes 8388608 | tf_op jit(solution)/shard_map/pallas_call | solution.py:395
  98.0 0.0 all-to-all-done.2
  98.0 2.0 %shard_map.129 = f32[8,256]{1,0:T(8,128)} custom-call(s32[8,256]{1,0:T(8,128)} %bitcast.26, s32[8,256]{1,0:T(8,128)} %bitcast.28, bf16[8,256]{1,0:T(8,128)(2,1)} %bitcast.30, f32[2,16,1,128]{3,2,1,0:T(1,128)S(1)} %bitcast.19), custom_call_target="tpu_custom_call" | custom-call | flops 16777216 | bytes 65536 | tf_op jit(solution)/shard_map/pallas_call | solution.py:458
  100.0 0.0 collective-permute-done.4.refs_1_
  100.0 2.5 %shard_map.128 = bf16[192,2048]{1,0:T(8,128)(2,1)} custom-call(bf16[192,2048]{1,0:T(8,128)(2,1)} %bitcast.22, bf16[192,512]{1,0:T(8,128)(2,1)} %get-tuple-element.40.refs_0_, bf16[192,512]{1,0:T(8,128)(2,1)S(1)} %collective-permute-done.4.refs_1_), custom_call_target="tpu_custom_call" | custom-call | flops 4718592 | bytes 1966080 | tf_op jit(solution)/shard_map/pallas_call | solution.py:424
  (2 shorter events, 0.1 us)
Async XLA Ops:
  4.1 29.2 %all-to-all-start.1 = ((bf16[16,16,1920]{2,1,0:T(8,128)(2,1)}), bf16[16,16,1920]{2,1,0:T(8,128)(2,1)S(1)}, u32[]{:S(2)}, u32[]{:S(2)}) async-start(bf16[16,16,1920]{2,1,0:T(8,128)(2,1)} %bitcast.23), calls=%async_computation.1 | async-start | bytes 1966080 | tf_op jit(solution)/shard_map/all_to_all | solution.py:484
  11.5 15.9 %collective-permute-start = (bf16[256,768]{1,0:T(8,128)(2,1)}, bf16[256,768]{1,0:T(8,128)(2,1)S(1)}, u32[]{:S(2)}, u32[]{:S(2)}) collective-permute-start(bf16[256,768]{1,0:T(8,128)(2,1)} %get-tuple-element.30.after_ref), channel_id=1, source_target_pairs={{0,16},{16,0},{1,17},{17,1},{2,18},{18,2},{3,19},{19,3},{4,20},{20... | collective-permute-start | bytes 1179656 | tf_op jit(solution)/shard_map/ppermute | solution.py:481
  15.0 12.3 %collective-permute-start.1 = (bf16[192,512]{1,0:T(8,128)(2,1)}, bf16[192,512]{1,0:T(8,128)(2,1)S(1)}, u32[]{:S(2)}, u32[]{:S(2)}) collective-permute-start(bf16[192,512]{1,0:T(8,128)(2,1)} %get-tuple-element.31), channel_id=1, source_target_pairs={{0,16},{16,0},{1,17},{17,1},{2,18},{18,2},{3,19},{19,3},{4,20},{20... | collective-permute-start | bytes 589832 | tf_op jit(solution)/shard_map/ppermute | solution.py:481
  33.3 41.5 %all-to-all-start = ((bf16[16,32,768]{2,1,0:T(8,128)(2,1)}), bf16[16,32,768]{2,1,0:T(8,128)(2,1)S(1)}, u32[]{:S(2)}, u32[]{:S(2)}) async-start(bf16[16,32,768]{2,1,0:T(8,128)(2,1)} %shard_map.122), calls=%async_computation | async-start | bytes 1572864 | tf_op jit(solution)/shard_map/all_to_all | solution.py:484
  39.9 31.7 %collective-permute-start.2 = (bf16[256,1152]{1,0:T(8,128)(2,1)S(1)}, bf16[256,1152]{1,0:T(8,128)(2,1)S(1)}, u32[]{:S(2)}, u32[]{:S(2)}) collective-permute-start(bf16[256,1152]{1,0:T(8,128)(2,1)S(1)} %slice.8), channel_id=1, source_target_pairs={{0,16},{16,0},{1,17},{17,1},{2,18},{18,2},{3,19},{19,3},{4,20},{20... | collective-permute-start | bytes 1769480 | tf_op jit(solution)/shard_map/ppermute | solution.py:481
  41.5 22.5 %collective-permute-start.3 = (bf16[256,768]{1,0:T(8,128)(2,1)S(1)}, bf16[256,768]{1,0:T(8,128)(2,1)S(1)}, u32[]{:S(2)}, u32[]{:S(2)}) collective-permute-start(bf16[256,768]{1,0:T(8,128)(2,1)S(1)} %slice.9), channel_id=1, source_target_pairs={{0,16},{16,0},{1,17},{17,1},{2,18},{18,2},{3,19},{19,3},{4,20},{20... | collective-permute-start | bytes 1179656 | tf_op jit(solution)/shard_map/ppermute | solution.py:481
  46.1 20.6 %copy-start = (bf16[192,512]{1,0:T(8,128)(2,1)S(1)}, bf16[192,512]{1,0:T(8,128)(2,1)}, u32[]{:S(2)}) copy-start(bf16[192,512]{1,0:T(8,128)(2,1)} %get-tuple-element.36.refs_0_.refs_4_) | copy-start | bytes 589828
  78.7 21.4 %collective-permute-start.4 = (bf16[192,512]{1,0:T(8,128)(2,1)}, bf16[192,512]{1,0:T(8,128)(2,1)S(1)}, u32[]{:S(2)}, u32[]{:S(2)}) collective-permute-start(bf16[192,512]{1,0:T(8,128)(2,1)} %get-tuple-element.41), channel_id=1, source_target_pairs={{0,16},{16,0},{1,17},{17,1},{2,18},{18,2},{3,19},{19,3},{4,20},{20... | collective-permute-start | bytes 589832 | tf_op jit(solution)/shard_map/ppermute | solution.py:481
  80.2 17.8 %all-to-all-start.2 = ((f32[32,1,128]{2,1,0:T(1,128)}), f32[32,1,128]{2,1,0:T(1,128)S(1)}, u32[]{:S(2)}, u32[]{:S(2)}) async-start(f32[32,1,128]{2,1,0:T(1,128)} %get-tuple-element.42), calls=%async_computation.2 | async-start | bytes 32768 | tf_op jit(solution)/shard_map/all_to_all | solution.py:519

commit v4 on v3

v4 whole, which is shorter than its diff:
```python
import functools

import jax
import jax.numpy as jnp
from jax import lax
from jax.experimental import pallas as pl
from jax.experimental.pallas import tpu as pltpu
from jax.sharding import PartitionSpec as P

TOPK = 8
EXP_LOCAL = 8
SEND = 12
LANE = 128
UNIT = 512
MIX_COST = 50
SETTLE_COST = 44
ROWS = 16

beta_one = 0.9
beta_two = 0.95
learn_rate = 0.002
decay_rate = 0.1
adam_eps = 1e-08
adam_step = 50

f32 = jnp.float32
bf16 = jnp.bfloat16
HBM = pl.BlockSpec(memory_space=pltpu.HBM)
ANY = pl.BlockSpec(memory_space=pl.ANY)


def in_hbm(*arrays):
    return [pltpu.with_memory_space_constraint(array, pltpu.HBM) for array in arrays]


def out_hbm(dims, dtype):
    return pltpu.HBM(tuple(dims), dtype)


def block(dims, at=None):
    at = at or (0,) * len(dims)
    return pl.BlockSpec(tuple(dims), lambda i: at, pipeline_mode=pl.Buffered(1))


def params(nbytes):
    mib = min(60, max(16, 10 + 5 * int(nbytes) // 2**22))
    return pltpu.CompilerParams(vmem_limit_bytes=mib * 2**20)


def cost(flops, nbytes, transcendentals=0):
    return pl.CostEstimate(
        flops=int(flops), bytes_accessed=int(nbytes), transcendentals=int(transcendentals)
    )


def div_send(index):
    return lax.shift_right_logical(index * 10923, 17)


def pack(cols):
    return cols // 4 * 3


def chunk_edges(width):
    units = width // UNIT
    return (0, (units - max(1, units * 3 // 7)) * UNIT, width)


def tail_order(count, total, j, slots_first):
    a = lax.broadcasted_iota(jnp.int32, (count, total), 0)
    b = lax.broadcasted_iota(jnp.int32, (count, total), 1)
    if slots_first:
        block_of = div_send(a)
        inner = a - SEND * block_of
        hit = b == block_of * ROWS + SEND + inner - 4 * j
    else:
        inner = (a & (ROWS - 1)) - SEND + 4 * j
        hit = (b == a - SEND + 4 * j) & ((a & (ROWS - 1)) >= SEND)
    return jnp.where(hit & (inner >= 4 * j) & (inner < 4 * j + 4), 1.0, 0.0).astype(bf16)


def dispatch_kernel(edges, ids_hbm, slots_hbm, gates_hbm, grad_hbm, *refs):
    outs, (ids_ref, slots_ref, gates_ref, grad_ref) = refs[:2], refs[2:6]
    sends, sems, out_sems = refs[6:8], refs[8], refs[9]
    pairs = [
        (ids_hbm, ids_ref),
        (slots_hbm, slots_ref),
        (gates_hbm, gates_ref),
        (grad_hbm, grad_ref),
    ]
    copies = [
        pltpu.make_async_copy(source, target, sems.at[i])
        for i, (source, target) in enumerate(pairs)
    ]
    for copy in copies:
        copy.start()
    rows = outs[0].shape[0]
    tok = ids_ref.shape[1]
    orders = [tail_order(rows, rows, j, False) for j in range(3)]
    for copy in copies[:3]:
        copy.wait()
    ids = ids_ref[...]
    slots = slots_ref[...]
    gates = gates_ref[...].astype(f32)
    live = ((ids & (EXP_LOCAL - 1)) == 0) & (slots >= 0)
    place = jnp.where(live, ids // EXP_LOCAL * ROWS + slots, -1)
    row = lax.broadcasted_iota(jnp.int32, (rows, tok), 0)
    main = jnp.zeros((rows, tok), f32)
    for k in range(TOPK):
        main = jnp.where(row == place[k : k + 1], gates[k : k + 1], main)
    main = main.astype(bf16)
    tails = [
        jnp.dot(order, main, preferred_element_type=f32).astype(bf16) for order in orders
    ]
    copies[3].wait()
    out_copies = []
    for c in (1, 0):
        low, high = edges[c], edges[c + 1]
        part = (high - low) // 4
        for j in range(3):
            total = jnp.dot(
                main,
                grad_ref[:, low + j * part : low + (j + 1) * part],
                preferred_element_type=f32,
            )
            total += jnp.dot(
                tails[j], grad_ref[:, low + 3 * part : high], preferred_element_type=f32
            )
            own = (slice(None), pl.ds(j * part, part))
            sends[c][own] = total.astype(bf16)
            copy = pltpu.make_async_copy(
                sends[c].at[own], outs[c].at[own], out_sems.at[c, j]
            )
            copy.start()
            out_copies.append(copy)
    for copy in out_copies:
        copy.wait()


def dispatch(blocks, edges, ids, slots, gates, out_grad):
    tok, width = out_grad.shape
    rows = blocks * ROWS
    shapes = [(rows, pack(high - low)) for low, high in zip(edges[:-1], edges[1:])]
    return pl.pallas_call(
        functools.partial(dispatch_kernel, edges),
        in_specs=[HBM] * 4,
        out_specs=[HBM] * 2,
        out_shape=[out_hbm(shape, bf16) for shape in shapes],
        scratch_shapes=[
            pltpu.VMEM(ids.shape, jnp.int32),
            pltpu.VMEM(slots.shape, jnp.int32),
            pltpu.VMEM(gates.shape, bf16),
            pltpu.VMEM(out_grad.shape, bf16),
        ]
        + [pltpu.VMEM(shape, bf16) for shape in shapes]
        + [pltpu.SemaphoreType.DMA((4,)), pltpu.SemaphoreType.DMA((2, 3))],
        compiler_params=params(2 * rows * width + 2 * tok * width),
        cost_estimate=cost(2 * rows * tok * width, 4 * tok * width),
    )(*in_hbm(ids, slots, gates, out_grad))


def swiglu_part(gate_up_ref, shards, step, part):
    at = lax.rem(lax.axis_index("rep") + step, shards)
    low = pl.multiple_of(at * part, part)
    high = pl.multiple_of((shards + at) * part, part)
    gate = gate_up_ref[:, pl.ds(low, part)].astype(f32)
    up = gate_up_ref[:, pl.ds(high, part)].astype(f32)
    return low, high, gate, up, jax.nn.sigmoid(gate)


def hidden_kernel(gate_up_ref, after_ref, *out_refs):
    del after_ref
    for s, out_ref in enumerate(out_refs):
        _, _, gate, up, sig = swiglu_part(gate_up_ref, len(out_refs), s, out_ref.shape[1])
        out_ref[...] = (gate * sig * up).astype(bf16)


def hidden_parts(gate_up, shards, after):
    slots, width = gate_up.shape
    shape = (slots, width // 2 // shards)
    return pl.pallas_call(
        hidden_kernel,
        grid=(1,),
        in_specs=[block(gate_up.shape), HBM],
        out_specs=[block(shape)] * shards,
        out_shape=[out_hbm(shape, bf16)] * shards,
        compiler_params=params(3 * slots * width),
        cost_estimate=cost(8 * slots * width, 3 * slots * width, slots * width),
    )(*in_hbm(gate_up, after))


def cast_kernel(master_ref, after_ref, weight_ref):
    del after_ref
    weight_ref[...] = master_ref[0].astype(bf16)


def cast_weight(master, after):
    _, part, width = master.shape
    rows = part // 4
    return pl.pallas_call(
        cast_kernel,
        grid=(4,),
        in_specs=[pl.BlockSpec((1, rows, width), lambda i: (0, i, 0)), HBM],
        out_specs=pl.BlockSpec((rows, width), lambda i: (i, 0)),
        out_shape=out_hbm((part, width), bf16),
        compiler_params=params(6 * rows * width),
        cost_estimate=cost(part * width, 6 * part * width),
    )(*in_hbm(master, after))


def mixed_place(index, shards):
    group = div_send(index)
    bits = shards.bit_length() - 1
    step = group & (shards - 1)
    return lax.shift_right_logical(group, bits), step, index - SEND * group


def mix_kernel(shards, *refs):
    parts, out_ref = refs[:shards], refs[-1]
    part = parts[0].shape[1] // 3
    blocks = parts[0].shape[0] // ROWS
    some = max(1, min(blocks, 32 // shards))
    rows, packed = some * shards * SEND, some * shards * ROWS
    row = lax.broadcasted_iota(jnp.int32, (rows, packed), 0)
    col = lax.broadcasted_iota(jnp.int32, (rows, packed), 1)
    at, step, slot = mixed_place(row, shards)
    base = (step * some + at) * ROWS
    orders = [jnp.where(col == base + slot, 1.0, 0.0).astype(bf16)]
    for j in range(3):
        hit = (col == base + SEND + slot - 4 * j) & (slot >= 4 * j) & (slot < 4 * j + 4)
        orders.append(jnp.where(hit, 1.0, 0.0).astype(bf16))
    for first in range(0, blocks, some):
        stack = jnp.concatenate(
            [ref[first * ROWS : (first + some) * ROWS, :] for ref in parts], axis=0
        )
        own = slice(first * shards * SEND, (first + some) * shards * SEND)
        out_ref[own, : 3 * part] = jnp.dot(
            orders[0], stack, preferred_element_type=f32
        ).astype(bf16)
        tail = jnp.zeros((rows, part), f32)
        for j in range(3):
            tail += jnp.dot(
                orders[1 + j],
                stack[:, j * part : (j + 1) * part],
                preferred_element_type=f32,
            )
        out_ref[own, 3 * part :] = tail.astype(bf16)


def mix(parts, weight, after):
    shards = len(parts)
    rows, packed = parts[0].shape
    shape = (rows // ROWS * SEND * shards, packed // 3 * 4)
    return pl.pallas_call(
        functools.partial(mix_kernel, shards),
        grid=(1,),
        in_specs=[block(part.shape) for part in parts] + [HBM] + [ANY] * len(after),
        out_specs=block(shape),
        out_shape=out_hbm(shape, bf16),
        compiler_params=params(12 * rows * packed * shards),
        cost_estimate=cost(0, MIX_COST * rows * packed * shards),
    )(*in_hbm(parts[0]), *parts[1:], *in_hbm(weight), *after)


def reorder(arrived, rows_ref):
    count, width = rows_ref.shape
    part = width // 4
    total = arrived.shape[0]
    slot = lax.broadcasted_iota(jnp.int32, (count, total), 0)
    col = lax.broadcasted_iota(jnp.int32, (count, total), 1)
    order = jnp.where(col == slot + (ROWS - SEND) * div_send(slot), 1.0, 0.0).astype(bf16)
    rows_ref[:, : 3 * part] = jnp.dot(order, arrived, preferred_element_type=f32).astype(bf16)
    tail = jnp.zeros((count, part), f32)
    for j in range(3):
        tail += jnp.dot(
            tail_order(count, total, j, True),
            arrived[:, j * part : (j + 1) * part],
            preferred_element_type=f32,
        )
    rows_ref[:, 3 * part :] = tail.astype(bf16)


def times_weight(rows_ref, weight_ref):
    return lax.dot_general(
        rows_ref[...], weight_ref[...], (((1,), (1,)), ((), ())), preferred_element_type=f32
    )


def score_block(blocks, proj, hidden, picked):
    count = proj.shape[0]
    score = jnp.sum(proj * hidden.astype(f32), axis=1, keepdims=True)
    row = lax.broadcasted_iota(jnp.int32, (count, LANE), 0)
    lane = lax.broadcasted_iota(jnp.int32, (count, LANE), 1)
    spread = jnp.where(row - SEND * div_send(row) == lane, score, 0.0)
    at = lax.broadcasted_iota(jnp.int32, (blocks, count), 1)
    out = []
    for pick in picked:
        gather = (div_send(at) == pick).astype(f32)
        value = jnp.dot(
            gather, spread, precision=lax.Precision.HIGHEST, preferred_element_type=f32
        )
        out.append(value.reshape(blocks, 1, LANE))
    return out


def block_index(blocks, count):
    return lax.broadcasted_iota(jnp.int32, (blocks, count), 0)


def begin_kernel(blocks, arrived_ref, weight_ref, *refs):
    hidden, (rows_ref, proj_ref, score_ref, mixed_ref) = refs[:-4], refs[-4:]
    reorder(arrived_ref[...], rows_ref)
    proj = times_weight(rows_ref, weight_ref)
    proj_ref[...] = proj
    count = proj.shape[0]
    score_ref[...] = score_block(
        blocks, proj, hidden[0][...], [block_index(blocks, count)]
    )[0]
    shards = len(hidden)
    row = lax.broadcasted_iota(jnp.int32, (shards * count, count), 0)
    col = lax.broadcasted_iota(jnp.int32, (shards * count, count), 1)
    at, step, slot = mixed_place(row, shards)
    mixed = 0.0
    for s in range(shards):
        order = jnp.where((step == s) & (col == at * SEND + slot), 1.0, 0.0).astype(bf16)
        mixed += jnp.dot(order, hidden[s][...], preferred_element_type=f32)
    mixed_ref[...] = mixed.astype(bf16)


def begin(blocks, cols, arrived, weight, hidden):
    count = blocks * SEND
    part = weight.shape[0]
    shards = len(hidden)
    out = [
        ((count, cols), bf16),
        ((count, part), f32),
        ((blocks, 1, LANE), f32),
        ((shards * count, part), bf16),
    ]
    nbytes = 4 * count * cols + 2 * part * cols + 4 * count * part * (1 + 3 * shards)
    return pl.pallas_call(
        functools.partial(begin_kernel, blocks),
        grid=(1,),
        in_specs=[block(arrived.shape), block((part, cols))]
        + [block((count, part))] * shards,
        out_specs=[block(shape) for shape, _ in out],
        out_shape=[out_hbm(shape, dtype) for shape, dtype in out],
        compiler_params=params(nbytes),
        cost_estimate=cost(4 * count * part * cols, nbytes),
    )(arrived, *in_hbm(weight, hidden[0]), *hidden[1:])


def finish_kernel(shards, blocks, low, arrived_ref, hidden_ref, weight_ref, *refs):
    before, score_in = refs[:shards], refs[shards : 2 * shards]
    projs, score_ref = refs[2 * shards : 3 * shards], refs[-1]
    proj = times_weight(arrived_ref, weight_ref)
    rounded = proj.astype(bf16)
    total = proj.shape[0]
    count = total // shards
    picked = [block_index(blocks, total) * shards + s for s in range(shards)]
    scores = score_block(blocks, proj, hidden_ref[...], picked)
    me = lax.axis_index("rep")
    slot = lax.broadcasted_iota(jnp.int32, (count, total), 0)
    row = lax.broadcasted_iota(jnp.int32, (count, total), 1)
    for s in range(shards):
        order = row == slot + SEND * (div_send(slot) * (shards - 1) + s)
        order = jnp.where(order, 1.0, 0.0).astype(bf16)
        own = before[s][...] + jnp.dot(order, rounded, preferred_element_type=f32)
        projs[s][...] = own.astype(bf16)
        at = lax.rem(me + shards - s, shards)
        score_ref[pl.ds(at * blocks, blocks)] = score_in[s][...] + scores[s]


def finish(edges, blocks, arrived, hidden, weight, before, scores):
    low, high = edges[-2:]
    shards = len(before)
    total, part = hidden.shape
    count = total // shards
    out = [((count, part), bf16)] * shards + [((shards * blocks, 1, LANE), f32)]
    nbytes = 2 * (total + part) * (high - low) + 14 * total * part
    outs = pl.pallas_call(
        functools.partial(finish_kernel, shards, blocks, low),
        grid=(1,),
        in_specs=[
            block(arrived.shape),
            block(hidden.shape),
            pl.BlockSpec(
                (pl.Element(part), pl.Element(high - low)),
                lambda i: (0, low),
                pipeline_mode=pl.Buffered(1),
            ),
        ]
        + [block((count, part))] * shards
        + [block((blocks, 1, LANE))] * shards,
        out_specs=[block(shape) for shape, _ in out],
        out_shape=[out_hbm(shape, dtype) for shape, dtype in out[:-1]]
        + [jax.ShapeDtypeStruct(*out[-1])],
        compiler_params=params(nbytes),
        cost_estimate=cost(2 * total * part * (high - low), nbytes),
    )(*in_hbm(arrived, hidden, weight, *before, *scores))
    return list(outs[:-1]), outs[-1]


def settle_kernel(low, fresh, blocks, *refs):
    refs = list(refs)

    def take(number):
        out = refs[:number]
        del refs[:number]
        return out

    arrived = take(len(fresh))
    hidden = take(1 + len(fresh))
    given_hbm, *state_hbm = take(4)
    weight_hbm = take(1)[0] if fresh else None
    take(3 if low else 0)
    projs, scores, outs = take(len(fresh)), take(len(fresh)), take(3)
    rows_ref, hidden_t, weight_ref = take(3)
    state, news = take(3), take(3)
    sem, in_sems, out_sems = refs
    cols = rows_ref.shape[1]
    given = given_hbm.shape[0]
    loads = [
        pltpu.make_async_copy(given_hbm, rows_ref.at[pl.ds(0, given)], sem.at[0])
    ]
    if fresh:
        loads.append(
            pltpu.make_async_copy(weight_hbm.at[:, pl.ds(low, cols)], weight_ref, sem.at[1])
        )
    for copy in loads:
        copy.start()

    def load(i):
        return [
            pltpu.make_async_copy(
                source.at[0, :, pl.ds(low + i * UNIT, UNIT)],
                target.at[:, pl.ds(i * UNIT, UNIT)],
                in_sems.at[j, i],
            )
            for j, (source, target) in enumerate(zip(state_hbm, state))
        ]

    def store(i):
        return [
            pltpu.make_async_copy(
                source.at[:, pl.ds(i * UNIT, UNIT)],
                target.at[0, :, pl.ds(low + i * UNIT, UNIT)],
                out_sems.at[j, i],
            )
            for j, (source, target) in enumerate(zip(news, outs))
        ]

    units = cols // UNIT
    for i in range(units):
        for copy in load(i):
            copy.start()
    base = 0
    for ref in hidden:
        count = ref.shape[0]
        hidden_t[:, base : base + count] = ref[...].astype(f32).T.astype(bf16)
        base += count
    for copy in loads:
        copy.wait()
    base = given
    for i, arrived_ref in enumerate(arrived):
        count = blocks * SEND
        own = rows_ref.at[base : base + count]
        base += count
        reorder(arrived_ref[...], own)
        proj = times_weight(own, weight_ref)
        projs[i][...] = proj
        scores[i][...] = score_block(
            blocks, proj, hidden[1 + i][...], [block_index(blocks, count)]
        )[0]

    corr_one = 1.0 - beta_one**adam_step
    corr_two = 1.0 - beta_two**adam_step
    rate = learn_rate * corr_two**0.5 / corr_one
    keep = 1.0 - learn_rate * decay_rate
    for i in range(units):
        for copy in load(i):
            copy.wait()
        own = slice(i * UNIT, (i + 1) * UNIT)
        grad = jnp.dot(hidden_t[...], rows_ref[:, own], preferred_element_type=f32)
        m_new = beta_one * state[1][:, own].astype(f32) + (1.0 - beta_one) * grad
        v_new = beta_two * state[2][:, own].astype(f32) + (1.0 - beta_two) * (grad * grad)
        root = v_new * lax.rsqrt(v_new) + adam_eps * corr_two**0.5
        news[0][:, own] = keep * state[0][:, own] - rate * m_new / root
        news[1][:, own] = m_new.astype(bf16)
        news[2][:, own] = v_new.astype(bf16)
        for copy in store(i):
            copy.start()
    for i in range(units):
        for copy in store(i):
            copy.wait()


def settle(low, blocks, arrived, given, hidden, weight, state, done):
    cols = given.shape[1]
    part = weight.shape[0]
    count = blocks * SEND
    fresh = tuple(range(1, 1 + len(arrived)))
    total = given.shape[0] + count * len(fresh)
    args = list(arrived) + in_hbm(hidden[0]) + list(hidden[1:])
    specs = [block(array.shape) for array in args]
    args += in_hbm(given, *state, *([weight] if fresh else []), *done)
    specs += [HBM] * (4 + bool(fresh) + len(done))
    out = [((count, part), f32)] * len(fresh) + [((blocks, 1, LANE), f32)] * len(fresh)
    kinds = [f32, bf16, bf16]
    scratch = [
        pltpu.VMEM((total, cols), bf16),
        pltpu.VMEM((part, total), bf16),
        pltpu.VMEM((part, cols) if fresh else (ROWS, LANE), bf16),
    ]
    scratch += [pltpu.VMEM((part, cols), kind) for kind in kinds * 2]
    scratch += [pltpu.SemaphoreType.DMA((2,))]
    scratch += [pltpu.SemaphoreType.DMA((3, cols // UNIT))] * 2
    nbytes = 18 * part * cols + 4 * total * cols + 8 * total * part
    outs = pl.pallas_call(
        functools.partial(settle_kernel, low, fresh, blocks),
        grid=(1,),
        in_specs=specs,
        out_specs=[block(shape) for shape, _ in out] + [HBM] * 3,
        out_shape=[out_hbm(shape, dtype) for shape, dtype in out]
        + [out_hbm(array.shape, array.dtype) for array in state],
        scratch_shapes=scratch,
        input_output_aliases={
            len(args) - len(done) + i: len(out) + i for i in range(len(done))
        },
        compiler_params=params(nbytes),
        cost_estimate=cost(4 * total * part * cols, SETTLE_COST * part * cols, part * cols),
    )(*args)
    outs = list(outs)
    return outs[: len(fresh)], outs[len(fresh) : 2 * len(fresh)], outs[-3:]


def close_kernel(shards, gate_up_ref, ids_ref, slots_ref, gates_ref, score_ref, *refs):
    grad_refs, (out_ref, gate_ref) = refs[:-2], refs[-2:]
    part = grad_refs[0].shape[1]
    for s, grad_ref in enumerate(grad_refs):
        low, high, gate, up, sig = swiglu_part(gate_up_ref, shards, s, part)
        grad = grad_ref[...].astype(f32)
        out_ref[:, pl.ds(low, part)] = (
            grad * up * sig * (1.0 + gate * (1.0 - sig))
        ).astype(bf16)
        out_ref[:, pl.ds(high, part)] = (grad * (gate * sig)).astype(bf16)

    blocks = score_ref.shape[1]
    score = score_ref[0].reshape(blocks, LANE)
    for s in range(1, shards):
        score += score_ref[s].reshape(blocks, LANE)
    ids = ids_ref[...]
    slots = slots_ref[...]
    tok = ids.shape[1]
    live = ((ids & (EXP_LOCAL - 1)) == 0) & (slots >= 0)
    owner = ids // EXP_LOCAL
    lane = lax.broadcasted_iota(jnp.int32, (LANE, tok), 0)
    block_of = lax.broadcasted_iota(jnp.int32, (blocks, tok), 0)
    for k in range(TOPK):
        pick = (lane == slots[k : k + 1]).astype(f32)
        value = jnp.dot(score, pick, precision=lax.Precision.HIGHEST, preferred_element_type=f32)
        value = jnp.where(block_of == owner[k : k + 1], value, 0.0)
        value = jnp.sum(value, axis=0, keepdims=True)
        gate_ref[k : k + 1] = jnp.where(
            live[k : k + 1], value / gates_ref[k : k + 1].astype(f32), 0.0
        )


def close(gate_up, ids, slots, gates, score, grads):
    size = gate_up.size
    args = in_hbm(gate_up, ids, slots, gates) + [score] + in_hbm(grads[0]) + grads[1:]
    shapes = [(gate_up.shape, bf16), (ids.shape, f32)]
    return pl.pallas_call(
        functools.partial(close_kernel, len(grads)),
        grid=(1,),
        in_specs=[block(array.shape) for array in args],
        out_specs=[block(shape) for shape, _ in shapes],
        out_shape=[out_hbm(shape, dtype) for shape, dtype in shapes],
        compiler_params=params(8 * size),
        cost_estimate=cost(12 * size, 5 * size, size),
    )(*args)


def per_device(out_grad, expert_ids, slots, gate_weights, saved_gate_up, master, moment1, moment2):
    ep_size = lax.axis_size("ep")
    rep_size = lax.axis_size("rep")
    ids_t, slots_t, gates_t = expert_ids.T, slots.T, gate_weights.T
    gate_up = saved_gate_up[0, 0]
    state = (master, moment1, moment2)
    edges = chunk_edges(out_grad.shape[1])
    steps = range(1, rep_size)

    def shift(value, step):
        perm = [(i, (i + step) % rep_size) for i in range(rep_size)]
        return lax.ppermute(value, "rep", perm)

    def exchange(value):
        return lax.all_to_all(value, "ep", split_axis=0, concat_axis=0, tiled=True)

    send_a, send_b = dispatch(ep_size, edges, ids_t, slots_t, gates_t, out_grad)
    mixed = [send_b] + [shift(send_b, s) for s in steps]
    parts = hidden_parts(gate_up, rep_size, send_b)
    hidden = [parts[0]] + [shift(parts[s], s) for s in steps]
    weight = cast_weight(master, send_b)
    arrived = exchange(send_a.reshape(ep_size, ROWS, -1)).reshape(send_a.shape)
    mixed = mix(mixed, weight, hidden[1:])
    arrived_b = exchange(mixed.reshape(ep_size, rep_size * SEND, -1)).reshape(mixed.shape)

    peers = [shift(arrived, s) for s in steps]
    rows, proj, score_own, hidden_mixed = begin(ep_size, edges[1], arrived, weight, hidden)
    before, scores, done = settle(0, ep_size, peers, rows, hidden, weight, state, ())
    projs, score = finish(
        edges,
        ep_size,
        arrived_b,
        hidden_mixed,
        weight,
        [proj] + before,
        [score_own] + scores,
    )
    grads = [projs[0]] + [shift(projs[s], rep_size - s) for s in steps]
    score = lax.all_to_all(score, ("rep", "ep"), split_axis=0, concat_axis=0, tiled=True)

    _, _, done = settle(
        edges[1], ep_size, [], arrived_b, [hidden_mixed], weight, state, done
    )
    grad_gate_up, gate_grad = close(
        gate_up, ids_t, slots_t, gates_t, score.reshape(rep_size, ep_size, 1, LANE), grads
    )
    return (grad_gate_up.reshape(saved_gate_up.shape), gate_grad.T) + tuple(done)


def solution(mesh):
    in_specs = (
        P(("rep", "ep"), None),
        P(("rep", "ep"), None),
        P(("rep", "ep"), None),
        P(("rep", "ep"), None),
        P("rep", "ep", None, None),
        P("ep", "rep", None),
        P("ep", "rep", None),
        P("ep", "rep", None),
    )
    out_specs = (
        P("rep", "ep", None, None),
        P(("rep", "ep"), None),
        P("ep", "rep", None),
        P("ep", "rep", None),
        P("ep", "rep", None),
    )
    return jax.shard_map(
        per_device, mesh=mesh, in_specs=in_specs, out_specs=out_specs, check_vma=False
    )
```

time: 103 us -> 96.9 us (0.941)
  waiting for transfers between devices: 28.5 us -> 24.9 us
  Pallas kernels: 48.9 us -> 46.4 us
  starting transfers between devices: 24.4 us -> 23.2 us
    all_to_all x2, waiting for transfers between devices: 4.09 us -> 0.01 us  [exchange(): return lax.all_to_all(value, 'ep', split_axis=0, concat_axis=0, tiled=True)]
    pallas_call x11 -> x7, Pallas kernels: 41.5 us -> 39.1 us  [the longest x2 20.7 us: settle(): pl.pallas_call(functools.partial(settle_kernel, low, fresh, blocks), grid...]
    ppermute x5 -> x4, starting transfers between devices: 5.77 us -> 5.19 us  [shift(): return lax.ppermute(value, 'rep', perm)]
    ppermute x5 -> x4, waiting for transfers between devices: 24.4 us -> 24.9 us  [shift(): return lax.ppermute(value, 'rep', perm)]
  transfers between devices with their start and end apart: 8 -> 7, of which waited for: 3 -> 2; matrix products, arithmetic and copies ran while one was open for 0% -> 0% of each run, Pallas kernels for 38% -> 37%
where the time goes in v4:
time: 96.9 us; the launch traced here: 96.3 us
  Pallas kernels  46.4 us (48%)
  waiting for transfers between devices  24.9 us (26%)
  starting transfers between devices  23.2 us (24%)
  local copies, waits for them, and re-layouts  1.02 us (1%)
    ppermute x4, waiting for transfers between devices, shift(): return lax.ppermute(value, 'rep', perm)  24.9 us
    pallas_call x2, Pallas kernels, settle(): pl.pallas_call(functools.partial(settle_kernel, low, fresh, blocks), grid...  20.7 us
    all_to_all x2, starting transfers between devices, exchange(): return lax.all_to_all(value, 'ep', split_axis=0, concat_axis=0, tiled=True)  13.1 us
    pallas_call x1, Pallas kernels, cast_weight(): pl.pallas_call(cast_kernel, grid=(4,), in_specs=[pl.BlockSpec((1, rows, w...  5.36 us
    ppermute x4, starting transfers between devices, shift(): return lax.ppermute(value, 'rep', perm)  5.19 us
    all_to_all x1, starting transfers between devices, per_device(): lax.all_to_all(score, ('rep', 'ep'), split_axis=0, concat_axis=0, tiled=T...  4.91 us
    pallas_call x1, Pallas kernels, finish(): pl.pallas_call(functools.partial(finish_kernel, shards, blocks, low), gri...  4.18 us
    pallas_call x1, Pallas kernels, begin(): pl.pallas_call(functools.partial(begin_kernel, blocks), grid=(1,), in_spe...  4.03 us
  transfers between devices with their start and end apart: 7, of which 2 were waited for; matrix products, arithmetic and copies ran while one was open for 0% of the time, Pallas kernels for 37%

profile of v4, /device:TPU:0, one launch (start us, length us, event | category | flops | bytes accessed | tf_op | source)
XLA Modules:
  0.0 96.3 jit_solution(10953441748110992615)
XLA Ops:
  0.6 3.3 %shard_map.119 = (bf16[256,1536]{1,0:T(8,128)(2,1)}, bf16[256,1152]{1,0:T(8,128)(2,1)}) custom-call(s32[8,256]{1,0:T(8,128)} %bitcast.20, s32[8,256]{1,0:T(8,128)} %bitcast.22, bf16[8,256]{1,0:T(8,128)(2,1)} %bitcast.24, bf16[256,3584]{1,0:T(8,128)(2,1)} %grad_hbm.1), custom_call_target="tpu_custom_call" | custom-call | flops 469762048 | bytes 3670016 | tf_op jit(solution)/shard_map/pallas_call | solution.py:144
  4.0 7.4 %all-to-all-start.1 = ((bf16[16,16,1536]{2,1,0:T(8,128)(2,1)}), bf16[16,16,1536]{2,1,0:T(8,128)(2,1)S(1)}, u32[]{:S(2)}, u32[]{:S(2)}) async-start(bf16[16,16,1536]{2,1,0:T(8,128)(2,1)} %bitcast.19), calls=%async_computation.1 | async-start | bytes 1572864 | tf_op jit(solution)/shard_map/all_to_all | solution.py:598
  11.3 1.6 %collective-permute-start = (bf16[256,1152]{1,0:T(8,128)(2,1)}, bf16[256,1152]{1,0:T(8,128)(2,1)S(1)}, u32[]{:S(2)}, u32[]{:S(2)}) collective-permute-start(bf16[256,1152]{1,0:T(8,128)(2,1)} %get-tuple-element.26.after_ref.refs_0_), channel_id=1, source_target_pairs={{0,16},{16,0},{1,17},{17,1},{2,18},{18,2},{3,19},{19,3},{4,20},{20... | collective-permute-start | bytes 1769480 | tf_op jit(solution)/shard_map/ppermute | solution.py:595
  12.9 2.0 %shard_map.121 = (bf16[192,512]{1,0:T(8,128)(2,1)}, bf16[192,512]{1,0:T(8,128)(2,1)}) custom-call(bf16[192,2048]{1,0:T(8,128)(2,1)} %bitcast.17, bf16[256,1152]{1,0:T(8,128)(2,1)} %get-tuple-element.26.after_ref.refs_0_), custom_call_target="tpu_custom_call" | custom-call | flops 3145728 | bytes 1179648 | tf_op jit(solution)/shard_map/pallas_call | solution.py:181
  14.9 0.5 collective-permute-start.1
  15.4 5.4 %shard_map.120.refs_2_.weight_ref.refs_7_ = bf16[512,3584]{1,0:T(8,128)(2,1)} custom-call(f32[1,512,3584]{2,1,0:T(8,128)} %refs_2_.1, bf16[256,1152]{1,0:T(8,128)(2,1)} %get-tuple-element.26.after_ref.refs_0_), custom_call_target="tpu_custom_call" | custom-call | flops 1835008 | bytes 11010048 | tf_op jit(solution)/shard_map/pallas_call | solution.py:200
  20.8 10.6 %collective-permute-done.1.refs_3_.refs_1_.refs_2_ = bf16[192,512]{1,0:T(8,128)(2,1)S(1)} collective-permute-done((bf16[192,512]{1,0:T(8,128)(2,1)}, bf16[192,512]{1,0:T(8,128)(2,1)S(1)}, u32[]{:S(2)}, u32[]{:S(2)}) %collective-permute-start.1) | collective-permute-done | bytes 196640 | tf_op jit(solution)/shard_map/ppermute | solution.py:595
  31.4 0.0 collective-permute-done.refs_1_
  31.4 3.4 %shard_map.122 = bf16[384,1536]{1,0:T(8,128)(2,1)} custom-call(bf16[256,1152]{1,0:T(8,128)(2,1)} %get-tuple-element.26.after_ref.refs_0_, bf16[256,1152]{1,0:T(8,128)(2,1)S(1)} %collective-permute-done.refs_1_, bf16[512,3584]{1,0:T(8,128)(2,1)} %shard_map.120.refs_2_.weight_ref.refs_7_, bf16[192,512]{1,0:T(8,128)(2,1)S(1)} %collective-permute-done.1.refs_3_.refs_1_.refs_2_), custom_call_target="tpu_custom_call" | custom-call | bytes 29491200 | tf_op jit(solution)/shard_map/pallas_call | solution.py:254
  34.8 0.0 all-to-all-done.1
  34.8 5.8 %all-to-all-start = ((bf16[16,24,1536]{2,1,0:T(8,128)(2,1)}), bf16[16,24,1536]{2,1,0:T(8,128)(2,1)S(1)}, u32[]{:S(2)}, u32[]{:S(2)}) async-start(bf16[16,24,1536]{2,1,0:T(8,128)(2,1)} %bitcast.16), calls=%async_computation | async-start | bytes 2359296 | tf_op jit(solution)/shard_map/all_to_all | solution.py:598
  40.6 1.6 %collective-permute-start.2 = (bf16[256,1536]{1,0:T(8,128)(2,1)S(1)}, bf16[256,1536]{1,0:T(8,128)(2,1)S(1)}, u32[]{:S(2)}, u32[]{:S(2)}) collective-permute-start(bf16[256,1536]{1,0:T(8,128)(2,1)S(1)} %bitcast.11), channel_id=1, source_target_pairs={{0,16},{16,0},{1,17},{17,1},{2,18},{18,2},{3,19},{19,3},{4,20},{20... | collective-permute-start | bytes 2359304 | tf_op jit(solution)/shard_map/ppermute | solution.py:595
  42.2 4.0 %shard_map.123 = (bf16[192,2048]{1,0:T(8,128)(2,1)}, f32[192,512]{1,0:T(8,128)}, f32[16,1,128]{2,1,0:T(1,128)}, bf16[384,512]{1,0:T(8,128)(2,1)}) custom-call(bf16[256,1536]{1,0:T(8,128)(2,1)S(1)} %bitcast.12, bf16[512,3584]{1,0:T(8,128)(2,1)} %shard_map.120.refs_2_.weight_ref.refs_7_, bf16[192,512]{1,0:T(8,128)(2,1)} %get-tuple-element.29.refs_0_.refs_1_, ...), custom_call_target="tpu_custom_call" | custom-call | flops 805306368 | bytes 6422528 | tf_op jit(solution)/shard_map/pallas_call | solution.py:341
  46.2 14.2 %collective-permute-done.2.refs_0_ = bf16[256,1536]{1,0:T(8,128)(2,1)S(1)} collective-permute-done((bf16[256,1536]{1,0:T(8,128)(2,1)S(1)}, bf16[256,1536]{1,0:T(8,128)(2,1)S(1)}, u32[]{:S(2)}, u32[]{:S(2)}) %collective-permute-start.2) | collective-permute-done | bytes 786464 | tf_op jit(solution)/shard_map/ppermute | solution.py:595
  60.4 12.5 %shard_map.124 = (f32[192,512]{1,0:T(8,128)}, f32[16,1,128]{2,1,0:T(1,128)}, f32[1,512,3584]{2,1,0:T(8,128)}, bf16[1,512,3584]{2,1,0:T(8,128)(2,1)}, bf16[1,512,3584]{2,1,0:T(8,128)(2,1)}) custom-call(bf16[256,1536]{1,0:T(8,128)(2,1)S(1)} %collective-permute-done.2.refs_0_, bf16[192,512]{1,0:T(8,128)(2,1)} %get-tuple-element.29.refs_0_.refs_1_, ...), custom_call_target="tpu_custom_call" | custom-call | flops 1610612736 | bytes 46137344 | tf_op jit(solution)/shard_map/pallas_call | solution.py:519
  72.9 0.0 all-to-all-done
  73.0 0.0 copy-start
  73.0 1.0 %copy-done = bf16[16,24,1536]{2,1,0:T(8,128)(2,1)} copy-done((bf16[16,24,1536]{2,1,0:T(8,128)(2,1)}, bf16[16,24,1536]{2,1,0:T(8,128)(2,1)S(1)}, u32[]{:S(2)}) %copy-start) | copy-done | bytes 1179672
  74.0 4.2 %shard_map.125 = (bf16[192,512]{1,0:T(8,128)(2,1)}, bf16[192,512]{1,0:T(8,128)(2,1)}, f32[32,1,128]{2,1,0:T(1,128)}) custom-call(bf16[384,1536]{1,0:T(8,128)(2,1)} %bitcast.14, bf16[384,512]{1,0:T(8,128)(2,1)} %get-tuple-element.30.hidden_ref.refs_0_, bf16[512,3584]{1,0:T(8,128)(2,1)} %shard_map.120.refs_2_.weight_ref.refs_7_, ...), custom_call_target="tpu_custom_call" | custom-call | flops 603979776 | bytes 5505024 | tf_op jit(solution)/shard_map/pallas_call | solution.py:381
  78.2 1.5 %collective-permute-start.3 = (bf16[192,512]{1,0:T(8,128)(2,1)}, bf16[192,512]{1,0:T(8,128)(2,1)S(1)}, u32[]{:S(2)}, u32[]{:S(2)}) collective-permute-start(bf16[192,512]{1,0:T(8,128)(2,1)} %get-tuple-element.38), channel_id=1, source_target_pairs={{0,16},{16,0},{1,17},{17,1},{2,18},{18,2},{3,19},{19,3},{4,20},{20... | collective-permute-start | bytes 589832 | tf_op jit(solution)/shard_map/ppermute | solution.py:595
  79.7 4.9 %all-to-all-start.2 = ((f32[32,1,128]{2,1,0:T(1,128)}), f32[32,1,128]{2,1,0:T(1,128)S(1)}, u32[]{:S(2)}, u32[]{:S(2)}) async-start(f32[32,1,128]{2,1,0:T(1,128)} %get-tuple-element.36), calls=%async_computation.2 | async-start | bytes 32768 | tf_op jit(solution)/shard_map/all_to_all | solution.py:622
  84.6 8.2 %shard_map.127 = (f32[1,512,3584]{2,1,0:T(8,128)}, bf16[1,512,3584]{2,1,0:T(8,128)(2,1)}, bf16[1,512,3584]{2,1,0:T(8,128)(2,1)}) custom-call(bf16[384,512]{1,0:T(8,128)(2,1)} %get-tuple-element.30.hidden_ref.refs_0_, bf16[384,1536]{1,0:T(8,128)(2,1)} %bitcast.15, ...), custom_call_target="tpu_custom_call", output_to_operand_aliasing={{0}: (5, {}), {1}: (6, {}), {2}: (7, {})} | custom-call | flops 1207959552 | bytes 34603008 | tf_op jit(solution)/shard_map/pallas_call | solution.py:519
  92.8 0.0 all-to-all-done.2
  92.8 0.0 collective-permute-done.3.refs_1_
  92.8 3.4 %shard_map.126 = (bf16[192,2048]{1,0:T(8,128)(2,1)}, f32[8,256]{1,0:T(8,128)}) custom-call(bf16[192,2048]{1,0:T(8,128)(2,1)} %bitcast.18, s32[8,256]{1,0:T(8,128)} %bitcast.21, s32[8,256]{1,0:T(8,128)} %bitcast.23, bf16[8,256]{1,0:T(8,128)(2,1)} %bitcast.25, f32[2,16,1,128]{3,2,1,0:T(1,128)S(1)} %bitcast.13, bf16[192,512]{1,0:T(8,128)(2,1)} %get-tuple-element.37.refs_0_, ...), custom_call_target="tpu_custom_call" | custom-call | flops 4718592 | bytes 1966080 | tf_op jit(solution)/shard_map/pallas_call | solution.py:573
Async XLA Ops:
  4.0 30.8 %all-to-all-start.1 = ((bf16[16,16,1536]{2,1,0:T(8,128)(2,1)}), bf16[16,16,1536]{2,1,0:T(8,128)(2,1)S(1)}, u32[]{:S(2)}, u32[]{:S(2)}) async-start(bf16[16,16,1536]{2,1,0:T(8,128)(2,1)} %bitcast.19), calls=%async_computation.1 | async-start | bytes 1572864 | tf_op jit(solution)/shard_map/all_to_all | solution.py:598
  11.3 20.1 %collective-permute-start = (bf16[256,1152]{1,0:T(8,128)(2,1)}, bf16[256,1152]{1,0:T(8,128)(2,1)S(1)}, u32[]{:S(2)}, u32[]{:S(2)}) collective-permute-start(bf16[256,1152]{1,0:T(8,128)(2,1)} %get-tuple-element.26.after_ref.refs_0_), channel_id=1, source_target_pairs={{0,16},{16,0},{1,17},{17,1},{2,18},{18,2},{3,19},{19,3},{4,20},{20... | collective-permute-start | bytes 1769480 | tf_op jit(solution)/shard_map/ppermute | solution.py:595
  14.9 16.5 %collective-permute-start.1 = (bf16[192,512]{1,0:T(8,128)(2,1)}, bf16[192,512]{1,0:T(8,128)(2,1)S(1)}, u32[]{:S(2)}, u32[]{:S(2)}) collective-permute-start(bf16[192,512]{1,0:T(8,128)(2,1)} %get-tuple-element.27), channel_id=1, source_target_pairs={{0,16},{16,0},{1,17},{17,1},{2,18},{18,2},{3,19},{19,3},{4,20},{20... | collective-permute-start | bytes 589832 | tf_op jit(solution)/shard_map/ppermute | solution.py:595
  34.8 38.1 %all-to-all-start = ((bf16[16,24,1536]{2,1,0:T(8,128)(2,1)}), bf16[16,24,1536]{2,1,0:T(8,128)(2,1)S(1)}, u32[]{:S(2)}, u32[]{:S(2)}) async-start(bf16[16,24,1536]{2,1,0:T(8,128)(2,1)} %bitcast.16), calls=%async_computation | async-start | bytes 2359296 | tf_op jit(solution)/shard_map/all_to_all | solution.py:598
  40.6 19.9 %collective-permute-start.2 = (bf16[256,1536]{1,0:T(8,128)(2,1)S(1)}, bf16[256,1536]{1,0:T(8,128)(2,1)S(1)}, u32[]{:S(2)}, u32[]{:S(2)}) collective-permute-start(bf16[256,1536]{1,0:T(8,128)(2,1)S(1)} %bitcast.11), channel_id=1, source_target_pairs={{0,16},{16,0},{1,17},{17,1},{2,18},{18,2},{3,19},{19,3},{4,20},{20... | collective-permute-start | bytes 2359304 | tf_op jit(solution)/shard_map/ppermute | solution.py:595
  73.0 1.0 %copy-start = (bf16[16,24,1536]{2,1,0:T(8,128)(2,1)}, bf16[16,24,1536]{2,1,0:T(8,128)(2,1)S(1)}, u32[]{:S(2)}) copy-start(bf16[16,24,1536]{2,1,0:T(8,128)(2,1)S(1)} %all-to-all-done) | copy-start | bytes 3538948
  78.2 14.7 %collective-permute-start.3 = (bf16[192,512]{1,0:T(8,128)(2,1)}, bf16[192,512]{1,0:T(8,128)(2,1)S(1)}, u32[]{:S(2)}, u32[]{:S(2)}) collective-permute-start(bf16[192,512]{1,0:T(8,128)(2,1)} %get-tuple-element.38), channel_id=1, source_target_pairs={{0,16},{16,0},{1,17},{17,1},{2,18},{18,2},{3,19},{19,3},{4,20},{20... | collective-permute-start | bytes 589832 | tf_op jit(solution)/shard_map/ppermute | solution.py:595
  79.7 13.1 %all-to-all-start.2 = ((f32[32,1,128]{2,1,0:T(1,128)}), f32[32,1,128]{2,1,0:T(1,128)S(1)}, u32[]{:S(2)}, u32[]{:S(2)}) async-start(f32[32,1,128]{2,1,0:T(1,128)} %get-tuple-element.36), calls=%async_computation.2 | async-start | bytes 32768 | tf_op jit(solution)/shard_map/all_to_all | solution.py:622

commit v5 on v4

--- a/solution.py
+++ b/solution.py
@@ -12,8 +12,7 @@
 SEND = 12
 LANE = 128
 UNIT = 512
-MIX_COST = 50
-SETTLE_COST = 44
+DEPTH = 4
 ROWS = 16
 
 beta_one = 0.9
@@ -26,7 +25,6 @@
 f32 = jnp.float32
 bf16 = jnp.bfloat16
 HBM = pl.BlockSpec(memory_space=pltpu.HBM)
-ANY = pl.BlockSpec(memory_space=pl.ANY)
 
 
 def in_hbm(*arrays):
@@ -247,19 +245,19 @@
         out_ref[own, 3 * part :] = tail.astype(bf16)
 
 
-def mix(parts, weight, after):
+def mix(parts, weight):
     shards = len(parts)
     rows, packed = parts[0].shape
     shape = (rows // ROWS * SEND * shards, packed // 3 * 4)
     return pl.pallas_call(
         functools.partial(mix_kernel, shards),
         grid=(1,),
-        in_specs=[block(part.shape) for part in parts] + [HBM] + [ANY] * len(after),
+        in_specs=[block(part.shape) for part in parts] + [HBM],
         out_specs=block(shape),
         out_shape=out_hbm(shape, bf16),
         compiler_params=params(12 * rows * packed * shards),
-        cost_estimate=cost(0, MIX_COST * rows * packed * shards),
-    )(*in_hbm(parts[0]), *parts[1:], *in_hbm(weight), *after)
+        cost_estimate=cost(0, 5 * rows * packed * shards),
+    )(*in_hbm(parts[0]), *parts[1:], *in_hbm(weight))
 
 
 def reorder(arrived, rows_ref):
@@ -292,15 +290,17 @@
     row = lax.broadcasted_iota(jnp.int32, (count, LANE), 0)
     lane = lax.broadcasted_iota(jnp.int32, (count, LANE), 1)
     spread = jnp.where(row - SEND * div_send(row) == lane, score, 0.0)
+    high = spread.astype(bf16)
+    rest = (spread - high.astype(f32)).astype(bf16)
     at = lax.broadcasted_iota(jnp.int32, (blocks, count), 1)
-    out = []
-    for pick in picked:
-        gather = (div_send(at) == pick).astype(f32)
-        value = jnp.dot(
-            gather, spread, precision=lax.Precision.HIGHEST, preferred_element_type=f32
-        )
-        out.append(value.reshape(blocks, 1, LANE))
-    return out
+    gather = [jnp.where(div_send(at) == pick, 1.0, 0.0) for pick in picked]
+    gather = jnp.concatenate(gather, axis=0).astype(bf16)
+    value = jnp.dot(gather, high, preferred_element_type=f32)
+    value += jnp.dot(gather, rest, preferred_element_type=f32)
+    return [
+        value[i * blocks : (i + 1) * blocks].reshape(blocks, 1, LANE)
+        for i in range(len(picked))
+    ]
 
 
 def block_index(blocks, count):
@@ -397,7 +397,7 @@
         + [jax.ShapeDtypeStruct(*out[-1])],
         compiler_params=params(nbytes),
         cost_estimate=cost(2 * total * part * (high - low), nbytes),
-    )(*in_hbm(arrived, hidden, weight, *before, *scores))
+    )(arrived, *in_hbm(hidden, weight, *before, *scores))
     return list(outs[:-1]), outs[-1]
 
 
@@ -411,86 +411,112 @@
 
     arrived = take(len(fresh))
     hidden = take(1 + len(fresh))
-    given_hbm, *state_hbm = take(4)
+    given_ref, *state_hbm = take(4)
     weight_hbm = take(1)[0] if fresh else None
     take(3 if low else 0)
     projs, scores, outs = take(len(fresh)), take(len(fresh)), take(3)
-    rows_ref, hidden_t, weight_ref = take(3)
-    state, news = take(3), take(3)
-    sem, in_sems, out_sems = refs
-    cols = rows_ref.shape[1]
-    given = given_hbm.shape[0]
-    loads = [
-        pltpu.make_async_copy(given_hbm, rows_ref.at[pl.ds(0, given)], sem.at[0])
-    ]
-    if fresh:
-        loads.append(
-            pltpu.make_async_copy(weight_hbm.at[:, pl.ds(low, cols)], weight_ref, sem.at[1])
-        )
-    for copy in loads:
-        copy.start()
+    hidden_t, grad_ref = take(2)
+    state = take(3)
+    in_sems, out_sems = take(2)
+    part, cols = grad_ref.shape
+    given = given_ref.shape[0]
+    step = part // out_sems.shape[1]
+    steps = part // step
 
     def load(i):
+        rows = pl.ds(pl.multiple_of(i * step, step), step)
         return [
             pltpu.make_async_copy(
-                source.at[0, :, pl.ds(low + i * UNIT, UNIT)],
-                target.at[:, pl.ds(i * UNIT, UNIT)],
-                in_sems.at[j, i],
+                source.at[0, rows, pl.ds(low, cols)], target.at[rows], in_sems.at[j, i]
             )
             for j, (source, target) in enumerate(zip(state_hbm, state))
         ]
 
     def store(i):
+        rows = pl.ds(pl.multiple_of(i * step, step), step)
         return [
             pltpu.make_async_copy(
-                source.at[:, pl.ds(i * UNIT, UNIT)],
-                target.at[0, :, pl.ds(low + i * UNIT, UNIT)],
-                out_sems.at[j, i],
+                source.at[rows], target.at[0, rows, pl.ds(low, cols)], out_sems.at[j, i]
             )
-            for j, (source, target) in enumerate(zip(news, outs))
+            for j, (source, target) in enumerate(zip(state, outs))
         ]
 
-    units = cols // UNIT
-    for i in range(units):
-        for copy in load(i):
+    def start_loads(first, end):
+        for i in range(first, end):
+            for copy in load(i):
+                copy.start()
+
+    if fresh:
+        rows_ref, weight_ref, sems = take(3)
+        loads = [
+            pltpu.make_async_copy(weight_hbm.at[:, pl.ds(low, cols)], weight_ref, sems.at[0]),
+            pltpu.make_async_copy(given_ref, rows_ref.at[pl.ds(0, given)], sems.at[1]),
+        ]
+        for copy in loads:
             copy.start()
+    else:
+        rows_ref = given_ref
+        start_loads(0, min(DEPTH, steps))
     base = 0
     for ref in hidden:
         count = ref.shape[0]
         hidden_t[:, base : base + count] = ref[...].astype(f32).T.astype(bf16)
         base += count
-    for copy in loads:
-        copy.wait()
-    base = given
-    for i, arrived_ref in enumerate(arrived):
+    if fresh:
         count = blocks * SEND
-        own = rows_ref.at[base : base + count]
-        base += count
-        reorder(arrived_ref[...], own)
-        proj = times_weight(own, weight_ref)
-        projs[i][...] = proj
-        scores[i][...] = score_block(
-            blocks, proj, hidden[1 + i][...], [block_index(blocks, count)]
-        )[0]
+        for i, arrived_ref in enumerate(arrived):
+            reorder(
+                arrived_ref[...],
+                rows_ref.at[given + i * count : given + (i + 1) * count],
+            )
+        loads[0].wait()
+        start_loads(0, min(DEPTH, steps))
+        for i in range(len(fresh)):
+            own = rows_ref.at[given + i * count : given + (i + 1) * count]
+            proj = times_weight(own, weight_ref)
+            projs[i][...] = proj
+            scores[i][...] = score_block(
+                blocks, proj, hidden[1 + i][...], [block_index(blocks, count)]
+            )[0]
+        loads[1].wait()
+    for i in range(cols // UNIT):
+        own = slice(i * UNIT, (i + 1) * UNIT)
+        grad_ref[:, own] = jnp.dot(
+            hidden_t[...], rows_ref[:, own], preferred_element_type=f32
+        )
 
     corr_one = 1.0 - beta_one**adam_step
     corr_two = 1.0 - beta_two**adam_step
     rate = learn_rate * corr_two**0.5 / corr_one
     keep = 1.0 - learn_rate * decay_rate
-    for i in range(units):
+    eps = adam_eps * corr_two**0.5
+
+    @pl.loop(0, steps)
+    def _(i):
         for copy in load(i):
             copy.wait()
-        own = slice(i * UNIT, (i + 1) * UNIT)
-        grad = jnp.dot(hidden_t[...], rows_ref[:, own], preferred_element_type=f32)
-        m_new = beta_one * state[1][:, own].astype(f32) + (1.0 - beta_one) * grad
-        v_new = beta_two * state[2][:, own].astype(f32) + (1.0 - beta_two) * (grad * grad)
-        root = v_new * lax.rsqrt(v_new) + adam_eps * corr_two**0.5
-        news[0][:, own] = keep * state[0][:, own] - rate * m_new / root
-        news[1][:, own] = m_new.astype(bf16)
-        news[2][:, own] = v_new.astype(bf16)
+
+        @pl.when(i + DEPTH < steps)
+        def _():
+            for copy in load(i + DEPTH):
+                copy.start()
+
+        own = pl.ds(pl.multiple_of(i * step, step), step)
+        grad = grad_ref[own, :]
+        m_new = beta_one * state[1][own, :].astype(f32) + (1.0 - beta_one) * grad
+        v_new = beta_two * state[2][own, :].astype(f32) + (1.0 - beta_two) * (grad * grad)
+        root = lax.rsqrt(v_new)
+        below = 1.0 + eps * root
+        inverse = pl.reciprocal(below, approx=True)
+        inverse = inverse * (2.0 - below * inverse)
+        state[0][own, :] = keep * state[0][own, :] - (rate * m_new) * (root * inverse)
+        state[1][own, :] = m_new.astype(bf16)
+        state[2][own, :] = v_new.astype(bf16)
         for copy in store(i):
             copy.start()
-    for i in range(units):
+
+    @pl.loop(0, steps)
+    def _(i):
         for copy in store(i):
             copy.wait()
 
@@ -501,21 +527,28 @@
     count = blocks * SEND
     fresh = tuple(range(1, 1 + len(arrived)))
     total = given.shape[0] + count * len(fresh)
+    steps = max(1, part // 64)
     args = list(arrived) + in_hbm(hidden[0]) + list(hidden[1:])
     specs = [block(array.shape) for array in args]
-    args += in_hbm(given, *state, *([weight] if fresh else []), *done)
-    specs += [HBM] * (4 + bool(fresh) + len(done))
+    if fresh:
+        args += in_hbm(given)
+        specs.append(HBM)
+    else:
+        args.append(given)
+        specs.append(block(given.shape))
+    args += in_hbm(*state, *([weight] if fresh else []), *done)
+    specs += [HBM] * (3 + bool(fresh) + len(done))
     out = [((count, part), f32)] * len(fresh) + [((blocks, 1, LANE), f32)] * len(fresh)
-    kinds = [f32, bf16, bf16]
-    scratch = [
-        pltpu.VMEM((total, cols), bf16),
-        pltpu.VMEM((part, total), bf16),
-        pltpu.VMEM((part, cols) if fresh else (ROWS, LANE), bf16),
-    ]
-    scratch += [pltpu.VMEM((part, cols), kind) for kind in kinds * 2]
-    scratch += [pltpu.SemaphoreType.DMA((2,))]
-    scratch += [pltpu.SemaphoreType.DMA((3, cols // UNIT))] * 2
-    nbytes = 18 * part * cols + 4 * total * cols + 8 * total * part
+    scratch = [pltpu.VMEM((part, total), bf16), pltpu.VMEM((part, cols), f32)]
+    scratch += [pltpu.VMEM((part, cols), kind) for kind in (f32, bf16, bf16)]
+    scratch += [pltpu.SemaphoreType.DMA((3, steps))] * 2
+    if fresh:
+        scratch += [
+            pltpu.VMEM((total, cols), bf16),
+            pltpu.VMEM((part, cols), bf16),
+            pltpu.SemaphoreType.DMA((2,)),
+        ]
+    nbytes = 14 * part * cols + 4 * total * cols + 8 * total * part
     outs = pl.pallas_call(
         functools.partial(settle_kernel, low, fresh, blocks),
         grid=(1,),
@@ -528,7 +561,7 @@
             len(args) - len(done) + i: len(out) + i for i in range(len(done))
         },
         compiler_params=params(nbytes),
-        cost_estimate=cost(4 * total * part * cols, SETTLE_COST * part * cols, part * cols),
+        cost_estimate=cost(4 * total * part * cols, 22 * part * cols, part * cols),
     )(*args)
     outs = list(outs)
     return outs[: len(fresh)], outs[len(fresh) : 2 * len(fresh)], outs[-3:]
@@ -545,25 +578,19 @@
         ).astype(bf16)
         out_ref[:, pl.ds(high, part)] = (grad * (gate * sig)).astype(bf16)
 
-    blocks = score_ref.shape[1]
-    score = score_ref[0].reshape(blocks, LANE)
-    for s in range(1, shards):
-        score += score_ref[s].reshape(blocks, LANE)
     ids = ids_ref[...]
     slots = slots_ref[...]
-    tok = ids.shape[1]
     live = ((ids & (EXP_LOCAL - 1)) == 0) & (slots >= 0)
-    owner = ids // EXP_LOCAL
-    lane = lax.broadcasted_iota(jnp.int32, (LANE, tok), 0)
-    block_of = lax.broadcasted_iota(jnp.int32, (blocks, tok), 0)
-    for k in range(TOPK):
-        pick = (lane == slots[k : k + 1]).astype(f32)
-        value = jnp.dot(score, pick, precision=lax.Precision.HIGHEST, preferred_element_type=f32)
-        value = jnp.where(block_of == owner[k : k + 1], value, 0.0)
-        value = jnp.sum(value, axis=0, keepdims=True)
-        gate_ref[k : k + 1] = jnp.where(
-            live[k : k + 1], value / gates_ref[k : k + 1].astype(f32), 0.0
-        )
+    place = jnp.where(live, ids // EXP_LOCAL * SEND + slots, -1)
+    blocks = score_ref.shape[0] // shards
+    value = jnp.zeros(ids.shape, f32)
+    for b in range(blocks):
+        for slot in range(SEND):
+            score = score_ref[b, 0, slot]
+            for s in range(1, shards):
+                score += score_ref[s * blocks + b, 0, slot]
+            value = jnp.where(place == b * SEND + slot, score, value)
+    gate_ref[...] = jnp.where(live, value / gates_ref[...].astype(f32), 0.0)
 
 
 def close(gate_up, ids, slots, gates, score, grads):
@@ -573,7 +600,9 @@
     return pl.pallas_call(
         functools.partial(close_kernel, len(grads)),
         grid=(1,),
-        in_specs=[block(array.shape) for array in args],
+        in_specs=[block(array.shape) for array in args[:4]]
+        + [pl.BlockSpec(memory_space=pltpu.SMEM)]
+        + [block(grad.shape) for grad in grads],
         out_specs=[block(shape) for shape, _ in shapes],
         out_shape=[out_hbm(shape, dtype) for shape, dtype in shapes],
         compiler_params=params(8 * size),
@@ -603,9 +632,10 @@
     hidden = [parts[0]] + [shift(parts[s], s) for s in steps]
     weight = cast_weight(master, send_b)
     arrived = exchange(send_a.reshape(ep_size, ROWS, -1)).reshape(send_a.shape)
-    mixed = mix(mixed, weight, hidden[1:])
+    mixed = mix(mixed, weight)
     arrived_b = exchange(mixed.reshape(ep_size, rep_size * SEND, -1)).reshape(mixed.shape)
 
+    arrived, *hidden[1:] = lax.optimization_barrier([arrived] + hidden[1:])
     peers = [shift(arrived, s) for s in steps]
     rows, proj, score_own, hidden_mixed = begin(ep_size, edges[1], arrived, weight, hidden)
     before, scores, done = settle(0, ep_size, peers, rows, hidden, weight, state, ())
@@ -625,7 +655,7 @@
         edges[1], ep_size, [], arrived_b, [hidden_mixed], weight, state, done
     )
     grad_gate_up, gate_grad = close(
-        gate_up, ids_t, slots_t, gates_t, score.reshape(rep_size, ep_size, 1, LANE), grads
+        gate_up, ids_t, slots_t, gates_t, score, grads
     )
     return (grad_gate_up.reshape(saved_gate_up.shape), gate_grad.T) + tuple(done)
 

time: 96.9 us -> 97.8 us (level)
  waiting for transfers between devices: 24.9 us -> 28.4 us
  Pallas kernels: 46.4 us -> 44.2 us
  local copies, waits for them, and re-layouts: 1.02 us -> 0 us
    ppermute x4, waiting for transfers between devices: 24.9 us -> 28.4 us  [shift(): return lax.ppermute(value, 'rep', perm)]
    unnamed x2 -> x0, local copies, waits for them, and re-layouts: 1.02 us -> none
  transfers between devices with their start and end apart: 7 -> 7, of which waited for: 2 -> 3; matrix products, arithmetic and copies ran while one was open for 0% -> 0% of each run, Pallas kernels for 37% -> 36%
where the time goes in v5:
time: 97.8 us; the launch traced here: 97 us
  Pallas kernels  44.2 us (45%)
  waiting for transfers between devices  28.4 us (29%)
  starting transfers between devices  23.7 us (24%)
    ppermute x4, waiting for transfers between devices, shift(): return lax.ppermute(value, 'rep', perm)  28.4 us
    pallas_call x2, Pallas kernels, settle(): pl.pallas_call(functools.partial(settle_kernel, low, fresh, blocks), grid...  19.8 us
    all_to_all x2, starting transfers between devices, exchange(): return lax.all_to_all(value, 'ep', split_axis=0, concat_axis=0, tiled=True)  13.1 us
    ppermute x4, starting transfers between devices, shift(): return lax.ppermute(value, 'rep', perm)  6.14 us
    pallas_call x1, Pallas kernels, cast_weight(): pl.pallas_call(cast_kernel, grid=(4,), in_specs=[pl.BlockSpec((1, rows, w...  5.37 us
    all_to_all x1, starting transfers between devices, per_device(): lax.all_to_all(score, ('rep', 'ep'), split_axis=0, concat_axis=0, tiled=T...  4.4 us
    pallas_call x1, Pallas kernels, begin(): pl.pallas_call(functools.partial(begin_kernel, blocks), grid=(1,), in_spe...  3.97 us
    pallas_call x1, Pallas kernels, finish(): pl.pallas_call(functools.partial(finish_kernel, shards, blocks, low), gri...  3.67 us
  transfers between devices with their start and end apart: 7, of which 3 were waited for; matrix products, arithmetic and copies ran while one was open for 0% of the time, Pallas kernels for 36%

profile of v5, /device:TPU:0, one launch (start us, length us, event | category | flops | bytes accessed | tf_op | source)
XLA Modules:
  0.0 97.0 jit_solution(3693190777029648033)
XLA Ops:
  0.6 3.3 %shard_map.119 = (bf16[256,1536]{1,0:T(8,128)(2,1)}, bf16[256,1152]{1,0:T(8,128)(2,1)}) custom-call(s32[8,256]{1,0:T(8,128)} %bitcast.18, s32[8,256]{1,0:T(8,128)} %bitcast.20, bf16[8,256]{1,0:T(8,128)(2,1)} %bitcast.22, bf16[256,3584]{1,0:T(8,128)(2,1)} %grad_hbm.1), custom_call_target="tpu_custom_call" | custom-call | flops 469762048 | bytes 3670016 | tf_op jit(solution)/shard_map/pallas_call | solution.py:142
  4.0 7.4 %all-to-all-start.1 = ((bf16[16,16,1536]{2,1,0:T(8,128)(2,1)}), bf16[16,16,1536]{2,1,0:T(8,128)(2,1)S(1)}, u32[]{:S(2)}, u32[]{:S(2)}) async-start(bf16[16,16,1536]{2,1,0:T(8,128)(2,1)} %bitcast.17), calls=%async_computation.1 | async-start | bytes 1572864 | tf_op jit(solution)/shard_map/all_to_all | solution.py:627
  11.3 1.6 %collective-permute-start = (bf16[256,1152]{1,0:T(8,128)(2,1)}, bf16[256,1152]{1,0:T(8,128)(2,1)S(1)}, u32[]{:S(2)}, u32[]{:S(2)}) collective-permute-start(bf16[256,1152]{1,0:T(8,128)(2,1)} %get-tuple-element.28.after_ref.refs_0_), channel_id=1, source_target_pairs={{0,16},{16,0},{1,17},{17,1},{2,18},{18,2},{3,19},{19,3},{4,20},{20... | collective-permute-start | bytes 1769480 | tf_op jit(solution)/shard_map/ppermute | solution.py:624
  12.9 5.4 %shard_map.120.refs_2_.weight_ref.refs_7_ = bf16[512,3584]{1,0:T(8,128)(2,1)} custom-call(f32[1,512,3584]{2,1,0:T(8,128)} %refs_2_.1, bf16[256,1152]{1,0:T(8,128)(2,1)} %get-tuple-element.28.after_ref.refs_0_), custom_call_target="tpu_custom_call" | custom-call | flops 1835008 | bytes 11010048 | tf_op jit(solution)/shard_map/pallas_call | solution.py:198
  18.3 8.9 %collective-permute-done.refs_1_ = bf16[256,1152]{1,0:T(8,128)(2,1)S(1)} collective-permute-done((bf16[256,1152]{1,0:T(8,128)(2,1)}, bf16[256,1152]{1,0:T(8,128)(2,1)S(1)}, u32[]{:S(2)}, u32[]{:S(2)}) %collective-permute-start) | collective-permute-done | bytes 589856 | tf_op jit(solution)/shard_map/ppermute | solution.py:624
  27.2 3.4 %shard_map.121 = bf16[384,1536]{1,0:T(8,128)(2,1)} custom-call(bf16[256,1152]{1,0:T(8,128)(2,1)} %get-tuple-element.28.after_ref.refs_0_, bf16[256,1152]{1,0:T(8,128)(2,1)S(1)} %collective-permute-done.refs_1_, bf16[512,3584]{1,0:T(8,128)(2,1)} %shard_map.120.refs_2_.weight_ref.refs_7_), custom_call_target="tpu_custom_call" | custom-call | bytes 2949120 | tf_op jit(solution)/shard_map/pallas_call | solution.py:252
  30.6 0.0 all-to-all-done.1
  30.6 5.8 %all-to-all-start = ((bf16[16,24,1536]{2,1,0:T(8,128)(2,1)}), bf16[16,24,1536]{2,1,0:T(8,128)(2,1)S(1)}, u32[]{:S(2)}, u32[]{:S(2)}) async-start(bf16[16,24,1536]{2,1,0:T(8,128)(2,1)} %bitcast.14), calls=%async_computation | async-start | bytes 2359296 | tf_op jit(solution)/shard_map/all_to_all | solution.py:627
  36.4 2.0 %shard_map.122 = (bf16[192,512]{1,0:T(8,128)(2,1)}, bf16[192,512]{1,0:T(8,128)(2,1)}) custom-call(bf16[192,2048]{1,0:T(8,128)(2,1)} %bitcast.15, bf16[256,1152]{1,0:T(8,128)(2,1)} %get-tuple-element.28.after_ref.refs_0_), custom_call_target="tpu_custom_call" | custom-call | flops 3145728 | bytes 1179648 | tf_op jit(solution)/shard_map/pallas_call | solution.py:179
  38.3 1.5 %collective-permute-start.1 = (bf16[192,512]{1,0:T(8,128)(2,1)}, bf16[192,512]{1,0:T(8,128)(2,1)S(1)}, u32[]{:S(2)}, u32[]{:S(2)}) collective-permute-start(bf16[192,512]{1,0:T(8,128)(2,1)} %get-tuple-element.30), channel_id=1, source_target_pairs={{0,16},{16,0},{1,17},{17,1},{2,18},{18,2},{3,19},{19,3},{4,20},{20... | collective-permute-start | bytes 589832 | tf_op jit(solution)/shard_map/ppermute | solution.py:624
  39.9 5.9 %collective-permute-done.1.refs_1_.refs_2_ = bf16[192,512]{1,0:T(8,128)(2,1)S(1)} collective-permute-done((bf16[192,512]{1,0:T(8,128)(2,1)}, bf16[192,512]{1,0:T(8,128)(2,1)S(1)}, u32[]{:S(2)}, u32[]{:S(2)}) %collective-permute-start.1) | collective-permute-done | bytes 196640 | tf_op jit(solution)/shard_map/ppermute | solution.py:624
  45.8 1.5 %collective-permute-start.2 = (bf16[256,1536]{1,0:T(8,128)(2,1)S(1)}, bf16[256,1536]{1,0:T(8,128)(2,1)S(1)}, u32[]{:S(2)}, u32[]{:S(2)}) collective-permute-start(bf16[256,1536]{1,0:T(8,128)(2,1)S(1)} %bitcast.12), channel_id=1, source_target_pairs={{0,16},{16,0},{1,17},{17,1},{2,18},{18,2},{3,19},{19,3},{4,20},{20... | collective-permute-start | bytes 2359304 | tf_op jit(solution)/shard_map/ppermute | solution.py:624
  47.3 4.0 %shard_map.123 = (bf16[192,2048]{1,0:T(8,128)(2,1)}, f32[192,512]{1,0:T(8,128)}, f32[16,1,128]{2,1,0:T(1,128)}, bf16[384,512]{1,0:T(8,128)(2,1)}) custom-call(bf16[256,1536]{1,0:T(8,128)(2,1)S(1)} %bitcast.13, bf16[512,3584]{1,0:T(8,128)(2,1)} %shard_map.120.refs_2_.weight_ref.refs_7_, bf16[192,512]{1,0:T(8,128)(2,1)} %get-tuple-element.32.refs_0_.refs_1_, ...), custom_call_target="tpu_custom_call" | custom-call | flops 805306368 | bytes 6422528 | tf_op jit(solution)/shard_map/pallas_call | solution.py:341
  51.3 13.6 %collective-permute-done.2.refs_0_ = bf16[256,1536]{1,0:T(8,128)(2,1)S(1)} collective-permute-done((bf16[256,1536]{1,0:T(8,128)(2,1)S(1)}, bf16[256,1536]{1,0:T(8,128)(2,1)S(1)}, u32[]{:S(2)}, u32[]{:S(2)}) %collective-permute-start.2) | collective-permute-done | bytes 786464 | tf_op jit(solution)/shard_map/ppermute | solution.py:624
  64.9 11.9 %shard_map.124 = (f32[192,512]{1,0:T(8,128)}, f32[16,1,128]{2,1,0:T(1,128)}, f32[1,512,3584]{2,1,0:T(8,128)}, bf16[1,512,3584]{2,1,0:T(8,128)(2,1)}, bf16[1,512,3584]{2,1,0:T(8,128)(2,1)}) custom-call(bf16[256,1536]{1,0:T(8,128)(2,1)S(1)} %collective-permute-done.2.refs_0_, bf16[192,512]{1,0:T(8,128)(2,1)} %get-tuple-element.32.refs_0_.refs_1_, ...), custom_call_target="tpu_custom_call" | custom-call | flops 1610612736 | bytes 23068672 | tf_op jit(solution)/shard_map/pallas_call | solution.py:552
  76.8 0.0 all-to-all-done
  76.8 3.7 %shard_map.125 = (bf16[192,512]{1,0:T(8,128)(2,1)}, bf16[192,512]{1,0:T(8,128)(2,1)}, f32[32,1,128]{2,1,0:T(1,128)}) custom-call(bf16[384,1536]{1,0:T(8,128)(2,1)S(1)} %bitcast.10, bf16[384,512]{1,0:T(8,128)(2,1)} %get-tuple-element.34.hidden_ref.refs_0_, bf16[512,3584]{1,0:T(8,128)(2,1)} %shard_map.120.refs_2_.weight_ref.refs_7_, ...), custom_call_target="tpu_custom_call" | custom-call | flops 603979776 | bytes 5505024 | tf_op jit(solution)/shard_map/pallas_call | solution.py:381
  80.5 1.5 %collective-permute-start.3 = (bf16[192,512]{1,0:T(8,128)(2,1)}, bf16[192,512]{1,0:T(8,128)(2,1)S(1)}, u32[]{:S(2)}, u32[]{:S(2)}) collective-permute-start(bf16[192,512]{1,0:T(8,128)(2,1)} %get-tuple-element.42), channel_id=1, source_target_pairs={{0,16},{16,0},{1,17},{17,1},{2,18},{18,2},{3,19},{19,3},{4,20},{20... | collective-permute-start | bytes 589832 | tf_op jit(solution)/shard_map/ppermute | solution.py:624
  82.0 4.4 %all-to-all-start.2 = ((f32[32,1,128]{2,1,0:T(1,128)}), f32[32,1,128]{2,1,0:T(1,128)S(1)}, u32[]{:S(2)}, u32[]{:S(2)}) async-start(f32[32,1,128]{2,1,0:T(1,128)} %get-tuple-element.40), calls=%async_computation.2 | async-start | bytes 32768 | tf_op jit(solution)/shard_map/all_to_all | solution.py:652
  86.4 7.8 %shard_map.127 = (f32[1,512,3584]{2,1,0:T(8,128)}, bf16[1,512,3584]{2,1,0:T(8,128)(2,1)}, bf16[1,512,3584]{2,1,0:T(8,128)(2,1)}) custom-call(bf16[384,512]{1,0:T(8,128)(2,1)} %get-tuple-element.34.hidden_ref.refs_0_, bf16[384,1536]{1,0:T(8,128)(2,1)S(1)} %bitcast.11, ...), custom_call_target="tpu_custom_call", output_to_operand_aliasing={{0}: (5, {}), {1}: (6, {}), {2}: (7, {})} | custom-call | flops 1207959552 | bytes 17301504 | tf_op jit(solution)/shard_map/pallas_call | solution.py:552
  94.3 0.0 all-to-all-done.2.score_ref
  94.3 0.0 collective-permute-done.3.refs_1_
  94.3 2.8 %shard_map.126 = (bf16[192,2048]{1,0:T(8,128)(2,1)}, f32[8,256]{1,0:T(8,128)}) custom-call(bf16[192,2048]{1,0:T(8,128)(2,1)} %bitcast.16, s32[8,256]{1,0:T(8,128)} %bitcast.19, s32[8,256]{1,0:T(8,128)} %bitcast.21, bf16[8,256]{1,0:T(8,128)(2,1)} %bitcast.23, f32[32,1,128]{2,1,0:T(1,128)S(1)} %all-to-all-done.2.score_ref, ...), custom_call_target="tpu_custom_call" | custom-call | flops 4718592 | bytes 1966080 | tf_op jit(solution)/shard_map/pallas_call | solution.py:600
Async XLA Ops:
  4.0 26.6 %all-to-all-start.1 = ((bf16[16,16,1536]{2,1,0:T(8,128)(2,1)}), bf16[16,16,1536]{2,1,0:T(8,128)(2,1)S(1)}, u32[]{:S(2)}, u32[]{:S(2)}) async-start(bf16[16,16,1536]{2,1,0:T(8,128)(2,1)} %bitcast.17), calls=%async_computation.1 | async-start | bytes 1572864 | tf_op jit(solution)/shard_map/all_to_all | solution.py:627
  11.3 15.9 %collective-permute-start = (bf16[256,1152]{1,0:T(8,128)(2,1)}, bf16[256,1152]{1,0:T(8,128)(2,1)S(1)}, u32[]{:S(2)}, u32[]{:S(2)}) collective-permute-start(bf16[256,1152]{1,0:T(8,128)(2,1)} %get-tuple-element.28.after_ref.refs_0_), channel_id=1, source_target_pairs={{0,16},{16,0},{1,17},{17,1},{2,18},{18,2},{3,19},{19,3},{4,20},{20... | collective-permute-start | bytes 1769480 | tf_op jit(solution)/shard_map/ppermute | solution.py:624
  30.6 46.2 %all-to-all-start = ((bf16[16,24,1536]{2,1,0:T(8,128)(2,1)}), bf16[16,24,1536]{2,1,0:T(8,128)(2,1)S(1)}, u32[]{:S(2)}, u32[]{:S(2)}) async-start(bf16[16,24,1536]{2,1,0:T(8,128)(2,1)} %bitcast.14), calls=%async_computation | async-start | bytes 2359296 | tf_op jit(solution)/shard_map/all_to_all | solution.py:627
  38.3 7.4 %collective-permute-start.1 = (bf16[192,512]{1,0:T(8,128)(2,1)}, bf16[192,512]{1,0:T(8,128)(2,1)S(1)}, u32[]{:S(2)}, u32[]{:S(2)}) collective-permute-start(bf16[192,512]{1,0:T(8,128)(2,1)} %get-tuple-element.30), channel_id=1, source_target_pairs={{0,16},{16,0},{1,17},{17,1},{2,18},{18,2},{3,19},{19,3},{4,20},{20... | collective-permute-start | bytes 589832 | tf_op jit(solution)/shard_map/ppermute | solution.py:624
  45.8 19.1 %collective-permute-start.2 = (bf16[256,1536]{1,0:T(8,128)(2,1)S(1)}, bf16[256,1536]{1,0:T(8,128)(2,1)S(1)}, u32[]{:S(2)}, u32[]{:S(2)}) collective-permute-start(bf16[256,1536]{1,0:T(8,128)(2,1)S(1)} %bitcast.12), channel_id=1, source_target_pairs={{0,16},{16,0},{1,17},{17,1},{2,18},{18,2},{3,19},{19,3},{4,20},{20... | collective-permute-start | bytes 2359304 | tf_op jit(solution)/shard_map/ppermute | solution.py:624
  80.5 13.7 %collective-permute-start.3 = (bf16[192,512]{1,0:T(8,128)(2,1)}, bf16[192,512]{1,0:T(8,128)(2,1)S(1)}, u32[]{:S(2)}, u32[]{:S(2)}) collective-permute-start(bf16[192,512]{1,0:T(8,128)(2,1)} %get-tuple-element.42), channel_id=1, source_target_pairs={{0,16},{16,0},{1,17},{17,1},{2,18},{18,2},{3,19},{19,3},{4,20},{20... | collective-permute-start | bytes 589832 | tf_op jit(solution)/shard_map/ppermute | solution.py:624
  82.0 12.2 %all-to-all-start.2 = ((f32[32,1,128]{2,1,0:T(1,128)}), f32[32,1,128]{2,1,0:T(1,128)S(1)}, u32[]{:S(2)}, u32[]{:S(2)}) async-start(f32[32,1,128]{2,1,0:T(1,128)} %get-tuple-element.40), calls=%async_computation.2 | async-start | bytes 32768 | tf_op jit(solution)/shard_map/all_to_all | solution.py:652

commit v6 on v5

--- a/solution.py
+++ b/solution.py
@@ -12,7 +12,7 @@
 SEND = 12
 LANE = 128
 UNIT = 512
-DEPTH = 4
+SETTLE_COST = 140
 ROWS = 16
 
 beta_one = 0.9
@@ -25,10 +25,16 @@
 f32 = jnp.float32
 bf16 = jnp.bfloat16
 HBM = pl.BlockSpec(memory_space=pltpu.HBM)
+ANY = pl.BlockSpec(memory_space=pl.ANY)
+VMEM = pl.BlockSpec(memory_space=pltpu.VMEM)
 
 
 def in_hbm(*arrays):
     return [pltpu.with_memory_space_constraint(array, pltpu.HBM) for array in arrays]
+
+
+def plain(dims, dtype):
+    return jax.ShapeDtypeStruct(tuple(dims), dtype)
 
 
 def out_hbm(dims, dtype):
@@ -181,29 +187,53 @@
         grid=(1,),
         in_specs=[block(gate_up.shape), HBM],
         out_specs=[block(shape)] * shards,
-        out_shape=[out_hbm(shape, bf16)] * shards,
+        out_shape=[plain(shape, bf16)] * shards,
         compiler_params=params(3 * slots * width),
         cost_estimate=cost(8 * slots * width, 3 * slots * width, slots * width),
     )(*in_hbm(gate_up, after))
 
 
-def cast_kernel(master_ref, after_ref, weight_ref):
+def load_kernel(middle, after_ref, master_hbm, one_hbm, two_hbm, *refs):
     del after_ref
-    weight_ref[...] = master_ref[0].astype(bf16)
-
-
-def cast_weight(master, after):
+    master_ref, one_ref, two_ref, weight_a, weight_b, sems = refs
+    part = master_ref.shape[0]
+    step = part // 4
+    copies = []
+    for i in range(4):
+        own = pl.ds(i * step, step)
+        copies.append(
+            pltpu.make_async_copy(master_hbm.at[0, own], master_ref.at[own], sems.at[i])
+        )
+    copies.append(pltpu.make_async_copy(one_hbm.at[0], one_ref, sems.at[4]))
+    copies.append(pltpu.make_async_copy(two_hbm.at[0], two_ref, sems.at[5]))
+    for copy in copies:
+        copy.start()
+    for i in range(4):
+        copies[i].wait()
+        own = slice(i * step, (i + 1) * step)
+        weight_a[own, :] = master_ref[own, :middle].astype(bf16)
+        weight_b[own, :] = master_ref[own, middle:].astype(bf16)
+    copies[4].wait()
+    copies[5].wait()
+
+
+def load_state(middle, master, one, two, after):
     _, part, width = master.shape
-    rows = part // 4
     return pl.pallas_call(
-        cast_kernel,
-        grid=(4,),
-        in_specs=[pl.BlockSpec((1, rows, width), lambda i: (0, i, 0)), HBM],
-        out_specs=pl.BlockSpec((rows, width), lambda i: (i, 0)),
-        out_shape=out_hbm((part, width), bf16),
-        compiler_params=params(6 * rows * width),
-        cost_estimate=cost(part * width, 6 * part * width),
-    )(*in_hbm(master, after))
+        functools.partial(load_kernel, middle),
+        in_specs=[HBM] * 4,
+        out_specs=[VMEM] * 5,
+        out_shape=[
+            pltpu.VMEM((part, width), f32),
+            pltpu.VMEM((part, width), bf16),
+            pltpu.VMEM((part, width), bf16),
+            pltpu.VMEM((part, middle), bf16),
+            pltpu.VMEM((part, width - middle), bf16),
+        ],
+        scratch_shapes=[pltpu.SemaphoreType.DMA((6,))],
+        compiler_params=params(0),
+        cost_estimate=cost(part * width, 14 * part * width),
+    )(*in_hbm(after, master, one, two))
 
 
 def mixed_place(index, shards):
@@ -245,19 +275,19 @@
         out_ref[own, 3 * part :] = tail.astype(bf16)
 
 
-def mix(parts, weight):
+def mix(parts, after):
     shards = len(parts)
     rows, packed = parts[0].shape
     shape = (rows // ROWS * SEND * shards, packed // 3 * 4)
     return pl.pallas_call(
         functools.partial(mix_kernel, shards),
         grid=(1,),
-        in_specs=[block(part.shape) for part in parts] + [HBM],
+        in_specs=[block(part.shape) for part in parts] + [ANY] * len(after),
         out_specs=block(shape),
         out_shape=out_hbm(shape, bf16),
         compiler_params=params(12 * rows * packed * shards),
         cost_estimate=cost(0, 5 * rows * packed * shards),
-    )(*in_hbm(parts[0]), *parts[1:], *in_hbm(weight))
+    )(*in_hbm(parts[0]), *parts[1:], *after)
 
 
 def reorder(arrived, rows_ref):
@@ -307,50 +337,33 @@
     return lax.broadcasted_iota(jnp.int32, (blocks, count), 0)
 
 
-def begin_kernel(blocks, arrived_ref, weight_ref, *refs):
-    hidden, (rows_ref, proj_ref, score_ref, mixed_ref) = refs[:-4], refs[-4:]
+def begin_kernel(blocks, arrived_ref, weight_ref, hidden_ref, rows_ref, proj_ref, score_ref):
     reorder(arrived_ref[...], rows_ref)
     proj = times_weight(rows_ref, weight_ref)
     proj_ref[...] = proj
-    count = proj.shape[0]
     score_ref[...] = score_block(
-        blocks, proj, hidden[0][...], [block_index(blocks, count)]
+        blocks, proj, hidden_ref[...], [block_index(blocks, proj.shape[0])]
     )[0]
-    shards = len(hidden)
-    row = lax.broadcasted_iota(jnp.int32, (shards * count, count), 0)
-    col = lax.broadcasted_iota(jnp.int32, (shards * count, count), 1)
-    at, step, slot = mixed_place(row, shards)
-    mixed = 0.0
-    for s in range(shards):
-        order = jnp.where((step == s) & (col == at * SEND + slot), 1.0, 0.0).astype(bf16)
-        mixed += jnp.dot(order, hidden[s][...], preferred_element_type=f32)
-    mixed_ref[...] = mixed.astype(bf16)
-
-
-def begin(blocks, cols, arrived, weight, hidden):
+
+
+def begin(blocks, arrived, weight, hidden):
     count = blocks * SEND
-    part = weight.shape[0]
-    shards = len(hidden)
-    out = [
-        ((count, cols), bf16),
-        ((count, part), f32),
-        ((blocks, 1, LANE), f32),
-        ((shards * count, part), bf16),
-    ]
-    nbytes = 4 * count * cols + 2 * part * cols + 4 * count * part * (1 + 3 * shards)
+    part, cols = weight.shape
     return pl.pallas_call(
         functools.partial(begin_kernel, blocks),
-        grid=(1,),
-        in_specs=[block(arrived.shape), block((part, cols))]
-        + [block((count, part))] * shards,
-        out_specs=[block(shape) for shape, _ in out],
-        out_shape=[out_hbm(shape, dtype) for shape, dtype in out],
-        compiler_params=params(nbytes),
-        cost_estimate=cost(4 * count * part * cols, nbytes),
-    )(arrived, *in_hbm(weight, hidden[0]), *hidden[1:])
-
-
-def finish_kernel(shards, blocks, low, arrived_ref, hidden_ref, weight_ref, *refs):
+        in_specs=[VMEM] * 3,
+        out_specs=[VMEM] * 3,
+        out_shape=[
+            plain((count, cols), bf16),
+            plain((count, part), f32),
+            plain((blocks, 1, LANE), f32),
+        ],
+        compiler_params=params(8 * count * cols + 8 * count * part),
+        cost_estimate=cost(4 * count * part * cols, 2 * part * cols),
+    )(arrived, weight, hidden)
+
+
+def finish_kernel(shards, blocks, arrived_ref, hidden_ref, weight_ref, *refs):
     before, score_in = refs[:shards], refs[shards : 2 * shards]
     projs, score_ref = refs[2 * shards : 3 * shards], refs[-1]
     proj = times_weight(arrived_ref, weight_ref)
@@ -371,33 +384,20 @@
         score_ref[pl.ds(at * blocks, blocks)] = score_in[s][...] + scores[s]
 
 
-def finish(edges, blocks, arrived, hidden, weight, before, scores):
-    low, high = edges[-2:]
+def finish(blocks, arrived, hidden, weight, before, scores):
     shards = len(before)
     total, part = hidden.shape
     count = total // shards
-    out = [((count, part), bf16)] * shards + [((shards * blocks, 1, LANE), f32)]
-    nbytes = 2 * (total + part) * (high - low) + 14 * total * part
+    cols = weight.shape[1]
     outs = pl.pallas_call(
-        functools.partial(finish_kernel, shards, blocks, low),
-        grid=(1,),
-        in_specs=[
-            block(arrived.shape),
-            block(hidden.shape),
-            pl.BlockSpec(
-                (pl.Element(part), pl.Element(high - low)),
-                lambda i: (0, low),
-                pipeline_mode=pl.Buffered(1),
-            ),
-        ]
-        + [block((count, part))] * shards
-        + [block((blocks, 1, LANE))] * shards,
-        out_specs=[block(shape) for shape, _ in out],
-        out_shape=[out_hbm(shape, dtype) for shape, dtype in out[:-1]]
-        + [jax.ShapeDtypeStruct(*out[-1])],
-        compiler_params=params(nbytes),
-        cost_estimate=cost(2 * total * part * (high - low), nbytes),
-    )(arrived, *in_hbm(hidden, weight, *before, *scores))
+        functools.partial(finish_kernel, shards, blocks),
+        in_specs=[VMEM] * (3 + 2 * shards),
+        out_specs=[VMEM] * (shards + 1),
+        out_shape=[plain((count, part), bf16)] * shards
+        + [plain((shards * blocks, 1, LANE), f32)],
+        compiler_params=params(20 * total * part),
+        cost_estimate=cost(2 * total * part * cols, 2 * part * cols),
+    )(arrived, hidden, weight, *before, *scores)
     return list(outs[:-1]), outs[-1]
 
 
@@ -411,160 +411,127 @@
 
     arrived = take(len(fresh))
     hidden = take(1 + len(fresh))
-    given_ref, *state_hbm = take(4)
-    weight_hbm = take(1)[0] if fresh else None
+    given_ref, weight_ref, *state = take(5)
     take(3 if low else 0)
-    projs, scores, outs = take(len(fresh)), take(len(fresh)), take(3)
-    hidden_t, grad_ref = take(2)
-    state = take(3)
-    in_sems, out_sems = take(2)
+    projs, scores, mixed = take(len(fresh)), take(len(fresh)), take(min(1, len(fresh)))
+    outs, news = take(3), take(3)
+    rows_refs = take(len(fresh))
+    hidden_t, grad_ref, sems = refs
     part, cols = grad_ref.shape
-    given = given_ref.shape[0]
-    step = part // out_sems.shape[1]
-    steps = part // step
-
-    def load(i):
-        rows = pl.ds(pl.multiple_of(i * step, step), step)
-        return [
-            pltpu.make_async_copy(
-                source.at[0, rows, pl.ds(low, cols)], target.at[rows], in_sems.at[j, i]
-            )
-            for j, (source, target) in enumerate(zip(state_hbm, state))
-        ]
-
-    def store(i):
-        rows = pl.ds(pl.multiple_of(i * step, step), step)
-        return [
-            pltpu.make_async_copy(
-                source.at[rows], target.at[0, rows, pl.ds(low, cols)], out_sems.at[j, i]
-            )
-            for j, (source, target) in enumerate(zip(state, outs))
-        ]
-
-    def start_loads(first, end):
-        for i in range(first, end):
-            for copy in load(i):
-                copy.start()
-
-    if fresh:
-        rows_ref, weight_ref, sems = take(3)
-        loads = [
-            pltpu.make_async_copy(weight_hbm.at[:, pl.ds(low, cols)], weight_ref, sems.at[0]),
-            pltpu.make_async_copy(given_ref, rows_ref.at[pl.ds(0, given)], sems.at[1]),
-        ]
-        for copy in loads:
-            copy.start()
-    else:
-        rows_ref = given_ref
-        start_loads(0, min(DEPTH, steps))
+    count = blocks * SEND
+    shards = 1 + len(fresh)
+    for i, s in enumerate(fresh):
+        reorder(arrived[i][...], rows_refs[i])
+        proj = times_weight(rows_refs[i], weight_ref)
+        projs[i][...] = proj
+        scores[i][...] = score_block(
+            blocks, proj, hidden[s][...], [block_index(blocks, count)]
+        )[0]
     base = 0
     for ref in hidden:
-        count = ref.shape[0]
-        hidden_t[:, base : base + count] = ref[...].astype(f32).T.astype(bf16)
-        base += count
-    if fresh:
-        count = blocks * SEND
-        for i, arrived_ref in enumerate(arrived):
-            reorder(
-                arrived_ref[...],
-                rows_ref.at[given + i * count : given + (i + 1) * count],
-            )
-        loads[0].wait()
-        start_loads(0, min(DEPTH, steps))
-        for i in range(len(fresh)):
-            own = rows_ref.at[given + i * count : given + (i + 1) * count]
-            proj = times_weight(own, weight_ref)
-            projs[i][...] = proj
-            scores[i][...] = score_block(
-                blocks, proj, hidden[1 + i][...], [block_index(blocks, count)]
-            )[0]
-        loads[1].wait()
+        high = base + ref.shape[0]
+        hidden_t[:, base:high] = ref[...].astype(f32).T.astype(bf16)
+        base = high
     for i in range(cols // UNIT):
         own = slice(i * UNIT, (i + 1) * UNIT)
-        grad_ref[:, own] = jnp.dot(
-            hidden_t[...], rows_ref[:, own], preferred_element_type=f32
-        )
-
+        base = 0
+        grad = 0.0
+        for rows_ref in [given_ref] + rows_refs:
+            high = base + rows_ref.shape[0]
+            grad += jnp.dot(
+                hidden_t[:, base:high], rows_ref[:, own], preferred_element_type=f32
+            )
+            base = high
+        grad_ref[:, own] = grad
+
+    step = part // sems.shape[1]
     corr_one = 1.0 - beta_one**adam_step
     corr_two = 1.0 - beta_two**adam_step
     rate = learn_rate * corr_two**0.5 / corr_one
     keep = 1.0 - learn_rate * decay_rate
     eps = adam_eps * corr_two**0.5
 
-    @pl.loop(0, steps)
+    def store(i):
+        rows = pl.ds(pl.multiple_of(i * step, step), step)
+        return [
+            pltpu.make_async_copy(
+                source.at[rows], target.at[0, rows, pl.ds(low, cols)], sems.at[j, i]
+            )
+            for j, (source, target) in enumerate(zip(news, outs))
+        ]
+
+    @pl.loop(0, part // step)
     def _(i):
-        for copy in load(i):
-            copy.wait()
-
-        @pl.when(i + DEPTH < steps)
-        def _():
-            for copy in load(i + DEPTH):
-                copy.start()
-
         own = pl.ds(pl.multiple_of(i * step, step), step)
+        at = (own, pl.ds(low, cols))
         grad = grad_ref[own, :]
-        m_new = beta_one * state[1][own, :].astype(f32) + (1.0 - beta_one) * grad
-        v_new = beta_two * state[2][own, :].astype(f32) + (1.0 - beta_two) * (grad * grad)
+        m_new = beta_one * state[1][at].astype(f32) + (1.0 - beta_one) * grad
+        v_new = beta_two * state[2][at].astype(f32) + (1.0 - beta_two) * (grad * grad)
         root = lax.rsqrt(v_new)
         below = 1.0 + eps * root
         inverse = pl.reciprocal(below, approx=True)
         inverse = inverse * (2.0 - below * inverse)
-        state[0][own, :] = keep * state[0][own, :] - (rate * m_new) * (root * inverse)
-        state[1][own, :] = m_new.astype(bf16)
-        state[2][own, :] = v_new.astype(bf16)
+        news[0][own, :] = keep * state[0][at] - (rate * m_new) * (root * inverse)
+        news[1][own, :] = m_new.astype(bf16)
+        news[2][own, :] = v_new.astype(bf16)
         for copy in store(i):
             copy.start()
 
-    @pl.loop(0, steps)
+    if mixed:
+        row = lax.broadcasted_iota(jnp.int32, (shards * count, count), 0)
+        col = lax.broadcasted_iota(jnp.int32, (shards * count, count), 1)
+        at, step_of, slot = mixed_place(row, shards)
+        total = 0.0
+        for s in range(shards):
+            order = (step_of == s) & (col == at * SEND + slot)
+            order = jnp.where(order, 1.0, 0.0).astype(bf16)
+            total += jnp.dot(order, hidden[s][...], preferred_element_type=f32)
+        mixed[0][...] = total.astype(bf16)
+
+    @pl.loop(0, part // step)
     def _(i):
         for copy in store(i):
             copy.wait()
 
 
-def settle(low, blocks, arrived, given, hidden, weight, state, done):
+def settle(low, blocks, arrived, given, hidden, weight, state, shapes, done):
     cols = given.shape[1]
     part = weight.shape[0]
     count = blocks * SEND
     fresh = tuple(range(1, 1 + len(arrived)))
     total = given.shape[0] + count * len(fresh)
-    steps = max(1, part // 64)
-    args = list(arrived) + in_hbm(hidden[0]) + list(hidden[1:])
-    specs = [block(array.shape) for array in args]
-    if fresh:
-        args += in_hbm(given)
-        specs.append(HBM)
-    else:
-        args.append(given)
-        specs.append(block(given.shape))
-    args += in_hbm(*state, *([weight] if fresh else []), *done)
-    specs += [HBM] * (3 + bool(fresh) + len(done))
-    out = [((count, part), f32)] * len(fresh) + [((blocks, 1, LANE), f32)] * len(fresh)
-    scratch = [pltpu.VMEM((part, total), bf16), pltpu.VMEM((part, cols), f32)]
-    scratch += [pltpu.VMEM((part, cols), kind) for kind in (f32, bf16, bf16)]
-    scratch += [pltpu.SemaphoreType.DMA((3, steps))] * 2
-    if fresh:
-        scratch += [
-            pltpu.VMEM((total, cols), bf16),
-            pltpu.VMEM((part, cols), bf16),
-            pltpu.SemaphoreType.DMA((2,)),
-        ]
+    step = min(part, 64)
+    args = [*arrived, *hidden, given, weight, *state] + in_hbm(*done)
+    out = [plain((count, part), f32)] * len(fresh)
+    out += [plain((blocks, 1, LANE), f32)] * len(fresh)
+    out += [plain((total, part), bf16)] * min(1, len(fresh))
+    scratch = [pltpu.VMEM((part, cols), kind) for kind in (f32, bf16, bf16)]
+    scratch += [pltpu.VMEM((count, cols), bf16)] * len(fresh)
+    scratch += [
+        pltpu.VMEM((part, total), bf16),
+        pltpu.VMEM((part, cols), f32),
+        pltpu.SemaphoreType.DMA((3, part // step)),
+    ]
     nbytes = 14 * part * cols + 4 * total * cols + 8 * total * part
     outs = pl.pallas_call(
         functools.partial(settle_kernel, low, fresh, blocks),
-        grid=(1,),
-        in_specs=specs,
-        out_specs=[block(shape) for shape, _ in out] + [HBM] * 3,
-        out_shape=[out_hbm(shape, dtype) for shape, dtype in out]
-        + [out_hbm(array.shape, array.dtype) for array in state],
+        in_specs=[VMEM] * (len(args) - len(done)) + [HBM] * len(done),
+        out_specs=[VMEM] * len(out) + [HBM] * 3,
+        out_shape=out + [out_hbm(array.shape, array.dtype) for array in shapes],
         scratch_shapes=scratch,
         input_output_aliases={
             len(args) - len(done) + i: len(out) + i for i in range(len(done))
         },
         compiler_params=params(nbytes),
-        cost_estimate=cost(4 * total * part * cols, 22 * part * cols, part * cols),
+        cost_estimate=cost(
+            4 * total * part * cols,
+            (SETTLE_COST if fresh else 16) * part * cols,
+            part * cols,
+        ),
     )(*args)
     outs = list(outs)
-    return outs[: len(fresh)], outs[len(fresh) : 2 * len(fresh)], outs[-3:]
+    size = len(fresh)
+    return outs[:size], outs[size : 2 * size], outs[2 * size : -3], outs[-3:]
 
 
 def close_kernel(shards, gate_up_ref, ids_ref, slots_ref, gates_ref, score_ref, *refs):
@@ -595,7 +562,7 @@
 
 def close(gate_up, ids, slots, gates, score, grads):
     size = gate_up.size
-    args = in_hbm(gate_up, ids, slots, gates) + [score] + in_hbm(grads[0]) + grads[1:]
+    args = in_hbm(gate_up, ids, slots, gates) + [score] + list(grads)
     shapes = [(gate_up.shape, bf16), (ids.shape, f32)]
     return pl.pallas_call(
         functools.partial(close_kernel, len(grads)),
@@ -628,31 +595,26 @@
 
     send_a, send_b = dispatch(ep_size, edges, ids_t, slots_t, gates_t, out_grad)
     mixed = [send_b] + [shift(send_b, s) for s in steps]
-    parts = hidden_parts(gate_up, rep_size, send_b)
+    parts = list(hidden_parts(gate_up, rep_size, send_b))
     hidden = [parts[0]] + [shift(parts[s], s) for s in steps]
-    weight = cast_weight(master, send_b)
+    *held, weight_a, weight_b = load_state(edges[1], *state, send_b)
     arrived = exchange(send_a.reshape(ep_size, ROWS, -1)).reshape(send_a.shape)
-    mixed = mix(mixed, weight)
+    mixed = mix(mixed, [weight_a] + parts[1:])
     arrived_b = exchange(mixed.reshape(ep_size, rep_size * SEND, -1)).reshape(mixed.shape)
 
-    arrived, *hidden[1:] = lax.optimization_barrier([arrived] + hidden[1:])
     peers = [shift(arrived, s) for s in steps]
-    rows, proj, score_own, hidden_mixed = begin(ep_size, edges[1], arrived, weight, hidden)
-    before, scores, done = settle(0, ep_size, peers, rows, hidden, weight, state, ())
+    rows, proj, score_own = begin(ep_size, arrived, weight_a, hidden[0])
+    before, scores, (hidden_mixed,), done = settle(
+        0, ep_size, peers, rows, hidden, weight_a, held, state, ()
+    )
     projs, score = finish(
-        edges,
-        ep_size,
-        arrived_b,
-        hidden_mixed,
-        weight,
-        [proj] + before,
-        [score_own] + scores,
+        ep_size, arrived_b, hidden_mixed, weight_b, [proj] + before, [score_own] + scores
     )
     grads = [projs[0]] + [shift(projs[s], rep_size - s) for s in steps]
     score = lax.all_to_all(score, ("rep", "ep"), split_axis=0, concat_axis=0, tiled=True)
 
-    _, _, done = settle(
-        edges[1], ep_size, [], arrived_b, [hidden_mixed], weight, state, done
+    *_, done = settle(
+        edges[1], ep_size, [], arrived_b, [hidden_mixed], weight_b, held, state, done
     )
     grad_gate_up, gate_grad = close(
         gate_up, ids_t, slots_t, gates_t, score, grads

time: 97.8 us -> 106 us (1.084)
  local copies, waits for them, and re-layouts: 0 us -> 30.2 us
  Pallas kernels: 44.2 us -> 31.9 us
  waiting for transfers between devices: 28.4 us -> 18.9 us
    unnamed x0 -> x40, local copies, waits for them, and re-layouts: none -> 30.2 us
    pallas_call x5, Pallas kernels: 32.8 us -> 21.1 us  [the longest x2 11.6 us: settle(): pl.pallas_call(functools.partial(settle_kernel, low, fresh, blocks), in_s...]
    ppermute x4, waiting for transfers between devices: 28.4 us -> 18.9 us  [shift(): return lax.ppermute(value, 'rep', perm)]
    ppermute x4, starting transfers between devices: 6.14 us -> 4.67 us  [shift(): return lax.ppermute(value, 'rep', perm)]
  transfers between devices with their start and end apart: 7 -> 7, of which waited for: 3 -> 1; matrix products, arithmetic and copies ran while one was open for 0% -> 0% of each run, Pallas kernels for 36% -> 23%
where the time goes in v6:
time: 106 us; the launch traced here: 105 us
  Pallas kernels  31.9 us (30%)
  local copies, waits for them, and re-layouts  30.2 us (28%)
  starting transfers between devices  23.2 us (22%)
  waiting for transfers between devices  18.9 us (18%)
    unnamed x40, local copies, waits for them, and re-layouts  30.2 us
    ppermute x4, waiting for transfers between devices, shift(): return lax.ppermute(value, 'rep', perm)  18.9 us
    all_to_all x2, starting transfers between devices, exchange(): return lax.all_to_all(value, 'ep', split_axis=0, concat_axis=0, tiled=True)  13.3 us
    pallas_call x2, Pallas kernels, settle(): pl.pallas_call(functools.partial(settle_kernel, low, fresh, blocks), in_s...  11.6 us
    pallas_call x1, Pallas kernels, load_state(): pl.pallas_call(functools.partial(load_kernel, middle), in_specs=[HBM] * 4...  5.31 us
    all_to_all x1, starting transfers between devices, per_device(): lax.all_to_all(score, ('rep', 'ep'), split_axis=0, concat_axis=0, tiled=T...  5.2 us
    ppermute x4, starting transfers between devices, shift(): return lax.ppermute(value, 'rep', perm)  4.67 us
    pallas_call x1, Pallas kernels, mix(): pl.pallas_call(functools.partial(mix_kernel, shards), grid=(1,), in_specs...  3.46 us
  transfers between devices with their start and end apart: 7, of which 1 were waited for; matrix products, arithmetic and copies ran while one was open for 0% of the time, Pallas kernels for 23%

profile of v6, /device:TPU:0, one launch (start us, length us, event | category | flops | bytes accessed | tf_op | source)
XLA Modules:
  0.0 105.1 jit_solution(4924551203716567605)
XLA Ops:
  0.6 3.3 %shard_map.119 = (bf16[256,1536]{1,0:T(8,128)(2,1)}, bf16[256,1152]{1,0:T(8,128)(2,1)}) custom-call(s32[8,256]{1,0:T(8,128)} %bitcast.16, s32[8,256]{1,0:T(8,128)} %bitcast.18, bf16[8,256]{1,0:T(8,128)(2,1)} %bitcast.20, bf16[256,3584]{1,0:T(8,128)(2,1)} %grad_hbm.1), custom_call_target="tpu_custom_call" | custom-call | flops 469762048 | bytes 3670016 | tf_op jit(solution)/shard_map/pallas_call | solution.py:148
  4.0 7.4 %all-to-all-start.1 = ((bf16[16,16,1536]{2,1,0:T(8,128)(2,1)}), bf16[16,16,1536]{2,1,0:T(8,128)(2,1)}, u32[]{:S(2)}, u32[]{:S(2)}) async-start(bf16[16,16,1536]{2,1,0:T(8,128)(2,1)} %bitcast.15), calls=%async_computation.1 | async-start | bytes 1572864 | tf_op jit(solution)/shard_map/all_to_all | solution.py:594
  11.4 1.6 %collective-permute-start = (bf16[256,1152]{1,0:T(8,128)(2,1)}, bf16[256,1152]{1,0:T(8,128)(2,1)S(1)}, u32[]{:S(2)}, u32[]{:S(2)}) collective-permute-start(bf16[256,1152]{1,0:T(8,128)(2,1)} %get-tuple-element.31.after_ref.refs_0_), channel_id=1, source_target_pairs={{0,16},{16,0},{1,17},{17,1},{2,18},{18,2},{3,19},{19,3},{4,20},{20... | collective-permute-start | bytes 1769480 | tf_op jit(solution)/shard_map/ppermute | solution.py:591
  13.0 5.3 %shard_map.120 = (f32[512,3584]{1,0:T(8,128)S(1)}, bf16[512,3584]{1,0:T(8,128)(2,1)S(1)}, bf16[512,3584]{1,0:T(8,128)(2,1)S(1)}, bf16[512,2048]{1,0:T(8,128)(2,1)S(1)}, bf16[512,1536]{1,0:T(8,128)(2,1)S(1)}) custom-call(bf16[256,1152]{1,0:T(8,128)(2,1)} %get-tuple-element.31.after_ref.refs_0_, f32[1,512,3584]{2,1,0:T(8,128)} %master_hbm.1, ...), custom_call_target="tpu_custom_call" | custom-call | flops 1835008 | bytes 25690112 | tf_op jit(solution)/shard_map/pallas_call | solution.py:222
  18.3 0.0 copy-start
  18.3 2.9 %copy-done = f32[512,3584]{1,0:T(8,128)} copy-done((f32[512,3584]{1,0:T(8,128)}, f32[512,3584]{1,0:T(8,128)S(1)}, u32[]{:S(2)}) %copy-start) | copy-done | bytes 7340056
  21.2 1.9 %copy-done.3 = bf16[512,3584]{1,0:T(8,128)(2,1)} copy-done((bf16[512,3584]{1,0:T(8,128)(2,1)}, bf16[512,3584]{1,0:T(8,128)(2,1)S(1)}, u32[]{:S(2)}) %copy-start.3) | copy-done | bytes 3670040
  23.1 1.9 %copy-done.6 = bf16[512,3584]{1,0:T(8,128)(2,1)} copy-done((bf16[512,3584]{1,0:T(8,128)(2,1)}, bf16[512,3584]{1,0:T(8,128)(2,1)S(1)}, u32[]{:S(2)}) %copy-start.6) | copy-done | bytes 3670040
  25.0 1.2 %copy-done.9 = bf16[512,1536]{1,0:T(8,128)(2,1)} copy-done((bf16[512,1536]{1,0:T(8,128)(2,1)}, bf16[512,1536]{1,0:T(8,128)(2,1)S(1)}, u32[]{:S(2)}) %copy-start.9) | copy-done | bytes 1572888
  26.2 1.3 %shard_map.121 = (bf16[192,512]{1,0:T(8,128)(2,1)S(1)}, bf16[192,512]{1,0:T(8,128)(2,1)S(1)}) custom-call(bf16[192,2048]{1,0:T(8,128)(2,1)} %bitcast.13, bf16[256,1152]{1,0:T(8,128)(2,1)} %get-tuple-element.31.after_ref.refs_0_), custom_call_target="tpu_custom_call" | custom-call | flops 3145728 | bytes 1179648 | tf_op jit(solution)/shard_map/pallas_call | solution.py:185
  27.5 0.0 copy-start.19
  27.5 0.0 collective-permute-done.refs_1_
  27.5 3.5 %shard_map.122 = bf16[384,1536]{1,0:T(8,128)(2,1)} custom-call(bf16[256,1152]{1,0:T(8,128)(2,1)} %get-tuple-element.31.after_ref.refs_0_, bf16[256,1152]{1,0:T(8,128)(2,1)S(1)} %collective-permute-done.refs_1_, bf16[512,2048]{1,0:T(8,128)(2,1)S(1)} %get-tuple-element.32.refs_2_.weight_ref.refs_4_, bf16[192,512]{1,0:T(8,128)(2,1)S(1)} %get-tuple-element.33.refs_3_), custom_call_target="tpu_custom_call" | custom-call | bytes 2949120 | tf_op jit(solution)/shard_map/pallas_call | solution.py:282
  31.0 0.0 all-to-all-done.1
  31.0 0.0 copy-done.19
  31.0 5.9 %all-to-all-start = ((bf16[16,24,1536]{2,1,0:T(8,128)(2,1)}), bf16[16,24,1536]{2,1,0:T(8,128)(2,1)S(1)}, u32[]{:S(2)}, u32[]{:S(2)}) async-start(bf16[16,24,1536]{2,1,0:T(8,128)(2,1)} %bitcast.12), calls=%async_computation | async-start | bytes 2359296 | tf_op jit(solution)/shard_map/all_to_all | solution.py:594
  36.9 1.1 %collective-permute-start.1 = (bf16[256,1536]{1,0:T(8,128)(2,1)}, bf16[256,1536]{1,0:T(8,128)(2,1)S(1)}, u32[]{:S(2)}, u32[]{:S(2)}) collective-permute-start(bf16[256,1536]{1,0:T(8,128)(2,1)} %bitcast.7.arrived_ref), channel_id=1, source_target_pairs={{0,16},{16,0},{1,17},{17,1},{2,18},{18,2},{3,19},{19,3},{4,20},{20... | collective-permute-start | bytes 2359304 | tf_op jit(solution)/shard_map/ppermute | solution.py:591
  37.9 1.0 collective-permute-start.2
  39.0 2.5 %shard_map.123 = (bf16[192,2048]{1,0:T(8,128)(2,1)S(1)}, f32[192,512]{1,0:T(8,128)S(1)}, f32[16,1,128]{2,1,0:T(1,128)S(1)}) custom-call(bf16[256,1536]{1,0:T(8,128)(2,1)} %bitcast.7.arrived_ref, bf16[512,2048]{1,0:T(8,128)(2,1)S(1)} %get-tuple-element.32.refs_2_.weight_ref.refs_4_, bf16[192,512]{1,0:T(8,128)(2,1)S(1)} %get-tuple-element.35.hidden_ref.refs_1_), custom_call_target="tpu_custom_call" | custom-call | flops 805306368 | bytes 2097152 | tf_op jit(solution)/shard_map/pallas_call | solution.py:352
  41.5 0.0 copy-start.15
  41.5 0.8 copy-done.15
  42.2 18.9 %collective-permute-done.2.refs_2_ = bf16[192,512]{1,0:T(8,128)(2,1)S(1)} collective-permute-done((bf16[192,512]{1,0:T(8,128)(2,1)}, bf16[192,512]{1,0:T(8,128)(2,1)S(1)}, u32[]{:S(2)}, u32[]{:S(2)}) %collective-permute-start.2) | collective-permute-done | bytes 196640 | tf_op jit(solution)/shard_map/ppermute | solution.py:591
  61.2 0.0 collective-permute-done.1.refs_0_
  61.2 3.1 %copy-done.1 = f32[512,3584]{1,0:T(8,128)S(1)} copy-done((f32[512,3584]{1,0:T(8,128)S(1)}, f32[512,3584]{1,0:T(8,128)}, u32[]{:S(2)}) %copy-start.1) | copy-done | bytes 7340056
  64.2 2.0 %copy-done.4 = bf16[512,3584]{1,0:T(8,128)(2,1)S(1)} copy-done((bf16[512,3584]{1,0:T(8,128)(2,1)S(1)}, bf16[512,3584]{1,0:T(8,128)(2,1)}, u32[]{:S(2)}) %copy-start.4) | copy-done | bytes 3670040
  66.3 2.0 %copy-done.7 = bf16[512,3584]{1,0:T(8,128)(2,1)S(1)} copy-done((bf16[512,3584]{1,0:T(8,128)(2,1)S(1)}, bf16[512,3584]{1,0:T(8,128)(2,1)}, u32[]{:S(2)}) %copy-start.7) | copy-done | bytes 3670040
  68.3 7.1 %shard_map.124 = (f32[192,512]{1,0:T(8,128)S(1)}, f32[16,1,128]{2,1,0:T(1,128)S(1)}, bf16[384,512]{1,0:T(8,128)(2,1)S(1)}, f32[1,512,3584]{2,1,0:T(8,128)}, bf16...) custom-call(bf16[256,1536]{1,0:T(8,128)(2,1)S(1)} %collective-permute-done.1.refs_0_, ...), custom_call_target="tpu_custom_call" | custom-call | flops 1610612736 | bytes 146800640 | tf_op jit(solution)/shard_map/pallas_call | solution.py:516
  75.4 0.0 copy-start.12
  75.5 0.7 copy-done.12
  76.2 0.8 copy-done.17
  77.0 0.0 all-to-all-done
  77.0 1.4 %copy-done.10 = bf16[512,1536]{1,0:T(8,128)(2,1)S(1)} copy-done((bf16[512,1536]{1,0:T(8,128)(2,1)S(1)}, bf16[512,1536]{1,0:T(8,128)(2,1)}, u32[]{:S(2)}) %copy-start.10) | copy-done | bytes 1572888
  78.4 1.0 copy-done.13
  79.4 1.0 copy-done.16
  80.4 1.0 copy-done.18
  81.4 1.7 %shard_map.125 = (bf16[192,512]{1,0:T(8,128)(2,1)S(1)}, bf16[192,512]{1,0:T(8,128)(2,1)S(1)}, f32[32,1,128]{2,1,0:T(1,128)}) custom-call(bf16[384,1536]{1,0:T(8,128)(2,1)S(1)} %bitcast.10, bf16[384,512]{1,0:T(8,128)(2,1)S(1)} %copy-done.13, bf16[512,1536]{1,0:T(8,128)(2,1)S(1)} %copy-done.10, f32[192,512]{1,0:T(8,128)S(1)} %copy-done.16, ...), custom_call_target="tpu_custom_call" | custom-call | flops 603979776 | bytes 1572864 | tf_op jit(solution)/shard_map/pallas_call | solution.py:392
  83.0 1.0 collective-permute-start.3
  84.0 5.2 %all-to-all-start.2 = ((f32[32,1,128]{2,1,0:T(1,128)}), f32[32,1,128]{2,1,0:T(1,128)S(1)}, u32[]{:S(2)}, u32[]{:S(2)}) async-start(f32[32,1,128]{2,1,0:T(1,128)} %get-tuple-element.46), calls=%async_computation.2 | async-start | bytes 32768 | tf_op jit(solution)/shard_map/all_to_all | solution.py:614
  89.2 0.0 copy-done.14
  89.2 0.0 copy-start.2
  89.2 3.1 %copy-done.2 = f32[512,3584]{1,0:T(8,128)S(1)} copy-done((f32[512,3584]{1,0:T(8,128)S(1)}, f32[512,3584]{1,0:T(8,128)}, u32[]{:S(2)}) %copy-start.2) | copy-done | bytes 7340056
  92.3 2.0 %copy-done.5 = bf16[512,3584]{1,0:T(8,128)(2,1)S(1)} copy-done((bf16[512,3584]{1,0:T(8,128)(2,1)S(1)}, bf16[512,3584]{1,0:T(8,128)(2,1)}, u32[]{:S(2)}) %copy-start.5) | copy-done | bytes 3670040
  94.4 2.0 %copy-done.8 = bf16[512,3584]{1,0:T(8,128)(2,1)S(1)} copy-done((bf16[512,3584]{1,0:T(8,128)(2,1)S(1)}, bf16[512,3584]{1,0:T(8,128)(2,1)}, u32[]{:S(2)}) %copy-start.8) | copy-done | bytes 3670040
  96.4 1.4 %copy-done.11 = bf16[512,1536]{1,0:T(8,128)(2,1)S(1)} copy-done((bf16[512,1536]{1,0:T(8,128)(2,1)S(1)}, bf16[512,1536]{1,0:T(8,128)(2,1)}, u32[]{:S(2)}) %copy-start.11) | copy-done | bytes 1572888
  97.8 4.5 %shard_map.127 = (f32[1,512,3584]{2,1,0:T(8,128)}, bf16[1,512,3584]{2,1,0:T(8,128)(2,1)}, bf16[1,512,3584]{2,1,0:T(8,128)(2,1)}) custom-call(bf16[384,512]{1,0:T(8,128)(2,1)S(1)} %copy-done.14, bf16[384,1536]{1,0:T(8,128)(2,1)S(1)} %bitcast.11, bf16[512,1536]{1,0:T(8,128)(2,1)S(1)} %copy-done.11, ...), custom_call_target="tpu_custom_call", output_to_operand_aliasing={{0}: (6, {}), {1}: (7, {}), {2}: (8, {})} | custom-call | flops 1207959552 | bytes 12582912 | tf_op jit(solution)/shard_map/pallas_call | solution.py:516
  102.3 0.0 all-to-all-done.2.score_ref
  102.4 0.0 collective-permute-done.3.refs_1_
  102.4 2.7 %shard_map.126 = (bf16[192,2048]{1,0:T(8,128)(2,1)}, f32[8,256]{1,0:T(8,128)}) custom-call(bf16[192,2048]{1,0:T(8,128)(2,1)} %bitcast.14, s32[8,256]{1,0:T(8,128)} %bitcast.17, s32[8,256]{1,0:T(8,128)} %bitcast.19, bf16[8,256]{1,0:T(8,128)(2,1)} %bitcast.21, f32[32,1,128]{2,1,0:T(1,128)S(1)} %all-to-all-done.2.score_ref, ...), custom_call_target="tpu_custom_call" | custom-call | flops 4718592 | bytes 1966080 | tf_op jit(solution)/shard_map/pallas_call | solution.py:567
  (15 shorter events, 0.0 us)
Async XLA Ops:
  4.0 27.0 %all-to-all-start.1 = ((bf16[16,16,1536]{2,1,0:T(8,128)(2,1)}), bf16[16,16,1536]{2,1,0:T(8,128)(2,1)}, u32[]{:S(2)}, u32[]{:S(2)}) async-start(bf16[16,16,1536]{2,1,0:T(8,128)(2,1)} %bitcast.15), calls=%async_computation.1 | async-start | bytes 1572864 | tf_op jit(solution)/shard_map/all_to_all | solution.py:594
  11.4 16.1 %collective-permute-start = (bf16[256,1152]{1,0:T(8,128)(2,1)}, bf16[256,1152]{1,0:T(8,128)(2,1)S(1)}, u32[]{:S(2)}, u32[]{:S(2)}) collective-permute-start(bf16[256,1152]{1,0:T(8,128)(2,1)} %get-tuple-element.31.after_ref.refs_0_), channel_id=1, source_target_pairs={{0,16},{16,0},{1,17},{17,1},{2,18},{18,2},{3,19},{19,3},{4,20},{20... | collective-permute-start | bytes 1769480 | tf_op jit(solution)/shard_map/ppermute | solution.py:591
  18.3 2.9 %copy-start = (f32[512,3584]{1,0:T(8,128)}, f32[512,3584]{1,0:T(8,128)S(1)}, u32[]{:S(2)}) copy-start(f32[512,3584]{1,0:T(8,128)S(1)} %get-tuple-element.37.refs_5_.refs_3_) | copy-start | bytes 22020100
  21.2 1.9 %copy-start.3 = (bf16[512,3584]{1,0:T(8,128)(2,1)}, bf16[512,3584]{1,0:T(8,128)(2,1)S(1)}, u32[]{:S(2)}) copy-start(bf16[512,3584]{1,0:T(8,128)(2,1)S(1)} %get-tuple-element.38.refs_6_.refs_4_) | copy-start | bytes 11010052
  23.1 1.9 %copy-start.6 = (bf16[512,3584]{1,0:T(8,128)(2,1)}, bf16[512,3584]{1,0:T(8,128)(2,1)S(1)}, u32[]{:S(2)}) copy-start(bf16[512,3584]{1,0:T(8,128)(2,1)S(1)} %get-tuple-element.39.refs_7_.refs_5_) | copy-start | bytes 11010052
  25.0 1.2 %copy-start.9 = (bf16[512,1536]{1,0:T(8,128)(2,1)}, bf16[512,1536]{1,0:T(8,128)(2,1)S(1)}, u32[]{:S(2)}) copy-start(bf16[512,1536]{1,0:T(8,128)(2,1)S(1)} %get-tuple-element.41.weight_ref.refs_2_) | copy-start | bytes 4718596
  27.5 3.5 %copy-start.19 = (bf16[192,512]{1,0:T(8,128)(2,1)}, bf16[192,512]{1,0:T(8,128)(2,1)S(1)}, u32[]{:S(2)}) copy-start(bf16[192,512]{1,0:T(8,128)(2,1)S(1)} %get-tuple-element.33.refs_3_) | copy-start | bytes 589828
  31.0 46.0 %all-to-all-start = ((bf16[16,24,1536]{2,1,0:T(8,128)(2,1)}), bf16[16,24,1536]{2,1,0:T(8,128)(2,1)S(1)}, u32[]{:S(2)}, u32[]{:S(2)}) async-start(bf16[16,24,1536]{2,1,0:T(8,128)(2,1)} %bitcast.12), calls=%async_computation | async-start | bytes 2359296 | tf_op jit(solution)/shard_map/all_to_all | solution.py:594
  36.9 24.3 %collective-permute-start.1 = (bf16[256,1536]{1,0:T(8,128)(2,1)}, bf16[256,1536]{1,0:T(8,128)(2,1)S(1)}, u32[]{:S(2)}, u32[]{:S(2)}) collective-permute-start(bf16[256,1536]{1,0:T(8,128)(2,1)} %bitcast.7.arrived_ref), channel_id=1, source_target_pairs={{0,16},{16,0},{1,17},{17,1},{2,18},{18,2},{3,19},{19,3},{4,20},{20... | collective-permute-start | bytes 2359304 | tf_op jit(solution)/shard_map/ppermute | solution.py:591
  37.9 23.2 %collective-permute-start.2 = (bf16[192,512]{1,0:T(8,128)(2,1)}, bf16[192,512]{1,0:T(8,128)(2,1)S(1)}, u32[]{:S(2)}, u32[]{:S(2)}) collective-permute-start(bf16[192,512]{1,0:T(8,128)(2,1)} %copy-done.19), channel_id=1, source_target_pairs={{0,16},{16,0},{1,17},{17,1},{2,18},{18,2},{3,19},{19,3},{4,20},{20... | collective-permute-start | bytes 589832 | tf_op jit(solution)/shard_map/ppermute | solution.py:591
  41.5 0.8 copy-start.15
  61.2 3.1 %copy-start.1 = (f32[512,3584]{1,0:T(8,128)S(1)}, f32[512,3584]{1,0:T(8,128)}, u32[]{:S(2)}) copy-start(f32[512,3584]{1,0:T(8,128)} %copy-done) | copy-start | bytes 22020100
  64.2 2.0 %copy-start.4 = (bf16[512,3584]{1,0:T(8,128)(2,1)S(1)}, bf16[512,3584]{1,0:T(8,128)(2,1)}, u32[]{:S(2)}) copy-start(bf16[512,3584]{1,0:T(8,128)(2,1)} %copy-done.3) | copy-start | bytes 11010052
  66.3 2.0 %copy-start.7 = (bf16[512,3584]{1,0:T(8,128)(2,1)S(1)}, bf16[512,3584]{1,0:T(8,128)(2,1)}, u32[]{:S(2)}) copy-start(bf16[512,3584]{1,0:T(8,128)(2,1)} %copy-done.6) | copy-start | bytes 11010052
  75.4 0.7 copy-start.12
  76.2 0.8 copy-start.17
  77.0 1.4 %copy-start.10 = (bf16[512,1536]{1,0:T(8,128)(2,1)S(1)}, bf16[512,1536]{1,0:T(8,128)(2,1)}, u32[]{:S(2)}) copy-start(bf16[512,1536]{1,0:T(8,128)(2,1)} %copy-done.9) | copy-start | bytes 4718596
  78.4 1.0 copy-start.13
  79.4 1.0 copy-start.16
  80.4 1.0 copy-start.18
  81.4 7.9 %copy-start.14 = (bf16[384,512]{1,0:T(8,128)(2,1)S(1)}, bf16[384,512]{1,0:T(8,128)(2,1)}, u32[]{:S(2)}) copy-start(bf16[384,512]{1,0:T(8,128)(2,1)} %copy-done.12) | copy-start | bytes 1179652
  83.0 19.3 %collective-permute-start.3 = (bf16[192,512]{1,0:T(8,128)(2,1)S(1)}, bf16[192,512]{1,0:T(8,128)(2,1)S(1)}, u32[]{:S(2)}, u32[]{:S(2)}) collective-permute-start(bf16[192,512]{1,0:T(8,128)(2,1)S(1)} %get-tuple-element.48), channel_id=1, source_target_pairs={{0,16},{16,0},{1,17},{17,1},{2,18},{18,2},{3,19},{19,3},{4,20},{20... | collective-permute-start | bytes 589832 | tf_op jit(solution)/shard_map/ppermute | solution.py:591
  84.0 18.3 %all-to-all-start.2 = ((f32[32,1,128]{2,1,0:T(1,128)}), f32[32,1,128]{2,1,0:T(1,128)S(1)}, u32[]{:S(2)}, u32[]{:S(2)}) async-start(f32[32,1,128]{2,1,0:T(1,128)} %get-tuple-element.46), calls=%async_computation.2 | async-start | bytes 32768 | tf_op jit(solution)/shard_map/all_to_all | solution.py:614
  89.2 3.1 %copy-start.2 = (f32[512,3584]{1,0:T(8,128)S(1)}, f32[512,3584]{1,0:T(8,128)}, u32[]{:S(2)}) copy-start(f32[512,3584]{1,0:T(8,128)} %copy-done) | copy-start | bytes 22020100
  92.3 2.0 %copy-start.5 = (bf16[512,3584]{1,0:T(8,128)(2,1)S(1)}, bf16[512,3584]{1,0:T(8,128)(2,1)}, u32[]{:S(2)}) copy-start(bf16[512,3584]{1,0:T(8,128)(2,1)} %copy-done.3) | copy-start | bytes 11010052
  94.4 2.0 %copy-start.8 = (bf16[512,3584]{1,0:T(8,128)(2,1)S(1)}, bf16[512,3584]{1,0:T(8,128)(2,1)}, u32[]{:S(2)}) copy-start(bf16[512,3584]{1,0:T(8,128)(2,1)} %copy-done.6) | copy-start | bytes 11010052
  96.4 1.4 %copy-start.11 = (bf16[512,1536]{1,0:T(8,128)(2,1)S(1)}, bf16[512,1536]{1,0:T(8,128)(2,1)}, u32[]{:S(2)}) copy-start(bf16[512,1536]{1,0:T(8,128)(2,1)} %copy-done.9) | copy-start | bytes 4718596

commit v7 on v6

--- a/solution.py
+++ b/solution.py
@@ -12,7 +12,6 @@
 SEND = 12
 LANE = 128
 UNIT = 512
-SETTLE_COST = 140
 ROWS = 16
 
 beta_one = 0.9
@@ -195,45 +194,63 @@
 
 def load_kernel(middle, after_ref, master_hbm, one_hbm, two_hbm, *refs):
     del after_ref
-    master_ref, one_ref, two_ref, weight_a, weight_b, sems = refs
+    master_ref, one_ref, two_ref, weight_a, weight_b, rest_ref, sems = refs
     part = master_ref.shape[0]
+    rest = rest_ref.shape[1]
     step = part // 4
     copies = []
     for i in range(4):
         own = pl.ds(i * step, step)
         copies.append(
-            pltpu.make_async_copy(master_hbm.at[0, own], master_ref.at[own], sems.at[i])
+            pltpu.make_async_copy(
+                master_hbm.at[0, own, pl.ds(0, middle)], master_ref.at[own], sems.at[i]
+            )
         )
-    copies.append(pltpu.make_async_copy(one_hbm.at[0], one_ref, sems.at[4]))
-    copies.append(pltpu.make_async_copy(two_hbm.at[0], two_ref, sems.at[5]))
+    for i in range(4):
+        own = pl.ds(i * step, step)
+        copies.append(
+            pltpu.make_async_copy(
+                master_hbm.at[0, own, pl.ds(middle, rest)], rest_ref.at[own], sems.at[4 + i]
+            )
+        )
+    for i, (source, target) in enumerate([(one_hbm, one_ref), (two_hbm, two_ref)]):
+        copies.append(
+            pltpu.make_async_copy(source.at[0, :, pl.ds(0, middle)], target, sems.at[8 + i])
+        )
     for copy in copies:
         copy.start()
     for i in range(4):
         copies[i].wait()
         own = slice(i * step, (i + 1) * step)
-        weight_a[own, :] = master_ref[own, :middle].astype(bf16)
-        weight_b[own, :] = master_ref[own, middle:].astype(bf16)
-    copies[4].wait()
-    copies[5].wait()
+        weight_a[own, :] = master_ref[own, :].astype(bf16)
+    for i in range(4):
+        copies[4 + i].wait()
+        own = slice(i * step, (i + 1) * step)
+        weight_b[own, :] = rest_ref[own, :].astype(bf16)
+    copies[8].wait()
+    copies[9].wait()
 
 
 def load_state(middle, master, one, two, after):
     _, part, width = master.shape
     return pl.pallas_call(
         functools.partial(load_kernel, middle),
-        in_specs=[HBM] * 4,
+        in_specs=[ANY] + [HBM] * 3,
         out_specs=[VMEM] * 5,
         out_shape=[
-            pltpu.VMEM((part, width), f32),
-            pltpu.VMEM((part, width), bf16),
-            pltpu.VMEM((part, width), bf16),
+            pltpu.VMEM((part, middle), f32),
+            pltpu.VMEM((part, middle), bf16),
+            pltpu.VMEM((part, middle), bf16),
             pltpu.VMEM((part, middle), bf16),
             pltpu.VMEM((part, width - middle), bf16),
         ],
-        scratch_shapes=[pltpu.SemaphoreType.DMA((6,))],
-        compiler_params=params(0),
+        scratch_shapes=[
+            pltpu.VMEM((part, width - middle), f32),
+            pltpu.SemaphoreType.DMA((10,)),
+        ],
+        compiler_params=params(4 * part * (width - middle)),
         cost_estimate=cost(part * width, 14 * part * width),
-    )(*in_hbm(after, master, one, two))
+    )(after, *in_hbm(master, one, two))
 
 
 def mixed_place(index, shards):
@@ -337,13 +354,17 @@
     return lax.broadcasted_iota(jnp.int32, (blocks, count), 0)
 
 
-def begin_kernel(blocks, arrived_ref, weight_ref, hidden_ref, rows_ref, proj_ref, score_ref):
+def begin_kernel(blocks, arrived_ref, weight_ref, hidden_ref, *refs):
+    rows_ref, score_ref, proj_hbm, proj_ref, sem = refs
     reorder(arrived_ref[...], rows_ref)
     proj = times_weight(rows_ref, weight_ref)
     proj_ref[...] = proj
+    copy = pltpu.make_async_copy(proj_ref, proj_hbm, sem.at[0])
+    copy.start()
     score_ref[...] = score_block(
         blocks, proj, hidden_ref[...], [block_index(blocks, proj.shape[0])]
     )[0]
+    copy.wait()
 
 
 def begin(blocks, arrived, weight, hidden):
@@ -352,20 +373,28 @@
     return pl.pallas_call(
         functools.partial(begin_kernel, blocks),
         in_specs=[VMEM] * 3,
-        out_specs=[VMEM] * 3,
+        out_specs=[VMEM] * 2 + [HBM],
         out_shape=[
             plain((count, cols), bf16),
-            plain((count, part), f32),
             plain((blocks, 1, LANE), f32),
+            out_hbm((count, part), f32),
         ],
+        scratch_shapes=[pltpu.VMEM((count, part), f32), pltpu.SemaphoreType.DMA((1,))],
         compiler_params=params(8 * count * cols + 8 * count * part),
         cost_estimate=cost(4 * count * part * cols, 2 * part * cols),
     )(arrived, weight, hidden)
 
 
 def finish_kernel(shards, blocks, arrived_ref, hidden_ref, weight_ref, *refs):
-    before, score_in = refs[:shards], refs[shards : 2 * shards]
-    projs, score_ref = refs[2 * shards : 3 * shards], refs[-1]
+    before_hbm, score_in = refs[:shards], refs[shards : 2 * shards]
+    projs, score_ref = refs[2 * shards : 3 * shards], refs[3 * shards]
+    before, sems = refs[3 * shards + 1 :]
+    copies = [
+        pltpu.make_async_copy(ref, before.at[s], sems.at[s])
+        for s, ref in enumerate(before_hbm)
+    ]
+    for copy in copies:
+        copy.start()
     proj = times_weight(arrived_ref, weight_ref)
     rounded = proj.astype(bf16)
     total = proj.shape[0]
@@ -378,7 +407,8 @@
     for s in range(shards):
         order = row == slot + SEND * (div_send(slot) * (shards - 1) + s)
         order = jnp.where(order, 1.0, 0.0).astype(bf16)
-        own = before[s][...] + jnp.dot(order, rounded, preferred_element_type=f32)
+        copies[s].wait()
+        own = before[s] + jnp.dot(order, rounded, preferred_element_type=f32)
         projs[s][...] = own.astype(bf16)
         at = lax.rem(me + shards - s, shards)
         score_ref[pl.ds(at * blocks, blocks)] = score_in[s][...] + scores[s]
@@ -391,52 +421,50 @@
     cols = weight.shape[1]
     outs = pl.pallas_call(
         functools.partial(finish_kernel, shards, blocks),
-        in_specs=[VMEM] * (3 + 2 * shards),
+        in_specs=[VMEM] * 3 + [HBM] * shards + [VMEM] * shards,
         out_specs=[VMEM] * (shards + 1),
         out_shape=[plain((count, part), bf16)] * shards
         + [plain((shards * blocks, 1, LANE), f32)],
+        scratch_shapes=[
+            pltpu.VMEM((shards, count, part), f32),
+            pltpu.SemaphoreType.DMA((shards,)),
+        ],
         compiler_params=params(20 * total * part),
         cost_estimate=cost(2 * total * part * cols, 2 * part * cols),
-    )(arrived, hidden, weight, *before, *scores)
+    )(arrived, hidden, weight, *in_hbm(*before), *scores)
     return list(outs[:-1]), outs[-1]
 
 
-def settle_kernel(low, fresh, blocks, *refs):
-    refs = list(refs)
-
-    def take(number):
-        out = refs[:number]
-        del refs[:number]
-        return out
-
-    arrived = take(len(fresh))
-    hidden = take(1 + len(fresh))
-    given_ref, weight_ref, *state = take(5)
-    take(3 if low else 0)
-    projs, scores, mixed = take(len(fresh)), take(len(fresh)), take(min(1, len(fresh)))
-    outs, news = take(3), take(3)
-    rows_refs = take(len(fresh))
-    hidden_t, grad_ref, sems = refs
-    part, cols = grad_ref.shape
-    count = blocks * SEND
-    shards = 1 + len(fresh)
-    for i, s in enumerate(fresh):
-        reorder(arrived[i][...], rows_refs[i])
-        proj = times_weight(rows_refs[i], weight_ref)
-        projs[i][...] = proj
-        scores[i][...] = score_block(
-            blocks, proj, hidden[s][...], [block_index(blocks, count)]
-        )[0]
+def new_state(master, one, two, grad):
+    corr_one = 1.0 - beta_one**adam_step
+    corr_two = 1.0 - beta_two**adam_step
+    rate = learn_rate * corr_two**0.5 / corr_one
+    keep = 1.0 - learn_rate * decay_rate
+    eps = adam_eps * corr_two**0.5
+    m_new = beta_one * one.astype(f32) + (1.0 - beta_one) * grad
+    v_new = beta_two * two.astype(f32) + (1.0 - beta_two) * (grad * grad)
+    root = lax.rsqrt(v_new)
+    below = 1.0 + eps * root
+    inverse = pl.reciprocal(below, approx=True)
+    inverse = inverse * (2.0 - below * inverse)
+    master = keep * master - (rate * m_new) * (root * inverse)
+    return master, m_new.astype(bf16), v_new.astype(bf16)
+
+
+def transpose_rows(hidden, hidden_t):
     base = 0
     for ref in hidden:
         high = base + ref.shape[0]
         hidden_t[:, base:high] = ref[...].astype(f32).T.astype(bf16)
         base = high
-    for i in range(cols // UNIT):
+
+
+def form_grad(hidden_t, rows_refs, grad_ref):
+    for i in range(grad_ref.shape[1] // UNIT):
         own = slice(i * UNIT, (i + 1) * UNIT)
         base = 0
         grad = 0.0
-        for rows_ref in [given_ref] + rows_refs:
+        for rows_ref in rows_refs:
             high = base + rows_ref.shape[0]
             grad += jnp.dot(
                 hidden_t[:, base:high], rows_ref[:, own], preferred_element_type=f32
@@ -444,94 +472,159 @@
             base = high
         grad_ref[:, own] = grad
 
+
+def state_copies(i, step, low, hbm, vmem, sems, into):
+    cols = vmem[0].shape[1]
+    rows = pl.ds(pl.multiple_of(i * step, step), step)
+    out = []
+    for j, (far, near) in enumerate(zip(hbm, vmem)):
+        ends = (far.at[0, rows, pl.ds(low, cols)], near.at[rows])
+        source, target = ends if into else ends[::-1]
+        out.append(pltpu.make_async_copy(source, target, sems.at[j, i]))
+    return out
+
+
+def settle_kernel(fresh, blocks, *refs):
+    refs = list(refs)
+
+    def take(number):
+        out = refs[:number]
+        del refs[:number]
+        return out
+
+    size = len(fresh)
+    arrived, hidden = take(size), take(1 + size)
+    given_ref, weight_ref, *state = take(5)
+    scores, (mixed_ref,) = take(size), take(1)
+    projs_hbm, outs, news = take(size), take(3), take(3)
+    rows_refs, projs = take(size), take(size)
+    hidden_t, grad_ref, sems, proj_sems = refs
+    part = grad_ref.shape[0]
+    count = blocks * SEND
+    shards = 1 + size
+    proj_copies = []
+    for i, s in enumerate(fresh):
+        reorder(arrived[i][...], rows_refs[i])
+        proj = times_weight(rows_refs[i], weight_ref)
+        projs[i][...] = proj
+        proj_copies.append(pltpu.make_async_copy(projs[i], projs_hbm[i], proj_sems.at[i]))
+        proj_copies[i].start()
+        scores[i][...] = score_block(
+            blocks, proj, hidden[s][...], [block_index(blocks, count)]
+        )[0]
+    transpose_rows(hidden, hidden_t)
+    form_grad(hidden_t, [given_ref] + rows_refs, grad_ref)
+
     step = part // sems.shape[1]
-    corr_one = 1.0 - beta_one**adam_step
-    corr_two = 1.0 - beta_two**adam_step
-    rate = learn_rate * corr_two**0.5 / corr_one
-    keep = 1.0 - learn_rate * decay_rate
-    eps = adam_eps * corr_two**0.5
-
-    def store(i):
-        rows = pl.ds(pl.multiple_of(i * step, step), step)
-        return [
-            pltpu.make_async_copy(
-                source.at[rows], target.at[0, rows, pl.ds(low, cols)], sems.at[j, i]
-            )
-            for j, (source, target) in enumerate(zip(news, outs))
-        ]
 
     @pl.loop(0, part // step)
     def _(i):
         own = pl.ds(pl.multiple_of(i * step, step), step)
-        at = (own, pl.ds(low, cols))
-        grad = grad_ref[own, :]
-        m_new = beta_one * state[1][at].astype(f32) + (1.0 - beta_one) * grad
-        v_new = beta_two * state[2][at].astype(f32) + (1.0 - beta_two) * (grad * grad)
-        root = lax.rsqrt(v_new)
-        below = 1.0 + eps * root
-        inverse = pl.reciprocal(below, approx=True)
-        inverse = inverse * (2.0 - below * inverse)
-        news[0][own, :] = keep * state[0][at] - (rate * m_new) * (root * inverse)
-        news[1][own, :] = m_new.astype(bf16)
-        news[2][own, :] = v_new.astype(bf16)
-        for copy in store(i):
+        values = new_state(*[ref[own, :] for ref in state], grad_ref[own, :])
+        for ref, value in zip(news, values):
+            ref[own, :] = value
+        for copy in state_copies(i, step, 0, outs, news, sems, False):
             copy.start()
 
-    if mixed:
-        row = lax.broadcasted_iota(jnp.int32, (shards * count, count), 0)
-        col = lax.broadcasted_iota(jnp.int32, (shards * count, count), 1)
-        at, step_of, slot = mixed_place(row, shards)
-        total = 0.0
-        for s in range(shards):
-            order = (step_of == s) & (col == at * SEND + slot)
-            order = jnp.where(order, 1.0, 0.0).astype(bf16)
-            total += jnp.dot(order, hidden[s][...], preferred_element_type=f32)
-        mixed[0][...] = total.astype(bf16)
+    row = lax.broadcasted_iota(jnp.int32, (shards * count, count), 0)
+    col = lax.broadcasted_iota(jnp.int32, (shards * count, count), 1)
+    at, step_of, slot = mixed_place(row, shards)
+    total = 0.0
+    for s in range(shards):
+        order = (step_of == s) & (col == at * SEND + slot)
+        order = jnp.where(order, 1.0, 0.0).astype(bf16)
+        total += jnp.dot(order, hidden[s][...], preferred_element_type=f32)
+    mixed_ref[...] = total.astype(bf16)
 
     @pl.loop(0, part // step)
     def _(i):
-        for copy in store(i):
+        for copy in state_copies(i, step, 0, outs, news, sems, False):
             copy.wait()
 
-
-def settle(low, blocks, arrived, given, hidden, weight, state, shapes, done):
-    cols = given.shape[1]
-    part = weight.shape[0]
+    for copy in proj_copies:
+        copy.wait()
+
+
+def settle(blocks, arrived, given, hidden, weight, held, shapes):
+    part, cols = weight.shape
     count = blocks * SEND
     fresh = tuple(range(1, 1 + len(arrived)))
-    total = given.shape[0] + count * len(fresh)
+    size = len(fresh)
+    total = count * (1 + size)
     step = min(part, 64)
-    args = [*arrived, *hidden, given, weight, *state] + in_hbm(*done)
-    out = [plain((count, part), f32)] * len(fresh)
-    out += [plain((blocks, 1, LANE), f32)] * len(fresh)
-    out += [plain((total, part), bf16)] * min(1, len(fresh))
+    args = [*arrived, *hidden, given, weight, *held]
+    near = [plain((blocks, 1, LANE), f32)] * size + [plain((total, part), bf16)]
+    far = [out_hbm((count, part), f32)] * size
+    far += [out_hbm(array.shape, array.dtype) for array in shapes]
     scratch = [pltpu.VMEM((part, cols), kind) for kind in (f32, bf16, bf16)]
-    scratch += [pltpu.VMEM((count, cols), bf16)] * len(fresh)
+    scratch += [pltpu.VMEM((count, cols), bf16)] * size
+    scratch += [pltpu.VMEM((count, part), f32)] * size
     scratch += [
         pltpu.VMEM((part, total), bf16),
         pltpu.VMEM((part, cols), f32),
         pltpu.SemaphoreType.DMA((3, part // step)),
+        pltpu.SemaphoreType.DMA((max(1, size),)),
     ]
-    nbytes = 14 * part * cols + 4 * total * cols + 8 * total * part
+    nbytes = 12 * part * cols + 4 * total * cols + 8 * total * part
     outs = pl.pallas_call(
-        functools.partial(settle_kernel, low, fresh, blocks),
-        in_specs=[VMEM] * (len(args) - len(done)) + [HBM] * len(done),
-        out_specs=[VMEM] * len(out) + [HBM] * 3,
-        out_shape=out + [out_hbm(array.shape, array.dtype) for array in shapes],
+        functools.partial(settle_kernel, fresh, blocks),
+        in_specs=[VMEM] * len(args),
+        out_specs=[VMEM] * len(near) + [HBM] * len(far),
+        out_shape=near + far,
         scratch_shapes=scratch,
-        input_output_aliases={
-            len(args) - len(done) + i: len(out) + i for i in range(len(done))
-        },
         compiler_params=params(nbytes),
-        cost_estimate=cost(
-            4 * total * part * cols,
-            (SETTLE_COST if fresh else 16) * part * cols,
-            part * cols,
-        ),
+        cost_estimate=cost(4 * total * part * cols, 16 * part * cols, part * cols),
     )(*args)
     outs = list(outs)
-    size = len(fresh)
-    return outs[:size], outs[size : 2 * size], outs[2 * size : -3], outs[-3:]
+    return outs[:size], outs[size], outs[size + 1 : -3], outs[-3:]
+
+
+def update_kernel(low, hidden_ref, rows_ref, *refs):
+    state_hbm, outs, state = refs[:3], refs[6:9], refs[9:12]
+    hidden_t, grad_ref, in_sems, out_sems = refs[12:]
+    part = grad_ref.shape[0]
+    steps = in_sems.shape[1]
+    step = part // steps
+    for i in range(steps):
+        for copy in state_copies(i, step, low, state_hbm, state, in_sems, True):
+            copy.start()
+    transpose_rows([hidden_ref], hidden_t)
+    form_grad(hidden_t, [rows_ref], grad_ref)
+
+    @pl.loop(0, steps)
+    def _(i):
+        for copy in state_copies(i, step, low, state_hbm, state, in_sems, True):
+            copy.wait()
+        own = pl.ds(pl.multiple_of(i * step, step), step)
+        values = new_state(*[ref[own, :] for ref in state], grad_ref[own, :])
+        for ref, value in zip(state, values):
+            ref[own, :] = value
+        for copy in state_copies(i, step, low, outs, state, out_sems, False):
+            copy.start()
+
+    @pl.loop(0, steps)
+    def _(i):
+        for copy in state_copies(i, step, low, outs, state, out_sems, False):
+            copy.wait()
+
+
+def update(low, hidden, rows, state, done):
+    total, part = hidden.shape
+    cols = rows.shape[1]
+    step = min(part, 64)
+    scratch = [pltpu.VMEM((part, cols), kind) for kind in (f32, bf16, bf16)]
+    scratch += [pltpu.VMEM((part, total), bf16), pltpu.VMEM((part, cols), f32)]
+    scratch += [pltpu.SemaphoreType.DMA((3, part // step))] * 2
+    return pl.pallas_call(
+        functools.partial(update_kernel, low),
+        in_specs=[VMEM] * 2 + [HBM] * 6,
+        out_specs=[HBM] * 3,
+        out_shape=[out_hbm(array.shape, array.dtype) for array in state],
+        scratch_shapes=scratch,
+        input_output_aliases={5 + i: i for i in range(3)},
+        compiler_params=params(12 * part * cols + 2 * total * part),
+        cost_estimate=cost(2 * total * part * cols, 16 * part * cols, part * cols),
+    )(hidden, rows, *in_hbm(*state, *done))
 
 
 def close_kernel(shards, gate_up_ref, ids_ref, slots_ref, gates_ref, score_ref, *refs):
@@ -597,15 +690,15 @@
     mixed = [send_b] + [shift(send_b, s) for s in steps]
     parts = list(hidden_parts(gate_up, rep_size, send_b))
     hidden = [parts[0]] + [shift(parts[s], s) for s in steps]
-    *held, weight_a, weight_b = load_state(edges[1], *state, send_b)
     arrived = exchange(send_a.reshape(ep_size, ROWS, -1)).reshape(send_a.shape)
-    mixed = mix(mixed, [weight_a] + parts[1:])
+    mixed = mix(mixed, parts[1:])
     arrived_b = exchange(mixed.reshape(ep_size, rep_size * SEND, -1)).reshape(mixed.shape)
 
     peers = [shift(arrived, s) for s in steps]
-    rows, proj, score_own = begin(ep_size, arrived, weight_a, hidden[0])
-    before, scores, (hidden_mixed,), done = settle(
-        0, ep_size, peers, rows, hidden, weight_a, held, state, ()
+    *held, weight_a, weight_b = load_state(edges[1], *state, arrived)
+    rows, score_own, proj = begin(ep_size, arrived, weight_a, hidden[0])
+    scores, hidden_mixed, before, done = settle(
+        ep_size, peers, rows, hidden, weight_a, held, state
     )
     projs, score = finish(
         ep_size, arrived_b, hidden_mixed, weight_b, [proj] + before, [score_own] + scores
@@ -613,9 +706,7 @@
     grads = [projs[0]] + [shift(projs[s], rep_size - s) for s in steps]
     score = lax.all_to_all(score, ("rep", "ep"), split_axis=0, concat_axis=0, tiled=True)
 
-    *_, done = settle(
-        edges[1], ep_size, [], arrived_b, [hidden_mixed], weight_b, held, state, done
-    )
+    done = update(edges[1], hidden_mixed, arrived_b, state, done)
     grad_gate_up, gate_grad = close(
         gate_up, ids_t, slots_t, gates_t, score, grads
     )

time: 106 us -> 86.7 us (0.82)
  local copies, waits for them, and re-layouts: 30.2 us -> 0.68 us
  waiting for transfers between devices: 18.9 us -> 28.3 us
  Pallas kernels: 31.9 us -> 33.5 us
    unnamed x40 -> x4, local copies, waits for them, and re-layouts: 30.2 us -> 0.68 us
    ppermute x4, waiting for transfers between devices: 18.9 us -> 27.3 us  [shift(): return lax.ppermute(value, 'rep', perm)]
  transfers between devices with their start and end apart: 7 -> 7, of which waited for: 1 -> 3; matrix products, arithmetic and copies ran while one was open for 0% -> 0% of each run, Pallas kernels for 23% -> 29%
where the time goes in v7:
time: 86.7 us; the launch traced here: 86.3 us
  Pallas kernels  33.5 us (39%)
  waiting for transfers between devices  28.3 us (33%)
  starting transfers between devices  23.1 us (27%)
    ppermute x4, waiting for transfers between devices, shift(): return lax.ppermute(value, 'rep', perm)  27.3 us
    all_to_all x2, starting transfers between devices, exchange(): return lax.all_to_all(value, 'ep', split_axis=0, concat_axis=0, tiled=True)  13.1 us
    pallas_call x1, Pallas kernels, settle(): pl.pallas_call(functools.partial(settle_kernel, fresh, blocks), in_specs=...  7.15 us
    pallas_call x1, Pallas kernels, update(): pl.pallas_call(functools.partial(update_kernel, low), in_specs=[VMEM] * 2...  6.23 us
    ppermute x4, starting transfers between devices, shift(): return lax.ppermute(value, 'rep', perm)  5.26 us
    all_to_all x1, starting transfers between devices, per_device(): lax.all_to_all(score, ('rep', 'ep'), split_axis=0, concat_axis=0, tiled=T...  4.71 us
    pallas_call x1, Pallas kernels, load_state(): pl.pallas_call(functools.partial(load_kernel, middle), in_specs=[ANY] + [...  4.47 us
    pallas_call x1, Pallas kernels, mix(): pl.pallas_call(functools.partial(mix_kernel, shards), grid=(1,), in_specs...  3.43 us
  transfers between devices with their start and end apart: 7, of which 3 were waited for; matrix products, arithmetic and copies ran while one was open for 0% of the time, Pallas kernels for 29%

profile of v7, /device:TPU:0, one launch (start us, length us, event | category | flops | bytes accessed | tf_op | source)
XLA Modules:
  0.0 86.3 jit_solution(15189377575951866027)
XLA Ops:
  0.6 3.3 %shard_map.119 = (bf16[256,1536]{1,0:T(8,128)(2,1)}, bf16[256,1152]{1,0:T(8,128)(2,1)}) custom-call(s32[8,256]{1,0:T(8,128)} %bitcast.19, s32[8,256]{1,0:T(8,128)} %bitcast.21, bf16[8,256]{1,0:T(8,128)(2,1)} %bitcast.23, bf16[256,3584]{1,0:T(8,128)(2,1)} %grad_hbm.1), custom_call_target="tpu_custom_call" | custom-call | flops 469762048 | bytes 3670016 | tf_op jit(solution)/shard_map/pallas_call | solution.py:147
  4.0 7.4 %all-to-all-start.1 = ((bf16[16,16,1536]{2,1,0:T(8,128)(2,1)}), bf16[16,16,1536]{2,1,0:T(8,128)(2,1)S(1)}, u32[]{:S(2)}, u32[]{:S(2)}) async-start(bf16[16,16,1536]{2,1,0:T(8,128)(2,1)} %bitcast.18), calls=%async_computation.1 | async-start | bytes 1572864 | tf_op jit(solution)/shard_map/all_to_all | solution.py:687
  11.3 1.6 %collective-permute-start = (bf16[256,1152]{1,0:T(8,128)(2,1)}, bf16[256,1152]{1,0:T(8,128)(2,1)S(1)}, u32[]{:S(2)}, u32[]{:S(2)}) collective-permute-start(bf16[256,1152]{1,0:T(8,128)(2,1)} %get-tuple-element.31.after_ref.refs_0_), channel_id=1, source_target_pairs={{0,16},{16,0},{1,17},{17,1},{2,18},{18,2},{3,19},{19,3},{4,20},{20... | collective-permute-start | bytes 1769480 | tf_op jit(solution)/shard_map/ppermute | solution.py:684
  12.9 1.9 %shard_map.120 = (bf16[192,512]{1,0:T(8,128)(2,1)S(1)}, bf16[192,512]{1,0:T(8,128)(2,1)}) custom-call(bf16[192,2048]{1,0:T(8,128)(2,1)} %bitcast.16, bf16[256,1152]{1,0:T(8,128)(2,1)} %get-tuple-element.31.after_ref.refs_0_), custom_call_target="tpu_custom_call" | custom-call | flops 3145728 | bytes 1179648 | tf_op jit(solution)/shard_map/pallas_call | solution.py:184
  14.8 0.0 copy-start
  14.8 0.7 copy-done
  15.5 11.7 %collective-permute-done.refs_1_ = bf16[256,1152]{1,0:T(8,128)(2,1)S(1)} collective-permute-done((bf16[256,1152]{1,0:T(8,128)(2,1)}, bf16[256,1152]{1,0:T(8,128)(2,1)S(1)}, u32[]{:S(2)}, u32[]{:S(2)}) %collective-permute-start) | collective-permute-done | bytes 589856 | tf_op jit(solution)/shard_map/ppermute | solution.py:684
  27.2 3.4 %shard_map.121 = bf16[384,1536]{1,0:T(8,128)(2,1)} custom-call(bf16[256,1152]{1,0:T(8,128)(2,1)} %get-tuple-element.31.after_ref.refs_0_, bf16[256,1152]{1,0:T(8,128)(2,1)S(1)} %collective-permute-done.refs_1_, bf16[192,512]{1,0:T(8,128)(2,1)} %get-tuple-element.32.refs_2_), custom_call_target="tpu_custom_call" | custom-call | bytes 2949120 | tf_op jit(solution)/shard_map/pallas_call | solution.py:299
  30.6 0.0 all-to-all-done.1
  30.6 5.8 %all-to-all-start = ((bf16[16,24,1536]{2,1,0:T(8,128)(2,1)}), bf16[16,24,1536]{2,1,0:T(8,128)(2,1)S(1)}, u32[]{:S(2)}, u32[]{:S(2)}) async-start(bf16[16,24,1536]{2,1,0:T(8,128)(2,1)} %bitcast.15), calls=%async_computation | async-start | bytes 2359296 | tf_op jit(solution)/shard_map/all_to_all | solution.py:687
  36.4 0.0 copy-start.1
  36.4 1.6 %collective-permute-start.1 = (bf16[256,1536]{1,0:T(8,128)(2,1)S(1)}, bf16[256,1536]{1,0:T(8,128)(2,1)S(1)}, u32[]{:S(2)}, u32[]{:S(2)}) collective-permute-start(bf16[256,1536]{1,0:T(8,128)(2,1)S(1)} %bitcast.12), channel_id=1, source_target_pairs={{0,16},{16,0},{1,17},{17,1},{2,18},{18,2},{3,19},{19,3},{4,20},{20... | collective-permute-start | bytes 2359304 | tf_op jit(solution)/shard_map/ppermute | solution.py:684
  38.0 0.5 collective-permute-start.2
  38.5 4.5 %shard_map.122 = (f32[512,2048]{1,0:T(8,128)S(1)}, bf16[512,2048]{1,0:T(8,128)(2,1)S(1)}, bf16[512,2048]{1,0:T(8,128)(2,1)S(1)}, bf16[512,2048]{1,0:T(8,128)(2,1)S(1)}, bf16[512,1536]{1,0:T(8,128)(2,1)S(1)}) custom-call(bf16[256,1536]{1,0:T(8,128)(2,1)S(1)} %bitcast.13, f32[1,512,3584]{2,1,0:T(8,128)} %refs_0_.1, bf16[1,512,3584]{2,1,0:T(8,128)(2,1)} %refs_1_.1, ...), custom_call_target="tpu_custom_call" | custom-call | flops 1835008 | bytes 25690112 | tf_op jit(solution)/shard_map/pallas_call | solution.py:236
  43.0 0.0 copy-done.1
  43.0 1.9 %shard_map.123 = (bf16[192,2048]{1,0:T(8,128)(2,1)S(1)}, f32[16,1,128]{2,1,0:T(1,128)S(1)}, f32[192,512]{1,0:T(8,128)}) custom-call(bf16[256,1536]{1,0:T(8,128)(2,1)S(1)} %bitcast.14, bf16[512,2048]{1,0:T(8,128)(2,1)S(1)} %get-tuple-element.35.weight_ref.refs_4_, bf16[192,512]{1,0:T(8,128)(2,1)S(1)} %copy-done.1), custom_call_target="tpu_custom_call" | custom-call | flops 805306368 | bytes 2097152 | tf_op jit(solution)/shard_map/pallas_call | solution.py:373
  44.9 15.7 %collective-permute-done.2.refs_2_ = bf16[192,512]{1,0:T(8,128)(2,1)S(1)} collective-permute-done((bf16[192,512]{1,0:T(8,128)(2,1)}, bf16[192,512]{1,0:T(8,128)(2,1)S(1)}, u32[]{:S(2)}, u32[]{:S(2)}) %collective-permute-start.2) | collective-permute-done | bytes 196640 | tf_op jit(solution)/shard_map/ppermute | solution.py:684
  60.5 0.0 collective-permute-done.1.refs_0_
  60.6 7.2 %shard_map.124 = (f32[16,1,128]{2,1,0:T(1,128)S(1)}, bf16[384,512]{1,0:T(8,128)(2,1)S(1)}, f32[192,512]{1,0:T(8,128)}, f32[1,512,3584]{2,1,0:T(8,128)}, bf16[1,5...) custom-call(bf16[256,1536]{1,0:T(8,128)(2,1)S(1)} %collective-permute-done.1.refs_0_, ...), custom_call_target="tpu_custom_call" | custom-call | flops 1610612736 | bytes 16777216 | tf_op jit(solution)/shard_map/pallas_call | solution.py:569
  67.7 0.0 all-to-all-done
  67.7 2.4 %shard_map.125 = (bf16[192,512]{1,0:T(8,128)(2,1)S(1)}, bf16[192,512]{1,0:T(8,128)(2,1)}, f32[32,1,128]{2,1,0:T(1,128)}) custom-call(bf16[384,1536]{1,0:T(8,128)(2,1)S(1)} %bitcast.10, bf16[384,512]{1,0:T(8,128)(2,1)S(1)} %get-tuple-element.40.hidden_ref, bf16[512,1536]{1,0:T(8,128)(2,1)S(1)} %get-tuple-element.41.weight_ref, ...), custom_call_target="tpu_custom_call" | custom-call | flops 603979776 | bytes 1572864 | tf_op jit(solution)/shard_map/pallas_call | solution.py:422
  70.1 1.6 %collective-permute-start.3 = (bf16[192,512]{1,0:T(8,128)(2,1)}, bf16[192,512]{1,0:T(8,128)(2,1)S(1)}, u32[]{:S(2)}, u32[]{:S(2)}) collective-permute-start(bf16[192,512]{1,0:T(8,128)(2,1)} %get-tuple-element.48), channel_id=1, source_target_pairs={{0,16},{16,0},{1,17},{17,1},{2,18},{18,2},{3,19},{19,3},{4,20},{20... | collective-permute-start | bytes 589832 | tf_op jit(solution)/shard_map/ppermute | solution.py:684
  71.7 4.7 %all-to-all-start.2 = ((f32[32,1,128]{2,1,0:T(1,128)}), f32[32,1,128]{2,1,0:T(1,128)S(1)}, u32[]{:S(2)}, u32[]{:S(2)}) async-start(f32[32,1,128]{2,1,0:T(1,128)} %get-tuple-element.46), calls=%async_computation.2 | async-start | bytes 32768 | tf_op jit(solution)/shard_map/all_to_all | solution.py:707
  76.4 6.2 %shard_map.127 = (f32[1,512,3584]{2,1,0:T(8,128)}, bf16[1,512,3584]{2,1,0:T(8,128)(2,1)}, bf16[1,512,3584]{2,1,0:T(8,128)(2,1)}) custom-call(bf16[384,512]{1,0:T(8,128)(2,1)S(1)} %get-tuple-element.40.hidden_ref, bf16[384,1536]{1,0:T(8,128)(2,1)S(1)} %bitcast.11, ...), custom_call_target="tpu_custom_call", output_to_operand_aliasing={{0}: (5, {}), {1}: (6, {}), {2}: (7, {})} | custom-call | flops 603979776 | bytes 12582912 | tf_op jit(solution)/shard_map/pallas_call | solution.py:618
  82.7 0.9 %all-to-all-done.2.score_ref = f32[32,1,128]{2,1,0:T(1,128)S(1)} async-done(((f32[32,1,128]{2,1,0:T(1,128)}), f32[32,1,128]{2,1,0:T(1,128)S(1)}, u32[]{:S(2)}, u32[]{:S(2)}) %all-to-all-start.2) | async-done | bytes 16416 | tf_op jit(solution)/shard_map/all_to_all | solution.py:707
  83.6 0.0 collective-permute-done.3.refs_1_
  83.6 2.7 %shard_map.126 = (bf16[192,2048]{1,0:T(8,128)(2,1)}, f32[8,256]{1,0:T(8,128)}) custom-call(bf16[192,2048]{1,0:T(8,128)(2,1)} %bitcast.17, s32[8,256]{1,0:T(8,128)} %bitcast.20, s32[8,256]{1,0:T(8,128)} %bitcast.22, bf16[8,256]{1,0:T(8,128)(2,1)} %bitcast.24, f32[32,1,128]{2,1,0:T(1,128)S(1)} %all-to-all-done.2.score_ref, ...), custom_call_target="tpu_custom_call" | custom-call | flops 4718592 | bytes 1966080 | tf_op jit(solution)/shard_map/pallas_call | solution.py:660
Async XLA Ops:
  4.0 26.7 %all-to-all-start.1 = ((bf16[16,16,1536]{2,1,0:T(8,128)(2,1)}), bf16[16,16,1536]{2,1,0:T(8,128)(2,1)S(1)}, u32[]{:S(2)}, u32[]{:S(2)}) async-start(bf16[16,16,1536]{2,1,0:T(8,128)(2,1)} %bitcast.18), calls=%async_computation.1 | async-start | bytes 1572864 | tf_op jit(solution)/shard_map/all_to_all | solution.py:687
  11.3 15.9 %collective-permute-start = (bf16[256,1152]{1,0:T(8,128)(2,1)}, bf16[256,1152]{1,0:T(8,128)(2,1)S(1)}, u32[]{:S(2)}, u32[]{:S(2)}) collective-permute-start(bf16[256,1152]{1,0:T(8,128)(2,1)} %get-tuple-element.31.after_ref.refs_0_), channel_id=1, source_target_pairs={{0,16},{16,0},{1,17},{17,1},{2,18},{18,2},{3,19},{19,3},{4,20},{20... | collective-permute-start | bytes 1769480 | tf_op jit(solution)/shard_map/ppermute | solution.py:684
  14.8 0.7 copy-start
  30.6 37.1 %all-to-all-start = ((bf16[16,24,1536]{2,1,0:T(8,128)(2,1)}), bf16[16,24,1536]{2,1,0:T(8,128)(2,1)S(1)}, u32[]{:S(2)}, u32[]{:S(2)}) async-start(bf16[16,24,1536]{2,1,0:T(8,128)(2,1)} %bitcast.15), calls=%async_computation | async-start | bytes 2359296 | tf_op jit(solution)/shard_map/all_to_all | solution.py:687
  36.4 6.6 %copy-start.1 = (bf16[192,512]{1,0:T(8,128)(2,1)S(1)}, bf16[192,512]{1,0:T(8,128)(2,1)}, u32[]{:S(2)}) copy-start(bf16[192,512]{1,0:T(8,128)(2,1)} %copy-done) | copy-start | bytes 589828
  36.4 24.2 %collective-permute-start.1 = (bf16[256,1536]{1,0:T(8,128)(2,1)S(1)}, bf16[256,1536]{1,0:T(8,128)(2,1)S(1)}, u32[]{:S(2)}, u32[]{:S(2)}) collective-permute-start(bf16[256,1536]{1,0:T(8,128)(2,1)S(1)} %bitcast.12), channel_id=1, source_target_pairs={{0,16},{16,0},{1,17},{17,1},{2,18},{18,2},{3,19},{19,3},{4,20},{20... | collective-permute-start | bytes 2359304 | tf_op jit(solution)/shard_map/ppermute | solution.py:684
  38.0 22.6 %collective-permute-start.2 = (bf16[192,512]{1,0:T(8,128)(2,1)}, bf16[192,512]{1,0:T(8,128)(2,1)S(1)}, u32[]{:S(2)}, u32[]{:S(2)}) collective-permute-start(bf16[192,512]{1,0:T(8,128)(2,1)} %get-tuple-element.32.refs_2_), channel_id=1, source_target_pairs={{0,16},{16,0},{1,17},{17,1},{2,18},{18,2},{3,19},{19,3},{4,20},{20... | collective-permute-start | bytes 589832 | tf_op jit(solution)/shard_map/ppermute | solution.py:684
  70.1 13.4 %collective-permute-start.3 = (bf16[192,512]{1,0:T(8,128)(2,1)}, bf16[192,512]{1,0:T(8,128)(2,1)S(1)}, u32[]{:S(2)}, u32[]{:S(2)}) collective-permute-start(bf16[192,512]{1,0:T(8,128)(2,1)} %get-tuple-element.48), channel_id=1, source_target_pairs={{0,16},{16,0},{1,17},{17,1},{2,18},{18,2},{3,19},{19,3},{4,20},{20... | collective-permute-start | bytes 589832 | tf_op jit(solution)/shard_map/ppermute | solution.py:684
  71.7 11.9 %all-to-all-start.2 = ((f32[32,1,128]{2,1,0:T(1,128)}), f32[32,1,128]{2,1,0:T(1,128)S(1)}, u32[]{:S(2)}, u32[]{:S(2)}) async-start(f32[32,1,128]{2,1,0:T(1,128)} %get-tuple-element.46), calls=%async_computation.2 | async-start | bytes 32768 | tf_op jit(solution)/shard_map/all_to_all | solution.py:707

commit v8 on v7

--- a/solution.py
+++ b/solution.py
@@ -12,6 +12,7 @@
 SEND = 12
 LANE = 128
 UNIT = 512
+SETTLE_COST = 525
 ROWS = 16
 
 beta_one = 0.9
@@ -573,23 +574,37 @@
         out_shape=near + far,
         scratch_shapes=scratch,
         compiler_params=params(nbytes),
-        cost_estimate=cost(4 * total * part * cols, 16 * part * cols, part * cols),
+        cost_estimate=cost(4 * total * part * cols, SETTLE_COST * part * cols, part * cols),
     )(*args)
     outs = list(outs)
     return outs[:size], outs[size], outs[size + 1 : -3], outs[-3:]
 
 
-def update_kernel(low, hidden_ref, rows_ref, *refs):
-    state_hbm, outs, state = refs[:3], refs[6:9], refs[9:12]
-    hidden_t, grad_ref, in_sems, out_sems = refs[12:]
+def update_kernel(low, shards, hidden_ref, rows_ref, *refs):
+    grad_refs, refs = refs[:shards], refs[shards:]
+    gate_up_hbm, state_hbm, outs, gate_out = refs[0], refs[1:4], refs[7:10], refs[10]
+    state, refs = refs[11:14], refs[14:]
+    hidden_t, grad_ref, gate_up_ref, gate_new, in_sems, out_sems, sems = refs
     part = grad_ref.shape[0]
     steps = in_sems.shape[1]
     step = part // steps
+    gate_load = pltpu.make_async_copy(gate_up_hbm, gate_up_ref, sems.at[0])
+    gate_store = pltpu.make_async_copy(gate_new, gate_out, sems.at[1])
+    gate_load.start()
     for i in range(steps):
         for copy in state_copies(i, step, low, state_hbm, state, in_sems, True):
             copy.start()
     transpose_rows([hidden_ref], hidden_t)
     form_grad(hidden_t, [rows_ref], grad_ref)
+    gate_load.wait()
+    for s, ref in enumerate(grad_refs):
+        first, second, gate, up, sig = swiglu_part(gate_up_ref, shards, s, ref.shape[1])
+        grad = ref[...].astype(f32)
+        gate_new[:, pl.ds(first, ref.shape[1])] = (
+            grad * up * sig * (1.0 + gate * (1.0 - sig))
+        ).astype(bf16)
+        gate_new[:, pl.ds(second, ref.shape[1])] = (grad * (gate * sig)).astype(bf16)
+    gate_store.start()
 
     @pl.loop(0, steps)
     def _(i):
@@ -607,37 +622,34 @@
         for copy in state_copies(i, step, low, outs, state, out_sems, False):
             copy.wait()
 
-
-def update(low, hidden, rows, state, done):
+    gate_store.wait()
+
+
+def update(low, hidden, rows, grads, gate_up, state, done):
     total, part = hidden.shape
     cols = rows.shape[1]
     step = min(part, 64)
+    shards = len(grads)
     scratch = [pltpu.VMEM((part, cols), kind) for kind in (f32, bf16, bf16)]
     scratch += [pltpu.VMEM((part, total), bf16), pltpu.VMEM((part, cols), f32)]
+    scratch += [pltpu.VMEM(gate_up.shape, bf16)] * 2
     scratch += [pltpu.SemaphoreType.DMA((3, part // step))] * 2
+    scratch += [pltpu.SemaphoreType.DMA((2,))]
     return pl.pallas_call(
-        functools.partial(update_kernel, low),
-        in_specs=[VMEM] * 2 + [HBM] * 6,
-        out_specs=[HBM] * 3,
-        out_shape=[out_hbm(array.shape, array.dtype) for array in state],
+        functools.partial(update_kernel, low, shards),
+        in_specs=[VMEM] * (2 + shards) + [HBM] * 7,
+        out_specs=[HBM] * 4,
+        out_shape=[out_hbm(array.shape, array.dtype) for array in state]
+        + [out_hbm(gate_up.shape, bf16)],
         scratch_shapes=scratch,
-        input_output_aliases={5 + i: i for i in range(3)},
-        compiler_params=params(12 * part * cols + 2 * total * part),
+        input_output_aliases={2 + shards + 4 + i: i for i in range(3)},
+        compiler_params=params(12 * part * cols + 2 * total * part + 4 * gate_up.size),
         cost_estimate=cost(2 * total * part * cols, 16 * part * cols, part * cols),
-    )(hidden, rows, *in_hbm(*state, *done))
-
-
-def close_kernel(shards, gate_up_ref, ids_ref, slots_ref, gates_ref, score_ref, *refs):
-    grad_refs, (out_ref, gate_ref) = refs[:-2], refs[-2:]
-    part = grad_refs[0].shape[1]
-    for s, grad_ref in enumerate(grad_refs):
-        low, high, gate, up, sig = swiglu_part(gate_up_ref, shards, s, part)
-        grad = grad_ref[...].astype(f32)
-        out_ref[:, pl.ds(low, part)] = (
-            grad * up * sig * (1.0 + gate * (1.0 - sig))
-        ).astype(bf16)
-        out_ref[:, pl.ds(high, part)] = (grad * (gate * sig)).astype(bf16)
-
+    )(hidden, rows, *grads, *in_hbm(gate_up, *state, *done))
+
+
+def close_kernel(shards, ids_ref, slots_ref, gates_ref, score_ref, after_ref, gate_ref):
+    del after_ref
     ids = ids_ref[...]
     slots = slots_ref[...]
     live = ((ids & (EXP_LOCAL - 1)) == 0) & (slots >= 0)
@@ -653,21 +665,16 @@
     gate_ref[...] = jnp.where(live, value / gates_ref[...].astype(f32), 0.0)
 
 
-def close(gate_up, ids, slots, gates, score, grads):
-    size = gate_up.size
-    args = in_hbm(gate_up, ids, slots, gates) + [score] + list(grads)
-    shapes = [(gate_up.shape, bf16), (ids.shape, f32)]
+def close(shards, ids, slots, gates, score, after):
     return pl.pallas_call(
-        functools.partial(close_kernel, len(grads)),
+        functools.partial(close_kernel, shards),
         grid=(1,),
-        in_specs=[block(array.shape) for array in args[:4]]
-        + [pl.BlockSpec(memory_space=pltpu.SMEM)]
-        + [block(grad.shape) for grad in grads],
-        out_specs=[block(shape) for shape, _ in shapes],
-        out_shape=[out_hbm(shape, dtype) for shape, dtype in shapes],
-        compiler_params=params(8 * size),
-        cost_estimate=cost(12 * size, 5 * size, size),
-    )(*args)
+        in_specs=[block(ids.shape)] * 3 + [pl.BlockSpec(memory_space=pltpu.SMEM), HBM],
+        out_specs=block(ids.shape),
+        out_shape=out_hbm(ids.shape, f32),
+        compiler_params=params(0),
+        cost_estimate=cost(1 << 20, 1 << 16),
+    )(*in_hbm(ids, slots, gates), score, *in_hbm(after))
 
 
 def per_device(out_grad, expert_ids, slots, gate_weights, saved_gate_up, master, moment1, moment2):
@@ -706,11 +713,11 @@
     grads = [projs[0]] + [shift(projs[s], rep_size - s) for s in steps]
     score = lax.all_to_all(score, ("rep", "ep"), split_axis=0, concat_axis=0, tiled=True)
 
-    done = update(edges[1], hidden_mixed, arrived_b, state, done)
-    grad_gate_up, gate_grad = close(
-        gate_up, ids_t, slots_t, gates_t, score, grads
+    *done, grad_gate_up = update(
+        edges[1], hidden_mixed, arrived_b, grads, gate_up, state, done
     )
-    return (grad_gate_up.reshape(saved_gate_up.shape), gate_grad.T) + tuple(done)
+    gate_grad = close(rep_size, ids_t, slots_t, gates_t, score, grad_gate_up).T
+    return (grad_gate_up.reshape(saved_gate_up.shape), gate_grad) + tuple(done)
 
 
 def solution(mesh):

time: 86.7 us -> 86.8 us (level)
    all_to_all x1, waiting for transfers between devices: 0.91 us -> 0.01 us  [per_device(): lax.all_to_all(score, ('rep', 'ep'), split_axis=0, concat_axis=0, tiled=T...]
  transfers between devices with their start and end apart: 7 -> 7, of which waited for: 3 -> 3; matrix products, arithmetic and copies ran while one was open for 0% -> 0% of each run, Pallas kernels for 29% -> 31%
where the time goes in v8:
time: 86.8 us; the launch traced here: 86.3 us
  Pallas kernels  34 us (39%)
  waiting for transfers between devices  27.8 us (32%)
  starting transfers between devices  23.1 us (27%)
    ppermute x4, waiting for transfers between devices, shift(): return lax.ppermute(value, 'rep', perm)  27.8 us
    all_to_all x2, starting transfers between devices, exchange(): return lax.all_to_all(value, 'ep', split_axis=0, concat_axis=0, tiled=True)  13.1 us
    pallas_call x1, Pallas kernels, update(): pl.pallas_call(functools.partial(update_kernel, low, shards), in_specs=[V...  7.86 us
    pallas_call x1, Pallas kernels, settle(): pl.pallas_call(functools.partial(settle_kernel, fresh, blocks), in_specs=...  7.16 us
    ppermute x4, starting transfers between devices, shift(): return lax.ppermute(value, 'rep', perm)  5.26 us
    all_to_all x1, starting transfers between devices, per_device(): lax.all_to_all(score, ('rep', 'ep'), split_axis=0, concat_axis=0, tiled=T...  4.71 us
    pallas_call x1, Pallas kernels, load_state(): pl.pallas_call(functools.partial(load_kernel, middle), in_specs=[ANY] + [...  4.47 us
    pallas_call x1, Pallas kernels, mix(): pl.pallas_call(functools.partial(mix_kernel, shards), grid=(1,), in_specs...  3.43 us
  transfers between devices with their start and end apart: 7, of which 3 were waited for; matrix products, arithmetic and copies ran while one was open for 0% of the time, Pallas kernels for 31%

profile of v8, /device:TPU:0, one launch (start us, length us, event | category | flops | bytes accessed | tf_op | source)
XLA Modules:
  0.0 86.3 jit_solution(5808286974694745195)
XLA Ops:
  0.6 3.3 %shard_map.119 = (bf16[256,1536]{1,0:T(8,128)(2,1)}, bf16[256,1152]{1,0:T(8,128)(2,1)}) custom-call(s32[8,256]{1,0:T(8,128)} %bitcast.20, s32[8,256]{1,0:T(8,128)} %bitcast.22, bf16[8,256]{1,0:T(8,128)(2,1)} %bitcast.24, bf16[256,3584]{1,0:T(8,128)(2,1)} %grad_hbm.1), custom_call_target="tpu_custom_call" | custom-call | flops 469762048 | bytes 3670016 | tf_op jit(solution)/shard_map/pallas_call | solution.py:148
  4.0 7.4 %all-to-all-start = ((bf16[16,16,1536]{2,1,0:T(8,128)(2,1)}), bf16[16,16,1536]{2,1,0:T(8,128)(2,1)S(1)}, u32[]{:S(2)}, u32[]{:S(2)}) async-start(bf16[16,16,1536]{2,1,0:T(8,128)(2,1)} %bitcast.19), calls=%async_computation | async-start | bytes 1572864 | tf_op jit(solution)/shard_map/all_to_all | solution.py:694
  11.3 1.6 %collective-permute-start.2 = (bf16[256,1152]{1,0:T(8,128)(2,1)}, bf16[256,1152]{1,0:T(8,128)(2,1)S(1)}, u32[]{:S(2)}, u32[]{:S(2)}) collective-permute-start(bf16[256,1152]{1,0:T(8,128)(2,1)} %get-tuple-element.31.after_ref.refs_0_), channel_id=1, source_target_pairs={{0,16},{16,0},{1,17},{17,1},{2,18},{18,2},{3,19},{19,3},{4,20},{20... | collective-permute-start | bytes 1769480 | tf_op jit(solution)/shard_map/ppermute | solution.py:691
  12.9 1.9 %shard_map.120 = (bf16[192,512]{1,0:T(8,128)(2,1)S(1)}, bf16[192,512]{1,0:T(8,128)(2,1)}) custom-call(bf16[192,2048]{1,0:T(8,128)(2,1)} %bitcast.16, bf16[256,1152]{1,0:T(8,128)(2,1)} %get-tuple-element.31.after_ref.refs_0_), custom_call_target="tpu_custom_call" | custom-call | flops 3145728 | bytes 1179648 | tf_op jit(solution)/shard_map/pallas_call | solution.py:185
  14.8 0.0 copy-start
  14.8 0.7 copy-done
  15.5 11.7 %collective-permute-done.2.refs_1_ = bf16[256,1152]{1,0:T(8,128)(2,1)S(1)} collective-permute-done((bf16[256,1152]{1,0:T(8,128)(2,1)}, bf16[256,1152]{1,0:T(8,128)(2,1)S(1)}, u32[]{:S(2)}, u32[]{:S(2)}) %collective-permute-start.2) | collective-permute-done | bytes 589856 | tf_op jit(solution)/shard_map/ppermute | solution.py:691
  27.2 3.4 %shard_map.124 = bf16[384,1536]{1,0:T(8,128)(2,1)} custom-call(bf16[256,1152]{1,0:T(8,128)(2,1)} %get-tuple-element.31.after_ref.refs_0_, bf16[256,1152]{1,0:T(8,128)(2,1)S(1)} %collective-permute-done.2.refs_1_, bf16[192,512]{1,0:T(8,128)(2,1)} %get-tuple-element.33.refs_2_), custom_call_target="tpu_custom_call" | custom-call | bytes 2949120 | tf_op jit(solution)/shard_map/pallas_call | solution.py:300
  30.6 0.0 all-to-all-done
  30.6 5.8 %all-to-all-start.1 = ((bf16[16,24,1536]{2,1,0:T(8,128)(2,1)}), bf16[16,24,1536]{2,1,0:T(8,128)(2,1)S(1)}, u32[]{:S(2)}, u32[]{:S(2)}) async-start(bf16[16,24,1536]{2,1,0:T(8,128)(2,1)} %bitcast.15), calls=%async_computation.1 | async-start | bytes 2359296 | tf_op jit(solution)/shard_map/all_to_all | solution.py:694
  36.4 0.0 copy-start.1
  36.4 1.6 %collective-permute-start = (bf16[256,1536]{1,0:T(8,128)(2,1)S(1)}, bf16[256,1536]{1,0:T(8,128)(2,1)S(1)}, u32[]{:S(2)}, u32[]{:S(2)}) collective-permute-start(bf16[256,1536]{1,0:T(8,128)(2,1)S(1)} %bitcast.12), channel_id=1, source_target_pairs={{0,16},{16,0},{1,17},{17,1},{2,18},{18,2},{3,19},{19,3},{4,20},{20... | collective-permute-start | bytes 2359304 | tf_op jit(solution)/shard_map/ppermute | solution.py:691
  38.0 0.5 collective-permute-start.1
  38.5 4.5 %shard_map.121 = (f32[512,2048]{1,0:T(8,128)S(1)}, bf16[512,2048]{1,0:T(8,128)(2,1)S(1)}, bf16[512,2048]{1,0:T(8,128)(2,1)S(1)}, bf16[512,2048]{1,0:T(8,128)(2,1)S(1)}, bf16[512,1536]{1,0:T(8,128)(2,1)S(1)}) custom-call(bf16[256,1536]{1,0:T(8,128)(2,1)S(1)} %bitcast.13, f32[1,512,3584]{2,1,0:T(8,128)} %refs_3_.1, bf16[1,512,3584]{2,1,0:T(8,128)(2,1)} %refs_4_.1, ...), custom_call_target="tpu_custom_call" | custom-call | flops 1835008 | bytes 25690112 | tf_op jit(solution)/shard_map/pallas_call | solution.py:237
  43.0 0.0 copy-done.1
  43.0 1.9 %shard_map.122 = (bf16[192,2048]{1,0:T(8,128)(2,1)S(1)}, f32[16,1,128]{2,1,0:T(1,128)S(1)}, f32[192,512]{1,0:T(8,128)}) custom-call(bf16[256,1536]{1,0:T(8,128)(2,1)S(1)} %bitcast.14, bf16[512,2048]{1,0:T(8,128)(2,1)S(1)} %get-tuple-element.34.weight_ref.refs_4_, bf16[192,512]{1,0:T(8,128)(2,1)S(1)} %copy-done.1), custom_call_target="tpu_custom_call" | custom-call | flops 805306368 | bytes 2097152 | tf_op jit(solution)/shard_map/pallas_call | solution.py:374
  44.9 15.7 %collective-permute-done.1.refs_2_ = bf16[192,512]{1,0:T(8,128)(2,1)S(1)} collective-permute-done((bf16[192,512]{1,0:T(8,128)(2,1)}, bf16[192,512]{1,0:T(8,128)(2,1)S(1)}, u32[]{:S(2)}, u32[]{:S(2)}) %collective-permute-start.1) | collective-permute-done | bytes 196640 | tf_op jit(solution)/shard_map/ppermute | solution.py:691
  60.6 0.0 collective-permute-done.refs_0_
  60.6 7.2 %shard_map.123 = (f32[16,1,128]{2,1,0:T(1,128)S(1)}, bf16[384,512]{1,0:T(8,128)(2,1)S(1)}, f32[192,512]{1,0:T(8,128)}, f32[1,512,3584]{2,1,0:T(8,128)}, bf16[1,5...) custom-call(bf16[256,1536]{1,0:T(8,128)(2,1)S(1)} %collective-permute-done.refs_0_, bf16[192,512]{1,0:T(8,128)(2,1)S(1)} %copy-done.1, ...), custom_call_target="tpu_custom_call" | custom-call | flops 1610612736 | bytes 550502400 | tf_op jit(solution)/shard_map/pallas_call | solution.py:570
  67.7 0.0 all-to-all-done.1
  67.7 2.4 %shard_map.125 = (bf16[192,512]{1,0:T(8,128)(2,1)S(1)}, bf16[192,512]{1,0:T(8,128)(2,1)}, f32[32,1,128]{2,1,0:T(1,128)}) custom-call(bf16[384,1536]{1,0:T(8,128)(2,1)S(1)} %bitcast.10, bf16[384,512]{1,0:T(8,128)(2,1)S(1)} %get-tuple-element.39.hidden_ref, bf16[512,1536]{1,0:T(8,128)(2,1)S(1)} %get-tuple-element.40.weight_ref, ...), custom_call_target="tpu_custom_call" | custom-call | flops 603979776 | bytes 1572864 | tf_op jit(solution)/shard_map/pallas_call | solution.py:423
  70.1 1.6 %collective-permute-start.3 = (bf16[192,512]{1,0:T(8,128)(2,1)}, bf16[192,512]{1,0:T(8,128)(2,1)S(1)}, u32[]{:S(2)}, u32[]{:S(2)}) collective-permute-start(bf16[192,512]{1,0:T(8,128)(2,1)} %get-tuple-element.46), channel_id=1, source_target_pairs={{0,16},{16,0},{1,17},{17,1},{2,18},{18,2},{3,19},{19,3},{4,20},{20... | collective-permute-start | bytes 589832 | tf_op jit(solution)/shard_map/ppermute | solution.py:691
  71.7 4.7 %all-to-all-start.2 = ((f32[32,1,128]{2,1,0:T(1,128)}), f32[32,1,128]{2,1,0:T(1,128)S(1)}, u32[]{:S(2)}, u32[]{:S(2)}) async-start(f32[32,1,128]{2,1,0:T(1,128)} %get-tuple-element.51), calls=%async_computation.2 | async-start | bytes 32768 | tf_op jit(solution)/shard_map/all_to_all | solution.py:714
  76.5 0.4 collective-permute-done.3.refs_1_
  76.9 7.9 %shard_map.126 = (f32[1,512,3584]{2,1,0:T(8,128)}, bf16[1,512,3584]{2,1,0:T(8,128)(2,1)}, bf16[1,512,3584]{2,1,0:T(8,128)(2,1)}, bf16[192,2048]{1,0:T(8,128)(2,1)}) custom-call(bf16[384,512]{1,0:T(8,128)(2,1)S(1)} %get-tuple-element.39.hidden_ref, bf16[384,1536]{1,0:T(8,128)(2,1)S(1)} %bitcast.11, ...), custom_call_target="tpu_custom_call", output_to_operand_aliasing={{0}: (8, {}), {1}: (9, {}), {2}: (10, {})} | custom-call | flops 603979776 | bytes 12582912 | tf_op jit(solution)/shard_map/pallas_call | solution.py:638
  84.7 0.0 all-to-all-done.2.score_ref
  84.7 1.6 %shard_map.127 = f32[8,256]{1,0:T(8,128)} custom-call(s32[8,256]{1,0:T(8,128)} %bitcast.21, s32[8,256]{1,0:T(8,128)} %bitcast.23, bf16[8,256]{1,0:T(8,128)(2,1)} %bitcast.25, f32[32,1,128]{2,1,0:T(1,128)S(1)} %all-to-all-done.2.score_ref, bf16[192,2048]{1,0:T(8,128)(2,1)} %get-tuple-element.50.after_ref), custom_call_target="tpu_custom_call" | custom-call | flops 1048576 | bytes 65536 | tf_op jit(solution)/shard_map/pallas_call | solution.py:669
Async XLA Ops:
  4.0 26.7 %all-to-all-start = ((bf16[16,16,1536]{2,1,0:T(8,128)(2,1)}), bf16[16,16,1536]{2,1,0:T(8,128)(2,1)S(1)}, u32[]{:S(2)}, u32[]{:S(2)}) async-start(bf16[16,16,1536]{2,1,0:T(8,128)(2,1)} %bitcast.19), calls=%async_computation | async-start | bytes 1572864 | tf_op jit(solution)/shard_map/all_to_all | solution.py:694
  11.3 15.9 %collective-permute-start.2 = (bf16[256,1152]{1,0:T(8,128)(2,1)}, bf16[256,1152]{1,0:T(8,128)(2,1)S(1)}, u32[]{:S(2)}, u32[]{:S(2)}) collective-permute-start(bf16[256,1152]{1,0:T(8,128)(2,1)} %get-tuple-element.31.after_ref.refs_0_), channel_id=1, source_target_pairs={{0,16},{16,0},{1,17},{17,1},{2,18},{18,2},{3,19},{19,3},{4,20},{20... | collective-permute-start | bytes 1769480 | tf_op jit(solution)/shard_map/ppermute | solution.py:691
  14.8 0.7 copy-start
  30.6 37.1 %all-to-all-start.1 = ((bf16[16,24,1536]{2,1,0:T(8,128)(2,1)}), bf16[16,24,1536]{2,1,0:T(8,128)(2,1)S(1)}, u32[]{:S(2)}, u32[]{:S(2)}) async-start(bf16[16,24,1536]{2,1,0:T(8,128)(2,1)} %bitcast.15), calls=%async_computation.1 | async-start | bytes 2359296 | tf_op jit(solution)/shard_map/all_to_all | solution.py:694
  36.4 6.6 %copy-start.1 = (bf16[192,512]{1,0:T(8,128)(2,1)S(1)}, bf16[192,512]{1,0:T(8,128)(2,1)}, u32[]{:S(2)}) copy-start(bf16[192,512]{1,0:T(8,128)(2,1)} %copy-done) | copy-start | bytes 589828
  36.4 24.2 %collective-permute-start = (bf16[256,1536]{1,0:T(8,128)(2,1)S(1)}, bf16[256,1536]{1,0:T(8,128)(2,1)S(1)}, u32[]{:S(2)}, u32[]{:S(2)}) collective-permute-start(bf16[256,1536]{1,0:T(8,128)(2,1)S(1)} %bitcast.12), channel_id=1, source_target_pairs={{0,16},{16,0},{1,17},{17,1},{2,18},{18,2},{3,19},{19,3},{4,20},{20... | collective-permute-start | bytes 2359304 | tf_op jit(solution)/shard_map/ppermute | solution.py:691
  38.0 22.6 %collective-permute-start.1 = (bf16[192,512]{1,0:T(8,128)(2,1)}, bf16[192,512]{1,0:T(8,128)(2,1)S(1)}, u32[]{:S(2)}, u32[]{:S(2)}) collective-permute-start(bf16[192,512]{1,0:T(8,128)(2,1)} %get-tuple-element.33.refs_2_), channel_id=1, source_target_pairs={{0,16},{16,0},{1,17},{17,1},{2,18},{18,2},{3,19},{19,3},{4,20},{20... | collective-permute-start | bytes 589832 | tf_op jit(solution)/shard_map/ppermute | solution.py:691
  70.1 6.7 %collective-permute-start.3 = (bf16[192,512]{1,0:T(8,128)(2,1)}, bf16[192,512]{1,0:T(8,128)(2,1)S(1)}, u32[]{:S(2)}, u32[]{:S(2)}) collective-permute-start(bf16[192,512]{1,0:T(8,128)(2,1)} %get-tuple-element.46), channel_id=1, source_target_pairs={{0,16},{16,0},{1,17},{17,1},{2,18},{18,2},{3,19},{19,3},{4,20},{20... | collective-permute-start | bytes 589832 | tf_op jit(solution)/shard_map/ppermute | solution.py:691
  71.7 13.0 %all-to-all-start.2 = ((f32[32,1,128]{2,1,0:T(1,128)}), f32[32,1,128]{2,1,0:T(1,128)S(1)}, u32[]{:S(2)}, u32[]{:S(2)}) async-start(f32[32,1,128]{2,1,0:T(1,128)} %get-tuple-element.51), calls=%async_computation.2 | async-start | bytes 32768 | tf_op jit(solution)/shard_map/all_to_all | solution.py:714

commit v9 on v8

--- a/solution.py
+++ b/solution.py
@@ -12,7 +12,6 @@
 SEND = 12
 LANE = 128
 UNIT = 512
-SETTLE_COST = 525
 ROWS = 16
 
 beta_one = 0.9
@@ -84,8 +83,7 @@
 
 
 def dispatch_kernel(edges, ids_hbm, slots_hbm, gates_hbm, grad_hbm, *refs):
-    outs, (ids_ref, slots_ref, gates_ref, grad_ref) = refs[:2], refs[2:6]
-    sends, sems, out_sems = refs[6:8], refs[8], refs[9]
+    outs, (ids_ref, slots_ref, gates_ref, grad_ref, sems) = refs[:2], refs[2:]
     pairs = [
         (ids_hbm, ids_ref),
         (slots_hbm, slots_ref),
@@ -117,7 +115,6 @@
         jnp.dot(order, main, preferred_element_type=f32).astype(bf16) for order in orders
     ]
     copies[3].wait()
-    out_copies = []
     for c in (1, 0):
         low, high = edges[c], edges[c + 1]
         part = (high - low) // 4
@@ -130,15 +127,7 @@
             total += jnp.dot(
                 tails[j], grad_ref[:, low + 3 * part : high], preferred_element_type=f32
             )
-            own = (slice(None), pl.ds(j * part, part))
-            sends[c][own] = total.astype(bf16)
-            copy = pltpu.make_async_copy(
-                sends[c].at[own], outs[c].at[own], out_sems.at[c, j]
-            )
-            copy.start()
-            out_copies.append(copy)
-    for copy in out_copies:
-        copy.wait()
+            outs[c][:, j * part : (j + 1) * part] = total.astype(bf16)
 
 
 def dispatch(blocks, edges, ids, slots, gates, out_grad):
@@ -148,16 +137,15 @@
     return pl.pallas_call(
         functools.partial(dispatch_kernel, edges),
         in_specs=[HBM] * 4,
-        out_specs=[HBM] * 2,
-        out_shape=[out_hbm(shape, bf16) for shape in shapes],
+        out_specs=[VMEM] * 2,
+        out_shape=[plain(shape, bf16) for shape in shapes],
         scratch_shapes=[
             pltpu.VMEM(ids.shape, jnp.int32),
             pltpu.VMEM(slots.shape, jnp.int32),
             pltpu.VMEM(gates.shape, bf16),
             pltpu.VMEM(out_grad.shape, bf16),
-        ]
-        + [pltpu.VMEM(shape, bf16) for shape in shapes]
-        + [pltpu.SemaphoreType.DMA((4,)), pltpu.SemaphoreType.DMA((2, 3))],
+            pltpu.SemaphoreType.DMA((4,)),
+        ],
         compiler_params=params(2 * rows * width + 2 * tok * width),
         cost_estimate=cost(2 * rows * tok * width, 4 * tok * width),
     )(*in_hbm(ids, slots, gates, out_grad))
@@ -185,12 +173,12 @@
     return pl.pallas_call(
         hidden_kernel,
         grid=(1,),
-        in_specs=[block(gate_up.shape), HBM],
+        in_specs=[block(gate_up.shape), ANY],
         out_specs=[block(shape)] * shards,
         out_shape=[plain(shape, bf16)] * shards,
         compiler_params=params(3 * slots * width),
         cost_estimate=cost(8 * slots * width, 3 * slots * width, slots * width),
-    )(*in_hbm(gate_up, after))
+    )(*in_hbm(gate_up), after)
 
 
 def load_kernel(middle, after_ref, master_hbm, one_hbm, two_hbm, *refs):
@@ -293,19 +281,18 @@
         out_ref[own, 3 * part :] = tail.astype(bf16)
 
 
-def mix(parts, after):
+def mix(parts):
     shards = len(parts)
     rows, packed = parts[0].shape
     shape = (rows // ROWS * SEND * shards, packed // 3 * 4)
     return pl.pallas_call(
         functools.partial(mix_kernel, shards),
-        grid=(1,),
-        in_specs=[block(part.shape) for part in parts] + [ANY] * len(after),
-        out_specs=block(shape),
-        out_shape=out_hbm(shape, bf16),
+        in_specs=[VMEM] * shards,
+        out_specs=VMEM,
+        out_shape=plain(shape, bf16),
         compiler_params=params(12 * rows * packed * shards),
         cost_estimate=cost(0, 5 * rows * packed * shards),
-    )(*in_hbm(parts[0]), *parts[1:], *after)
+    )(*parts)
 
 
 def reorder(arrived, rows_ref):
@@ -445,10 +432,9 @@
     m_new = beta_one * one.astype(f32) + (1.0 - beta_one) * grad
     v_new = beta_two * two.astype(f32) + (1.0 - beta_two) * (grad * grad)
     root = lax.rsqrt(v_new)
-    below = 1.0 + eps * root
-    inverse = pl.reciprocal(below, approx=True)
-    inverse = inverse * (2.0 - below * inverse)
-    master = keep * master - (rate * m_new) * (root * inverse)
+    below = v_new * root + eps
+    inverse = root * (2.0 - below * root)
+    master = keep * master - (rate * m_new) * inverse
     return master, m_new.astype(bf16), v_new.astype(bf16)
 
 
@@ -574,7 +560,7 @@
         out_shape=near + far,
         scratch_shapes=scratch,
         compiler_params=params(nbytes),
-        cost_estimate=cost(4 * total * part * cols, SETTLE_COST * part * cols, part * cols),
+        cost_estimate=cost(4 * total * part * cols, 16 * part * cols, part * cols),
     )(*args)
     outs = list(outs)
     return outs[:size], outs[size], outs[size + 1 : -3], outs[-3:]
@@ -694,11 +680,13 @@
         return lax.all_to_all(value, "ep", split_axis=0, concat_axis=0, tiled=True)
 
     send_a, send_b = dispatch(ep_size, edges, ids_t, slots_t, gates_t, out_grad)
-    mixed = [send_b] + [shift(send_b, s) for s in steps]
+    mixed = [shift(send_b, s) for s in steps]
     parts = list(hidden_parts(gate_up, rep_size, send_b))
+    arrived = exchange(send_a.reshape(ep_size, ROWS, -1)).reshape(send_a.shape)
+    parts[1:], mixed = lax.optimization_barrier((parts[1:], mixed))
     hidden = [parts[0]] + [shift(parts[s], s) for s in steps]
-    arrived = exchange(send_a.reshape(ep_size, ROWS, -1)).reshape(send_a.shape)
-    mixed = mix(mixed, parts[1:])
+    mixed = mix([send_b] + mixed)
+    hidden[1:], mixed = lax.optimization_barrier((hidden[1:], mixed))
     arrived_b = exchange(mixed.reshape(ep_size, rep_size * SEND, -1)).reshape(mixed.shape)
 
     peers = [shift(arrived, s) for s in steps]

time: 86.8 us -> 85.7 us (0.987)
  Pallas kernels: 34 us -> 32 us
    pallas_call x1, Pallas kernels: 3.43 us -> 2.36 us  [mix(): pl.pallas_call(functools.partial(mix_kernel, shards), in_specs=[VMEM] * s...]
    ppermute x4, starting transfers between devices: 5.26 us -> 6.25 us  [shift(): return lax.ppermute(value, 'rep', perm)]
  transfers between devices with their start and end apart: 7 -> 7, of which waited for: 3 -> 4; matrix products, arithmetic and copies ran while one was open for 0% -> 0% of each run, Pallas kernels for 31% -> 29%
where the time goes in v9:
time: 85.7 us; the launch traced here: 84.9 us
  Pallas kernels  32 us (37%)
  waiting for transfers between devices  27.5 us (32%)
  starting transfers between devices  23.9 us (28%)
    ppermute x4, waiting for transfers between devices, shift(): return lax.ppermute(value, 'rep', perm)  27.5 us
    all_to_all x2, starting transfers between devices, exchange(): return lax.all_to_all(value, 'ep', split_axis=0, concat_axis=0, tiled=True)  12.9 us
    pallas_call x1, Pallas kernels, update(): pl.pallas_call(functools.partial(update_kernel, low, shards), in_specs=[V...  7.66 us
    pallas_call x1, Pallas kernels, settle(): pl.pallas_call(functools.partial(settle_kernel, fresh, blocks), in_specs=...  6.86 us
    ppermute x4, starting transfers between devices, shift(): return lax.ppermute(value, 'rep', perm)  6.25 us
    all_to_all x1, starting transfers between devices, per_device(): lax.all_to_all(score, ('rep', 'ep'), split_axis=0, concat_axis=0, tiled=T...  4.76 us
    pallas_call x1, Pallas kernels, load_state(): pl.pallas_call(functools.partial(load_kernel, middle), in_specs=[ANY] + [...  4.47 us
    pallas_call x1, Pallas kernels, dispatch(): pl.pallas_call(functools.partial(dispatch_kernel, edges), in_specs=[HBM]...  3.45 us
  transfers between devices with their start and end apart: 7, of which 4 were waited for; matrix products, arithmetic and copies ran while one was open for 0% of the time, Pallas kernels for 29%

profile of v9, /device:TPU:0, one launch (start us, length us, event | category | flops | bytes accessed | tf_op | source)
XLA Modules:
  0.0 84.9 jit_solution(13705448777866558205)
XLA Ops:
  0.6 3.4 %shard_map.119 = (bf16[256,1536]{1,0:T(8,128)(2,1)}, bf16[256,1152]{1,0:T(8,128)(2,1)S(1)}) custom-call(s32[8,256]{1,0:T(8,128)} %bitcast.18, s32[8,256]{1,0:T(8,128)} %bitcast.20, bf16[8,256]{1,0:T(8,128)(2,1)} %bitcast.22, bf16[256,3584]{1,0:T(8,128)(2,1)} %grad_hbm.1), custom_call_target="tpu_custom_call" | custom-call | flops 469762048 | bytes 3670016 | tf_op jit(solution)/shard_map/pallas_call | solution.py:137
  4.1 7.4 %all-to-all-start = ((bf16[16,16,1536]{2,1,0:T(8,128)(2,1)}), bf16[16,16,1536]{2,1,0:T(8,128)(2,1)S(1)}, u32[]{:S(2)}, u32[]{:S(2)}) async-start(bf16[16,16,1536]{2,1,0:T(8,128)(2,1)} %bitcast.3), calls=%async_computation | async-start | bytes 1572864 | tf_op jit(solution)/shard_map/all_to_all | solution.py:680
  11.5 1.6 %collective-permute-start.1 = (bf16[256,1152]{1,0:T(8,128)(2,1)S(1)}, bf16[256,1152]{1,0:T(8,128)(2,1)S(1)}, u32[]{:S(2)}, u32[]{:S(2)}) collective-permute-start(bf16[256,1152]{1,0:T(8,128)(2,1)S(1)} %get-tuple-element.35.after_ref.refs_0_), channel_id=1, source_target_pairs={{0,16},{16,0},{1,17},{17,1},{2,18},{18,2},{3,19},{19,3},{4,20},{20... | collective-permute-start | bytes 1769480 | tf_op jit(solution)/shard_map/ppermute | solution.py:677
  13.0 1.3 %shard_map.120 = (bf16[192,512]{1,0:T(8,128)(2,1)S(1)}, bf16[192,512]{1,0:T(8,128)(2,1)S(1)}) custom-call(bf16[192,2048]{1,0:T(8,128)(2,1)} %bitcast.15, bf16[256,1152]{1,0:T(8,128)(2,1)S(1)} %get-tuple-element.35.after_ref.refs_0_), custom_call_target="tpu_custom_call" | custom-call | flops 3145728 | bytes 1179648 | tf_op jit(solution)/shard_map/pallas_call | solution.py:173
  14.4 0.0 copy-start
  14.4 12.7 %collective-permute-done.1.refs_1_ = bf16[256,1152]{1,0:T(8,128)(2,1)S(1)} collective-permute-done((bf16[256,1152]{1,0:T(8,128)(2,1)S(1)}, bf16[256,1152]{1,0:T(8,128)(2,1)S(1)}, u32[]{:S(2)}, u32[]{:S(2)}) %collective-permute-start.1) | collective-permute-done | bytes 589856 | tf_op jit(solution)/shard_map/ppermute | solution.py:677
  27.1 1.5 %collective-permute-start.2 = (bf16[192,512]{1,0:T(8,128)(2,1)S(1)}, bf16[192,512]{1,0:T(8,128)(2,1)S(1)}, u32[]{:S(2)}, u32[]{:S(2)}) collective-permute-start(bf16[192,512]{1,0:T(8,128)(2,1)S(1)} %get-tuple-element.38), channel_id=1, source_target_pairs={{0,16},{16,0},{1,17},{17,1},{2,18},{18,2},{3,19},{19,3},{4,20},{20... | collective-permute-start | bytes 589832 | tf_op jit(solution)/shard_map/ppermute | solution.py:677
  28.6 2.4 %shard_map.121 = bf16[384,1536]{1,0:T(8,128)(2,1)} custom-call(bf16[256,1152]{1,0:T(8,128)(2,1)S(1)} %get-tuple-element.35.after_ref.refs_0_, bf16[256,1152]{1,0:T(8,128)(2,1)S(1)} %collective-permute-done.1.refs_1_), custom_call_target="tpu_custom_call" | custom-call | bytes 2949120 | tf_op jit(solution)/shard_map/pallas_call | solution.py:288
  31.0 2.5 %collective-permute-done.2.refs_2_ = bf16[192,512]{1,0:T(8,128)(2,1)S(1)} collective-permute-done((bf16[192,512]{1,0:T(8,128)(2,1)S(1)}, bf16[192,512]{1,0:T(8,128)(2,1)S(1)}, u32[]{:S(2)}, u32[]{:S(2)}) %collective-permute-start.2) | collective-permute-done | bytes 196640 | tf_op jit(solution)/shard_map/ppermute | solution.py:677
  33.5 0.0 copy-start.2
  33.5 0.7 copy-done.2
  34.1 0.0 all-to-all-done
  34.1 0.0 copy-done
  34.1 5.5 %all-to-all-start.1 = ((bf16[16,24,1536]{2,1,0:T(8,128)(2,1)}), bf16[16,24,1536]{2,1,0:T(8,128)(2,1)S(1)}, u32[]{:S(2)}, u32[]{:S(2)}) async-start(bf16[16,24,1536]{2,1,0:T(8,128)(2,1)} %bitcast.6), calls=%async_computation.1 | async-start | bytes 2359296 | tf_op jit(solution)/shard_map/all_to_all | solution.py:680
  39.7 0.0 copy-start.1
  39.7 0.0 copy-start.3
  39.7 1.6 %collective-permute-start = (bf16[256,1536]{1,0:T(8,128)(2,1)S(1)}, bf16[256,1536]{1,0:T(8,128)(2,1)S(1)}, u32[]{:S(2)}, u32[]{:S(2)}) collective-permute-start(bf16[256,1536]{1,0:T(8,128)(2,1)S(1)} %bitcast.12), channel_id=1, source_target_pairs={{0,16},{16,0},{1,17},{17,1},{2,18},{18,2},{3,19},{19,3},{4,20},{20... | collective-permute-start | bytes 2359304 | tf_op jit(solution)/shard_map/ppermute | solution.py:677
  41.3 4.5 %shard_map.122 = (f32[512,2048]{1,0:T(8,128)S(1)}, bf16[512,2048]{1,0:T(8,128)(2,1)S(1)}, bf16[512,2048]{1,0:T(8,128)(2,1)S(1)}, bf16[512,2048]{1,0:T(8,128)(2,1)S(1)}, bf16[512,1536]{1,0:T(8,128)(2,1)S(1)}) custom-call(bf16[256,1536]{1,0:T(8,128)(2,1)S(1)} %bitcast.13, f32[1,512,3584]{2,1,0:T(8,128)} %refs_3_.1, bf16[1,512,3584]{2,1,0:T(8,128)(2,1)} %refs_4_.1, ...), custom_call_target="tpu_custom_call" | custom-call | flops 1835008 | bytes 25690112 | tf_op jit(solution)/shard_map/pallas_call | solution.py:225
  45.8 0.0 copy-done.1
  45.8 1.9 %shard_map.123 = (bf16[192,2048]{1,0:T(8,128)(2,1)S(1)}, f32[16,1,128]{2,1,0:T(1,128)S(1)}, f32[192,512]{1,0:T(8,128)}) custom-call(bf16[256,1536]{1,0:T(8,128)(2,1)S(1)} %bitcast.14, bf16[512,2048]{1,0:T(8,128)(2,1)S(1)} %get-tuple-element.41.weight_ref.refs_4_, bf16[192,512]{1,0:T(8,128)(2,1)S(1)} %copy-done.1), custom_call_target="tpu_custom_call" | custom-call | flops 805306368 | bytes 2097152 | tf_op jit(solution)/shard_map/pallas_call | solution.py:361
  47.7 11.9 %collective-permute-done.refs_0_ = bf16[256,1536]{1,0:T(8,128)(2,1)S(1)} collective-permute-done((bf16[256,1536]{1,0:T(8,128)(2,1)S(1)}, bf16[256,1536]{1,0:T(8,128)(2,1)S(1)}, u32[]{:S(2)}, u32[]{:S(2)}) %collective-permute-start) | collective-permute-done | bytes 786464 | tf_op jit(solution)/shard_map/ppermute | solution.py:677
  59.6 0.0 copy-done.3
  59.6 6.9 %shard_map.124 = (f32[16,1,128]{2,1,0:T(1,128)S(1)}, bf16[384,512]{1,0:T(8,128)(2,1)S(1)}, f32[192,512]{1,0:T(8,128)}, f32[1,512,3584]{2,1,0:T(8,128)}, bf16[1,5...) custom-call(bf16[256,1536]{1,0:T(8,128)(2,1)S(1)} %collective-permute-done.refs_0_, bf16[192,512]{1,0:T(8,128)(2,1)S(1)} %copy-done.1, ...), custom_call_target="tpu_custom_call" | custom-call | flops 1610612736 | bytes 16777216 | tf_op jit(solution)/shard_map/pallas_call | solution.py:556
  66.5 0.0 all-to-all-done.1
  66.5 2.4 %shard_map.125 = (bf16[192,512]{1,0:T(8,128)(2,1)S(1)}, bf16[192,512]{1,0:T(8,128)(2,1)}, f32[32,1,128]{2,1,0:T(1,128)}) custom-call(bf16[384,1536]{1,0:T(8,128)(2,1)S(1)} %bitcast.10, bf16[384,512]{1,0:T(8,128)(2,1)S(1)} %get-tuple-element.46.hidden_ref, bf16[512,1536]{1,0:T(8,128)(2,1)S(1)} %get-tuple-element.48.weight_ref, ...), custom_call_target="tpu_custom_call" | custom-call | flops 603979776 | bytes 1572864 | tf_op jit(solution)/shard_map/pallas_call | solution.py:410
  68.9 1.6 %collective-permute-start.3 = (bf16[192,512]{1,0:T(8,128)(2,1)}, bf16[192,512]{1,0:T(8,128)(2,1)S(1)}, u32[]{:S(2)}, u32[]{:S(2)}) collective-permute-start(bf16[192,512]{1,0:T(8,128)(2,1)} %get-tuple-element.54), channel_id=1, source_target_pairs={{0,16},{16,0},{1,17},{17,1},{2,18},{18,2},{3,19},{19,3},{4,20},{20... | collective-permute-start | bytes 589832 | tf_op jit(solution)/shard_map/ppermute | solution.py:677
  70.5 4.8 %all-to-all-start.2 = ((f32[32,1,128]{2,1,0:T(1,128)}), f32[32,1,128]{2,1,0:T(1,128)S(1)}, u32[]{:S(2)}, u32[]{:S(2)}) async-start(f32[32,1,128]{2,1,0:T(1,128)} %get-tuple-element.59), calls=%async_computation.2 | async-start | bytes 32768 | tf_op jit(solution)/shard_map/all_to_all | solution.py:702
  75.3 0.4 collective-permute-done.3.refs_1_
  75.6 7.7 %shard_map.126 = (f32[1,512,3584]{2,1,0:T(8,128)}, bf16[1,512,3584]{2,1,0:T(8,128)(2,1)}, bf16[1,512,3584]{2,1,0:T(8,128)(2,1)}, bf16[192,2048]{1,0:T(8,128)(2,1)}) custom-call(bf16[384,512]{1,0:T(8,128)(2,1)S(1)} %get-tuple-element.46.hidden_ref, bf16[384,1536]{1,0:T(8,128)(2,1)S(1)} %bitcast.11, ...), custom_call_target="tpu_custom_call", output_to_operand_aliasing={{0}: (8, {}), {1}: (9, {}), {2}: (10, {})} | custom-call | flops 603979776 | bytes 12582912 | tf_op jit(solution)/shard_map/pallas_call | solution.py:624
  83.3 0.0 all-to-all-done.2.score_ref
  83.3 1.6 %shard_map.127 = f32[8,256]{1,0:T(8,128)} custom-call(s32[8,256]{1,0:T(8,128)} %bitcast.19, s32[8,256]{1,0:T(8,128)} %bitcast.21, bf16[8,256]{1,0:T(8,128)(2,1)} %bitcast.23, f32[32,1,128]{2,1,0:T(1,128)S(1)} %all-to-all-done.2.score_ref, bf16[192,2048]{1,0:T(8,128)(2,1)} %get-tuple-element.58.after_ref), custom_call_target="tpu_custom_call" | custom-call | flops 1048576 | bytes 65536 | tf_op jit(solution)/shard_map/pallas_call | solution.py:655
Async XLA Ops:
  4.1 30.1 %all-to-all-start = ((bf16[16,16,1536]{2,1,0:T(8,128)(2,1)}), bf16[16,16,1536]{2,1,0:T(8,128)(2,1)S(1)}, u32[]{:S(2)}, u32[]{:S(2)}) async-start(bf16[16,16,1536]{2,1,0:T(8,128)(2,1)} %bitcast.3), calls=%async_computation | async-start | bytes 1572864 | tf_op jit(solution)/shard_map/all_to_all | solution.py:680
  11.5 15.6 %collective-permute-start.1 = (bf16[256,1152]{1,0:T(8,128)(2,1)S(1)}, bf16[256,1152]{1,0:T(8,128)(2,1)S(1)}, u32[]{:S(2)}, u32[]{:S(2)}) collective-permute-start(bf16[256,1152]{1,0:T(8,128)(2,1)S(1)} %get-tuple-element.35.after_ref.refs_0_), channel_id=1, source_target_pairs={{0,16},{16,0},{1,17},{17,1},{2,18},{18,2},{3,19},{19,3},{4,20},{20... | collective-permute-start | bytes 1769480 | tf_op jit(solution)/shard_map/ppermute | solution.py:677
  14.4 19.8 %copy-start = (bf16[192,512]{1,0:T(8,128)(2,1)}, bf16[192,512]{1,0:T(8,128)(2,1)S(1)}, u32[]{:S(2)}) copy-start(bf16[192,512]{1,0:T(8,128)(2,1)S(1)} %get-tuple-element.36.hidden_ref.refs_1_) | copy-start | bytes 589828
  27.1 6.4 %collective-permute-start.2 = (bf16[192,512]{1,0:T(8,128)(2,1)S(1)}, bf16[192,512]{1,0:T(8,128)(2,1)S(1)}, u32[]{:S(2)}, u32[]{:S(2)}) collective-permute-start(bf16[192,512]{1,0:T(8,128)(2,1)S(1)} %get-tuple-element.38), channel_id=1, source_target_pairs={{0,16},{16,0},{1,17},{17,1},{2,18},{18,2},{3,19},{19,3},{4,20},{20... | collective-permute-start | bytes 589832 | tf_op jit(solution)/shard_map/ppermute | solution.py:677
  33.5 0.7 copy-start.2
  34.1 32.4 %all-to-all-start.1 = ((bf16[16,24,1536]{2,1,0:T(8,128)(2,1)}), bf16[16,24,1536]{2,1,0:T(8,128)(2,1)S(1)}, u32[]{:S(2)}, u32[]{:S(2)}) async-start(bf16[16,24,1536]{2,1,0:T(8,128)(2,1)} %bitcast.6), calls=%async_computation.1 | async-start | bytes 2359296 | tf_op jit(solution)/shard_map/all_to_all | solution.py:680
  39.7 6.1 %copy-start.1 = (bf16[192,512]{1,0:T(8,128)(2,1)S(1)}, bf16[192,512]{1,0:T(8,128)(2,1)}, u32[]{:S(2)}) copy-start(bf16[192,512]{1,0:T(8,128)(2,1)} %copy-done) | copy-start | bytes 589828
  39.7 20.0 %copy-start.3 = (bf16[192,512]{1,0:T(8,128)(2,1)S(1)}, bf16[192,512]{1,0:T(8,128)(2,1)}, u32[]{:S(2)}) copy-start(bf16[192,512]{1,0:T(8,128)(2,1)} %copy-done.2) | copy-start | bytes 589828
  39.7 19.9 %collective-permute-start = (bf16[256,1536]{1,0:T(8,128)(2,1)S(1)}, bf16[256,1536]{1,0:T(8,128)(2,1)S(1)}, u32[]{:S(2)}, u32[]{:S(2)}) collective-permute-start(bf16[256,1536]{1,0:T(8,128)(2,1)S(1)} %bitcast.12), channel_id=1, source_target_pairs={{0,16},{16,0},{1,17},{17,1},{2,18},{18,2},{3,19},{19,3},{4,20},{20... | collective-permute-start | bytes 2359304 | tf_op jit(solution)/shard_map/ppermute | solution.py:677
  68.9 6.7 %collective-permute-start.3 = (bf16[192,512]{1,0:T(8,128)(2,1)}, bf16[192,512]{1,0:T(8,128)(2,1)S(1)}, u32[]{:S(2)}, u32[]{:S(2)}) collective-permute-start(bf16[192,512]{1,0:T(8,128)(2,1)} %get-tuple-element.54), channel_id=1, source_target_pairs={{0,16},{16,0},{1,17},{17,1},{2,18},{18,2},{3,19},{19,3},{4,20},{20... | collective-permute-start | bytes 589832 | tf_op jit(solution)/shard_map/ppermute | solution.py:677
  70.5 12.8 %all-to-all-start.2 = ((f32[32,1,128]{2,1,0:T(1,128)}), f32[32,1,128]{2,1,0:T(1,128)S(1)}, u32[]{:S(2)}, u32[]{:S(2)}) async-start(f32[32,1,128]{2,1,0:T(1,128)} %get-tuple-element.59), calls=%async_computation.2 | async-start | bytes 32768 | tf_op jit(solution)/shard_map/all_to_all | solution.py:702

commit v10 on v9

--- a/solution.py
+++ b/solution.py
@@ -84,12 +84,10 @@
 
 def dispatch_kernel(edges, ids_hbm, slots_hbm, gates_hbm, grad_hbm, *refs):
     outs, (ids_ref, slots_ref, gates_ref, grad_ref, sems) = refs[:2], refs[2:]
-    pairs = [
-        (ids_hbm, ids_ref),
-        (slots_hbm, slots_ref),
-        (gates_hbm, gates_ref),
-        (grad_hbm, grad_ref),
-    ]
+    pairs = [(ids_hbm, ids_ref), (slots_hbm, slots_ref), (gates_hbm, gates_ref)]
+    for c in (1, 0):
+        own = (slice(None), pl.ds(edges[c], edges[c + 1] - edges[c]))
+        pairs.append((grad_hbm.at[own], grad_ref.at[own]))
     copies = [
         pltpu.make_async_copy(source, target, sems.at[i])
         for i, (source, target) in enumerate(pairs)
@@ -114,8 +112,8 @@
     tails = [
         jnp.dot(order, main, preferred_element_type=f32).astype(bf16) for order in orders
     ]
-    copies[3].wait()
     for c in (1, 0):
+        copies[4 - c].wait()
         low, high = edges[c], edges[c + 1]
         part = (high - low) // 4
         for j in range(3):
@@ -144,7 +142,7 @@
             pltpu.VMEM(slots.shape, jnp.int32),
             pltpu.VMEM(gates.shape, bf16),
             pltpu.VMEM(out_grad.shape, bf16),
-            pltpu.SemaphoreType.DMA((4,)),
+            pltpu.SemaphoreType.DMA((5,)),
         ],
         compiler_params=params(2 * rows * width + 2 * tok * width),
         cost_estimate=cost(2 * rows * tok * width, 4 * tok * width),
@@ -342,17 +340,13 @@
     return lax.broadcasted_iota(jnp.int32, (blocks, count), 0)
 
 
-def begin_kernel(blocks, arrived_ref, weight_ref, hidden_ref, *refs):
-    rows_ref, score_ref, proj_hbm, proj_ref, sem = refs
+def begin_kernel(blocks, arrived_ref, weight_ref, hidden_ref, rows_ref, proj_ref, score_ref):
     reorder(arrived_ref[...], rows_ref)
     proj = times_weight(rows_ref, weight_ref)
-    proj_ref[...] = proj
-    copy = pltpu.make_async_copy(proj_ref, proj_hbm, sem.at[0])
-    copy.start()
+    proj_ref[...] = proj.astype(bf16)
     score_ref[...] = score_block(
         blocks, proj, hidden_ref[...], [block_index(blocks, proj.shape[0])]
     )[0]
-    copy.wait()
 
 
 def begin(blocks, arrived, weight, hidden):
@@ -361,28 +355,20 @@
     return pl.pallas_call(
         functools.partial(begin_kernel, blocks),
         in_specs=[VMEM] * 3,
-        out_specs=[VMEM] * 2 + [HBM],
+        out_specs=[VMEM] * 3,
         out_shape=[
             plain((count, cols), bf16),
+            plain((count, part), bf16),
             plain((blocks, 1, LANE), f32),
-            out_hbm((count, part), f32),
         ],
-        scratch_shapes=[pltpu.VMEM((count, part), f32), pltpu.SemaphoreType.DMA((1,))],
         compiler_params=params(8 * count * cols + 8 * count * part),
         cost_estimate=cost(4 * count * part * cols, 2 * part * cols),
     )(arrived, weight, hidden)
 
 
 def finish_kernel(shards, blocks, arrived_ref, hidden_ref, weight_ref, *refs):
-    before_hbm, score_in = refs[:shards], refs[shards : 2 * shards]
-    projs, score_ref = refs[2 * shards : 3 * shards], refs[3 * shards]
-    before, sems = refs[3 * shards + 1 :]
-    copies = [
-        pltpu.make_async_copy(ref, before.at[s], sems.at[s])
-        for s, ref in enumerate(before_hbm)
-    ]
-    for copy in copies:
-        copy.start()
+    before, score_in = refs[:shards], refs[shards : 2 * shards]
+    projs, score_ref = refs[2 * shards : 3 * shards], refs[-1]
     proj = times_weight(arrived_ref, weight_ref)
     rounded = proj.astype(bf16)
     total = proj.shape[0]
@@ -395,8 +381,8 @@
     for s in range(shards):
         order = row == slot + SEND * (div_send(slot) * (shards - 1) + s)
         order = jnp.where(order, 1.0, 0.0).astype(bf16)
-        copies[s].wait()
-        own = before[s] + jnp.dot(order, rounded, preferred_element_type=f32)
+        own = jnp.dot(order, rounded, preferred_element_type=f32)
+        own += before[s][...].astype(f32)
         projs[s][...] = own.astype(bf16)
         at = lax.rem(me + shards - s, shards)
         score_ref[pl.ds(at * blocks, blocks)] = score_in[s][...] + scores[s]
@@ -409,17 +395,13 @@
     cols = weight.shape[1]
     outs = pl.pallas_call(
         functools.partial(finish_kernel, shards, blocks),
-        in_specs=[VMEM] * 3 + [HBM] * shards + [VMEM] * shards,
+        in_specs=[VMEM] * (3 + 2 * shards),
         out_specs=[VMEM] * (shards + 1),
         out_shape=[plain((count, part), bf16)] * shards
         + [plain((shards * blocks, 1, LANE), f32)],
-        scratch_shapes=[
-            pltpu.VMEM((shards, count, part), f32),
-            pltpu.SemaphoreType.DMA((shards,)),
-        ],
         compiler_params=params(20 * total * part),
         cost_estimate=cost(2 * total * part * cols, 2 * part * cols),
-    )(arrived, hidden, weight, *in_hbm(*before), *scores)
+    )(arrived, hidden, weight, *before, *scores)
     return list(outs[:-1]), outs[-1]
 
 
@@ -438,6 +420,19 @@
     return master, m_new.astype(bf16), v_new.astype(bf16)
 
 
+def update_rows(first, count, state, news, grad_ref):
+    cols = grad_ref.shape[1]
+
+    @pl.loop(0, count // ROWS)
+    def _(i):
+        own = pl.ds(pl.multiple_of(first + i * ROWS, ROWS), ROWS)
+        for low in range(0, cols, UNIT):
+            at = (own, slice(low, low + UNIT))
+            values = new_state(*[ref[at] for ref in state], grad_ref[at])
+            for ref, value in zip(news, values):
+                ref[at] = value
+
+
 def transpose_rows(hidden, hidden_t):
     base = 0
     for ref in hidden:
@@ -482,20 +477,16 @@
     size = len(fresh)
     arrived, hidden = take(size), take(1 + size)
     given_ref, weight_ref, *state = take(5)
-    scores, (mixed_ref,) = take(size), take(1)
-    projs_hbm, outs, news = take(size), take(3), take(3)
-    rows_refs, projs = take(size), take(size)
-    hidden_t, grad_ref, sems, proj_sems = refs
+    scores, projs, (mixed_ref,) = take(size), take(size), take(1)
+    outs, news, rows_refs = take(3), take(3), take(size)
+    hidden_t, grad_ref, sems = refs
     part = grad_ref.shape[0]
     count = blocks * SEND
     shards = 1 + size
-    proj_copies = []
     for i, s in enumerate(fresh):
         reorder(arrived[i][...], rows_refs[i])
         proj = times_weight(rows_refs[i], weight_ref)
-        projs[i][...] = proj
-        proj_copies.append(pltpu.make_async_copy(projs[i], projs_hbm[i], proj_sems.at[i]))
-        proj_copies[i].start()
+        projs[i][...] = proj.astype(bf16)
         scores[i][...] = score_block(
             blocks, proj, hidden[s][...], [block_index(blocks, count)]
         )[0]
@@ -506,10 +497,7 @@
 
     @pl.loop(0, part // step)
     def _(i):
-        own = pl.ds(pl.multiple_of(i * step, step), step)
-        values = new_state(*[ref[own, :] for ref in state], grad_ref[own, :])
-        for ref, value in zip(news, values):
-            ref[own, :] = value
+        update_rows(i * step, step, state, news, grad_ref)
         for copy in state_copies(i, step, 0, outs, news, sems, False):
             copy.start()
 
@@ -528,9 +516,6 @@
         for copy in state_copies(i, step, 0, outs, news, sems, False):
             copy.wait()
 
-    for copy in proj_copies:
-        copy.wait()
-
 
 def settle(blocks, arrived, given, hidden, weight, held, shapes):
     part, cols = weight.shape
@@ -540,17 +525,15 @@
     total = count * (1 + size)
     step = min(part, 64)
     args = [*arrived, *hidden, given, weight, *held]
-    near = [plain((blocks, 1, LANE), f32)] * size + [plain((total, part), bf16)]
-    far = [out_hbm((count, part), f32)] * size
-    far += [out_hbm(array.shape, array.dtype) for array in shapes]
+    near = [plain((blocks, 1, LANE), f32)] * size + [plain((count, part), bf16)] * size
+    near.append(plain((total, part), bf16))
+    far = [out_hbm(array.shape, array.dtype) for array in shapes]
     scratch = [pltpu.VMEM((part, cols), kind) for kind in (f32, bf16, bf16)]
     scratch += [pltpu.VMEM((count, cols), bf16)] * size
-    scratch += [pltpu.VMEM((count, part), f32)] * size
     scratch += [
         pltpu.VMEM((part, total), bf16),
         pltpu.VMEM((part, cols), f32),
         pltpu.SemaphoreType.DMA((3, part // step)),
-        pltpu.SemaphoreType.DMA((max(1, size),)),
     ]
     nbytes = 12 * part * cols + 4 * total * cols + 8 * total * part
     outs = pl.pallas_call(
@@ -563,13 +546,14 @@
         cost_estimate=cost(4 * total * part * cols, 16 * part * cols, part * cols),
     )(*args)
     outs = list(outs)
-    return outs[:size], outs[size], outs[size + 1 : -3], outs[-3:]
+    return outs[:size], outs[2 * size], outs[size : 2 * size], outs[-3:]
 
 
 def update_kernel(low, shards, hidden_ref, rows_ref, *refs):
     grad_refs, refs = refs[:shards], refs[shards:]
-    gate_up_hbm, state_hbm, outs, gate_out = refs[0], refs[1:4], refs[7:10], refs[10]
-    state, refs = refs[11:14], refs[14:]
+    gate_up_hbm, state_hbm, token_hbm, refs = refs[0], refs[1:4], refs[4:7], refs[10:]
+    outs, gate_out, place_ref, inverse_ref, refs = refs[:3], *refs[3:6], refs[6:]
+    state, tokens, refs = refs[:3], refs[3:6], refs[6:]
     hidden_t, grad_ref, gate_up_ref, gate_new, in_sems, out_sems, sems = refs
     part = grad_ref.shape[0]
     steps = in_sems.shape[1]
@@ -577,11 +561,23 @@
     gate_load = pltpu.make_async_copy(gate_up_hbm, gate_up_ref, sems.at[0])
     gate_store = pltpu.make_async_copy(gate_new, gate_out, sems.at[1])
     gate_load.start()
+    token_loads = [
+        pltpu.make_async_copy(source, target, sems.at[2 + i])
+        for i, (source, target) in enumerate(zip(token_hbm, tokens))
+    ]
+    for copy in token_loads:
+        copy.start()
     for i in range(steps):
         for copy in state_copies(i, step, low, state_hbm, state, in_sems, True):
             copy.start()
     transpose_rows([hidden_ref], hidden_t)
     form_grad(hidden_t, [rows_ref], grad_ref)
+    for copy in token_loads:
+        copy.wait()
+    ids, slots = tokens[0][...], tokens[1][...]
+    live = ((ids & (EXP_LOCAL - 1)) == 0) & (slots >= 0)
+    place_ref[...] = jnp.where(live, ids // EXP_LOCAL * SEND + slots, -1)
+    inverse_ref[...] = 1.0 / tokens[2][...].astype(f32)
     gate_load.wait()
     for s, ref in enumerate(grad_refs):
         first, second, gate, up, sig = swiglu_part(gate_up_ref, shards, s, ref.shape[1])
@@ -596,10 +592,7 @@
     def _(i):
         for copy in state_copies(i, step, low, state_hbm, state, in_sems, True):
             copy.wait()
-        own = pl.ds(pl.multiple_of(i * step, step), step)
-        values = new_state(*[ref[own, :] for ref in state], grad_ref[own, :])
-        for ref, value in zip(state, values):
-            ref[own, :] = value
+        update_rows(i * step, step, state, state, grad_ref)
         for copy in state_copies(i, step, low, outs, state, out_sems, False):
             copy.start()
 
@@ -611,56 +604,53 @@
     gate_store.wait()
 
 
-def update(low, hidden, rows, grads, gate_up, state, done):
+def update(low, hidden, rows, grads, gate_up, state, tokens, done):
     total, part = hidden.shape
     cols = rows.shape[1]
     step = min(part, 64)
     shards = len(grads)
     scratch = [pltpu.VMEM((part, cols), kind) for kind in (f32, bf16, bf16)]
+    scratch += [pltpu.VMEM(token.shape, token.dtype) for token in tokens]
     scratch += [pltpu.VMEM((part, total), bf16), pltpu.VMEM((part, cols), f32)]
     scratch += [pltpu.VMEM(gate_up.shape, bf16)] * 2
     scratch += [pltpu.SemaphoreType.DMA((3, part // step))] * 2
-    scratch += [pltpu.SemaphoreType.DMA((2,))]
+    scratch += [pltpu.SemaphoreType.DMA((5,))]
     return pl.pallas_call(
         functools.partial(update_kernel, low, shards),
-        in_specs=[VMEM] * (2 + shards) + [HBM] * 7,
-        out_specs=[HBM] * 4,
+        in_specs=[VMEM] * (2 + shards) + [HBM] * 10,
+        out_specs=[HBM] * 4 + [VMEM] * 2,
         out_shape=[out_hbm(array.shape, array.dtype) for array in state]
-        + [out_hbm(gate_up.shape, bf16)],
+        + [out_hbm(gate_up.shape, bf16)]
+        + [plain(tokens[0].shape, kind) for kind in (jnp.int32, f32)],
         scratch_shapes=scratch,
-        input_output_aliases={2 + shards + 4 + i: i for i in range(3)},
+        input_output_aliases={2 + shards + 7 + i: i for i in range(3)},
         compiler_params=params(12 * part * cols + 2 * total * part + 4 * gate_up.size),
         cost_estimate=cost(2 * total * part * cols, 16 * part * cols, part * cols),
-    )(hidden, rows, *grads, *in_hbm(gate_up, *state, *done))
-
-
-def close_kernel(shards, ids_ref, slots_ref, gates_ref, score_ref, after_ref, gate_ref):
-    del after_ref
-    ids = ids_ref[...]
-    slots = slots_ref[...]
-    live = ((ids & (EXP_LOCAL - 1)) == 0) & (slots >= 0)
-    place = jnp.where(live, ids // EXP_LOCAL * SEND + slots, -1)
+    )(hidden, rows, *grads, *in_hbm(gate_up, *state, *tokens, *done))
+
+
+def close_kernel(shards, place_ref, inverse_ref, score_ref, gate_ref):
+    place = place_ref[...]
     blocks = score_ref.shape[0] // shards
-    value = jnp.zeros(ids.shape, f32)
+    value = jnp.zeros(place.shape, f32)
     for b in range(blocks):
         for slot in range(SEND):
             score = score_ref[b, 0, slot]
             for s in range(1, shards):
                 score += score_ref[s * blocks + b, 0, slot]
             value = jnp.where(place == b * SEND + slot, score, value)
-    gate_ref[...] = jnp.where(live, value / gates_ref[...].astype(f32), 0.0)
-
-
-def close(shards, ids, slots, gates, score, after):
+    gate_ref[...] = value * inverse_ref[...]
+
+
+def close(shards, place, inverse, score):
     return pl.pallas_call(
         functools.partial(close_kernel, shards),
-        grid=(1,),
-        in_specs=[block(ids.shape)] * 3 + [pl.BlockSpec(memory_space=pltpu.SMEM), HBM],
-        out_specs=block(ids.shape),
-        out_shape=out_hbm(ids.shape, f32),
+        in_specs=[VMEM] * 2 + [pl.BlockSpec(memory_space=pltpu.SMEM)],
+        out_specs=VMEM,
+        out_shape=plain(place.shape, f32),
         compiler_params=params(0),
         cost_estimate=cost(1 << 20, 1 << 16),
-    )(*in_hbm(ids, slots, gates), score, *in_hbm(after))
+    )(place, inverse, score)
 
 
 def per_device(out_grad, expert_ids, slots, gate_weights, saved_gate_up, master, moment1, moment2):
@@ -691,7 +681,7 @@
 
     peers = [shift(arrived, s) for s in steps]
     *held, weight_a, weight_b = load_state(edges[1], *state, arrived)
-    rows, score_own, proj = begin(ep_size, arrived, weight_a, hidden[0])
+    rows, proj, score_own = begin(ep_size, arrived, weight_a, hidden[0])
     scores, hidden_mixed, before, done = settle(
         ep_size, peers, rows, hidden, weight_a, held, state
     )
@@ -701,10 +691,11 @@
     grads = [projs[0]] + [shift(projs[s], rep_size - s) for s in steps]
     score = lax.all_to_all(score, ("rep", "ep"), split_axis=0, concat_axis=0, tiled=True)
 
-    *done, grad_gate_up = update(
-        edges[1], hidden_mixed, arrived_b, grads, gate_up, state, done
+    tokens = (ids_t, slots_t, gates_t)
+    *done, grad_gate_up, place, inverse = update(
+        edges[1], hidden_mixed, arrived_b, grads, gate_up, state, tokens, done
     )
-    gate_grad = close(rep_size, ids_t, slots_t, gates_t, score, grad_gate_up).T
+    gate_grad = close(rep_size, place, inverse, score).T
     return (grad_gate_up.reshape(saved_gate_up.shape), gate_grad) + tuple(done)
 
 

time: 85.7 us -> 86.3 us (level)
  local copies, waits for them, and re-layouts: 0.7 us -> 2.98 us
  Pallas kernels: 32 us -> 30.9 us
    unnamed x8 -> x16, local copies, waits for them, and re-layouts: 0.7 us -> 2.98 us
  transfers between devices with their start and end apart: 7 -> 7, of which waited for: 4 -> 4; matrix products, arithmetic and copies ran while one was open for 0% -> 0% of each run, Pallas kernels for 29% -> 28%
where the time goes in v10:
time: 86.3 us; the launch traced here: 85.9 us
  Pallas kernels  30.9 us (36%)
  waiting for transfers between devices  27.5 us (32%)
  starting transfers between devices  23.8 us (28%)
  local copies, waits for them, and re-layouts  2.98 us (3%)
    ppermute x4, waiting for transfers between devices, shift(): return lax.ppermute(value, 'rep', perm)  27.5 us
    all_to_all x2, starting transfers between devices, exchange(): return lax.all_to_all(value, 'ep', split_axis=0, concat_axis=0, tiled=True)  12.9 us
    pallas_call x1, Pallas kernels, update(): pl.pallas_call(functools.partial(update_kernel, low, shards), in_specs=[V...  7.75 us
    pallas_call x1, Pallas kernels, settle(): pl.pallas_call(functools.partial(settle_kernel, fresh, blocks), in_specs=...  6.91 us
    ppermute x4, starting transfers between devices, shift(): return lax.ppermute(value, 'rep', perm)  6.19 us
    all_to_all x1, starting transfers between devices, per_device(): lax.all_to_all(score, ('rep', 'ep'), split_axis=0, concat_axis=0, tiled=T...  4.71 us
    pallas_call x1, Pallas kernels, load_state(): pl.pallas_call(functools.partial(load_kernel, middle), in_specs=[ANY] + [...  4.47 us
    pallas_call x1, Pallas kernels, dispatch(): pl.pallas_call(functools.partial(dispatch_kernel, edges), in_specs=[HBM]...  3.26 us
  transfers between devices with their start and end apart: 7, of which 4 were waited for; matrix products, arithmetic and copies ran while one was open for 0% of the time, Pallas kernels for 28%

profile of v10, /device:TPU:0, one launch (start us, length us, event | category | flops | bytes accessed | tf_op | source)
XLA Modules:
  0.0 85.9 jit_solution(15057737934993809663)
XLA Ops:
  0.6 3.3 %shard_map.119 = (bf16[256,1536]{1,0:T(8,128)(2,1)}, bf16[256,1152]{1,0:T(8,128)(2,1)S(1)}) custom-call(s32[8,256]{1,0:T(8,128)} %bitcast.17, s32[8,256]{1,0:T(8,128)} %bitcast.19, bf16[8,256]{1,0:T(8,128)(2,1)} %bitcast.21, bf16[256,3584]{1,0:T(8,128)(2,1)} %grad_hbm.1), custom_call_target="tpu_custom_call" | custom-call | flops 469762048 | bytes 3670016 | tf_op jit(solution)/shard_map/pallas_call | solution.py:135
  3.9 7.4 %all-to-all-start = ((bf16[16,16,1536]{2,1,0:T(8,128)(2,1)}), bf16[16,16,1536]{2,1,0:T(8,128)(2,1)S(1)}, u32[]{:S(2)}, u32[]{:S(2)}) async-start(bf16[16,16,1536]{2,1,0:T(8,128)(2,1)} %bitcast.3), calls=%async_computation | async-start | bytes 1572864 | tf_op jit(solution)/shard_map/all_to_all | solution.py:670
  11.3 1.6 %collective-permute-start.1 = (bf16[256,1152]{1,0:T(8,128)(2,1)S(1)}, bf16[256,1152]{1,0:T(8,128)(2,1)S(1)}, u32[]{:S(2)}, u32[]{:S(2)}) collective-permute-start(bf16[256,1152]{1,0:T(8,128)(2,1)S(1)} %get-tuple-element.37.after_ref.refs_0_), channel_id=1, source_target_pairs={{0,16},{16,0},{1,17},{17,1},{2,18},{18,2},{3,19},{19,3},{4,20},{20... | collective-permute-start | bytes 1769480 | tf_op jit(solution)/shard_map/ppermute | solution.py:667
  12.9 1.3 %shard_map.120 = (bf16[192,512]{1,0:T(8,128)(2,1)S(1)}, bf16[192,512]{1,0:T(8,128)(2,1)S(1)}) custom-call(bf16[192,2048]{1,0:T(8,128)(2,1)} %bitcast.15, bf16[256,1152]{1,0:T(8,128)(2,1)S(1)} %get-tuple-element.37.after_ref.refs_0_), custom_call_target="tpu_custom_call" | custom-call | flops 3145728 | bytes 1179648 | tf_op jit(solution)/shard_map/pallas_call | solution.py:171
  14.2 0.0 copy-start
  14.2 12.7 %collective-permute-done.1.refs_1_ = bf16[256,1152]{1,0:T(8,128)(2,1)S(1)} collective-permute-done((bf16[256,1152]{1,0:T(8,128)(2,1)S(1)}, bf16[256,1152]{1,0:T(8,128)(2,1)S(1)}, u32[]{:S(2)}, u32[]{:S(2)}) %collective-permute-start.1) | collective-permute-done | bytes 589856 | tf_op jit(solution)/shard_map/ppermute | solution.py:667
  26.9 1.5 %collective-permute-start.2 = (bf16[192,512]{1,0:T(8,128)(2,1)S(1)}, bf16[192,512]{1,0:T(8,128)(2,1)S(1)}, u32[]{:S(2)}, u32[]{:S(2)}) collective-permute-start(bf16[192,512]{1,0:T(8,128)(2,1)S(1)} %get-tuple-element.40), channel_id=1, source_target_pairs={{0,16},{16,0},{1,17},{17,1},{2,18},{18,2},{3,19},{19,3},{4,20},{20... | collective-permute-start | bytes 589832 | tf_op jit(solution)/shard_map/ppermute | solution.py:667
  28.4 2.3 %shard_map.121 = bf16[384,1536]{1,0:T(8,128)(2,1)} custom-call(bf16[256,1152]{1,0:T(8,128)(2,1)S(1)} %get-tuple-element.37.after_ref.refs_0_, bf16[256,1152]{1,0:T(8,128)(2,1)S(1)} %collective-permute-done.1.refs_1_), custom_call_target="tpu_custom_call" | custom-call | bytes 2949120 | tf_op jit(solution)/shard_map/pallas_call | solution.py:286
  30.8 2.5 %collective-permute-done.2.refs_2_ = bf16[192,512]{1,0:T(8,128)(2,1)S(1)} collective-permute-done((bf16[192,512]{1,0:T(8,128)(2,1)S(1)}, bf16[192,512]{1,0:T(8,128)(2,1)S(1)}, u32[]{:S(2)}, u32[]{:S(2)}) %collective-permute-start.2) | collective-permute-done | bytes 196640 | tf_op jit(solution)/shard_map/ppermute | solution.py:667
  33.3 0.0 copy-start.6
  33.3 0.7 copy-done.6
  33.9 0.0 all-to-all-done
  33.9 0.0 copy-done
  34.0 5.5 %all-to-all-start.1 = ((bf16[16,24,1536]{2,1,0:T(8,128)(2,1)}), bf16[16,24,1536]{2,1,0:T(8,128)(2,1)S(1)}, u32[]{:S(2)}, u32[]{:S(2)}) async-start(bf16[16,24,1536]{2,1,0:T(8,128)(2,1)} %bitcast.6), calls=%async_computation.1 | async-start | bytes 2359296 | tf_op jit(solution)/shard_map/all_to_all | solution.py:670
  39.5 0.0 copy-start.1
  39.5 0.0 copy-start.7
  39.5 1.6 %collective-permute-start = (bf16[256,1536]{1,0:T(8,128)(2,1)S(1)}, bf16[256,1536]{1,0:T(8,128)(2,1)S(1)}, u32[]{:S(2)}, u32[]{:S(2)}) collective-permute-start(bf16[256,1536]{1,0:T(8,128)(2,1)S(1)} %bitcast.12), channel_id=1, source_target_pairs={{0,16},{16,0},{1,17},{17,1},{2,18},{18,2},{3,19},{19,3},{4,20},{20... | collective-permute-start | bytes 2359304 | tf_op jit(solution)/shard_map/ppermute | solution.py:667
  41.1 4.5 %shard_map.122 = (f32[512,2048]{1,0:T(8,128)S(1)}, bf16[512,2048]{1,0:T(8,128)(2,1)S(1)}, bf16[512,2048]{1,0:T(8,128)(2,1)S(1)}, bf16[512,2048]{1,0:T(8,128)(2,1)S(1)}, bf16[512,1536]{1,0:T(8,128)(2,1)S(1)}) custom-call(bf16[256,1536]{1,0:T(8,128)(2,1)S(1)} %bitcast.13, f32[1,512,3584]{2,1,0:T(8,128)} %refs_3_.1, bf16[1,512,3584]{2,1,0:T(8,128)(2,1)} %refs_4_.1, ...), custom_call_target="tpu_custom_call" | custom-call | flops 1835008 | bytes 25690112 | tf_op jit(solution)/shard_map/pallas_call | solution.py:223
  45.6 0.0 copy-done.1
  45.6 1.4 %shard_map.123 = (bf16[192,2048]{1,0:T(8,128)(2,1)S(1)}, bf16[192,512]{1,0:T(8,128)(2,1)S(1)}, f32[16,1,128]{2,1,0:T(1,128)S(1)}) custom-call(bf16[256,1536]{1,0:T(8,128)(2,1)S(1)} %bitcast.14, bf16[512,2048]{1,0:T(8,128)(2,1)S(1)} %get-tuple-element.43.weight_ref.refs_4_, bf16[192,512]{1,0:T(8,128)(2,1)S(1)} %copy-done.1), custom_call_target="tpu_custom_call" | custom-call | flops 805306368 | bytes 2097152 | tf_op jit(solution)/shard_map/pallas_call | solution.py:355
  46.9 0.0 copy-start.2
  47.0 0.7 copy-done.2
  47.6 11.8 %collective-permute-done.refs_0_ = bf16[256,1536]{1,0:T(8,128)(2,1)S(1)} collective-permute-done((bf16[256,1536]{1,0:T(8,128)(2,1)S(1)}, bf16[256,1536]{1,0:T(8,128)(2,1)S(1)}, u32[]{:S(2)}, u32[]{:S(2)}) %collective-permute-start) | collective-permute-done | bytes 786464 | tf_op jit(solution)/shard_map/ppermute | solution.py:667
  59.5 0.0 copy-done.7
  59.5 0.0 copy-start.3
  59.5 6.9 %shard_map.124 = (f32[16,1,128]{2,1,0:T(1,128)S(1)}, bf16[192,512]{1,0:T(8,128)(2,1)S(1)}, bf16[384,512]{1,0:T(8,128)(2,1)S(1)}, f32[1,512,3584]{2,1,0:T(8,128)}...) custom-call(bf16[256,1536]{1,0:T(8,128)(2,1)S(1)} %collective-permute-done.refs_0_, ...), custom_call_target="tpu_custom_call" | custom-call | flops 1610612736 | bytes 16777216 | tf_op jit(solution)/shard_map/pallas_call | solution.py:539
  66.4 0.0 copy-start.4
  66.4 0.7 copy-done.4
  67.1 0.0 all-to-all-done.1
  67.1 0.0 copy-done.3
  67.1 0.0 copy-start.5
  67.1 0.9 %copy-done.5 = bf16[192,512]{1,0:T(8,128)(2,1)S(1)} copy-done((bf16[192,512]{1,0:T(8,128)(2,1)S(1)}, bf16[192,512]{1,0:T(8,128)(2,1)}, u32[]{:S(2)}) %copy-start.5) | copy-done | bytes 196632
  68.0 2.0 %shard_map.125 = (bf16[192,512]{1,0:T(8,128)(2,1)S(1)}, bf16[192,512]{1,0:T(8,128)(2,1)}, f32[32,1,128]{2,1,0:T(1,128)}) custom-call(bf16[384,1536]{1,0:T(8,128)(2,1)S(1)} %bitcast.10, bf16[384,512]{1,0:T(8,128)(2,1)S(1)} %get-tuple-element.48.hidden_ref, bf16[512,1536]{1,0:T(8,128)(2,1)S(1)} %get-tuple-element.50.weight_ref, ...), custom_call_target="tpu_custom_call" | custom-call | flops 603979776 | bytes 1572864 | tf_op jit(solution)/shard_map/pallas_call | solution.py:396
  70.0 1.5 %collective-permute-start.3 = (bf16[192,512]{1,0:T(8,128)(2,1)}, bf16[192,512]{1,0:T(8,128)(2,1)S(1)}, u32[]{:S(2)}, u32[]{:S(2)}) collective-permute-start(bf16[192,512]{1,0:T(8,128)(2,1)} %get-tuple-element.56), channel_id=1, source_target_pairs={{0,16},{16,0},{1,17},{17,1},{2,18},{18,2},{3,19},{19,3},{4,20},{20... | collective-permute-start | bytes 589832 | tf_op jit(solution)/shard_map/ppermute | solution.py:667
  71.5 4.7 %all-to-all-start.2 = ((f32[32,1,128]{2,1,0:T(1,128)}), f32[32,1,128]{2,1,0:T(1,128)S(1)}, u32[]{:S(2)}, u32[]{:S(2)}) async-start(f32[32,1,128]{2,1,0:T(1,128)} %get-tuple-element.63), calls=%async_computation.2 | async-start | bytes 32768 | tf_op jit(solution)/shard_map/all_to_all | solution.py:692
  76.2 0.4 collective-permute-done.3.refs_1_
  76.6 7.7 %shard_map.126 = (f32[1,512,3584]{2,1,0:T(8,128)}, bf16[1,512,3584]{2,1,0:T(8,128)(2,1)}, bf16[1,512,3584]{2,1,0:T(8,128)(2,1)}, bf16[192,2048]{1,0:T(8,128)(2,1...) custom-call(bf16[384,512]{1,0:T(8,128)(2,1)S(1)} %get-tuple-element., ...), custom_call_target="tpu_custom_call", output_to_operand_aliasing={{0}: (11, {}), {1}: (12, {}), {2}: (13, {})} | custom-call | flops 603979776 | bytes 12582912 | tf_op jit(solution)/shard_map/pallas_call | solution.py:618
  84.4 0.0 all-to-all-done.2.score_ref
  84.4 1.6 %shard_map.127 = f32[8,256]{1,0:T(8,128)} custom-call(s32[8,256]{1,0:T(8,128)S(1)} %get-tuple-element.61.place_ref, f32[8,256]{1,0:T(8,128)S(1)} %get-tuple-element.62.inverse_ref, f32[32,1,128]{2,1,0:T(1,128)S(1)} %all-to-all-done.2.score_ref), custom_call_target="tpu_custom_call" | custom-call | flops 1048576 | bytes 65536 | tf_op jit(solution)/shard_map/pallas_call | solution.py:646
Async XLA Ops:
  3.9 30.1 %all-to-all-start = ((bf16[16,16,1536]{2,1,0:T(8,128)(2,1)}), bf16[16,16,1536]{2,1,0:T(8,128)(2,1)S(1)}, u32[]{:S(2)}, u32[]{:S(2)}) async-start(bf16[16,16,1536]{2,1,0:T(8,128)(2,1)} %bitcast.3), calls=%async_computation | async-start | bytes 1572864 | tf_op jit(solution)/shard_map/all_to_all | solution.py:670
  11.3 15.6 %collective-permute-start.1 = (bf16[256,1152]{1,0:T(8,128)(2,1)S(1)}, bf16[256,1152]{1,0:T(8,128)(2,1)S(1)}, u32[]{:S(2)}, u32[]{:S(2)}) collective-permute-start(bf16[256,1152]{1,0:T(8,128)(2,1)S(1)} %get-tuple-element.37.after_ref.refs_0_), channel_id=1, source_target_pairs={{0,16},{16,0},{1,17},{17,1},{2,18},{18,2},{3,19},{19,3},{4,20},{20... | collective-permute-start | bytes 1769480 | tf_op jit(solution)/shard_map/ppermute | solution.py:667
  14.2 19.8 %copy-start = (bf16[192,512]{1,0:T(8,128)(2,1)}, bf16[192,512]{1,0:T(8,128)(2,1)S(1)}, u32[]{:S(2)}) copy-start(bf16[192,512]{1,0:T(8,128)(2,1)S(1)} %get-tuple-element.38.hidden_ref.refs_1_) | copy-start | bytes 589828
  26.9 6.4 %collective-permute-start.2 = (bf16[192,512]{1,0:T(8,128)(2,1)S(1)}, bf16[192,512]{1,0:T(8,128)(2,1)S(1)}, u32[]{:S(2)}, u32[]{:S(2)}) collective-permute-start(bf16[192,512]{1,0:T(8,128)(2,1)S(1)} %get-tuple-element.40), channel_id=1, source_target_pairs={{0,16},{16,0},{1,17},{17,1},{2,18},{18,2},{3,19},{19,3},{4,20},{20... | collective-permute-start | bytes 589832 | tf_op jit(solution)/shard_map/ppermute | solution.py:667
  33.3 0.7 copy-start.6
  34.0 33.1 %all-to-all-start.1 = ((bf16[16,24,1536]{2,1,0:T(8,128)(2,1)}), bf16[16,24,1536]{2,1,0:T(8,128)(2,1)S(1)}, u32[]{:S(2)}, u32[]{:S(2)}) async-start(bf16[16,24,1536]{2,1,0:T(8,128)(2,1)} %bitcast.6), calls=%async_computation.1 | async-start | bytes 2359296 | tf_op jit(solution)/shard_map/all_to_all | solution.py:670
  39.5 6.1 %copy-start.1 = (bf16[192,512]{1,0:T(8,128)(2,1)S(1)}, bf16[192,512]{1,0:T(8,128)(2,1)}, u32[]{:S(2)}) copy-start(bf16[192,512]{1,0:T(8,128)(2,1)} %copy-done) | copy-start | bytes 589828
  39.5 20.0 %copy-start.7 = (bf16[192,512]{1,0:T(8,128)(2,1)S(1)}, bf16[192,512]{1,0:T(8,128)(2,1)}, u32[]{:S(2)}) copy-start(bf16[192,512]{1,0:T(8,128)(2,1)} %copy-done.6) | copy-start | bytes 589828
  39.5 19.9 %collective-permute-start = (bf16[256,1536]{1,0:T(8,128)(2,1)S(1)}, bf16[256,1536]{1,0:T(8,128)(2,1)S(1)}, u32[]{:S(2)}, u32[]{:S(2)}) collective-permute-start(bf16[256,1536]{1,0:T(8,128)(2,1)S(1)} %bitcast.12), channel_id=1, source_target_pairs={{0,16},{16,0},{1,17},{17,1},{2,18},{18,2},{3,19},{19,3},{4,20},{20... | collective-permute-start | bytes 2359304 | tf_op jit(solution)/shard_map/ppermute | solution.py:667
  46.9 0.7 copy-start.2
  59.5 7.6 %copy-start.3 = (bf16[192,512]{1,0:T(8,128)(2,1)S(1)}, bf16[192,512]{1,0:T(8,128)(2,1)}, u32[]{:S(2)}) copy-start(bf16[192,512]{1,0:T(8,128)(2,1)} %copy-done.2) | copy-start | bytes 589828
  66.4 0.7 copy-start.4
  67.1 0.9 %copy-start.5 = (bf16[192,512]{1,0:T(8,128)(2,1)S(1)}, bf16[192,512]{1,0:T(8,128)(2,1)}, u32[]{:S(2)}) copy-start(bf16[192,512]{1,0:T(8,128)(2,1)} %copy-done.4) | copy-start | bytes 589828
  70.0 6.7 %collective-permute-start.3 = (bf16[192,512]{1,0:T(8,128)(2,1)}, bf16[192,512]{1,0:T(8,128)(2,1)S(1)}, u32[]{:S(2)}, u32[]{:S(2)}) collective-permute-start(bf16[192,512]{1,0:T(8,128)(2,1)} %get-tuple-element.56), channel_id=1, source_target_pairs={{0,16},{16,0},{1,17},{17,1},{2,18},{18,2},{3,19},{19,3},{4,20},{20... | collective-permute-start | bytes 589832 | tf_op jit(solution)/shard_map/ppermute | solution.py:667
  71.5 12.9 %all-to-all-start.2 = ((f32[32,1,128]{2,1,0:T(1,128)}), f32[32,1,128]{2,1,0:T(1,128)S(1)}, u32[]{:S(2)}, u32[]{:S(2)}) async-start(f32[32,1,128]{2,1,0:T(1,128)} %get-tuple-element.63), calls=%async_computation.2 | async-start | bytes 32768 | tf_op jit(solution)/shard_map/all_to_all | solution.py:692

commit v11 on v10

--- a/solution.py
+++ b/solution.py
@@ -248,10 +248,11 @@
 
 
 def mix_kernel(shards, *refs):
-    parts, out_ref = refs[:shards], refs[-1]
+    parts, (out_hbm_ref, out_ref, sems) = refs[:shards], refs[shards:]
     part = parts[0].shape[1] // 3
+    copies = []
     blocks = parts[0].shape[0] // ROWS
-    some = max(1, min(blocks, 32 // shards))
+    some = min(blocks, 32 // shards)
     rows, packed = some * shards * SEND, some * shards * ROWS
     row = lax.broadcasted_iota(jnp.int32, (rows, packed), 0)
     col = lax.broadcasted_iota(jnp.int32, (rows, packed), 1)
@@ -266,9 +267,20 @@
             [ref[first * ROWS : (first + some) * ROWS, :] for ref in parts], axis=0
         )
         own = slice(first * shards * SEND, (first + some) * shards * SEND)
-        out_ref[own, : 3 * part] = jnp.dot(
-            orders[0], stack, preferred_element_type=f32
-        ).astype(bf16)
+        place = pl.ds(first * shards * SEND, some * shards * SEND)
+        index = first // some
+
+        def send(j):
+            at = (place, pl.ds(j * part, part))
+            copy = pltpu.make_async_copy(out_ref.at[at], out_hbm_ref.at[at], sems.at[j, index])
+            copy.start()
+            copies.append(copy)
+
+        for j in range(3):
+            out_ref[own, j * part : (j + 1) * part] = jnp.dot(
+                orders[0], stack[:, j * part : (j + 1) * part], preferred_element_type=f32
+            ).astype(bf16)
+            send(j)
         tail = jnp.zeros((rows, part), f32)
         for j in range(3):
             tail += jnp.dot(
@@ -277,6 +289,9 @@
                 preferred_element_type=f32,
             )
         out_ref[own, 3 * part :] = tail.astype(bf16)
+        send(3)
+    for copy in copies:
+        copy.wait()
 
 
 def mix(parts):
@@ -286,8 +301,12 @@
     return pl.pallas_call(
         functools.partial(mix_kernel, shards),
         in_specs=[VMEM] * shards,
-        out_specs=VMEM,
-        out_shape=plain(shape, bf16),
+        out_specs=HBM,
+        out_shape=out_hbm(shape, bf16),
+        scratch_shapes=[
+            pltpu.VMEM(shape, bf16),
+            pltpu.SemaphoreType.DMA((4, rows // ROWS // min(rows // ROWS, 32 // shards))),
+        ],
         compiler_params=params(12 * rows * packed * shards),
         cost_estimate=cost(0, 5 * rows * packed * shards),
     )(*parts)
@@ -340,35 +359,62 @@
     return lax.broadcasted_iota(jnp.int32, (blocks, count), 0)
 
 
-def begin_kernel(blocks, arrived_ref, weight_ref, hidden_ref, rows_ref, proj_ref, score_ref):
+def begin_kernel(blocks, arrived_ref, weight_ref, *refs):
+    hidden, (rows_ref, hidden_t, mixed_ref, score_ref) = refs[:-7], refs[-7:-3]
+    proj_hbm, proj_ref, sem = refs[-3:]
     reorder(arrived_ref[...], rows_ref)
     proj = times_weight(rows_ref, weight_ref)
-    proj_ref[...] = proj.astype(bf16)
+    proj_ref[...] = proj
+    copy = pltpu.make_async_copy(proj_ref, proj_hbm, sem.at[0])
+    copy.start()
+    count = proj.shape[0]
     score_ref[...] = score_block(
-        blocks, proj, hidden_ref[...], [block_index(blocks, proj.shape[0])]
+        blocks, proj, hidden[0][...], [block_index(blocks, count)]
     )[0]
+    transpose_rows(hidden, hidden_t)
+    shards = len(hidden)
+    row = lax.broadcasted_iota(jnp.int32, (shards * count, count), 0)
+    col = lax.broadcasted_iota(jnp.int32, (shards * count, count), 1)
+    at, step_of, slot = mixed_place(row, shards)
+    total = 0.0
+    for s in range(shards):
+        order = (step_of == s) & (col == at * SEND + slot)
+        order = jnp.where(order, 1.0, 0.0).astype(bf16)
+        total += jnp.dot(order, hidden[s][...], preferred_element_type=f32)
+    mixed_ref[...] = total.astype(bf16)
+    copy.wait()
 
 
 def begin(blocks, arrived, weight, hidden):
     count = blocks * SEND
     part, cols = weight.shape
+    total = count * len(hidden)
     return pl.pallas_call(
         functools.partial(begin_kernel, blocks),
-        in_specs=[VMEM] * 3,
-        out_specs=[VMEM] * 3,
+        in_specs=[VMEM] * (2 + len(hidden)),
+        out_specs=[VMEM] * 4 + [HBM],
         out_shape=[
             plain((count, cols), bf16),
-            plain((count, part), bf16),
+            plain((part, total), bf16),
+            plain((total, part), bf16),
             plain((blocks, 1, LANE), f32),
+            out_hbm((count, part), f32),
         ],
-        compiler_params=params(8 * count * cols + 8 * count * part),
+        scratch_shapes=[pltpu.VMEM((count, part), f32), pltpu.SemaphoreType.DMA((1,))],
+        compiler_params=params(8 * count * cols + 16 * total * part),
         cost_estimate=cost(4 * count * part * cols, 2 * part * cols),
-    )(arrived, weight, hidden)
+    )(arrived, weight, *hidden)
 
 
 def finish_kernel(shards, blocks, arrived_ref, hidden_ref, weight_ref, *refs):
-    before, score_in = refs[:shards], refs[shards : 2 * shards]
-    projs, score_ref = refs[2 * shards : 3 * shards], refs[-1]
+    before_hbm, score_in = refs[:shards], refs[shards : 2 * shards]
+    projs, (score_ref, before, sems) = refs[2 * shards : 3 * shards], refs[3 * shards :]
+    copies = [
+        pltpu.make_async_copy(ref, before.at[s], sems.at[s])
+        for s, ref in enumerate(before_hbm)
+    ]
+    for copy in copies:
+        copy.start()
     proj = times_weight(arrived_ref, weight_ref)
     rounded = proj.astype(bf16)
     total = proj.shape[0]
@@ -382,7 +428,8 @@
         order = row == slot + SEND * (div_send(slot) * (shards - 1) + s)
         order = jnp.where(order, 1.0, 0.0).astype(bf16)
         own = jnp.dot(order, rounded, preferred_element_type=f32)
-        own += before[s][...].astype(f32)
+        copies[s].wait()
+        own += before[s]
         projs[s][...] = own.astype(bf16)
         at = lax.rem(me + shards - s, shards)
         score_ref[pl.ds(at * blocks, blocks)] = score_in[s][...] + scores[s]
@@ -395,13 +442,17 @@
     cols = weight.shape[1]
     outs = pl.pallas_call(
         functools.partial(finish_kernel, shards, blocks),
-        in_specs=[VMEM] * (3 + 2 * shards),
+        in_specs=[VMEM] * 3 + [HBM] * shards + [VMEM] * shards,
         out_specs=[VMEM] * (shards + 1),
         out_shape=[plain((count, part), bf16)] * shards
         + [plain((shards * blocks, 1, LANE), f32)],
+        scratch_shapes=[
+            pltpu.VMEM((shards, count, part), f32),
+            pltpu.SemaphoreType.DMA((shards,)),
+        ],
         compiler_params=params(20 * total * part),
         cost_estimate=cost(2 * total * part * cols, 2 * part * cols),
-    )(arrived, hidden, weight, *before, *scores)
+    )(arrived, hidden, weight, *in_hbm(*before), *scores)
     return list(outs[:-1]), outs[-1]
 
 
@@ -441,18 +492,20 @@
         base = high
 
 
-def form_grad(hidden_t, rows_refs, grad_ref):
-    for i in range(grad_ref.shape[1] // UNIT):
-        own = slice(i * UNIT, (i + 1) * UNIT)
+def form_grad(first, count, hidden_t, rows_refs, grad_ref):
+    own = slice(first, first + count)
+    for low in range(0, grad_ref.shape[1], UNIT):
         base = 0
         grad = 0.0
         for rows_ref in rows_refs:
             high = base + rows_ref.shape[0]
             grad += jnp.dot(
-                hidden_t[:, base:high], rows_ref[:, own], preferred_element_type=f32
+                hidden_t[own, base:high],
+                rows_ref[:, low : low + UNIT],
+                preferred_element_type=f32,
             )
             base = high
-        grad_ref[:, own] = grad
+        grad_ref[own, low : low + UNIT] = grad
 
 
 def state_copies(i, step, low, hbm, vmem, sems, into):
@@ -475,65 +528,54 @@
         return out
 
     size = len(fresh)
-    arrived, hidden = take(size), take(1 + size)
-    given_ref, weight_ref, *state = take(5)
-    scores, projs, (mixed_ref,) = take(size), take(size), take(1)
-    outs, news, rows_refs = take(3), take(3), take(size)
-    hidden_t, grad_ref, sems = refs
+    arrived, hidden = take(size), take(size)
+    hidden_t, given_ref, weight_ref, *state = take(6)
+    scores, projs_hbm, outs = take(size), take(size), take(3)
+    news, rows_refs, projs = take(3), take(size), take(size)
+    grad_ref, sems, proj_sems = refs
     part = grad_ref.shape[0]
     count = blocks * SEND
-    shards = 1 + size
-    for i, s in enumerate(fresh):
+    for i in range(size):
         reorder(arrived[i][...], rows_refs[i])
-        proj = times_weight(rows_refs[i], weight_ref)
-        projs[i][...] = proj.astype(bf16)
-        scores[i][...] = score_block(
-            blocks, proj, hidden[s][...], [block_index(blocks, count)]
-        )[0]
-    transpose_rows(hidden, hidden_t)
-    form_grad(hidden_t, [given_ref] + rows_refs, grad_ref)
-
-    step = part // sems.shape[1]
-
-    @pl.loop(0, part // step)
-    def _(i):
+    steps = sems.shape[1]
+    step = part // steps
+    copies = []
+    for i in range(steps):
+        form_grad(i * step, step, hidden_t, [given_ref] + rows_refs, grad_ref)
         update_rows(i * step, step, state, news, grad_ref)
         for copy in state_copies(i, step, 0, outs, news, sems, False):
             copy.start()
-
-    row = lax.broadcasted_iota(jnp.int32, (shards * count, count), 0)
-    col = lax.broadcasted_iota(jnp.int32, (shards * count, count), 1)
-    at, step_of, slot = mixed_place(row, shards)
-    total = 0.0
-    for s in range(shards):
-        order = (step_of == s) & (col == at * SEND + slot)
-        order = jnp.where(order, 1.0, 0.0).astype(bf16)
-        total += jnp.dot(order, hidden[s][...], preferred_element_type=f32)
-    mixed_ref[...] = total.astype(bf16)
-
-    @pl.loop(0, part // step)
-    def _(i):
-        for copy in state_copies(i, step, 0, outs, news, sems, False):
-            copy.wait()
-
-
-def settle(blocks, arrived, given, hidden, weight, held, shapes):
+            copies.append(copy)
+    for i in range(size):
+        proj = times_weight(rows_refs[i], weight_ref)
+        projs[i][...] = proj
+        copies.append(pltpu.make_async_copy(projs[i], projs_hbm[i], proj_sems.at[i]))
+        copies[-1].start()
+        scores[i][...] = score_block(
+            blocks, proj, hidden[i][...], [block_index(blocks, count)]
+        )[0]
+    for copy in copies:
+        copy.wait()
+
+
+def settle(blocks, arrived, given, hidden, hidden_t, weight, held, shapes):
     part, cols = weight.shape
     count = blocks * SEND
     fresh = tuple(range(1, 1 + len(arrived)))
     size = len(fresh)
     total = count * (1 + size)
-    step = min(part, 64)
-    args = [*arrived, *hidden, given, weight, *held]
-    near = [plain((blocks, 1, LANE), f32)] * size + [plain((count, part), bf16)] * size
-    near.append(plain((total, part), bf16))
-    far = [out_hbm(array.shape, array.dtype) for array in shapes]
+    step = min(part, 128)
+    args = [*arrived, *hidden, hidden_t, given, weight, *held]
+    near = [plain((blocks, 1, LANE), f32)] * size
+    far = [out_hbm((count, part), f32)] * size
+    far += [out_hbm(array.shape, array.dtype) for array in shapes]
     scratch = [pltpu.VMEM((part, cols), kind) for kind in (f32, bf16, bf16)]
     scratch += [pltpu.VMEM((count, cols), bf16)] * size
+    scratch += [pltpu.VMEM((count, part), f32)] * size
     scratch += [
-        pltpu.VMEM((part, total), bf16),
         pltpu.VMEM((part, cols), f32),
         pltpu.SemaphoreType.DMA((3, part // step)),
+        pltpu.SemaphoreType.DMA((max(1, size),)),
     ]
     nbytes = 12 * part * cols + 4 * total * cols + 8 * total * part
     outs = pl.pallas_call(
@@ -546,7 +588,7 @@
         cost_estimate=cost(4 * total * part * cols, 16 * part * cols, part * cols),
     )(*args)
     outs = list(outs)
-    return outs[:size], outs[2 * size], outs[size : 2 * size], outs[-3:]
+    return outs[:size], outs[size : 2 * size], outs[-3:]
 
 
 def update_kernel(low, shards, hidden_ref, rows_ref, *refs):
@@ -571,43 +613,41 @@
         for copy in state_copies(i, step, low, state_hbm, state, in_sems, True):
             copy.start()
     transpose_rows([hidden_ref], hidden_t)
-    form_grad(hidden_t, [rows_ref], grad_ref)
-    for copy in token_loads:
-        copy.wait()
-    ids, slots = tokens[0][...], tokens[1][...]
-    live = ((ids & (EXP_LOCAL - 1)) == 0) & (slots >= 0)
-    place_ref[...] = jnp.where(live, ids // EXP_LOCAL * SEND + slots, -1)
-    inverse_ref[...] = 1.0 / tokens[2][...].astype(f32)
-    gate_load.wait()
-    for s, ref in enumerate(grad_refs):
-        first, second, gate, up, sig = swiglu_part(gate_up_ref, shards, s, ref.shape[1])
-        grad = ref[...].astype(f32)
-        gate_new[:, pl.ds(first, ref.shape[1])] = (
-            grad * up * sig * (1.0 + gate * (1.0 - sig))
-        ).astype(bf16)
-        gate_new[:, pl.ds(second, ref.shape[1])] = (grad * (gate * sig)).astype(bf16)
-    gate_store.start()
-
-    @pl.loop(0, steps)
-    def _(i):
+    stores = []
+    for i in range(steps):
+        if i == min(1, steps - 1):
+            for copy in token_loads:
+                copy.wait()
+            ids, slots = tokens[0][...], tokens[1][...]
+            live = ((ids & (EXP_LOCAL - 1)) == 0) & (slots >= 0)
+            place_ref[...] = jnp.where(live, ids // EXP_LOCAL * SEND + slots, -1)
+            inverse_ref[...] = 1.0 / tokens[2][...].astype(f32)
+            gate_load.wait()
+            for s, ref in enumerate(grad_refs):
+                width = ref.shape[1]
+                first, second, gate, up, sig = swiglu_part(gate_up_ref, shards, s, width)
+                grad = ref[...].astype(f32)
+                gate_new[:, pl.ds(first, width)] = (
+                    grad * up * sig * (1.0 + gate * (1.0 - sig))
+                ).astype(bf16)
+                gate_new[:, pl.ds(second, width)] = (grad * (gate * sig)).astype(bf16)
+            gate_store.start()
+            stores.append(gate_store)
+        form_grad(i * step, step, hidden_t, [rows_ref], grad_ref)
         for copy in state_copies(i, step, low, state_hbm, state, in_sems, True):
             copy.wait()
         update_rows(i * step, step, state, state, grad_ref)
         for copy in state_copies(i, step, low, outs, state, out_sems, False):
             copy.start()
-
-    @pl.loop(0, steps)
-    def _(i):
-        for copy in state_copies(i, step, low, outs, state, out_sems, False):
-            copy.wait()
-
-    gate_store.wait()
+            stores.append(copy)
+    for copy in stores:
+        copy.wait()
 
 
 def update(low, hidden, rows, grads, gate_up, state, tokens, done):
     total, part = hidden.shape
     cols = rows.shape[1]
-    step = min(part, 64)
+    step = min(part, 128)
     shards = len(grads)
     scratch = [pltpu.VMEM((part, cols), kind) for kind in (f32, bf16, bf16)]
     scratch += [pltpu.VMEM(token.shape, token.dtype) for token in tokens]
@@ -681,9 +721,9 @@
 
     peers = [shift(arrived, s) for s in steps]
     *held, weight_a, weight_b = load_state(edges[1], *state, arrived)
-    rows, proj, score_own = begin(ep_size, arrived, weight_a, hidden[0])
-    scores, hidden_mixed, before, done = settle(
-        ep_size, peers, rows, hidden, weight_a, held, state
+    rows, hidden_t, hidden_mixed, score_own, proj = begin(ep_size, arrived, weight_a, hidden)
+    scores, before, done = settle(
+        ep_size, peers, rows, hidden[1:], hidden_t, weight_a, held, state
     )
     projs, score = finish(
         ep_size, arrived_b, hidden_mixed, weight_b, [proj] + before, [score_own] + scores

time: 86.3 us -> 86.4 us (level)
  Pallas kernels: 30.9 us -> 32.6 us
  local copies, waits for them, and re-layouts: 2.98 us -> 1.41 us
    unnamed x16 -> x4, local copies, waits for them, and re-layouts: 2.98 us -> 1.41 us
  transfers between devices with their start and end apart: 7 -> 7, of which waited for: 4 -> 4; matrix products, arithmetic and copies ran while one was open for 0% -> 0% of each run, Pallas kernels for 28% -> 30%
where the time goes in v11:
time: 86.4 us; the launch traced here: 86 us
  Pallas kernels  32.6 us (38%)
  waiting for transfers between devices  27.3 us (32%)
  starting transfers between devices  23.9 us (28%)
  local copies, waits for them, and re-layouts  1.41 us (2%)
    ppermute x4, waiting for transfers between devices, shift(): return lax.ppermute(value, 'rep', perm)  27.3 us
    all_to_all x2, starting transfers between devices, exchange(): return lax.all_to_all(value, 'ep', split_axis=0, concat_axis=0, tiled=True)  12.9 us
    pallas_call x1, Pallas kernels, update(): pl.pallas_call(functools.partial(update_kernel, low, shards), in_specs=[V...  8.04 us
    pallas_call x1, Pallas kernels, settle(): pl.pallas_call(functools.partial(settle_kernel, fresh, blocks), in_specs=...  7.68 us
    ppermute x4, starting transfers between devices, shift(): return lax.ppermute(value, 'rep', perm)  6.27 us
    all_to_all x1, starting transfers between devices, per_device(): lax.all_to_all(score, ('rep', 'ep'), split_axis=0, concat_axis=0, tiled=T...  4.74 us
    pallas_call x1, Pallas kernels, load_state(): pl.pallas_call(functools.partial(load_kernel, middle), in_specs=[ANY] + [...  4.47 us
    pallas_call x1, Pallas kernels, dispatch(): pl.pallas_call(functools.partial(dispatch_kernel, edges), in_specs=[HBM]...  3.26 us
  transfers between devices with their start and end apart: 7, of which 4 were waited for; matrix products, arithmetic and copies ran while one was open for 0% of the time, Pallas kernels for 30%

profile of v11, /device:TPU:0, one launch (start us, length us, event | category | flops | bytes accessed | tf_op | source)
XLA Modules:
  0.0 86.0 jit_solution(17862925655662032964)
XLA Ops:
  0.6 3.3 %shard_map.119 = (bf16[256,1536]{1,0:T(8,128)(2,1)}, bf16[256,1152]{1,0:T(8,128)(2,1)S(1)}) custom-call(s32[8,256]{1,0:T(8,128)} %bitcast.18, s32[8,256]{1,0:T(8,128)} %bitcast.20, bf16[8,256]{1,0:T(8,128)(2,1)} %bitcast.22, bf16[256,3584]{1,0:T(8,128)(2,1)} %grad_hbm.1), custom_call_target="tpu_custom_call" | custom-call | flops 469762048 | bytes 3670016 | tf_op jit(solution)/shard_map/pallas_call | solution.py:135
  3.9 7.4 %all-to-all-start = ((bf16[16,16,1536]{2,1,0:T(8,128)(2,1)}), bf16[16,16,1536]{2,1,0:T(8,128)(2,1)S(1)}, u32[]{:S(2)}, u32[]{:S(2)}) async-start(bf16[16,16,1536]{2,1,0:T(8,128)(2,1)} %bitcast.3), calls=%async_computation | async-start | bytes 1572864 | tf_op jit(solution)/shard_map/all_to_all | solution.py:710
  11.3 1.6 %collective-permute-start = (bf16[256,1152]{1,0:T(8,128)(2,1)S(1)}, bf16[256,1152]{1,0:T(8,128)(2,1)S(1)}, u32[]{:S(2)}, u32[]{:S(2)}) collective-permute-start(bf16[256,1152]{1,0:T(8,128)(2,1)S(1)} %get-tuple-element.39.after_ref.refs_0_), channel_id=1, source_target_pairs={{0,16},{16,0},{1,17},{17,1},{2,18},{18,2},{3,19},{19,3},{4,20},{20... | collective-permute-start | bytes 1769480 | tf_op jit(solution)/shard_map/ppermute | solution.py:707
  12.9 1.3 %shard_map.121 = (bf16[192,512]{1,0:T(8,128)(2,1)S(1)}, bf16[192,512]{1,0:T(8,128)(2,1)S(1)}) custom-call(bf16[192,2048]{1,0:T(8,128)(2,1)} %bitcast.16, bf16[256,1152]{1,0:T(8,128)(2,1)S(1)} %get-tuple-element.39.after_ref.refs_0_), custom_call_target="tpu_custom_call" | custom-call | flops 3145728 | bytes 1179648 | tf_op jit(solution)/shard_map/pallas_call | solution.py:171
  14.2 12.8 %collective-permute-done.refs_1_ = bf16[256,1152]{1,0:T(8,128)(2,1)S(1)} collective-permute-done((bf16[256,1152]{1,0:T(8,128)(2,1)S(1)}, bf16[256,1152]{1,0:T(8,128)(2,1)S(1)}, u32[]{:S(2)}, u32[]{:S(2)}) %collective-permute-start) | collective-permute-done | bytes 589856 | tf_op jit(solution)/shard_map/ppermute | solution.py:707
  26.9 1.5 %collective-permute-start.1 = (bf16[192,512]{1,0:T(8,128)(2,1)S(1)}, bf16[192,512]{1,0:T(8,128)(2,1)S(1)}, u32[]{:S(2)}, u32[]{:S(2)}) collective-permute-start(bf16[192,512]{1,0:T(8,128)(2,1)S(1)} %get-tuple-element.42), channel_id=1, source_target_pairs={{0,16},{16,0},{1,17},{17,1},{2,18},{18,2},{3,19},{19,3},{4,20},{20... | collective-permute-start | bytes 589832 | tf_op jit(solution)/shard_map/ppermute | solution.py:707
  28.4 2.2 %shard_map.122 = bf16[384,1536]{1,0:T(8,128)(2,1)} custom-call(bf16[256,1152]{1,0:T(8,128)(2,1)S(1)} %get-tuple-element.39.after_ref.refs_0_, bf16[256,1152]{1,0:T(8,128)(2,1)S(1)} %collective-permute-done.refs_1_), custom_call_target="tpu_custom_call" | custom-call | bytes 2949120 | tf_op jit(solution)/shard_map/pallas_call | solution.py:301
  30.6 2.6 %collective-permute-done.1.refs_1_ = bf16[192,512]{1,0:T(8,128)(2,1)S(1)} collective-permute-done((bf16[192,512]{1,0:T(8,128)(2,1)S(1)}, bf16[192,512]{1,0:T(8,128)(2,1)S(1)}, u32[]{:S(2)}, u32[]{:S(2)}) %collective-permute-start.1) | collective-permute-done | bytes 196640 | tf_op jit(solution)/shard_map/ppermute | solution.py:707
  33.3 0.0 all-to-all-done
  33.3 5.5 %all-to-all-start.1 = ((bf16[16,24,1536]{2,1,0:T(8,128)(2,1)}), bf16[16,24,1536]{2,1,0:T(8,128)(2,1)S(1)}, u32[]{:S(2)}, u32[]{:S(2)}) async-start(bf16[16,24,1536]{2,1,0:T(8,128)(2,1)} %bitcast.15), calls=%async_computation.1 | async-start | bytes 2359296 | tf_op jit(solution)/shard_map/all_to_all | solution.py:710
  38.8 1.6 %collective-permute-start.2 = (bf16[256,1536]{1,0:T(8,128)(2,1)S(1)}, bf16[256,1536]{1,0:T(8,128)(2,1)S(1)}, u32[]{:S(2)}, u32[]{:S(2)}) collective-permute-start(bf16[256,1536]{1,0:T(8,128)(2,1)S(1)} %bitcast.12), channel_id=1, source_target_pairs={{0,16},{16,0},{1,17},{17,1},{2,18},{18,2},{3,19},{19,3},{4,20},{20... | collective-permute-start | bytes 2359304 | tf_op jit(solution)/shard_map/ppermute | solution.py:707
  40.4 4.5 %shard_map.120 = (f32[512,2048]{1,0:T(8,128)S(1)}, bf16[512,2048]{1,0:T(8,128)(2,1)S(1)}, bf16[512,2048]{1,0:T(8,128)(2,1)S(1)}, bf16[512,2048]{1,0:T(8,128)(2,1)S(1)}, bf16[512,1536]{1,0:T(8,128)(2,1)S(1)}) custom-call(bf16[256,1536]{1,0:T(8,128)(2,1)S(1)} %bitcast.13, f32[1,512,3584]{2,1,0:T(8,128)} %refs_3_.1, bf16[1,512,3584]{2,1,0:T(8,128)(2,1)} %refs_4_.1, ...), custom_call_target="tpu_custom_call" | custom-call | flops 1835008 | bytes 25690112 | tf_op jit(solution)/shard_map/pallas_call | solution.py:223
  44.9 0.0 copy-start
  44.9 1.9 %shard_map.123 = (bf16[192,2048]{1,0:T(8,128)(2,1)S(1)}, bf16[512,384]{1,0:T(8,128)(2,1)S(1)}, bf16[384,512]{1,0:T(8,128)(2,1)S(1)}, f32[16,1,128]{2,1,0:T(1,128)S(1)}, f32[192,512]{1,0:T(8,128)}) custom-call(bf16[256,1536]{1,0:T(8,128)(2,1)S(1)} %bitcast.14, bf16[512,2048]{1,0:T(8,128)(2,1)S(1)} %get-tuple-element.38.weight_ref.refs_4_, ...), custom_call_target="tpu_custom_call" | custom-call | flops 805306368 | bytes 2097152 | tf_op jit(solution)/shard_map/pallas_call | solution.py:392
  46.8 11.9 %collective-permute-done.2.refs_0_ = bf16[256,1536]{1,0:T(8,128)(2,1)S(1)} collective-permute-done((bf16[256,1536]{1,0:T(8,128)(2,1)S(1)}, bf16[256,1536]{1,0:T(8,128)(2,1)S(1)}, u32[]{:S(2)}, u32[]{:S(2)}) %collective-permute-start.2) | collective-permute-done | bytes 786464 | tf_op jit(solution)/shard_map/ppermute | solution.py:707
  58.7 0.0 copy-done
  58.7 7.7 %shard_map.124 = (f32[16,1,128]{2,1,0:T(1,128)S(1)}, f32[192,512]{1,0:T(8,128)}, f32[1,512,3584]{2,1,0:T(8,128)}, bf16[1,512,3584]{2,1,0:T(8,128)(2,1)}, bf16[1,512,3584]{2,1,0:T(8,128)(2,1)}) custom-call(bf16[256,1536]{1,0:T(8,128)(2,1)S(1)} %collective-permute-done.2.refs_0_, bf16[192,512]{1,0:T(8,128)(2,1)S(1)} %collective-permute-done.1.refs_1_, ...), custom_call_target="tpu_custom_call" | custom-call | flops 1610612736 | bytes 16777216 | tf_op jit(solution)/shard_map/pallas_call | solution.py:581
  66.4 0.0 all-to-all-done.1
  66.4 0.0 copy-start.1
  66.4 1.4 %copy-done.1 = bf16[512,1536]{1,0:T(8,128)(2,1)S(1)} copy-done((bf16[512,1536]{1,0:T(8,128)(2,1)S(1)}, bf16[512,1536]{1,0:T(8,128)(2,1)}, u32[]{:S(2)}) %copy-start.1) | copy-done | bytes 1572888
  67.8 2.2 %shard_map.125 = (bf16[192,512]{1,0:T(8,128)(2,1)S(1)}, bf16[192,512]{1,0:T(8,128)(2,1)S(1)}, f32[32,1,128]{2,1,0:T(1,128)}) custom-call(bf16[384,1536]{1,0:T(8,128)(2,1)S(1)} %bitcast.10, bf16[384,512]{1,0:T(8,128)(2,1)S(1)} %get-tuple-element.45.hidden_ref, bf16[512,1536]{1,0:T(8,128)(2,1)S(1)} %copy-done.1, f32[192,512]{1,0:T(8,128)} %get-tuple-element.48.refs_0_, ...), custom_call_target="tpu_custom_call" | custom-call | flops 603979776 | bytes 1572864 | tf_op jit(solution)/shard_map/pallas_call | solution.py:443
  70.0 1.6 %collective-permute-start.3 = (bf16[192,512]{1,0:T(8,128)(2,1)S(1)}, bf16[192,512]{1,0:T(8,128)(2,1)S(1)}, u32[]{:S(2)}, u32[]{:S(2)}) collective-permute-start(bf16[192,512]{1,0:T(8,128)(2,1)S(1)} %get-tuple-element.58), channel_id=1, source_target_pairs={{0,16},{16,0},{1,17},{17,1},{2,18},{18,2},{3,19},{19,3},{4,20},{20... | collective-permute-start | bytes 589832 | tf_op jit(solution)/shard_map/ppermute | solution.py:707
  71.6 4.7 %all-to-all-start.2 = ((f32[32,1,128]{2,1,0:T(1,128)}), f32[32,1,128]{2,1,0:T(1,128)S(1)}, u32[]{:S(2)}, u32[]{:S(2)}) async-start(f32[32,1,128]{2,1,0:T(1,128)} %get-tuple-element.65), calls=%async_computation.2 | async-start | bytes 32768 | tf_op jit(solution)/shard_map/all_to_all | solution.py:732
  76.3 0.1 collective-permute-done.3.refs_1_
  76.4 8.0 %shard_map.126 = (f32[1,512,3584]{2,1,0:T(8,128)}, bf16[1,512,3584]{2,1,0:T(8,128)(2,1)}, bf16[1,512,3584]{2,1,0:T(8,128)(2,1)}, bf16[192,2048]{1,0:T(8,128)(2,1...) custom-call(bf16[384,512]{1,0:T(8,128)(2,1)S(1)} %get-tuple-element., ...), custom_call_target="tpu_custom_call", output_to_operand_aliasing={{0}: (11, {}), {1}: (12, {}), {2}: (13, {})} | custom-call | flops 603979776 | bytes 12582912 | tf_op jit(solution)/shard_map/pallas_call | solution.py:658
  84.4 0.0 all-to-all-done.2.score_ref
  84.5 1.6 %shard_map.127 = f32[8,256]{1,0:T(8,128)} custom-call(s32[8,256]{1,0:T(8,128)S(1)} %get-tuple-element.63.place_ref, f32[8,256]{1,0:T(8,128)S(1)} %get-tuple-element.64.inverse_ref, f32[32,1,128]{2,1,0:T(1,128)S(1)} %all-to-all-done.2.score_ref), custom_call_target="tpu_custom_call" | custom-call | flops 1048576 | bytes 65536 | tf_op jit(solution)/shard_map/pallas_call | solution.py:686
Async XLA Ops:
  3.9 29.4 %all-to-all-start = ((bf16[16,16,1536]{2,1,0:T(8,128)(2,1)}), bf16[16,16,1536]{2,1,0:T(8,128)(2,1)S(1)}, u32[]{:S(2)}, u32[]{:S(2)}) async-start(bf16[16,16,1536]{2,1,0:T(8,128)(2,1)} %bitcast.3), calls=%async_computation | async-start | bytes 1572864 | tf_op jit(solution)/shard_map/all_to_all | solution.py:710
  11.3 15.6 %collective-permute-start = (bf16[256,1152]{1,0:T(8,128)(2,1)S(1)}, bf16[256,1152]{1,0:T(8,128)(2,1)S(1)}, u32[]{:S(2)}, u32[]{:S(2)}) collective-permute-start(bf16[256,1152]{1,0:T(8,128)(2,1)S(1)} %get-tuple-element.39.after_ref.refs_0_), channel_id=1, source_target_pairs={{0,16},{16,0},{1,17},{17,1},{2,18},{18,2},{3,19},{19,3},{4,20},{20... | collective-permute-start | bytes 1769480 | tf_op jit(solution)/shard_map/ppermute | solution.py:707
  26.9 6.4 %collective-permute-start.1 = (bf16[192,512]{1,0:T(8,128)(2,1)S(1)}, bf16[192,512]{1,0:T(8,128)(2,1)S(1)}, u32[]{:S(2)}, u32[]{:S(2)}) collective-permute-start(bf16[192,512]{1,0:T(8,128)(2,1)S(1)} %get-tuple-element.42), channel_id=1, source_target_pairs={{0,16},{16,0},{1,17},{17,1},{2,18},{18,2},{3,19},{19,3},{4,20},{20... | collective-permute-start | bytes 589832 | tf_op jit(solution)/shard_map/ppermute | solution.py:707
  33.3 33.1 %all-to-all-start.1 = ((bf16[16,24,1536]{2,1,0:T(8,128)(2,1)}), bf16[16,24,1536]{2,1,0:T(8,128)(2,1)S(1)}, u32[]{:S(2)}, u32[]{:S(2)}) async-start(bf16[16,24,1536]{2,1,0:T(8,128)(2,1)} %bitcast.15), calls=%async_computation.1 | async-start | bytes 2359296 | tf_op jit(solution)/shard_map/all_to_all | solution.py:710
  38.8 19.9 %collective-permute-start.2 = (bf16[256,1536]{1,0:T(8,128)(2,1)S(1)}, bf16[256,1536]{1,0:T(8,128)(2,1)S(1)}, u32[]{:S(2)}, u32[]{:S(2)}) collective-permute-start(bf16[256,1536]{1,0:T(8,128)(2,1)S(1)} %bitcast.12), channel_id=1, source_target_pairs={{0,16},{16,0},{1,17},{17,1},{2,18},{18,2},{3,19},{19,3},{4,20},{20... | collective-permute-start | bytes 2359304 | tf_op jit(solution)/shard_map/ppermute | solution.py:707
  44.9 13.8 %copy-start = (bf16[512,1536]{1,0:T(8,128)(2,1)}, bf16[512,1536]{1,0:T(8,128)(2,1)S(1)}, u32[]{:S(2)}) copy-start(bf16[512,1536]{1,0:T(8,128)(2,1)S(1)} %get-tuple-element.47.weight_ref) | copy-start | bytes 4718596
  66.4 1.4 %copy-start.1 = (bf16[512,1536]{1,0:T(8,128)(2,1)S(1)}, bf16[512,1536]{1,0:T(8,128)(2,1)}, u32[]{:S(2)}) copy-start(bf16[512,1536]{1,0:T(8,128)(2,1)} %copy-done) | copy-start | bytes 4718596
  70.0 6.4 %collective-permute-start.3 = (bf16[192,512]{1,0:T(8,128)(2,1)S(1)}, bf16[192,512]{1,0:T(8,128)(2,1)S(1)}, u32[]{:S(2)}, u32[]{:S(2)}) collective-permute-start(bf16[192,512]{1,0:T(8,128)(2,1)S(1)} %get-tuple-element.58), channel_id=1, source_target_pairs={{0,16},{16,0},{1,17},{17,1},{2,18},{18,2},{3,19},{19,3},{4,20},{20... | collective-permute-start | bytes 589832 | tf_op jit(solution)/shard_map/ppermute | solution.py:707
  71.6 12.9 %all-to-all-start.2 = ((f32[32,1,128]{2,1,0:T(1,128)}), f32[32,1,128]{2,1,0:T(1,128)S(1)}, u32[]{:S(2)}, u32[]{:S(2)}) async-start(f32[32,1,128]{2,1,0:T(1,128)} %get-tuple-element.65), calls=%async_computation.2 | async-start | bytes 32768 | tf_op jit(solution)/shard_map/all_to_all | solution.py:732

commit v12 on v11

--- a/solution.py
+++ b/solution.py
@@ -360,7 +360,7 @@
 
 
 def begin_kernel(blocks, arrived_ref, weight_ref, *refs):
-    hidden, (rows_ref, hidden_t, mixed_ref, score_ref) = refs[:-7], refs[-7:-3]
+    hidden, (rows_ref, hidden_t, score_ref) = refs[:-6], refs[-6:-3]
     proj_hbm, proj_ref, sem = refs[-3:]
     reorder(arrived_ref[...], rows_ref)
     proj = times_weight(rows_ref, weight_ref)
@@ -372,16 +372,6 @@
         blocks, proj, hidden[0][...], [block_index(blocks, count)]
     )[0]
     transpose_rows(hidden, hidden_t)
-    shards = len(hidden)
-    row = lax.broadcasted_iota(jnp.int32, (shards * count, count), 0)
-    col = lax.broadcasted_iota(jnp.int32, (shards * count, count), 1)
-    at, step_of, slot = mixed_place(row, shards)
-    total = 0.0
-    for s in range(shards):
-        order = (step_of == s) & (col == at * SEND + slot)
-        order = jnp.where(order, 1.0, 0.0).astype(bf16)
-        total += jnp.dot(order, hidden[s][...], preferred_element_type=f32)
-    mixed_ref[...] = total.astype(bf16)
     copy.wait()
 
 
@@ -392,11 +382,10 @@
     return pl.pallas_call(
         functools.partial(begin_kernel, blocks),
         in_specs=[VMEM] * (2 + len(hidden)),
-        out_specs=[VMEM] * 4 + [HBM],
+        out_specs=[VMEM] * 3 + [HBM],
         out_shape=[
             plain((count, cols), bf16),
             plain((part, total), bf16),
-            plain((total, part), bf16),
             plain((blocks, 1, LANE), f32),
             out_hbm((count, part), f32),
         ],
@@ -492,20 +481,18 @@
         base = high
 
 
-def form_grad(first, count, hidden_t, rows_refs, grad_ref):
-    own = slice(first, first + count)
+def form_grad(hidden_t, rows_refs, grad_ref):
     for low in range(0, grad_ref.shape[1], UNIT):
+        own = slice(low, low + UNIT)
         base = 0
         grad = 0.0
         for rows_ref in rows_refs:
             high = base + rows_ref.shape[0]
             grad += jnp.dot(
-                hidden_t[own, base:high],
-                rows_ref[:, low : low + UNIT],
-                preferred_element_type=f32,
+                hidden_t[:, base:high], rows_ref[:, own], preferred_element_type=f32
             )
             base = high
-        grad_ref[own, low : low + UNIT] = grad
+        grad_ref[:, own] = grad
 
 
 def state_copies(i, step, low, hbm, vmem, sems, into):
@@ -528,32 +515,50 @@
         return out
 
     size = len(fresh)
-    arrived, hidden = take(size), take(size)
+    arrived, hidden = take(size), take(1 + size)
     hidden_t, given_ref, weight_ref, *state = take(6)
-    scores, projs_hbm, outs = take(size), take(size), take(3)
+    scores, (mixed_ref,), projs_hbm, outs = take(size), take(1), take(size), take(3)
     news, rows_refs, projs = take(3), take(size), take(size)
     grad_ref, sems, proj_sems = refs
     part = grad_ref.shape[0]
     count = blocks * SEND
+    shards = 1 + size
     for i in range(size):
         reorder(arrived[i][...], rows_refs[i])
+    form_grad(hidden_t, [given_ref] + rows_refs, grad_ref)
     steps = sems.shape[1]
     step = part // steps
-    copies = []
-    for i in range(steps):
-        form_grad(i * step, step, hidden_t, [given_ref] + rows_refs, grad_ref)
+
+    @pl.loop(0, steps)
+    def _(i):
         update_rows(i * step, step, state, news, grad_ref)
         for copy in state_copies(i, step, 0, outs, news, sems, False):
             copy.start()
-            copies.append(copy)
-    for i in range(size):
+
+    copies = []
+    for i, s in enumerate(fresh):
         proj = times_weight(rows_refs[i], weight_ref)
         projs[i][...] = proj
         copies.append(pltpu.make_async_copy(projs[i], projs_hbm[i], proj_sems.at[i]))
-        copies[-1].start()
+        copies[i].start()
         scores[i][...] = score_block(
-            blocks, proj, hidden[i][...], [block_index(blocks, count)]
+            blocks, proj, hidden[s][...], [block_index(blocks, count)]
         )[0]
+    row = lax.broadcasted_iota(jnp.int32, (shards * count, count), 0)
+    col = lax.broadcasted_iota(jnp.int32, (shards * count, count), 1)
+    at, step_of, slot = mixed_place(row, shards)
+    total = 0.0
+    for s in range(shards):
+        order = (step_of == s) & (col == at * SEND + slot)
+        order = jnp.where(order, 1.0, 0.0).astype(bf16)
+        total += jnp.dot(order, hidden[s][...], preferred_element_type=f32)
+    mixed_ref[...] = total.astype(bf16)
+
+    @pl.loop(0, steps)
+    def _(i):
+        for copy in state_copies(i, step, 0, outs, news, sems, False):
+            copy.wait()
+
     for copy in copies:
         copy.wait()
 
@@ -564,9 +569,9 @@
     fresh = tuple(range(1, 1 + len(arrived)))
     size = len(fresh)
     total = count * (1 + size)
-    step = min(part, 128)
+    step = min(part, 64)
     args = [*arrived, *hidden, hidden_t, given, weight, *held]
-    near = [plain((blocks, 1, LANE), f32)] * size
+    near = [plain((blocks, 1, LANE), f32)] * size + [plain((total, part), bf16)]
     far = [out_hbm((count, part), f32)] * size
     far += [out_hbm(array.shape, array.dtype) for array in shapes]
     scratch = [pltpu.VMEM((part, cols), kind) for kind in (f32, bf16, bf16)]
@@ -588,7 +593,7 @@
         cost_estimate=cost(4 * total * part * cols, 16 * part * cols, part * cols),
     )(*args)
     outs = list(outs)
-    return outs[:size], outs[size : 2 * size], outs[-3:]
+    return outs[:size], outs[size], outs[size + 1 : -3], outs[-3:]
 
 
 def update_kernel(low, shards, hidden_ref, rows_ref, *refs):
@@ -613,41 +618,45 @@
         for copy in state_copies(i, step, low, state_hbm, state, in_sems, True):
             copy.start()
     transpose_rows([hidden_ref], hidden_t)
-    stores = []
-    for i in range(steps):
-        if i == min(1, steps - 1):
-            for copy in token_loads:
-                copy.wait()
-            ids, slots = tokens[0][...], tokens[1][...]
-            live = ((ids & (EXP_LOCAL - 1)) == 0) & (slots >= 0)
-            place_ref[...] = jnp.where(live, ids // EXP_LOCAL * SEND + slots, -1)
-            inverse_ref[...] = 1.0 / tokens[2][...].astype(f32)
-            gate_load.wait()
-            for s, ref in enumerate(grad_refs):
-                width = ref.shape[1]
-                first, second, gate, up, sig = swiglu_part(gate_up_ref, shards, s, width)
-                grad = ref[...].astype(f32)
-                gate_new[:, pl.ds(first, width)] = (
-                    grad * up * sig * (1.0 + gate * (1.0 - sig))
-                ).astype(bf16)
-                gate_new[:, pl.ds(second, width)] = (grad * (gate * sig)).astype(bf16)
-            gate_store.start()
-            stores.append(gate_store)
-        form_grad(i * step, step, hidden_t, [rows_ref], grad_ref)
+    form_grad(hidden_t, [rows_ref], grad_ref)
+    for copy in token_loads:
+        copy.wait()
+    ids, slots = tokens[0][...], tokens[1][...]
+    live = ((ids & (EXP_LOCAL - 1)) == 0) & (slots >= 0)
+    place_ref[...] = jnp.where(live, ids // EXP_LOCAL * SEND + slots, -1)
+    inverse_ref[...] = 1.0 / tokens[2][...].astype(f32)
+
+    @pl.loop(0, steps)
+    def _(i):
         for copy in state_copies(i, step, low, state_hbm, state, in_sems, True):
             copy.wait()
         update_rows(i * step, step, state, state, grad_ref)
         for copy in state_copies(i, step, low, outs, state, out_sems, False):
             copy.start()
-            stores.append(copy)
-    for copy in stores:
-        copy.wait()
+
+    gate_load.wait()
+    for s, ref in enumerate(grad_refs):
+        width = ref.shape[1]
+        first, second, gate, up, sig = swiglu_part(gate_up_ref, shards, s, width)
+        grad = ref[...].astype(f32)
+        gate_new[:, pl.ds(first, width)] = (
+            grad * up * sig * (1.0 + gate * (1.0 - sig))
+        ).astype(bf16)
+        gate_new[:, pl.ds(second, width)] = (grad * (gate * sig)).astype(bf16)
+    gate_store.start()
+
+    @pl.loop(0, steps)
+    def _(i):
+        for copy in state_copies(i, step, low, outs, state, out_sems, False):
+            copy.wait()
+
+    gate_store.wait()
 
 
 def update(low, hidden, rows, grads, gate_up, state, tokens, done):
     total, part = hidden.shape
     cols = rows.shape[1]
-    step = min(part, 128)
+    step = min(part, 64)
     shards = len(grads)
     scratch = [pltpu.VMEM((part, cols), kind) for kind in (f32, bf16, bf16)]
     scratch += [pltpu.VMEM(token.shape, token.dtype) for token in tokens]
@@ -713,7 +722,6 @@
     mixed = [shift(send_b, s) for s in steps]
     parts = list(hidden_parts(gate_up, rep_size, send_b))
     arrived = exchange(send_a.reshape(ep_size, ROWS, -1)).reshape(send_a.shape)
-    parts[1:], mixed = lax.optimization_barrier((parts[1:], mixed))
     hidden = [parts[0]] + [shift(parts[s], s) for s in steps]
     mixed = mix([send_b] + mixed)
     hidden[1:], mixed = lax.optimization_barrier((hidden[1:], mixed))
@@ -721,9 +729,9 @@
 
     peers = [shift(arrived, s) for s in steps]
     *held, weight_a, weight_b = load_state(edges[1], *state, arrived)
-    rows, hidden_t, hidden_mixed, score_own, proj = begin(ep_size, arrived, weight_a, hidden)
-    scores, before, done = settle(
-        ep_size, peers, rows, hidden[1:], hidden_t, weight_a, held, state
+    rows, hidden_t, score_own, proj = begin(ep_size, arrived, weight_a, hidden)
+    scores, hidden_mixed, before, done = settle(
+        ep_size, peers, rows, hidden, hidden_t, weight_a, held, state
     )
     projs, score = finish(
         ep_size, arrived_b, hidden_mixed, weight_b, [proj] + before, [score_own] + scores

time: 86.4 us -> 83.6 us (0.968)
  Pallas kernels: 32.6 us -> 31.4 us
  waiting for transfers between devices: 27.3 us -> 26.1 us
    ppermute x4, waiting for transfers between devices: 27.3 us -> 26.1 us  [shift(): return lax.ppermute(value, 'rep', perm)]
    pallas_call x1, Pallas kernels: 7.68 us -> 6.51 us  [settle(): pl.pallas_call(functools.partial(settle_kernel, fresh, blocks), in_specs=...]
    ppermute x4, starting transfers between devices: 6.27 us -> 5.33 us  [shift(): return lax.ppermute(value, 'rep', perm)]
  transfers between devices with their start and end apart: 7 -> 7, of which waited for: 4 -> 3; matrix products, arithmetic and copies ran while one was open for 0% -> 0% of each run, Pallas kernels for 30% -> 29%
where the time goes in v12:
time: 83.6 us; the launch traced here: 82.6 us
  Pallas kernels  31.4 us (38%)
  waiting for transfers between devices  26.1 us (31%)
  starting transfers between devices  23.5 us (28%)
    ppermute x4, waiting for transfers between devices, shift(): return lax.ppermute(value, 'rep', perm)  26.1 us
    all_to_all x2, starting transfers between devices, exchange(): return lax.all_to_all(value, 'ep', split_axis=0, concat_axis=0, tiled=True)  13.1 us
    pallas_call x1, Pallas kernels, update(): pl.pallas_call(functools.partial(update_kernel, low, shards), in_specs=[V...  7.78 us
    pallas_call x1, Pallas kernels, settle(): pl.pallas_call(functools.partial(settle_kernel, fresh, blocks), in_specs=...  6.51 us
    ppermute x4, starting transfers between devices, shift(): return lax.ppermute(value, 'rep', perm)  5.33 us
    all_to_all x1, starting transfers between devices, per_device(): lax.all_to_all(score, ('rep', 'ep'), split_axis=0, concat_axis=0, tiled=T...  5.1 us
    pallas_call x1, Pallas kernels, load_state(): pl.pallas_call(functools.partial(load_kernel, middle), in_specs=[ANY] + [...  4.47 us
    pallas_call x1, Pallas kernels, dispatch(): pl.pallas_call(functools.partial(dispatch_kernel, edges), in_specs=[HBM]...  3.26 us
  transfers between devices with their start and end apart: 7, of which 3 were waited for; matrix products, arithmetic and copies ran while one was open for 0% of the time, Pallas kernels for 29%

profile of v12, /device:TPU:0, one launch (start us, length us, event | category | flops | bytes accessed | tf_op | source)
XLA Modules:
  0.0 82.6 jit_solution(5780245331687606920)
XLA Ops:
  0.6 3.3 %shard_map.119 = (bf16[256,1536]{1,0:T(8,128)(2,1)}, bf16[256,1152]{1,0:T(8,128)(2,1)S(1)}) custom-call(s32[8,256]{1,0:T(8,128)} %bitcast.18, s32[8,256]{1,0:T(8,128)} %bitcast.20, bf16[8,256]{1,0:T(8,128)(2,1)} %bitcast.22, bf16[256,3584]{1,0:T(8,128)(2,1)} %grad_hbm.1), custom_call_target="tpu_custom_call" | custom-call | flops 469762048 | bytes 3670016 | tf_op jit(solution)/shard_map/pallas_call | solution.py:135
  3.9 7.4 %all-to-all-start = ((bf16[16,16,1536]{2,1,0:T(8,128)(2,1)}), bf16[16,16,1536]{2,1,0:T(8,128)(2,1)S(1)}, u32[]{:S(2)}, u32[]{:S(2)}) async-start(bf16[16,16,1536]{2,1,0:T(8,128)(2,1)} %bitcast.3), calls=%async_computation | async-start | bytes 1572864 | tf_op jit(solution)/shard_map/all_to_all | solution.py:719
  11.3 1.6 %collective-permute-start.2 = (bf16[256,1152]{1,0:T(8,128)(2,1)S(1)}, bf16[256,1152]{1,0:T(8,128)(2,1)S(1)}, u32[]{:S(2)}, u32[]{:S(2)}) collective-permute-start(bf16[256,1152]{1,0:T(8,128)(2,1)S(1)} %get-tuple-element.36.after_ref.refs_0_), channel_id=1, source_target_pairs={{0,16},{16,0},{1,17},{17,1},{2,18},{18,2},{3,19},{19,3},{4,20},{20... | collective-permute-start | bytes 1769480 | tf_op jit(solution)/shard_map/ppermute | solution.py:716
  12.9 1.3 %shard_map.120 = (bf16[192,512]{1,0:T(8,128)(2,1)S(1)}, bf16[192,512]{1,0:T(8,128)(2,1)S(1)}) custom-call(bf16[192,2048]{1,0:T(8,128)(2,1)} %bitcast.16, bf16[256,1152]{1,0:T(8,128)(2,1)S(1)} %get-tuple-element.36.after_ref.refs_0_), custom_call_target="tpu_custom_call" | custom-call | flops 3145728 | bytes 1179648 | tf_op jit(solution)/shard_map/pallas_call | solution.py:171
  14.2 0.0 copy-start
  14.2 0.6 collective-permute-start.1
  14.7 12.7 %collective-permute-done.2.refs_1_ = bf16[256,1152]{1,0:T(8,128)(2,1)S(1)} collective-permute-done((bf16[256,1152]{1,0:T(8,128)(2,1)S(1)}, bf16[256,1152]{1,0:T(8,128)(2,1)S(1)}, u32[]{:S(2)}, u32[]{:S(2)}) %collective-permute-start.2) | collective-permute-done | bytes 589856 | tf_op jit(solution)/shard_map/ppermute | solution.py:716
  27.5 2.2 %shard_map.121 = bf16[384,1536]{1,0:T(8,128)(2,1)} custom-call(bf16[256,1152]{1,0:T(8,128)(2,1)S(1)} %get-tuple-element.36.after_ref.refs_0_, bf16[256,1152]{1,0:T(8,128)(2,1)S(1)} %collective-permute-done.2.refs_1_), custom_call_target="tpu_custom_call" | custom-call | bytes 2949120 | tf_op jit(solution)/shard_map/pallas_call | solution.py:301
  29.7 1.4 %collective-permute-done.1.refs_1_.refs_2_ = bf16[192,512]{1,0:T(8,128)(2,1)S(1)} collective-permute-done((bf16[192,512]{1,0:T(8,128)(2,1)S(1)}, bf16[192,512]{1,0:T(8,128)(2,1)S(1)}, u32[]{:S(2)}, u32[]{:S(2)}) %collective-permute-start.1) | collective-permute-done | bytes 196640 | tf_op jit(solution)/shard_map/ppermute | solution.py:716
  31.1 0.0 copy-start.2
  31.1 0.7 copy-done.2
  31.8 0.0 all-to-all-done
  31.8 0.0 copy-done
  31.8 5.8 %all-to-all-start.1 = ((bf16[16,24,1536]{2,1,0:T(8,128)(2,1)}), bf16[16,24,1536]{2,1,0:T(8,128)(2,1)S(1)}, u32[]{:S(2)}, u32[]{:S(2)}) async-start(bf16[16,24,1536]{2,1,0:T(8,128)(2,1)} %bitcast.15), calls=%async_computation.1 | async-start | bytes 2359296 | tf_op jit(solution)/shard_map/all_to_all | solution.py:719
  37.6 0.0 copy-start.1
  37.6 0.0 copy-start.3
  37.6 1.6 %collective-permute-start = (bf16[256,1536]{1,0:T(8,128)(2,1)S(1)}, bf16[256,1536]{1,0:T(8,128)(2,1)S(1)}, u32[]{:S(2)}, u32[]{:S(2)}) collective-permute-start(bf16[256,1536]{1,0:T(8,128)(2,1)S(1)} %bitcast.12), channel_id=1, source_target_pairs={{0,16},{16,0},{1,17},{17,1},{2,18},{18,2},{3,19},{19,3},{4,20},{20... | collective-permute-start | bytes 2359304 | tf_op jit(solution)/shard_map/ppermute | solution.py:716
  39.2 4.5 %shard_map.122 = (f32[512,2048]{1,0:T(8,128)S(1)}, bf16[512,2048]{1,0:T(8,128)(2,1)S(1)}, bf16[512,2048]{1,0:T(8,128)(2,1)S(1)}, bf16[512,2048]{1,0:T(8,128)(2,1)S(1)}, bf16[512,1536]{1,0:T(8,128)(2,1)S(1)}) custom-call(bf16[256,1536]{1,0:T(8,128)(2,1)S(1)} %bitcast.13, f32[1,512,3584]{2,1,0:T(8,128)} %refs_3_.1, bf16[1,512,3584]{2,1,0:T(8,128)(2,1)} %refs_4_.1, ...), custom_call_target="tpu_custom_call" | custom-call | flops 1835008 | bytes 25690112 | tf_op jit(solution)/shard_map/pallas_call | solution.py:223
  43.7 0.0 copy-done.1
  43.7 0.0 copy-done.3
  43.7 1.9 %shard_map.123 = (bf16[192,2048]{1,0:T(8,128)(2,1)S(1)}, bf16[512,384]{1,0:T(8,128)(2,1)S(1)}, f32[16,1,128]{2,1,0:T(1,128)S(1)}, f32[192,512]{1,0:T(8,128)}) custom-call(bf16[256,1536]{1,0:T(8,128)(2,1)S(1)} %bitcast.14, bf16[512,2048]{1,0:T(8,128)(2,1)S(1)} %get-tuple-element.40.weight_ref.refs_5_, bf16[192,512]{1,0:T(8,128)(2,1)S(1)} %copy-done.1, ...), custom_call_target="tpu_custom_call" | custom-call | flops 805306368 | bytes 2097152 | tf_op jit(solution)/shard_map/pallas_call | solution.py:382
  45.6 11.9 %collective-permute-done.refs_0_ = bf16[256,1536]{1,0:T(8,128)(2,1)S(1)} collective-permute-done((bf16[256,1536]{1,0:T(8,128)(2,1)S(1)}, bf16[256,1536]{1,0:T(8,128)(2,1)S(1)}, u32[]{:S(2)}, u32[]{:S(2)}) %collective-permute-start) | collective-permute-done | bytes 786464 | tf_op jit(solution)/shard_map/ppermute | solution.py:716
  57.5 6.5 %shard_map.124 = (f32[16,1,128]{2,1,0:T(1,128)S(1)}, bf16[384,512]{1,0:T(8,128)(2,1)S(1)}, f32[192,512]{1,0:T(8,128)}, f32[1,512,3584]{2,1,0:T(8,128)}, bf16[1,5...) custom-call(bf16[256,1536]{1,0:T(8,128)(2,1)S(1)} %collective-permute-done.refs_0_, bf16[192,512]{1,0:T(8,128)(2,1)S(1)} %copy-done.1, ...), custom_call_target="tpu_custom_call" | custom-call | flops 1610612736 | bytes 16777216 | tf_op jit(solution)/shard_map/pallas_call | solution.py:586
  64.1 0.0 all-to-all-done.1
  64.1 2.4 %shard_map.125 = (bf16[192,512]{1,0:T(8,128)(2,1)S(1)}, bf16[192,512]{1,0:T(8,128)(2,1)}, f32[32,1,128]{2,1,0:T(1,128)}) custom-call(bf16[384,1536]{1,0:T(8,128)(2,1)S(1)} %bitcast.10, bf16[384,512]{1,0:T(8,128)(2,1)S(1)} %get-tuple-element.46.hidden_ref, bf16[512,1536]{1,0:T(8,128)(2,1)S(1)} %get-tuple-element.48.weight_ref, ...), custom_call_target="tpu_custom_call" | custom-call | flops 603979776 | bytes 1572864 | tf_op jit(solution)/shard_map/pallas_call | solution.py:432
  66.5 1.6 %collective-permute-start.3 = (bf16[192,512]{1,0:T(8,128)(2,1)}, bf16[192,512]{1,0:T(8,128)(2,1)S(1)}, u32[]{:S(2)}, u32[]{:S(2)}) collective-permute-start(bf16[192,512]{1,0:T(8,128)(2,1)} %get-tuple-element.54), channel_id=1, source_target_pairs={{0,16},{16,0},{1,17},{17,1},{2,18},{18,2},{3,19},{19,3},{4,20},{20... | collective-permute-start | bytes 589832 | tf_op jit(solution)/shard_map/ppermute | solution.py:716
  68.1 5.1 %all-to-all-start.2 = ((f32[32,1,128]{2,1,0:T(1,128)}), f32[32,1,128]{2,1,0:T(1,128)S(1)}, u32[]{:S(2)}, u32[]{:S(2)}) async-start(f32[32,1,128]{2,1,0:T(1,128)} %get-tuple-element.61), calls=%async_computation.2 | async-start | bytes 32768 | tf_op jit(solution)/shard_map/all_to_all | solution.py:740
  73.2 0.0 collective-permute-done.3.refs_1_
  73.2 7.8 %shard_map.126 = (f32[1,512,3584]{2,1,0:T(8,128)}, bf16[1,512,3584]{2,1,0:T(8,128)(2,1)}, bf16[1,512,3584]{2,1,0:T(8,128)(2,1)}, bf16[192,2048]{1,0:T(8,128)(2,1...) custom-call(bf16[384,512]{1,0:T(8,128)(2,1)S(1)} %get-tuple-element., ...), custom_call_target="tpu_custom_call", output_to_operand_aliasing={{0}: (11, {}), {1}: (12, {}), {2}: (13, {})} | custom-call | flops 603979776 | bytes 12582912 | tf_op jit(solution)/shard_map/pallas_call | solution.py:667
  81.0 0.0 all-to-all-done.2.score_ref
  81.0 1.6 %shard_map.127 = f32[8,256]{1,0:T(8,128)} custom-call(s32[8,256]{1,0:T(8,128)S(1)} %get-tuple-element.59.place_ref, f32[8,256]{1,0:T(8,128)S(1)} %get-tuple-element.60.inverse_ref, f32[32,1,128]{2,1,0:T(1,128)S(1)} %all-to-all-done.2.score_ref), custom_call_target="tpu_custom_call" | custom-call | flops 1048576 | bytes 65536 | tf_op jit(solution)/shard_map/pallas_call | solution.py:695
Async XLA Ops:
  3.9 27.9 %all-to-all-start = ((bf16[16,16,1536]{2,1,0:T(8,128)(2,1)}), bf16[16,16,1536]{2,1,0:T(8,128)(2,1)S(1)}, u32[]{:S(2)}, u32[]{:S(2)}) async-start(bf16[16,16,1536]{2,1,0:T(8,128)(2,1)} %bitcast.3), calls=%async_computation | async-start | bytes 1572864 | tf_op jit(solution)/shard_map/all_to_all | solution.py:719
  11.3 16.2 %collective-permute-start.2 = (bf16[256,1152]{1,0:T(8,128)(2,1)S(1)}, bf16[256,1152]{1,0:T(8,128)(2,1)S(1)}, u32[]{:S(2)}, u32[]{:S(2)}) collective-permute-start(bf16[256,1152]{1,0:T(8,128)(2,1)S(1)} %get-tuple-element.36.after_ref.refs_0_), channel_id=1, source_target_pairs={{0,16},{16,0},{1,17},{17,1},{2,18},{18,2},{3,19},{19,3},{4,20},{20... | collective-permute-start | bytes 1769480 | tf_op jit(solution)/shard_map/ppermute | solution.py:716
  14.2 17.6 %copy-start = (bf16[192,512]{1,0:T(8,128)(2,1)}, bf16[192,512]{1,0:T(8,128)(2,1)S(1)}, u32[]{:S(2)}) copy-start(bf16[192,512]{1,0:T(8,128)(2,1)S(1)} %get-tuple-element.37.refs_0_.refs_1_) | copy-start | bytes 589828
  14.2 17.0 %collective-permute-start.1 = (bf16[192,512]{1,0:T(8,128)(2,1)S(1)}, bf16[192,512]{1,0:T(8,128)(2,1)S(1)}, u32[]{:S(2)}, u32[]{:S(2)}) collective-permute-start(bf16[192,512]{1,0:T(8,128)(2,1)S(1)} %get-tuple-element.38), channel_id=1, source_target_pairs={{0,16},{16,0},{1,17},{17,1},{2,18},{18,2},{3,19},{19,3},{4,20},{20... | collective-permute-start | bytes 589832 | tf_op jit(solution)/shard_map/ppermute | solution.py:716
  31.1 0.7 copy-start.2
  31.8 32.2 %all-to-all-start.1 = ((bf16[16,24,1536]{2,1,0:T(8,128)(2,1)}), bf16[16,24,1536]{2,1,0:T(8,128)(2,1)S(1)}, u32[]{:S(2)}, u32[]{:S(2)}) async-start(bf16[16,24,1536]{2,1,0:T(8,128)(2,1)} %bitcast.15), calls=%async_computation.1 | async-start | bytes 2359296 | tf_op jit(solution)/shard_map/all_to_all | solution.py:719
  37.6 6.1 %copy-start.1 = (bf16[192,512]{1,0:T(8,128)(2,1)S(1)}, bf16[192,512]{1,0:T(8,128)(2,1)}, u32[]{:S(2)}) copy-start(bf16[192,512]{1,0:T(8,128)(2,1)} %copy-done) | copy-start | bytes 589828
  37.6 6.1 %copy-start.3 = (bf16[192,512]{1,0:T(8,128)(2,1)S(1)}, bf16[192,512]{1,0:T(8,128)(2,1)}, u32[]{:S(2)}) copy-start(bf16[192,512]{1,0:T(8,128)(2,1)} %copy-done.2) | copy-start | bytes 589828
  37.6 19.9 %collective-permute-start = (bf16[256,1536]{1,0:T(8,128)(2,1)S(1)}, bf16[256,1536]{1,0:T(8,128)(2,1)S(1)}, u32[]{:S(2)}, u32[]{:S(2)}) collective-permute-start(bf16[256,1536]{1,0:T(8,128)(2,1)S(1)} %bitcast.12), channel_id=1, source_target_pairs={{0,16},{16,0},{1,17},{17,1},{2,18},{18,2},{3,19},{19,3},{4,20},{20... | collective-permute-start | bytes 2359304 | tf_op jit(solution)/shard_map/ppermute | solution.py:716
  66.5 6.7 %collective-permute-start.3 = (bf16[192,512]{1,0:T(8,128)(2,1)}, bf16[192,512]{1,0:T(8,128)(2,1)S(1)}, u32[]{:S(2)}, u32[]{:S(2)}) collective-permute-start(bf16[192,512]{1,0:T(8,128)(2,1)} %get-tuple-element.54), channel_id=1, source_target_pairs={{0,16},{16,0},{1,17},{17,1},{2,18},{18,2},{3,19},{19,3},{4,20},{20... | collective-permute-start | bytes 589832 | tf_op jit(solution)/shard_map/ppermute | solution.py:716
  68.1 12.9 %all-to-all-start.2 = ((f32[32,1,128]{2,1,0:T(1,128)}), f32[32,1,128]{2,1,0:T(1,128)S(1)}, u32[]{:S(2)}, u32[]{:S(2)}) async-start(f32[32,1,128]{2,1,0:T(1,128)} %get-tuple-element.61), calls=%async_computation.2 | async-start | bytes 32768 | tf_op jit(solution)/shard_map/all_to_all | solution.py:740

commit v13 on v12

--- a/solution.py
+++ b/solution.py
@@ -149,34 +149,39 @@
     )(*in_hbm(ids, slots, gates, out_grad))
 
 
-def swiglu_part(gate_up_ref, shards, step, part):
+def unit_columns(shards, step, part):
     at = lax.rem(lax.axis_index("rep") + step, shards)
-    low = pl.multiple_of(at * part, part)
-    high = pl.multiple_of((shards + at) * part, part)
-    gate = gate_up_ref[:, pl.ds(low, part)].astype(f32)
-    up = gate_up_ref[:, pl.ds(high, part)].astype(f32)
-    return low, high, gate, up, jax.nn.sigmoid(gate)
-
-
-def hidden_kernel(gate_up_ref, after_ref, *out_refs):
+    return pl.multiple_of(at * part, part), pl.multiple_of((shards + at) * part, part)
+
+
+def hidden_kernel(gate_up_ref, after_ref, *refs):
     del after_ref
+    out_refs, factor_ref = refs[:-1], refs[-1]
     for s, out_ref in enumerate(out_refs):
-        _, _, gate, up, sig = swiglu_part(gate_up_ref, len(out_refs), s, out_ref.shape[1])
-        out_ref[...] = (gate * sig * up).astype(bf16)
+        part = out_ref.shape[1]
+        low, high = unit_columns(len(out_refs), s, part)
+        gate = gate_up_ref[:, pl.ds(low, part)].astype(f32)
+        up = gate_up_ref[:, pl.ds(high, part)].astype(f32)
+        sig = jax.nn.sigmoid(gate)
+        silu = gate * sig
+        out_ref[...] = (silu * up).astype(bf16)
+        factor_ref[:, pl.ds(low, part)] = up * sig * (1.0 + gate * (1.0 - sig))
+        factor_ref[:, pl.ds(high, part)] = silu
 
 
 def hidden_parts(gate_up, shards, after):
     slots, width = gate_up.shape
     shape = (slots, width // 2 // shards)
-    return pl.pallas_call(
+    outs = pl.pallas_call(
         hidden_kernel,
         grid=(1,),
         in_specs=[block(gate_up.shape), ANY],
-        out_specs=[block(shape)] * shards,
-        out_shape=[plain(shape, bf16)] * shards,
-        compiler_params=params(3 * slots * width),
-        cost_estimate=cost(8 * slots * width, 3 * slots * width, slots * width),
+        out_specs=[block(shape)] * shards + [block(gate_up.shape)],
+        out_shape=[out_hbm(shape, bf16)] * shards + [out_hbm(gate_up.shape, f32)],
+        compiler_params=params(7 * slots * width),
+        cost_estimate=cost(8 * slots * width, 7 * slots * width, slots * width),
     )(*in_hbm(gate_up), after)
+    return list(outs[:-1]), outs[-1]
 
 
 def load_kernel(middle, after_ref, master_hbm, one_hbm, two_hbm, *refs):
@@ -360,18 +365,27 @@
 
 
 def begin_kernel(blocks, arrived_ref, weight_ref, *refs):
-    hidden, (rows_ref, hidden_t, score_ref) = refs[:-6], refs[-6:-3]
-    proj_hbm, proj_ref, sem = refs[-3:]
+    size = len(refs) - 7
+    hidden_hbm, (rows_ref, hidden_ref, hidden_t, score_ref) = refs[:size], refs[size:-3]
+    proj_hbm, proj_ref, sems = refs[-3:]
+    count = rows_ref.shape[0]
+    loads = [
+        pltpu.make_async_copy(ref, hidden_ref.at[pl.ds(s * count, count)], sems.at[1 + s])
+        for s, ref in enumerate(hidden_hbm)
+    ]
+    for copy in loads:
+        copy.start()
     reorder(arrived_ref[...], rows_ref)
     proj = times_weight(rows_ref, weight_ref)
     proj_ref[...] = proj
-    copy = pltpu.make_async_copy(proj_ref, proj_hbm, sem.at[0])
+    copy = pltpu.make_async_copy(proj_ref, proj_hbm, sems.at[0])
     copy.start()
-    count = proj.shape[0]
+    for load in loads:
+        load.wait()
     score_ref[...] = score_block(
-        blocks, proj, hidden[0][...], [block_index(blocks, count)]
+        blocks, proj, hidden_ref[:count], [block_index(blocks, count)]
     )[0]
-    transpose_rows(hidden, hidden_t)
+    transpose_rows([hidden_ref], hidden_t)
     copy.wait()
 
 
@@ -381,18 +395,22 @@
     total = count * len(hidden)
     return pl.pallas_call(
         functools.partial(begin_kernel, blocks),
-        in_specs=[VMEM] * (2 + len(hidden)),
-        out_specs=[VMEM] * 3 + [HBM],
+        in_specs=[VMEM] * 2 + [HBM] * len(hidden),
+        out_specs=[VMEM] * 4 + [HBM],
         out_shape=[
             plain((count, cols), bf16),
+            plain((total, part), bf16),
             plain((part, total), bf16),
             plain((blocks, 1, LANE), f32),
             out_hbm((count, part), f32),
         ],
-        scratch_shapes=[pltpu.VMEM((count, part), f32), pltpu.SemaphoreType.DMA((1,))],
+        scratch_shapes=[
+            pltpu.VMEM((count, part), f32),
+            pltpu.SemaphoreType.DMA((1 + len(hidden),)),
+        ],
         compiler_params=params(8 * count * cols + 16 * total * part),
         cost_estimate=cost(4 * count * part * cols, 2 * part * cols),
-    )(arrived, weight, *hidden)
+    )(arrived, weight, *in_hbm(*hidden))
 
 
 def finish_kernel(shards, blocks, arrived_ref, hidden_ref, weight_ref, *refs):
@@ -515,8 +533,8 @@
         return out
 
     size = len(fresh)
-    arrived, hidden = take(size), take(1 + size)
-    hidden_t, given_ref, weight_ref, *state = take(6)
+    arrived = take(size)
+    hidden_ref, hidden_t, given_ref, weight_ref, *state = take(7)
     scores, (mixed_ref,), projs_hbm, outs = take(size), take(1), take(size), take(3)
     news, rows_refs, projs = take(3), take(size), take(size)
     grad_ref, sems, proj_sems = refs
@@ -542,7 +560,10 @@
         copies.append(pltpu.make_async_copy(projs[i], projs_hbm[i], proj_sems.at[i]))
         copies[i].start()
         scores[i][...] = score_block(
-            blocks, proj, hidden[s][...], [block_index(blocks, count)]
+            blocks,
+            proj,
+            hidden_ref[s * count : (s + 1) * count],
+            [block_index(blocks, count)],
         )[0]
     row = lax.broadcasted_iota(jnp.int32, (shards * count, count), 0)
     col = lax.broadcasted_iota(jnp.int32, (shards * count, count), 1)
@@ -551,7 +572,8 @@
     for s in range(shards):
         order = (step_of == s) & (col == at * SEND + slot)
         order = jnp.where(order, 1.0, 0.0).astype(bf16)
-        total += jnp.dot(order, hidden[s][...], preferred_element_type=f32)
+        own = hidden_ref[s * count : (s + 1) * count]
+        total += jnp.dot(order, own, preferred_element_type=f32)
     mixed_ref[...] = total.astype(bf16)
 
     @pl.loop(0, steps)
@@ -570,7 +592,7 @@
     size = len(fresh)
     total = count * (1 + size)
     step = min(part, 64)
-    args = [*arrived, *hidden, hidden_t, given, weight, *held]
+    args = [*arrived, hidden, hidden_t, given, weight, *held]
     near = [plain((blocks, 1, LANE), f32)] * size + [plain((total, part), bf16)]
     far = [out_hbm((count, part), f32)] * size
     far += [out_hbm(array.shape, array.dtype) for array in shapes]
@@ -598,14 +620,14 @@
 
 def update_kernel(low, shards, hidden_ref, rows_ref, *refs):
     grad_refs, refs = refs[:shards], refs[shards:]
-    gate_up_hbm, state_hbm, token_hbm, refs = refs[0], refs[1:4], refs[4:7], refs[10:]
+    factor_hbm, state_hbm, token_hbm, refs = refs[0], refs[1:4], refs[4:7], refs[10:]
     outs, gate_out, place_ref, inverse_ref, refs = refs[:3], *refs[3:6], refs[6:]
     state, tokens, refs = refs[:3], refs[3:6], refs[6:]
-    hidden_t, grad_ref, gate_up_ref, gate_new, in_sems, out_sems, sems = refs
+    hidden_t, grad_ref, factor_ref, gate_new, in_sems, out_sems, sems = refs
     part = grad_ref.shape[0]
     steps = in_sems.shape[1]
     step = part // steps
-    gate_load = pltpu.make_async_copy(gate_up_hbm, gate_up_ref, sems.at[0])
+    gate_load = pltpu.make_async_copy(factor_hbm, factor_ref, sems.at[0])
     gate_store = pltpu.make_async_copy(gate_new, gate_out, sems.at[1])
     gate_load.start()
     token_loads = [
@@ -637,12 +659,10 @@
     gate_load.wait()
     for s, ref in enumerate(grad_refs):
         width = ref.shape[1]
-        first, second, gate, up, sig = swiglu_part(gate_up_ref, shards, s, width)
         grad = ref[...].astype(f32)
-        gate_new[:, pl.ds(first, width)] = (
-            grad * up * sig * (1.0 + gate * (1.0 - sig))
-        ).astype(bf16)
-        gate_new[:, pl.ds(second, width)] = (grad * (gate * sig)).astype(bf16)
+        for first in unit_columns(shards, s, width):
+            own = pl.ds(first, width)
+            gate_new[:, own] = (grad * factor_ref[:, own]).astype(bf16)
     gate_store.start()
 
     @pl.loop(0, steps)
@@ -653,7 +673,7 @@
     gate_store.wait()
 
 
-def update(low, hidden, rows, grads, gate_up, state, tokens, done):
+def update(low, hidden, rows, grads, factors, state, tokens, done):
     total, part = hidden.shape
     cols = rows.shape[1]
     step = min(part, 64)
@@ -661,7 +681,7 @@
     scratch = [pltpu.VMEM((part, cols), kind) for kind in (f32, bf16, bf16)]
     scratch += [pltpu.VMEM(token.shape, token.dtype) for token in tokens]
     scratch += [pltpu.VMEM((part, total), bf16), pltpu.VMEM((part, cols), f32)]
-    scratch += [pltpu.VMEM(gate_up.shape, bf16)] * 2
+    scratch += [pltpu.VMEM(factors.shape, kind) for kind in (f32, bf16)]
     scratch += [pltpu.SemaphoreType.DMA((3, part // step))] * 2
     scratch += [pltpu.SemaphoreType.DMA((5,))]
     return pl.pallas_call(
@@ -669,13 +689,13 @@
         in_specs=[VMEM] * (2 + shards) + [HBM] * 10,
         out_specs=[HBM] * 4 + [VMEM] * 2,
         out_shape=[out_hbm(array.shape, array.dtype) for array in state]
-        + [out_hbm(gate_up.shape, bf16)]
+        + [out_hbm(factors.shape, bf16)]
         + [plain(tokens[0].shape, kind) for kind in (jnp.int32, f32)],
         scratch_shapes=scratch,
         input_output_aliases={2 + shards + 7 + i: i for i in range(3)},
-        compiler_params=params(12 * part * cols + 2 * total * part + 4 * gate_up.size),
+        compiler_params=params(12 * part * cols + 2 * total * part + 6 * factors.size),
         cost_estimate=cost(2 * total * part * cols, 16 * part * cols, part * cols),
-    )(hidden, rows, *grads, *in_hbm(gate_up, *state, *tokens, *done))
+    )(hidden, rows, *grads, *in_hbm(factors, *state, *tokens, *done))
 
 
 def close_kernel(shards, place_ref, inverse_ref, score_ref, gate_ref):
@@ -720,7 +740,7 @@
 
     send_a, send_b = dispatch(ep_size, edges, ids_t, slots_t, gates_t, out_grad)
     mixed = [shift(send_b, s) for s in steps]
-    parts = list(hidden_parts(gate_up, rep_size, send_b))
+    parts, factors = hidden_parts(gate_up, rep_size, send_b)
     arrived = exchange(send_a.reshape(ep_size, ROWS, -1)).reshape(send_a.shape)
     hidden = [parts[0]] + [shift(parts[s], s) for s in steps]
     mixed = mix([send_b] + mixed)
@@ -729,7 +749,7 @@
 
     peers = [shift(arrived, s) for s in steps]
     *held, weight_a, weight_b = load_state(edges[1], *state, arrived)
-    rows, hidden_t, score_own, proj = begin(ep_size, arrived, weight_a, hidden)
+    rows, hidden, hidden_t, score_own, proj = begin(ep_size, arrived, weight_a, hidden)
     scores, hidden_mixed, before, done = settle(
         ep_size, peers, rows, hidden, hidden_t, weight_a, held, state
     )
@@ -741,7 +761,7 @@
 
     tokens = (ids_t, slots_t, gates_t)
     *done, grad_gate_up, place, inverse = update(
-        edges[1], hidden_mixed, arrived_b, grads, gate_up, state, tokens, done
+        edges[1], hidden_mixed, arrived_b, grads, factors, state, tokens, done
     )
     gate_grad = close(rep_size, place, inverse, score).T
     return (grad_gate_up.reshape(saved_gate_up.shape), gate_grad) + tuple(done)

time: 83.6 us -> 83.7 us (level)
  Pallas kernels: 31.4 us -> 32.9 us
  waiting for transfers between devices: 26.1 us -> 24.7 us
    pallas_call x1, Pallas kernels: 1.31 us -> 2.74 us  [hidden_parts(): pl.pallas_call(hidden_kernel, grid=(1,), in_specs=[block(gate_up.shape),...]
    ppermute x4, waiting for transfers between devices: 26.1 us -> 24.7 us  [shift(): return lax.ppermute(value, 'rep', perm)]
  transfers between devices with their start and end apart: 7 -> 7, of which waited for: 3 -> 3; matrix products, arithmetic and copies ran while one was open for 0% -> 0% of each run, Pallas kernels for 29% -> 31%
where the time goes in v13:
time: 83.7 us; the launch traced here: 82.6 us
  Pallas kernels  32.9 us (39%)
  waiting for transfers between devices  24.7 us (30%)
  starting transfers between devices  23.6 us (28%)
    ppermute x4, waiting for transfers between devices, shift(): return lax.ppermute(value, 'rep', perm)  24.7 us
    all_to_all x2, starting transfers between devices, exchange(): return lax.all_to_all(value, 'ep', split_axis=0, concat_axis=0, tiled=True)  13.1 us
    pallas_call x1, Pallas kernels, update(): pl.pallas_call(functools.partial(update_kernel, low, shards), in_specs=[V...  7.82 us
    pallas_call x1, Pallas kernels, settle(): pl.pallas_call(functools.partial(settle_kernel, fresh, blocks), in_specs=...  6.53 us
    ppermute x4, starting transfers between devices, shift(): return lax.ppermute(value, 'rep', perm)  5.27 us
    all_to_all x1, starting transfers between devices, per_device(): lax.all_to_all(score, ('rep', 'ep'), split_axis=0, concat_axis=0, tiled=T...  5.19 us
    pallas_call x1, Pallas kernels, load_state(): pl.pallas_call(functools.partial(load_kernel, middle), in_specs=[ANY] + [...  4.47 us
    pallas_call x1, Pallas kernels, dispatch(): pl.pallas_call(functools.partial(dispatch_kernel, edges), in_specs=[HBM]...  3.26 us
  transfers between devices with their start and end apart: 7, of which 3 were waited for; matrix products, arithmetic and copies ran while one was open for 0% of the time, Pallas kernels for 31%

profile of v13, /device:TPU:0, one launch (start us, length us, event | category | flops | bytes accessed | tf_op | source)
XLA Modules:
  0.0 82.6 jit_solution(2445548966415997049)
XLA Ops:
  0.6 3.3 %shard_map.119 = (bf16[256,1536]{1,0:T(8,128)(2,1)}, bf16[256,1152]{1,0:T(8,128)(2,1)S(1)}) custom-call(s32[8,256]{1,0:T(8,128)} %bitcast.17, s32[8,256]{1,0:T(8,128)} %bitcast.19, bf16[8,256]{1,0:T(8,128)(2,1)} %bitcast.21, bf16[256,3584]{1,0:T(8,128)(2,1)} %grad_hbm.1), custom_call_target="tpu_custom_call" | custom-call | flops 469762048 | bytes 3670016 | tf_op jit(solution)/shard_map/pallas_call | solution.py:135
  3.9 7.4 %all-to-all-start = ((bf16[16,16,1536]{2,1,0:T(8,128)(2,1)}), bf16[16,16,1536]{2,1,0:T(8,128)(2,1)S(1)}, u32[]{:S(2)}, u32[]{:S(2)}) async-start(bf16[16,16,1536]{2,1,0:T(8,128)(2,1)} %bitcast.3), calls=%async_computation | async-start | bytes 1572864 | tf_op jit(solution)/shard_map/all_to_all | solution.py:739
  11.3 1.6 %collective-permute-start.2 = (bf16[256,1152]{1,0:T(8,128)(2,1)S(1)}, bf16[256,1152]{1,0:T(8,128)(2,1)S(1)}, u32[]{:S(2)}, u32[]{:S(2)}) collective-permute-start(bf16[256,1152]{1,0:T(8,128)(2,1)S(1)} %get-tuple-element.39.after_ref.refs_0_), channel_id=1, source_target_pairs={{0,16},{16,0},{1,17},{17,1},{2,18},{18,2},{3,19},{19,3},{4,20},{20... | collective-permute-start | bytes 1769480 | tf_op jit(solution)/shard_map/ppermute | solution.py:736
  12.9 2.7 %shard_map.121 = (bf16[192,512]{1,0:T(8,128)(2,1)}, bf16[192,512]{1,0:T(8,128)(2,1)}, f32[192,2048]{1,0:T(8,128)}) custom-call(bf16[192,2048]{1,0:T(8,128)(2,1)} %bitcast.16, bf16[256,1152]{1,0:T(8,128)(2,1)S(1)} %get-tuple-element.39.after_ref.refs_0_), custom_call_target="tpu_custom_call" | custom-call | flops 3145728 | bytes 2752512 | tf_op jit(solution)/shard_map/pallas_call | solution.py:175
  15.6 0.5 collective-permute-start.1
  16.1 11.4 %collective-permute-done.2.refs_1_ = bf16[256,1152]{1,0:T(8,128)(2,1)S(1)} collective-permute-done((bf16[256,1152]{1,0:T(8,128)(2,1)S(1)}, bf16[256,1152]{1,0:T(8,128)(2,1)S(1)}, u32[]{:S(2)}, u32[]{:S(2)}) %collective-permute-start.2) | collective-permute-done | bytes 589856 | tf_op jit(solution)/shard_map/ppermute | solution.py:736
  27.5 2.2 %shard_map.122 = bf16[384,1536]{1,0:T(8,128)(2,1)} custom-call(bf16[256,1152]{1,0:T(8,128)(2,1)S(1)} %get-tuple-element.39.after_ref.refs_0_, bf16[256,1152]{1,0:T(8,128)(2,1)S(1)} %collective-permute-done.2.refs_1_), custom_call_target="tpu_custom_call" | custom-call | bytes 2949120 | tf_op jit(solution)/shard_map/pallas_call | solution.py:306
  29.6 1.5 %collective-permute-done.1.refs_1_ = bf16[192,512]{1,0:T(8,128)(2,1)S(1)} collective-permute-done((bf16[192,512]{1,0:T(8,128)(2,1)}, bf16[192,512]{1,0:T(8,128)(2,1)S(1)}, u32[]{:S(2)}, u32[]{:S(2)}) %collective-permute-start.1) | collective-permute-done | bytes 196640 | tf_op jit(solution)/shard_map/ppermute | solution.py:736
  31.1 0.0 copy-start
  31.1 0.0 all-to-all-done
  31.1 0.7 copy-done
  31.8 5.7 %all-to-all-start.1 = ((bf16[16,24,1536]{2,1,0:T(8,128)(2,1)}), bf16[16,24,1536]{2,1,0:T(8,128)(2,1)S(1)}, u32[]{:S(2)}, u32[]{:S(2)}) async-start(bf16[16,24,1536]{2,1,0:T(8,128)(2,1)} %bitcast.15), calls=%async_computation.1 | async-start | bytes 2359296 | tf_op jit(solution)/shard_map/all_to_all | solution.py:739
  37.6 1.6 %collective-permute-start = (bf16[256,1536]{1,0:T(8,128)(2,1)S(1)}, bf16[256,1536]{1,0:T(8,128)(2,1)S(1)}, u32[]{:S(2)}, u32[]{:S(2)}) collective-permute-start(bf16[256,1536]{1,0:T(8,128)(2,1)S(1)} %bitcast.12), channel_id=1, source_target_pairs={{0,16},{16,0},{1,17},{17,1},{2,18},{18,2},{3,19},{19,3},{4,20},{20... | collective-permute-start | bytes 2359304 | tf_op jit(solution)/shard_map/ppermute | solution.py:736
  39.1 4.5 %shard_map.120 = (f32[512,2048]{1,0:T(8,128)S(1)}, bf16[512,2048]{1,0:T(8,128)(2,1)S(1)}, bf16[512,2048]{1,0:T(8,128)(2,1)S(1)}, bf16[512,2048]{1,0:T(8,128)(2,1)S(1)}, bf16[512,1536]{1,0:T(8,128)(2,1)S(1)}) custom-call(bf16[256,1536]{1,0:T(8,128)(2,1)S(1)} %bitcast.13, f32[1,512,3584]{2,1,0:T(8,128)} %refs_3_.1, bf16[1,512,3584]{2,1,0:T(8,128)(2,1)} %refs_4_.1, ...), custom_call_target="tpu_custom_call" | custom-call | flops 1835008 | bytes 25690112 | tf_op jit(solution)/shard_map/pallas_call | solution.py:228
  43.6 1.9 %shard_map.123 = (bf16[192,2048]{1,0:T(8,128)(2,1)S(1)}, bf16[384,512]{1,0:T(8,128)(2,1)S(1)}, bf16[512,384]{1,0:T(8,128)(2,1)S(1)}, f32[16,1,128]{2,1,0:T(1,128)S(1)}, f32[192,512]{1,0:T(8,128)}) custom-call(bf16[256,1536]{1,0:T(8,128)(2,1)S(1)} %bitcast.14, bf16[512,2048]{1,0:T(8,128)(2,1)S(1)} %get-tuple-element.38.weight_ref.refs_4_, ...), custom_call_target="tpu_custom_call" | custom-call | flops 805306368 | bytes 2097152 | tf_op jit(solution)/shard_map/pallas_call | solution.py:396
  45.6 11.9 %collective-permute-done.refs_0_ = bf16[256,1536]{1,0:T(8,128)(2,1)S(1)} collective-permute-done((bf16[256,1536]{1,0:T(8,128)(2,1)S(1)}, bf16[256,1536]{1,0:T(8,128)(2,1)S(1)}, u32[]{:S(2)}, u32[]{:S(2)}) %collective-permute-start) | collective-permute-done | bytes 786464 | tf_op jit(solution)/shard_map/ppermute | solution.py:736
  57.4 6.5 %shard_map.124 = (f32[16,1,128]{2,1,0:T(1,128)S(1)}, bf16[384,512]{1,0:T(8,128)(2,1)S(1)}, f32[192,512]{1,0:T(8,128)}, f32[1,512,3584]{2,1,0:T(8,128)}, bf16[1,5...) custom-call(bf16[256,1536]{1,0:T(8,128)(2,1)S(1)} %collective-permute-done.refs_0_, ...), custom_call_target="tpu_custom_call" | custom-call | flops 1610612736 | bytes 16777216 | tf_op jit(solution)/shard_map/pallas_call | solution.py:608
  64.0 0.0 all-to-all-done.1
  64.0 2.4 %shard_map.125 = (bf16[192,512]{1,0:T(8,128)(2,1)S(1)}, bf16[192,512]{1,0:T(8,128)(2,1)}, f32[32,1,128]{2,1,0:T(1,128)}) custom-call(bf16[384,1536]{1,0:T(8,128)(2,1)S(1)} %bitcast.10, bf16[384,512]{1,0:T(8,128)(2,1)S(1)} %get-tuple-element.49.hidden_ref, bf16[512,1536]{1,0:T(8,128)(2,1)S(1)} %get-tuple-element.51.weight_ref, ...), custom_call_target="tpu_custom_call" | custom-call | flops 603979776 | bytes 1572864 | tf_op jit(solution)/shard_map/pallas_call | solution.py:450
  66.4 1.6 %collective-permute-start.3 = (bf16[192,512]{1,0:T(8,128)(2,1)}, bf16[192,512]{1,0:T(8,128)(2,1)S(1)}, u32[]{:S(2)}, u32[]{:S(2)}) collective-permute-start(bf16[192,512]{1,0:T(8,128)(2,1)} %get-tuple-element.57), channel_id=1, source_target_pairs={{0,16},{16,0},{1,17},{17,1},{2,18},{18,2},{3,19},{19,3},{4,20},{20... | collective-permute-start | bytes 589832 | tf_op jit(solution)/shard_map/ppermute | solution.py:736
  68.0 5.2 %all-to-all-start.2 = ((f32[32,1,128]{2,1,0:T(1,128)}), f32[32,1,128]{2,1,0:T(1,128)S(1)}, u32[]{:S(2)}, u32[]{:S(2)}) async-start(f32[32,1,128]{2,1,0:T(1,128)} %get-tuple-element.65), calls=%async_computation.2 | async-start | bytes 32768 | tf_op jit(solution)/shard_map/all_to_all | solution.py:760
  73.2 0.0 collective-permute-done.3.refs_1_
  73.2 7.8 %shard_map.126 = (f32[1,512,3584]{2,1,0:T(8,128)}, bf16[1,512,3584]{2,1,0:T(8,128)(2,1)}, bf16[1,512,3584]{2,1,0:T(8,128)(2,1)}, bf16[192,2048]{1,0:T(8,128)(2,1...) custom-call(bf16[384,512]{1,0:T(8,128)(2,1)S(1)} %get-tuple-element., ...), custom_call_target="tpu_custom_call", output_to_operand_aliasing={{0}: (11, {}), {1}: (12, {}), {2}: (13, {})} | custom-call | flops 603979776 | bytes 12582912 | tf_op jit(solution)/shard_map/pallas_call | solution.py:687
  81.0 0.0 all-to-all-done.2.score_ref
  81.0 1.6 %shard_map.127 = f32[8,256]{1,0:T(8,128)} custom-call(s32[8,256]{1,0:T(8,128)S(1)} %get-tuple-element.63.place_ref, f32[8,256]{1,0:T(8,128)S(1)} %get-tuple-element.64.inverse_ref, f32[32,1,128]{2,1,0:T(1,128)S(1)} %all-to-all-done.2.score_ref), custom_call_target="tpu_custom_call" | custom-call | flops 1048576 | bytes 65536 | tf_op jit(solution)/shard_map/pallas_call | solution.py:715
Async XLA Ops:
  3.9 27.2 %all-to-all-start = ((bf16[16,16,1536]{2,1,0:T(8,128)(2,1)}), bf16[16,16,1536]{2,1,0:T(8,128)(2,1)S(1)}, u32[]{:S(2)}, u32[]{:S(2)}) async-start(bf16[16,16,1536]{2,1,0:T(8,128)(2,1)} %bitcast.3), calls=%async_computation | async-start | bytes 1572864 | tf_op jit(solution)/shard_map/all_to_all | solution.py:739
  11.3 16.2 %collective-permute-start.2 = (bf16[256,1152]{1,0:T(8,128)(2,1)S(1)}, bf16[256,1152]{1,0:T(8,128)(2,1)S(1)}, u32[]{:S(2)}, u32[]{:S(2)}) collective-permute-start(bf16[256,1152]{1,0:T(8,128)(2,1)S(1)} %get-tuple-element.39.after_ref.refs_0_), channel_id=1, source_target_pairs={{0,16},{16,0},{1,17},{17,1},{2,18},{18,2},{3,19},{19,3},{4,20},{20... | collective-permute-start | bytes 1769480 | tf_op jit(solution)/shard_map/ppermute | solution.py:736
  15.6 15.5 %collective-permute-start.1 = (bf16[192,512]{1,0:T(8,128)(2,1)}, bf16[192,512]{1,0:T(8,128)(2,1)S(1)}, u32[]{:S(2)}, u32[]{:S(2)}) collective-permute-start(bf16[192,512]{1,0:T(8,128)(2,1)} %get-tuple-element.41), channel_id=1, source_target_pairs={{0,16},{16,0},{1,17},{17,1},{2,18},{18,2},{3,19},{19,3},{4,20},{20... | collective-permute-start | bytes 589832 | tf_op jit(solution)/shard_map/ppermute | solution.py:736
  31.1 0.7 copy-start
  31.8 32.2 %all-to-all-start.1 = ((bf16[16,24,1536]{2,1,0:T(8,128)(2,1)}), bf16[16,24,1536]{2,1,0:T(8,128)(2,1)S(1)}, u32[]{:S(2)}, u32[]{:S(2)}) async-start(bf16[16,24,1536]{2,1,0:T(8,128)(2,1)} %bitcast.15), calls=%async_computation.1 | async-start | bytes 2359296 | tf_op jit(solution)/shard_map/all_to_all | solution.py:739
  37.6 19.9 %collective-permute-start = (bf16[256,1536]{1,0:T(8,128)(2,1)S(1)}, bf16[256,1536]{1,0:T(8,128)(2,1)S(1)}, u32[]{:S(2)}, u32[]{:S(2)}) collective-permute-start(bf16[256,1536]{1,0:T(8,128)(2,1)S(1)} %bitcast.12), channel_id=1, source_target_pairs={{0,16},{16,0},{1,17},{17,1},{2,18},{18,2},{3,19},{19,3},{4,20},{20... | collective-permute-start | bytes 2359304 | tf_op jit(solution)/shard_map/ppermute | solution.py:736
  66.4 6.8 %collective-permute-start.3 = (bf16[192,512]{1,0:T(8,128)(2,1)}, bf16[192,512]{1,0:T(8,128)(2,1)S(1)}, u32[]{:S(2)}, u32[]{:S(2)}) collective-permute-start(bf16[192,512]{1,0:T(8,128)(2,1)} %get-tuple-element.57), channel_id=1, source_target_pairs={{0,16},{16,0},{1,17},{17,1},{2,18},{18,2},{3,19},{19,3},{4,20},{20... | collective-permute-start | bytes 589832 | tf_op jit(solution)/shard_map/ppermute | solution.py:736
  68.0 13.0 %all-to-all-start.2 = ((f32[32,1,128]{2,1,0:T(1,128)}), f32[32,1,128]{2,1,0:T(1,128)S(1)}, u32[]{:S(2)}, u32[]{:S(2)}) async-start(f32[32,1,128]{2,1,0:T(1,128)} %get-tuple-element.65), calls=%async_computation.2 | async-start | bytes 32768 | tf_op jit(solution)/shard_map/all_to_all | solution.py:760

commit v14 on v13

--- a/solution.py
+++ b/solution.py
@@ -513,8 +513,9 @@
         grad_ref[:, own] = grad
 
 
-def state_copies(i, step, low, hbm, vmem, sems, into):
-    cols = vmem[0].shape[1]
+def state_copies(i, low, hbm, vmem, sems, into):
+    part, cols = vmem[0].shape
+    step = part // sems.shape[1]
     rows = pl.ds(pl.multiple_of(i * step, step), step)
     out = []
     for j, (far, near) in enumerate(zip(hbm, vmem)):
@@ -550,7 +551,7 @@
     @pl.loop(0, steps)
     def _(i):
         update_rows(i * step, step, state, news, grad_ref)
-        for copy in state_copies(i, step, 0, outs, news, sems, False):
+        for copy in state_copies(i, 0, outs, news, sems, False):
             copy.start()
 
     copies = []
@@ -578,7 +579,7 @@
 
     @pl.loop(0, steps)
     def _(i):
-        for copy in state_copies(i, step, 0, outs, news, sems, False):
+        for copy in state_copies(i, 0, outs, news, sems, False):
             copy.wait()
 
     for copy in copies:
@@ -591,7 +592,7 @@
     fresh = tuple(range(1, 1 + len(arrived)))
     size = len(fresh)
     total = count * (1 + size)
-    step = min(part, 64)
+    step = min(part, 128)
     args = [*arrived, hidden, hidden_t, given, weight, *held]
     near = [plain((blocks, 1, LANE), f32)] * size + [plain((total, part), bf16)]
     far = [out_hbm((count, part), f32)] * size
@@ -625,8 +626,9 @@
     state, tokens, refs = refs[:3], refs[3:6], refs[6:]
     hidden_t, grad_ref, factor_ref, gate_new, in_sems, out_sems, sems = refs
     part = grad_ref.shape[0]
-    steps = in_sems.shape[1]
+    steps = out_sems.shape[1]
     step = part // steps
+    loads = in_sems.shape[1]
     gate_load = pltpu.make_async_copy(factor_hbm, factor_ref, sems.at[0])
     gate_store = pltpu.make_async_copy(gate_new, gate_out, sems.at[1])
     gate_load.start()
@@ -636,8 +638,8 @@
     ]
     for copy in token_loads:
         copy.start()
-    for i in range(steps):
-        for copy in state_copies(i, step, low, state_hbm, state, in_sems, True):
+    for i in range(loads):
+        for copy in state_copies(i, low, state_hbm, state, in_sems, True):
             copy.start()
     transpose_rows([hidden_ref], hidden_t)
     form_grad(hidden_t, [rows_ref], grad_ref)
@@ -648,12 +650,12 @@
     place_ref[...] = jnp.where(live, ids // EXP_LOCAL * SEND + slots, -1)
     inverse_ref[...] = 1.0 / tokens[2][...].astype(f32)
 
-    @pl.loop(0, steps)
-    def _(i):
-        for copy in state_copies(i, step, low, state_hbm, state, in_sems, True):
-            copy.wait()
+    for i in range(steps):
+        if i % (steps // loads) == 0:
+            for copy in state_copies(i * loads // steps, low, state_hbm, state, in_sems, True):
+                copy.wait()
         update_rows(i * step, step, state, state, grad_ref)
-        for copy in state_copies(i, step, low, outs, state, out_sems, False):
+        for copy in state_copies(i, low, outs, state, out_sems, False):
             copy.start()
 
     gate_load.wait()
@@ -667,7 +669,7 @@
 
     @pl.loop(0, steps)
     def _(i):
-        for copy in state_copies(i, step, low, outs, state, out_sems, False):
+        for copy in state_copies(i, low, outs, state, out_sems, False):
             copy.wait()
 
     gate_store.wait()
@@ -676,13 +678,14 @@
 def update(low, hidden, rows, grads, factors, state, tokens, done):
     total, part = hidden.shape
     cols = rows.shape[1]
-    step = min(part, 64)
+    step = min(part, 128)
     shards = len(grads)
     scratch = [pltpu.VMEM((part, cols), kind) for kind in (f32, bf16, bf16)]
     scratch += [pltpu.VMEM(token.shape, token.dtype) for token in tokens]
     scratch += [pltpu.VMEM((part, total), bf16), pltpu.VMEM((part, cols), f32)]
     scratch += [pltpu.VMEM(factors.shape, kind) for kind in (f32, bf16)]
-    scratch += [pltpu.SemaphoreType.DMA((3, part // step))] * 2
+    steps = part // step
+    scratch += [pltpu.SemaphoreType.DMA((3, count)) for count in (min(2, steps), steps)]
     scratch += [pltpu.SemaphoreType.DMA((5,))]
     return pl.pallas_call(
         functools.partial(update_kernel, low, shards),

time: 83.7 us -> 82.8 us (0.989)
  Pallas kernels: 32.9 us -> 31.9 us
    pallas_call x1, Pallas kernels: 7.82 us -> 6.95 us  [update(): pl.pallas_call(functools.partial(update_kernel, low, shards), in_specs=[V...]
  transfers between devices with their start and end apart: 7 -> 7, of which waited for: 3 -> 4; matrix products, arithmetic and copies ran while one was open for 0% -> 0% of each run, Pallas kernels for 31% -> 30%
where the time goes in v14:
time: 82.8 us; the launch traced here: 81.9 us
  Pallas kernels  31.9 us (39%)
  waiting for transfers between devices  24.9 us (30%)
  starting transfers between devices  23.7 us (29%)
    ppermute x4, waiting for transfers between devices, shift(): return lax.ppermute(value, 'rep', perm)  24.7 us
    all_to_all x2, starting transfers between devices, exchange(): return lax.all_to_all(value, 'ep', split_axis=0, concat_axis=0, tiled=True)  13.1 us
    pallas_call x1, Pallas kernels, update(): pl.pallas_call(functools.partial(update_kernel, low, shards), in_specs=[V...  6.95 us
    pallas_call x1, Pallas kernels, settle(): pl.pallas_call(functools.partial(settle_kernel, fresh, blocks), in_specs=...  6.4 us
    all_to_all x1, starting transfers between devices, per_device(): lax.all_to_all(score, ('rep', 'ep'), split_axis=0, concat_axis=0, tiled=T...  5.33 us
    ppermute x4, starting transfers between devices, shift(): return lax.ppermute(value, 'rep', perm)  5.26 us
    pallas_call x1, Pallas kernels, load_state(): pl.pallas_call(functools.partial(load_kernel, middle), in_specs=[ANY] + [...  4.47 us
    pallas_call x1, Pallas kernels, dispatch(): pl.pallas_call(functools.partial(dispatch_kernel, edges), in_specs=[HBM]...  3.26 us
  transfers between devices with their start and end apart: 7, of which 4 were waited for; matrix products, arithmetic and copies ran while one was open for 0% of the time, Pallas kernels for 30%

profile of v14, /device:TPU:0, one launch (start us, length us, event | category | flops | bytes accessed | tf_op | source)
XLA Modules:
  0.0 81.9 jit_solution(748355721468218523)
XLA Ops:
  0.6 3.3 %shard_map.119 = (bf16[256,1536]{1,0:T(8,128)(2,1)}, bf16[256,1152]{1,0:T(8,128)(2,1)S(1)}) custom-call(s32[8,256]{1,0:T(8,128)} %bitcast.17, s32[8,256]{1,0:T(8,128)} %bitcast.19, bf16[8,256]{1,0:T(8,128)(2,1)} %bitcast.21, bf16[256,3584]{1,0:T(8,128)(2,1)} %grad_hbm.1), custom_call_target="tpu_custom_call" | custom-call | flops 469762048 | bytes 3670016 | tf_op jit(solution)/shard_map/pallas_call | solution.py:135
  3.9 7.4 %all-to-all-start = ((bf16[16,16,1536]{2,1,0:T(8,128)(2,1)}), bf16[16,16,1536]{2,1,0:T(8,128)(2,1)S(1)}, u32[]{:S(2)}, u32[]{:S(2)}) async-start(bf16[16,16,1536]{2,1,0:T(8,128)(2,1)} %bitcast.3), calls=%async_computation | async-start | bytes 1572864 | tf_op jit(solution)/shard_map/all_to_all | solution.py:742
  11.3 1.6 %collective-permute-start.2 = (bf16[256,1152]{1,0:T(8,128)(2,1)S(1)}, bf16[256,1152]{1,0:T(8,128)(2,1)S(1)}, u32[]{:S(2)}, u32[]{:S(2)}) collective-permute-start(bf16[256,1152]{1,0:T(8,128)(2,1)S(1)} %get-tuple-element.39.after_ref.refs_0_), channel_id=1, source_target_pairs={{0,16},{16,0},{1,17},{17,1},{2,18},{18,2},{3,19},{19,3},{4,20},{20... | collective-permute-start | bytes 1769480 | tf_op jit(solution)/shard_map/ppermute | solution.py:739
  12.9 2.7 %shard_map.121 = (bf16[192,512]{1,0:T(8,128)(2,1)}, bf16[192,512]{1,0:T(8,128)(2,1)}, f32[192,2048]{1,0:T(8,128)}) custom-call(bf16[192,2048]{1,0:T(8,128)(2,1)} %bitcast.16, bf16[256,1152]{1,0:T(8,128)(2,1)S(1)} %get-tuple-element.39.after_ref.refs_0_), custom_call_target="tpu_custom_call" | custom-call | flops 3145728 | bytes 2752512 | tf_op jit(solution)/shard_map/pallas_call | solution.py:175
  15.6 0.5 collective-permute-start.1
  16.1 11.4 %collective-permute-done.2.refs_1_ = bf16[256,1152]{1,0:T(8,128)(2,1)S(1)} collective-permute-done((bf16[256,1152]{1,0:T(8,128)(2,1)S(1)}, bf16[256,1152]{1,0:T(8,128)(2,1)S(1)}, u32[]{:S(2)}, u32[]{:S(2)}) %collective-permute-start.2) | collective-permute-done | bytes 589856 | tf_op jit(solution)/shard_map/ppermute | solution.py:739
  27.5 2.2 %shard_map.122 = bf16[384,1536]{1,0:T(8,128)(2,1)} custom-call(bf16[256,1152]{1,0:T(8,128)(2,1)S(1)} %get-tuple-element.39.after_ref.refs_0_, bf16[256,1152]{1,0:T(8,128)(2,1)S(1)} %collective-permute-done.2.refs_1_), custom_call_target="tpu_custom_call" | custom-call | bytes 2949120 | tf_op jit(solution)/shard_map/pallas_call | solution.py:306
  29.6 1.5 %collective-permute-done.1.refs_1_ = bf16[192,512]{1,0:T(8,128)(2,1)S(1)} collective-permute-done((bf16[192,512]{1,0:T(8,128)(2,1)}, bf16[192,512]{1,0:T(8,128)(2,1)S(1)}, u32[]{:S(2)}, u32[]{:S(2)}) %collective-permute-start.1) | collective-permute-done | bytes 196640 | tf_op jit(solution)/shard_map/ppermute | solution.py:739
  31.1 0.0 copy-start
  31.1 0.0 all-to-all-done
  31.1 0.7 copy-done
  31.8 5.7 %all-to-all-start.1 = ((bf16[16,24,1536]{2,1,0:T(8,128)(2,1)}), bf16[16,24,1536]{2,1,0:T(8,128)(2,1)S(1)}, u32[]{:S(2)}, u32[]{:S(2)}) async-start(bf16[16,24,1536]{2,1,0:T(8,128)(2,1)} %bitcast.15), calls=%async_computation.1 | async-start | bytes 2359296 | tf_op jit(solution)/shard_map/all_to_all | solution.py:742
  37.6 1.6 %collective-permute-start = (bf16[256,1536]{1,0:T(8,128)(2,1)S(1)}, bf16[256,1536]{1,0:T(8,128)(2,1)S(1)}, u32[]{:S(2)}, u32[]{:S(2)}) collective-permute-start(bf16[256,1536]{1,0:T(8,128)(2,1)S(1)} %bitcast.12), channel_id=1, source_target_pairs={{0,16},{16,0},{1,17},{17,1},{2,18},{18,2},{3,19},{19,3},{4,20},{20... | collective-permute-start | bytes 2359304 | tf_op jit(solution)/shard_map/ppermute | solution.py:739
  39.1 4.5 %shard_map.120 = (f32[512,2048]{1,0:T(8,128)S(1)}, bf16[512,2048]{1,0:T(8,128)(2,1)S(1)}, bf16[512,2048]{1,0:T(8,128)(2,1)S(1)}, bf16[512,2048]{1,0:T(8,128)(2,1)S(1)}, bf16[512,1536]{1,0:T(8,128)(2,1)S(1)}) custom-call(bf16[256,1536]{1,0:T(8,128)(2,1)S(1)} %bitcast.13, f32[1,512,3584]{2,1,0:T(8,128)} %refs_3_.1, bf16[1,512,3584]{2,1,0:T(8,128)(2,1)} %refs_4_.1, ...), custom_call_target="tpu_custom_call" | custom-call | flops 1835008 | bytes 25690112 | tf_op jit(solution)/shard_map/pallas_call | solution.py:228
  43.6 1.9 %shard_map.123 = (bf16[192,2048]{1,0:T(8,128)(2,1)S(1)}, bf16[384,512]{1,0:T(8,128)(2,1)S(1)}, bf16[512,384]{1,0:T(8,128)(2,1)S(1)}, f32[16,1,128]{2,1,0:T(1,128)S(1)}, f32[192,512]{1,0:T(8,128)}) custom-call(bf16[256,1536]{1,0:T(8,128)(2,1)S(1)} %bitcast.14, bf16[512,2048]{1,0:T(8,128)(2,1)S(1)} %get-tuple-element.38.weight_ref.refs_4_, ...), custom_call_target="tpu_custom_call" | custom-call | flops 805306368 | bytes 2097152 | tf_op jit(solution)/shard_map/pallas_call | solution.py:396
  45.6 11.9 %collective-permute-done.refs_0_ = bf16[256,1536]{1,0:T(8,128)(2,1)S(1)} collective-permute-done((bf16[256,1536]{1,0:T(8,128)(2,1)S(1)}, bf16[256,1536]{1,0:T(8,128)(2,1)S(1)}, u32[]{:S(2)}, u32[]{:S(2)}) %collective-permute-start) | collective-permute-done | bytes 786464 | tf_op jit(solution)/shard_map/ppermute | solution.py:739
  57.4 6.4 %shard_map.124 = (f32[16,1,128]{2,1,0:T(1,128)S(1)}, bf16[384,512]{1,0:T(8,128)(2,1)S(1)}, f32[192,512]{1,0:T(8,128)}, f32[1,512,3584]{2,1,0:T(8,128)}, bf16[1,5...) custom-call(bf16[256,1536]{1,0:T(8,128)(2,1)S(1)} %collective-permute-done.refs_0_, ...), custom_call_target="tpu_custom_call" | custom-call | flops 1610612736 | bytes 16777216 | tf_op jit(solution)/shard_map/pallas_call | solution.py:609
  63.8 0.0 all-to-all-done.1
  63.8 2.4 %shard_map.125 = (bf16[192,512]{1,0:T(8,128)(2,1)S(1)}, bf16[192,512]{1,0:T(8,128)(2,1)}, f32[32,1,128]{2,1,0:T(1,128)}) custom-call(bf16[384,1536]{1,0:T(8,128)(2,1)S(1)} %bitcast.10, bf16[384,512]{1,0:T(8,128)(2,1)S(1)} %get-tuple-element.49.hidden_ref, bf16[512,1536]{1,0:T(8,128)(2,1)S(1)} %get-tuple-element.51.weight_ref, ...), custom_call_target="tpu_custom_call" | custom-call | flops 603979776 | bytes 1572864 | tf_op jit(solution)/shard_map/pallas_call | solution.py:450
  66.2 1.6 %collective-permute-start.3 = (bf16[192,512]{1,0:T(8,128)(2,1)}, bf16[192,512]{1,0:T(8,128)(2,1)S(1)}, u32[]{:S(2)}, u32[]{:S(2)}) collective-permute-start(bf16[192,512]{1,0:T(8,128)(2,1)} %get-tuple-element.57), channel_id=1, source_target_pairs={{0,16},{16,0},{1,17},{17,1},{2,18},{18,2},{3,19},{19,3},{4,20},{20... | collective-permute-start | bytes 589832 | tf_op jit(solution)/shard_map/ppermute | solution.py:739
  67.8 5.3 %all-to-all-start.2 = ((f32[32,1,128]{2,1,0:T(1,128)}), f32[32,1,128]{2,1,0:T(1,128)S(1)}, u32[]{:S(2)}, u32[]{:S(2)}) async-start(f32[32,1,128]{2,1,0:T(1,128)} %get-tuple-element.65), calls=%async_computation.2 | async-start | bytes 32768 | tf_op jit(solution)/shard_map/all_to_all | solution.py:763
  73.2 0.0 collective-permute-done.3.refs_1_
  73.2 7.0 %shard_map.126 = (f32[1,512,3584]{2,1,0:T(8,128)}, bf16[1,512,3584]{2,1,0:T(8,128)(2,1)}, bf16[1,512,3584]{2,1,0:T(8,128)(2,1)}, bf16[192,2048]{1,0:T(8,128)(2,1...) custom-call(bf16[384,512]{1,0:T(8,128)(2,1)S(1)} %get-tuple-element., ...), custom_call_target="tpu_custom_call", output_to_operand_aliasing={{0}: (11, {}), {1}: (12, {}), {2}: (13, {})} | custom-call | flops 603979776 | bytes 12582912 | tf_op jit(solution)/shard_map/pallas_call | solution.py:690
  80.1 0.2 all-to-all-done.2.score_ref
  80.3 1.6 %shard_map.127 = f32[8,256]{1,0:T(8,128)} custom-call(s32[8,256]{1,0:T(8,128)S(1)} %get-tuple-element.63.place_ref, f32[8,256]{1,0:T(8,128)S(1)} %get-tuple-element.64.inverse_ref, f32[32,1,128]{2,1,0:T(1,128)S(1)} %all-to-all-done.2.score_ref), custom_call_target="tpu_custom_call" | custom-call | flops 1048576 | bytes 65536 | tf_op jit(solution)/shard_map/pallas_call | solution.py:718
Async XLA Ops:
  3.9 27.2 %all-to-all-start = ((bf16[16,16,1536]{2,1,0:T(8,128)(2,1)}), bf16[16,16,1536]{2,1,0:T(8,128)(2,1)S(1)}, u32[]{:S(2)}, u32[]{:S(2)}) async-start(bf16[16,16,1536]{2,1,0:T(8,128)(2,1)} %bitcast.3), calls=%async_computation | async-start | bytes 1572864 | tf_op jit(solution)/shard_map/all_to_all | solution.py:742
  11.3 16.2 %collective-permute-start.2 = (bf16[256,1152]{1,0:T(8,128)(2,1)S(1)}, bf16[256,1152]{1,0:T(8,128)(2,1)S(1)}, u32[]{:S(2)}, u32[]{:S(2)}) collective-permute-start(bf16[256,1152]{1,0:T(8,128)(2,1)S(1)} %get-tuple-element.39.after_ref.refs_0_), channel_id=1, source_target_pairs={{0,16},{16,0},{1,17},{17,1},{2,18},{18,2},{3,19},{19,3},{4,20},{20... | collective-permute-start | bytes 1769480 | tf_op jit(solution)/shard_map/ppermute | solution.py:739
  15.6 15.5 %collective-permute-start.1 = (bf16[192,512]{1,0:T(8,128)(2,1)}, bf16[192,512]{1,0:T(8,128)(2,1)S(1)}, u32[]{:S(2)}, u32[]{:S(2)}) collective-permute-start(bf16[192,512]{1,0:T(8,128)(2,1)} %get-tuple-element.41), channel_id=1, source_target_pairs={{0,16},{16,0},{1,17},{17,1},{2,18},{18,2},{3,19},{19,3},{4,20},{20... | collective-permute-start | bytes 589832 | tf_op jit(solution)/shard_map/ppermute | solution.py:739
  31.1 0.7 copy-start
  31.8 32.0 %all-to-all-start.1 = ((bf16[16,24,1536]{2,1,0:T(8,128)(2,1)}), bf16[16,24,1536]{2,1,0:T(8,128)(2,1)S(1)}, u32[]{:S(2)}, u32[]{:S(2)}) async-start(bf16[16,24,1536]{2,1,0:T(8,128)(2,1)} %bitcast.15), calls=%async_computation.1 | async-start | bytes 2359296 | tf_op jit(solution)/shard_map/all_to_all | solution.py:742
  37.6 19.9 %collective-permute-start = (bf16[256,1536]{1,0:T(8,128)(2,1)S(1)}, bf16[256,1536]{1,0:T(8,128)(2,1)S(1)}, u32[]{:S(2)}, u32[]{:S(2)}) collective-permute-start(bf16[256,1536]{1,0:T(8,128)(2,1)S(1)} %bitcast.12), channel_id=1, source_target_pairs={{0,16},{16,0},{1,17},{17,1},{2,18},{18,2},{3,19},{19,3},{4,20},{20... | collective-permute-start | bytes 2359304 | tf_op jit(solution)/shard_map/ppermute | solution.py:739
  66.2 6.9 %collective-permute-start.3 = (bf16[192,512]{1,0:T(8,128)(2,1)}, bf16[192,512]{1,0:T(8,128)(2,1)S(1)}, u32[]{:S(2)}, u32[]{:S(2)}) collective-permute-start(bf16[192,512]{1,0:T(8,128)(2,1)} %get-tuple-element.57), channel_id=1, source_target_pairs={{0,16},{16,0},{1,17},{17,1},{2,18},{18,2},{3,19},{19,3},{4,20},{20... | collective-permute-start | bytes 589832 | tf_op jit(solution)/shard_map/ppermute | solution.py:739
  67.8 12.5 %all-to-all-start.2 = ((f32[32,1,128]{2,1,0:T(1,128)}), f32[32,1,128]{2,1,0:T(1,128)S(1)}, u32[]{:S(2)}, u32[]{:S(2)}) async-start(f32[32,1,128]{2,1,0:T(1,128)} %get-tuple-element.65), calls=%async_computation.2 | async-start | bytes 32768 | tf_op jit(solution)/shard_map/all_to_all | solution.py:763

commit v15 on v14

--- a/solution.py
+++ b/solution.py
@@ -366,22 +366,19 @@
 
 def begin_kernel(blocks, arrived_ref, weight_ref, *refs):
     size = len(refs) - 7
-    hidden_hbm, (rows_ref, hidden_ref, hidden_t, score_ref) = refs[:size], refs[size:-3]
+    hidden, (rows_ref, hidden_ref, hidden_t, score_ref) = refs[:size], refs[size:-3]
     proj_hbm, proj_ref, sems = refs[-3:]
     count = rows_ref.shape[0]
-    loads = [
-        pltpu.make_async_copy(ref, hidden_ref.at[pl.ds(s * count, count)], sems.at[1 + s])
-        for s, ref in enumerate(hidden_hbm)
-    ]
-    for copy in loads:
-        copy.start()
+    load = pltpu.make_async_copy(hidden[0], hidden_ref.at[pl.ds(0, count)], sems.at[1])
+    load.start()
+    for s in range(1, size):
+        hidden_ref[s * count : (s + 1) * count] = hidden[s][...]
     reorder(arrived_ref[...], rows_ref)
     proj = times_weight(rows_ref, weight_ref)
     proj_ref[...] = proj
     copy = pltpu.make_async_copy(proj_ref, proj_hbm, sems.at[0])
     copy.start()
-    for load in loads:
-        load.wait()
+    load.wait()
     score_ref[...] = score_block(
         blocks, proj, hidden_ref[:count], [block_index(blocks, count)]
     )[0]
@@ -395,7 +392,7 @@
     total = count * len(hidden)
     return pl.pallas_call(
         functools.partial(begin_kernel, blocks),
-        in_specs=[VMEM] * 2 + [HBM] * len(hidden),
+        in_specs=[VMEM] * 2 + [HBM] + [VMEM] * (len(hidden) - 1),
         out_specs=[VMEM] * 4 + [HBM],
         out_shape=[
             plain((count, cols), bf16),
@@ -406,16 +403,17 @@
         ],
         scratch_shapes=[
             pltpu.VMEM((count, part), f32),
-            pltpu.SemaphoreType.DMA((1 + len(hidden),)),
+            pltpu.SemaphoreType.DMA((2,)),
         ],
         compiler_params=params(8 * count * cols + 16 * total * part),
         cost_estimate=cost(4 * count * part * cols, 2 * part * cols),
-    )(arrived, weight, *in_hbm(*hidden))
+    )(arrived, weight, *in_hbm(hidden[0]), *hidden[1:])
 
 
 def finish_kernel(shards, blocks, arrived_ref, hidden_ref, weight_ref, *refs):
-    before_hbm, score_in = refs[:shards], refs[shards : 2 * shards]
-    projs, (score_ref, before, sems) = refs[2 * shards : 3 * shards], refs[3 * shards :]
+    before_hbm, refs = refs[: shards - 1], refs[shards - 1 :]
+    score_in, projs = refs[:shards], refs[shards : 2 * shards]
+    score_ref, before, sems = refs[2 * shards :]
     copies = [
         pltpu.make_async_copy(ref, before.at[s], sems.at[s])
         for s, ref in enumerate(before_hbm)
@@ -435,27 +433,28 @@
         order = row == slot + SEND * (div_send(slot) * (shards - 1) + s)
         order = jnp.where(order, 1.0, 0.0).astype(bf16)
         own = jnp.dot(order, rounded, preferred_element_type=f32)
-        copies[s].wait()
-        own += before[s]
+        if s > 0:
+            copies[s - 1].wait()
+            own += before[s - 1]
         projs[s][...] = own.astype(bf16)
         at = lax.rem(me + shards - s, shards)
         score_ref[pl.ds(at * blocks, blocks)] = score_in[s][...] + scores[s]
 
 
 def finish(blocks, arrived, hidden, weight, before, scores):
-    shards = len(before)
+    shards = len(scores)
     total, part = hidden.shape
     count = total // shards
     cols = weight.shape[1]
     outs = pl.pallas_call(
         functools.partial(finish_kernel, shards, blocks),
-        in_specs=[VMEM] * 3 + [HBM] * shards + [VMEM] * shards,
+        in_specs=[VMEM] * 3 + [HBM] * len(before) + [VMEM] * shards,
         out_specs=[VMEM] * (shards + 1),
         out_shape=[plain((count, part), bf16)] * shards
         + [plain((shards * blocks, 1, LANE), f32)],
         scratch_shapes=[
-            pltpu.VMEM((shards, count, part), f32),
-            pltpu.SemaphoreType.DMA((shards,)),
+            pltpu.VMEM((max(1, len(before)), count, part), f32),
+            pltpu.SemaphoreType.DMA((max(1, len(before)),)),
         ],
         compiler_params=params(20 * total * part),
         cost_estimate=cost(2 * total * part * cols, 2 * part * cols),
@@ -621,17 +620,18 @@
 
 def update_kernel(low, shards, hidden_ref, rows_ref, *refs):
     grad_refs, refs = refs[:shards], refs[shards:]
-    factor_hbm, state_hbm, token_hbm, refs = refs[0], refs[1:4], refs[4:7], refs[10:]
+    factor_hbm, before_hbm, state_hbm, token_hbm = refs[0], refs[1], refs[2:5], refs[5:8]
+    refs = refs[11:]
     outs, gate_out, place_ref, inverse_ref, refs = refs[:3], *refs[3:6], refs[6:]
     state, tokens, refs = refs[:3], refs[3:6], refs[6:]
-    hidden_t, grad_ref, factor_ref, gate_new, in_sems, out_sems, sems = refs
+    hidden_t, grad_ref, factor_ref, gate_new, before, in_sems, out_sems, sems = refs
     part = grad_ref.shape[0]
     steps = out_sems.shape[1]
     step = part // steps
     loads = in_sems.shape[1]
     gate_load = pltpu.make_async_copy(factor_hbm, factor_ref, sems.at[0])
     gate_store = pltpu.make_async_copy(gate_new, gate_out, sems.at[1])
-    gate_load.start()
+    before_load = pltpu.make_async_copy(before_hbm, before, sems.at[5])
     token_loads = [
         pltpu.make_async_copy(source, target, sems.at[2 + i])
         for i, (source, target) in enumerate(zip(token_hbm, tokens))
@@ -641,6 +641,8 @@
     for i in range(loads):
         for copy in state_copies(i, low, state_hbm, state, in_sems, True):
             copy.start()
+    gate_load.start()
+    before_load.start()
     transpose_rows([hidden_ref], hidden_t)
     form_grad(hidden_t, [rows_ref], grad_ref)
     for copy in token_loads:
@@ -659,9 +661,12 @@
             copy.start()
 
     gate_load.wait()
+    before_load.wait()
     for s, ref in enumerate(grad_refs):
         width = ref.shape[1]
         grad = ref[...].astype(f32)
+        if s == 0:
+            grad += before[...]
         for first in unit_columns(shards, s, width):
             own = pl.ds(first, width)
             gate_new[:, own] = (grad * factor_ref[:, own]).astype(bf16)
@@ -675,7 +680,7 @@
     gate_store.wait()
 
 
-def update(low, hidden, rows, grads, factors, state, tokens, done):
+def update(low, hidden, rows, grads, before, factors, state, tokens, done):
     total, part = hidden.shape
     cols = rows.shape[1]
     step = min(part, 128)
@@ -684,44 +689,52 @@
     scratch += [pltpu.VMEM(token.shape, token.dtype) for token in tokens]
     scratch += [pltpu.VMEM((part, total), bf16), pltpu.VMEM((part, cols), f32)]
     scratch += [pltpu.VMEM(factors.shape, kind) for kind in (f32, bf16)]
+    scratch += [pltpu.VMEM(before.shape, f32)]
     steps = part // step
     scratch += [pltpu.SemaphoreType.DMA((3, count)) for count in (min(2, steps), steps)]
-    scratch += [pltpu.SemaphoreType.DMA((5,))]
+    scratch += [pltpu.SemaphoreType.DMA((6,))]
     return pl.pallas_call(
         functools.partial(update_kernel, low, shards),
-        in_specs=[VMEM] * (2 + shards) + [HBM] * 10,
+        in_specs=[VMEM] * (2 + shards) + [HBM] * 11,
         out_specs=[HBM] * 4 + [VMEM] * 2,
         out_shape=[out_hbm(array.shape, array.dtype) for array in state]
         + [out_hbm(factors.shape, bf16)]
         + [plain(tokens[0].shape, kind) for kind in (jnp.int32, f32)],
         scratch_shapes=scratch,
-        input_output_aliases={2 + shards + 7 + i: i for i in range(3)},
+        input_output_aliases={2 + shards + 8 + i: i for i in range(3)},
         compiler_params=params(12 * part * cols + 2 * total * part + 6 * factors.size),
         cost_estimate=cost(2 * total * part * cols, 16 * part * cols, part * cols),
-    )(hidden, rows, *grads, *in_hbm(factors, *state, *tokens, *done))
+    )(hidden, rows, *grads, *in_hbm(factors, before, *state, *tokens, *done))
 
 
 def close_kernel(shards, place_ref, inverse_ref, score_ref, gate_ref):
-    place = place_ref[...]
     blocks = score_ref.shape[0] // shards
-    value = jnp.zeros(place.shape, f32)
-    for b in range(blocks):
-        for slot in range(SEND):
-            score = score_ref[b, 0, slot]
-            for s in range(1, shards):
-                score += score_ref[s * blocks + b, 0, slot]
-            value = jnp.where(place == b * SEND + slot, score, value)
-    gate_ref[...] = value * inverse_ref[...]
+    score = score_ref[:blocks].reshape(blocks, LANE)
+    for s in range(1, shards):
+        score += score_ref[s * blocks : (s + 1) * blocks].reshape(blocks, LANE)
+    high = score.astype(bf16)
+    rest = (score - high.astype(f32)).astype(bf16)
+    tok = place_ref.shape[1]
+    lane = lax.broadcasted_iota(jnp.int32, (LANE, tok), 0)
+    row = lax.broadcasted_iota(jnp.int32, (blocks, tok), 0)
+    for k in range(place_ref.shape[0]):
+        place = place_ref[k : k + 1]
+        owner = div_send(place)
+        pick = jnp.where(lane == place - SEND * owner, 1.0, 0.0).astype(bf16)
+        value = jnp.dot(high, pick, preferred_element_type=f32)
+        value += jnp.dot(rest, pick, preferred_element_type=f32)
+        value = jnp.sum(jnp.where(row == owner, value, 0.0), axis=0, keepdims=True)
+        gate_ref[k : k + 1] = value * inverse_ref[k : k + 1]
 
 
 def close(shards, place, inverse, score):
     return pl.pallas_call(
         functools.partial(close_kernel, shards),
-        in_specs=[VMEM] * 2 + [pl.BlockSpec(memory_space=pltpu.SMEM)],
+        in_specs=[VMEM] * 3,
         out_specs=VMEM,
         out_shape=plain(place.shape, f32),
         compiler_params=params(0),
-        cost_estimate=cost(1 << 20, 1 << 16),
+        cost_estimate=cost(1 << 24, 1 << 16),
     )(place, inverse, score)
 
 
@@ -757,14 +770,14 @@
         ep_size, peers, rows, hidden, hidden_t, weight_a, held, state
     )
     projs, score = finish(
-        ep_size, arrived_b, hidden_mixed, weight_b, [proj] + before, [score_own] + scores
+        ep_size, arrived_b, hidden_mixed, weight_b, before, [score_own] + scores
     )
     grads = [projs[0]] + [shift(projs[s], rep_size - s) for s in steps]
     score = lax.all_to_all(score, ("rep", "ep"), split_axis=0, concat_axis=0, tiled=True)
 
     tokens = (ids_t, slots_t, gates_t)
     *done, grad_gate_up, place, inverse = update(
-        edges[1], hidden_mixed, arrived_b, grads, factors, state, tokens, done
+        edges[1], hidden_mixed, arrived_b, grads, proj, factors, state, tokens, done
     )
     gate_grad = close(rep_size, place, inverse, score).T
     return (grad_gate_up.reshape(saved_gate_up.shape), gate_grad) + tuple(done)

time: 82.8 us -> 82.3 us (level)
  transfers between devices with their start and end apart: 7 -> 7, of which waited for: 4 -> 4; matrix products, arithmetic and copies ran while one was open for 0% -> 0% of each run, Pallas kernels for 30% -> 29%
where the time goes in v15:
time: 82.3 us; the launch traced here: 81.9 us
  Pallas kernels  31.2 us (38%)
  waiting for transfers between devices  25.6 us (31%)
  starting transfers between devices  23.6 us (29%)
    ppermute x4, waiting for transfers between devices, shift(): return lax.ppermute(value, 'rep', perm)  24.7 us
    all_to_all x2, starting transfers between devices, exchange(): return lax.all_to_all(value, 'ep', split_axis=0, concat_axis=0, tiled=True)  13.1 us
    pallas_call x1, Pallas kernels, settle(): pl.pallas_call(functools.partial(settle_kernel, fresh, blocks), in_specs=...  6.38 us
    pallas_call x1, Pallas kernels, update(): pl.pallas_call(functools.partial(update_kernel, low, shards), in_specs=[V...  6.24 us
    ppermute x4, starting transfers between devices, shift(): return lax.ppermute(value, 'rep', perm)  5.26 us
    all_to_all x1, starting transfers between devices, per_device(): lax.all_to_all(score, ('rep', 'ep'), split_axis=0, concat_axis=0, tiled=T...  5.24 us
    pallas_call x1, Pallas kernels, load_state(): pl.pallas_call(functools.partial(load_kernel, middle), in_specs=[ANY] + [...  4.47 us
    pallas_call x1, Pallas kernels, dispatch(): pl.pallas_call(functools.partial(dispatch_kernel, edges), in_specs=[HBM]...  3.26 us
  transfers between devices with their start and end apart: 7, of which 4 were waited for; matrix products, arithmetic and copies ran while one was open for 0% of the time, Pallas kernels for 29%

profile of v15, /device:TPU:0, one launch (start us, length us, event | category | flops | bytes accessed | tf_op | source)
XLA Modules:
  0.0 81.9 jit_solution(3661721490450193794)
XLA Ops:
  0.6 3.3 %shard_map.119 = (bf16[256,1536]{1,0:T(8,128)(2,1)}, bf16[256,1152]{1,0:T(8,128)(2,1)S(1)}) custom-call(s32[8,256]{1,0:T(8,128)} %bitcast.17, s32[8,256]{1,0:T(8,128)} %bitcast.19, bf16[8,256]{1,0:T(8,128)(2,1)} %bitcast.21, bf16[256,3584]{1,0:T(8,128)(2,1)} %grad_hbm.1), custom_call_target="tpu_custom_call" | custom-call | flops 469762048 | bytes 3670016 | tf_op jit(solution)/shard_map/pallas_call | solution.py:135
  3.9 7.4 %all-to-all-start = ((bf16[16,16,1536]{2,1,0:T(8,128)(2,1)}), bf16[16,16,1536]{2,1,0:T(8,128)(2,1)S(1)}, u32[]{:S(2)}, u32[]{:S(2)}) async-start(bf16[16,16,1536]{2,1,0:T(8,128)(2,1)} %bitcast.3), calls=%async_computation | async-start | bytes 1572864 | tf_op jit(solution)/shard_map/all_to_all | solution.py:755
  11.3 1.6 %collective-permute-start.2 = (bf16[256,1152]{1,0:T(8,128)(2,1)S(1)}, bf16[256,1152]{1,0:T(8,128)(2,1)S(1)}, u32[]{:S(2)}, u32[]{:S(2)}) collective-permute-start(bf16[256,1152]{1,0:T(8,128)(2,1)S(1)} %get-tuple-element.39.after_ref.refs_0_), channel_id=1, source_target_pairs={{0,16},{16,0},{1,17},{17,1},{2,18},{18,2},{3,19},{19,3},{4,20},{20... | collective-permute-start | bytes 1769480 | tf_op jit(solution)/shard_map/ppermute | solution.py:752
  12.9 2.7 %shard_map.121 = (bf16[192,512]{1,0:T(8,128)(2,1)}, bf16[192,512]{1,0:T(8,128)(2,1)}, f32[192,2048]{1,0:T(8,128)}) custom-call(bf16[192,2048]{1,0:T(8,128)(2,1)} %bitcast.16, bf16[256,1152]{1,0:T(8,128)(2,1)S(1)} %get-tuple-element.39.after_ref.refs_0_), custom_call_target="tpu_custom_call" | custom-call | flops 3145728 | bytes 2752512 | tf_op jit(solution)/shard_map/pallas_call | solution.py:175
  15.6 0.5 collective-permute-start.1
  16.1 11.4 %collective-permute-done.2.refs_1_ = bf16[256,1152]{1,0:T(8,128)(2,1)S(1)} collective-permute-done((bf16[256,1152]{1,0:T(8,128)(2,1)S(1)}, bf16[256,1152]{1,0:T(8,128)(2,1)S(1)}, u32[]{:S(2)}, u32[]{:S(2)}) %collective-permute-start.2) | collective-permute-done | bytes 589856 | tf_op jit(solution)/shard_map/ppermute | solution.py:752
  27.5 2.2 %shard_map.122 = bf16[384,1536]{1,0:T(8,128)(2,1)} custom-call(bf16[256,1152]{1,0:T(8,128)(2,1)S(1)} %get-tuple-element.39.after_ref.refs_0_, bf16[256,1152]{1,0:T(8,128)(2,1)S(1)} %collective-permute-done.2.refs_1_), custom_call_target="tpu_custom_call" | custom-call | bytes 2949120 | tf_op jit(solution)/shard_map/pallas_call | solution.py:306
  29.7 1.4 %collective-permute-done.1.refs_1_ = bf16[192,512]{1,0:T(8,128)(2,1)S(1)} collective-permute-done((bf16[192,512]{1,0:T(8,128)(2,1)}, bf16[192,512]{1,0:T(8,128)(2,1)S(1)}, u32[]{:S(2)}, u32[]{:S(2)}) %collective-permute-start.1) | collective-permute-done | bytes 196640 | tf_op jit(solution)/shard_map/ppermute | solution.py:752
  31.1 0.0 copy-start
  31.1 0.7 copy-done
  31.8 0.0 all-to-all-done
  31.8 5.8 %all-to-all-start.1 = ((bf16[16,24,1536]{2,1,0:T(8,128)(2,1)}), bf16[16,24,1536]{2,1,0:T(8,128)(2,1)S(1)}, u32[]{:S(2)}, u32[]{:S(2)}) async-start(bf16[16,24,1536]{2,1,0:T(8,128)(2,1)} %bitcast.15), calls=%async_computation.1 | async-start | bytes 2359296 | tf_op jit(solution)/shard_map/all_to_all | solution.py:755
  37.6 0.0 copy-start.1
  37.6 1.6 %collective-permute-start = (bf16[256,1536]{1,0:T(8,128)(2,1)S(1)}, bf16[256,1536]{1,0:T(8,128)(2,1)S(1)}, u32[]{:S(2)}, u32[]{:S(2)}) collective-permute-start(bf16[256,1536]{1,0:T(8,128)(2,1)S(1)} %bitcast.12), channel_id=1, source_target_pairs={{0,16},{16,0},{1,17},{17,1},{2,18},{18,2},{3,19},{19,3},{4,20},{20... | collective-permute-start | bytes 2359304 | tf_op jit(solution)/shard_map/ppermute | solution.py:752
  39.2 4.5 %shard_map.120 = (f32[512,2048]{1,0:T(8,128)S(1)}, bf16[512,2048]{1,0:T(8,128)(2,1)S(1)}, bf16[512,2048]{1,0:T(8,128)(2,1)S(1)}, bf16[512,2048]{1,0:T(8,128)(2,1)S(1)}, bf16[512,1536]{1,0:T(8,128)(2,1)S(1)}) custom-call(bf16[256,1536]{1,0:T(8,128)(2,1)S(1)} %bitcast.13, f32[1,512,3584]{2,1,0:T(8,128)} %refs_4_.1, bf16[1,512,3584]{2,1,0:T(8,128)(2,1)} %refs_5_.1, ...), custom_call_target="tpu_custom_call" | custom-call | flops 1835008 | bytes 25690112 | tf_op jit(solution)/shard_map/pallas_call | solution.py:228
  43.6 0.0 copy-done.1
  43.7 1.9 %shard_map.123 = (bf16[192,2048]{1,0:T(8,128)(2,1)S(1)}, bf16[384,512]{1,0:T(8,128)(2,1)S(1)}, bf16[512,384]{1,0:T(8,128)(2,1)S(1)}, f32[16,1,128]{2,1,0:T(1,128)S(1)}, f32[192,512]{1,0:T(8,128)}) custom-call(bf16[256,1536]{1,0:T(8,128)(2,1)S(1)} %bitcast.14, bf16[512,2048]{1,0:T(8,128)(2,1)S(1)} %get-tuple-element.38.weight_ref.refs_4_, ...), custom_call_target="tpu_custom_call" | custom-call | flops 805306368 | bytes 2097152 | tf_op jit(solution)/shard_map/pallas_call | solution.py:393
  45.6 11.9 %collective-permute-done.refs_0_ = bf16[256,1536]{1,0:T(8,128)(2,1)S(1)} collective-permute-done((bf16[256,1536]{1,0:T(8,128)(2,1)S(1)}, bf16[256,1536]{1,0:T(8,128)(2,1)S(1)}, u32[]{:S(2)}, u32[]{:S(2)}) %collective-permute-start) | collective-permute-done | bytes 786464 | tf_op jit(solution)/shard_map/ppermute | solution.py:752
  57.5 6.4 %shard_map.124 = (f32[16,1,128]{2,1,0:T(1,128)S(1)}, bf16[384,512]{1,0:T(8,128)(2,1)S(1)}, f32[192,512]{1,0:T(8,128)}, f32[1,512,3584]{2,1,0:T(8,128)}, bf16[1,5...) custom-call(bf16[256,1536]{1,0:T(8,128)(2,1)S(1)} %collective-permute-done.refs_0_, ...), custom_call_target="tpu_custom_call" | custom-call | flops 1610612736 | bytes 16777216 | tf_op jit(solution)/shard_map/pallas_call | solution.py:608
  63.9 0.0 all-to-all-done.1
  63.9 3.0 %shard_map.125 = (bf16[192,512]{1,0:T(8,128)(2,1)S(1)}, bf16[192,512]{1,0:T(8,128)(2,1)}, f32[32,1,128]{2,1,0:T(1,128)}) custom-call(bf16[384,1536]{1,0:T(8,128)(2,1)S(1)} %bitcast.10, bf16[384,512]{1,0:T(8,128)(2,1)S(1)} %get-tuple-element.49.hidden_ref, bf16[512,1536]{1,0:T(8,128)(2,1)S(1)} %get-tuple-element.51.weight_ref, ...), custom_call_target="tpu_custom_call" | custom-call | flops 603979776 | bytes 1572864 | tf_op jit(solution)/shard_map/pallas_call | solution.py:449
  67.0 1.6 %collective-permute-start.3 = (bf16[192,512]{1,0:T(8,128)(2,1)}, bf16[192,512]{1,0:T(8,128)(2,1)S(1)}, u32[]{:S(2)}, u32[]{:S(2)}) collective-permute-start(bf16[192,512]{1,0:T(8,128)(2,1)} %get-tuple-element.56), channel_id=1, source_target_pairs={{0,16},{16,0},{1,17},{17,1},{2,18},{18,2},{3,19},{19,3},{4,20},{20... | collective-permute-start | bytes 589832 | tf_op jit(solution)/shard_map/ppermute | solution.py:752
  68.5 5.2 %all-to-all-start.2 = ((f32[32,1,128]{2,1,0:T(1,128)}), f32[32,1,128]{2,1,0:T(1,128)S(1)}, u32[]{:S(2)}, u32[]{:S(2)}) async-start(f32[32,1,128]{2,1,0:T(1,128)} %get-tuple-element.65), calls=%async_computation.2 | async-start | bytes 32768 | tf_op jit(solution)/shard_map/all_to_all | solution.py:776
  73.8 0.0 collective-permute-done.3.refs_1_
  73.8 6.2 %shard_map.126 = (f32[1,512,3584]{2,1,0:T(8,128)}, bf16[1,512,3584]{2,1,0:T(8,128)(2,1)}, bf16[1,512,3584]{2,1,0:T(8,128)(2,1)}, bf16[192,2048]{1,0:T(8,128)(2,1...) custom-call(bf16[384,512]{1,0:T(8,128)(2,1)S(1)} %get-tuple-element., ...), custom_call_target="tpu_custom_call", output_to_operand_aliasing={{0}: (12, {}), {1}: (13, {}), {2}: (14, {})} | custom-call | flops 603979776 | bytes 12582912 | tf_op jit(solution)/shard_map/pallas_call | solution.py:696
  80.1 0.9 %all-to-all-done.2.score_ref = f32[32,1,128]{2,1,0:T(1,128)S(1)} async-done(((f32[32,1,128]{2,1,0:T(1,128)}), f32[32,1,128]{2,1,0:T(1,128)S(1)}, u32[]{:S(2)}, u32[]{:S(2)}) %all-to-all-start.2) | async-done | bytes 16416 | tf_op jit(solution)/shard_map/all_to_all | solution.py:776
  80.9 0.9 %shard_map.127 = f32[8,256]{1,0:T(8,128)} custom-call(s32[8,256]{1,0:T(8,128)S(1)} %get-tuple-element.63.place_ref, f32[8,256]{1,0:T(8,128)S(1)} %get-tuple-element.64.inverse_ref, f32[32,1,128]{2,1,0:T(1,128)S(1)} %all-to-all-done.2.score_ref), custom_call_target="tpu_custom_call" | custom-call | flops 16777216 | bytes 65536 | tf_op jit(solution)/shard_map/pallas_call | solution.py:731
Async XLA Ops:
  3.9 27.9 %all-to-all-start = ((bf16[16,16,1536]{2,1,0:T(8,128)(2,1)}), bf16[16,16,1536]{2,1,0:T(8,128)(2,1)S(1)}, u32[]{:S(2)}, u32[]{:S(2)}) async-start(bf16[16,16,1536]{2,1,0:T(8,128)(2,1)} %bitcast.3), calls=%async_computation | async-start | bytes 1572864 | tf_op jit(solution)/shard_map/all_to_all | solution.py:755
  11.3 16.2 %collective-permute-start.2 = (bf16[256,1152]{1,0:T(8,128)(2,1)S(1)}, bf16[256,1152]{1,0:T(8,128)(2,1)S(1)}, u32[]{:S(2)}, u32[]{:S(2)}) collective-permute-start(bf16[256,1152]{1,0:T(8,128)(2,1)S(1)} %get-tuple-element.39.after_ref.refs_0_), channel_id=1, source_target_pairs={{0,16},{16,0},{1,17},{17,1},{2,18},{18,2},{3,19},{19,3},{4,20},{20... | collective-permute-start | bytes 1769480 | tf_op jit(solution)/shard_map/ppermute | solution.py:752
  15.6 15.5 %collective-permute-start.1 = (bf16[192,512]{1,0:T(8,128)(2,1)}, bf16[192,512]{1,0:T(8,128)(2,1)S(1)}, u32[]{:S(2)}, u32[]{:S(2)}) collective-permute-start(bf16[192,512]{1,0:T(8,128)(2,1)} %get-tuple-element.41), channel_id=1, source_target_pairs={{0,16},{16,0},{1,17},{17,1},{2,18},{18,2},{3,19},{19,3},{4,20},{20... | collective-permute-start | bytes 589832 | tf_op jit(solution)/shard_map/ppermute | solution.py:752
  31.1 0.7 copy-start
  31.8 32.1 %all-to-all-start.1 = ((bf16[16,24,1536]{2,1,0:T(8,128)(2,1)}), bf16[16,24,1536]{2,1,0:T(8,128)(2,1)S(1)}, u32[]{:S(2)}, u32[]{:S(2)}) async-start(bf16[16,24,1536]{2,1,0:T(8,128)(2,1)} %bitcast.15), calls=%async_computation.1 | async-start | bytes 2359296 | tf_op jit(solution)/shard_map/all_to_all | solution.py:755
  37.6 6.1 %copy-start.1 = (bf16[192,512]{1,0:T(8,128)(2,1)S(1)}, bf16[192,512]{1,0:T(8,128)(2,1)}, u32[]{:S(2)}) copy-start(bf16[192,512]{1,0:T(8,128)(2,1)} %copy-done) | copy-start | bytes 589828
  37.6 19.9 %collective-permute-start = (bf16[256,1536]{1,0:T(8,128)(2,1)S(1)}, bf16[256,1536]{1,0:T(8,128)(2,1)S(1)}, u32[]{:S(2)}, u32[]{:S(2)}) collective-permute-start(bf16[256,1536]{1,0:T(8,128)(2,1)S(1)} %bitcast.12), channel_id=1, source_target_pairs={{0,16},{16,0},{1,17},{17,1},{2,18},{18,2},{3,19},{19,3},{4,20},{20... | collective-permute-start | bytes 2359304 | tf_op jit(solution)/shard_map/ppermute | solution.py:752
  67.0 6.8 %collective-permute-start.3 = (bf16[192,512]{1,0:T(8,128)(2,1)}, bf16[192,512]{1,0:T(8,128)(2,1)S(1)}, u32[]{:S(2)}, u32[]{:S(2)}) collective-permute-start(bf16[192,512]{1,0:T(8,128)(2,1)} %get-tuple-element.56), channel_id=1, source_target_pairs={{0,16},{16,0},{1,17},{17,1},{2,18},{18,2},{3,19},{19,3},{4,20},{20... | collective-permute-start | bytes 589832 | tf_op jit(solution)/shard_map/ppermute | solution.py:752
  68.5 12.4 %all-to-all-start.2 = ((f32[32,1,128]{2,1,0:T(1,128)}), f32[32,1,128]{2,1,0:T(1,128)S(1)}, u32[]{:S(2)}, u32[]{:S(2)}) async-start(f32[32,1,128]{2,1,0:T(1,128)} %get-tuple-element.65), calls=%async_computation.2 | async-start | bytes 32768 | tf_op jit(solution)/shard_map/all_to_all | solution.py:776

commit v16 on v15

--- a/solution.py
+++ b/solution.py
@@ -411,9 +411,8 @@
 
 
 def finish_kernel(shards, blocks, arrived_ref, hidden_ref, weight_ref, *refs):
-    before_hbm, refs = refs[: shards - 1], refs[shards - 1 :]
-    score_in, projs = refs[:shards], refs[shards : 2 * shards]
-    score_ref, before, sems = refs[2 * shards :]
+    before_hbm, score_in = refs[:shards], refs[shards : 2 * shards]
+    projs, (score_ref, before, sems) = refs[2 * shards : 3 * shards], refs[3 * shards :]
     copies = [
         pltpu.make_async_copy(ref, before.at[s], sems.at[s])
         for s, ref in enumerate(before_hbm)
@@ -433,28 +432,27 @@
         order = row == slot + SEND * (div_send(slot) * (shards - 1) + s)
         order = jnp.where(order, 1.0, 0.0).astype(bf16)
         own = jnp.dot(order, rounded, preferred_element_type=f32)
-        if s > 0:
-            copies[s - 1].wait()
-            own += before[s - 1]
+        copies[s].wait()
+        own += before[s]
         projs[s][...] = own.astype(bf16)
         at = lax.rem(me + shards - s, shards)
         score_ref[pl.ds(at * blocks, blocks)] = score_in[s][...] + scores[s]
 
 
 def finish(blocks, arrived, hidden, weight, before, scores):
-    shards = len(scores)
+    shards = len(before)
     total, part = hidden.shape
     count = total // shards
     cols = weight.shape[1]
     outs = pl.pallas_call(
         functools.partial(finish_kernel, shards, blocks),
-        in_specs=[VMEM] * 3 + [HBM] * len(before) + [VMEM] * shards,
+        in_specs=[VMEM] * 3 + [HBM] * shards + [VMEM] * shards,
         out_specs=[VMEM] * (shards + 1),
         out_shape=[plain((count, part), bf16)] * shards
         + [plain((shards * blocks, 1, LANE), f32)],
         scratch_shapes=[
-            pltpu.VMEM((max(1, len(before)), count, part), f32),
-            pltpu.SemaphoreType.DMA((max(1, len(before)),)),
+            pltpu.VMEM((shards, count, part), f32),
+            pltpu.SemaphoreType.DMA((shards,)),
         ],
         compiler_params=params(20 * total * part),
         cost_estimate=cost(2 * total * part * cols, 2 * part * cols),
@@ -620,18 +618,17 @@
 
 def update_kernel(low, shards, hidden_ref, rows_ref, *refs):
     grad_refs, refs = refs[:shards], refs[shards:]
-    factor_hbm, before_hbm, state_hbm, token_hbm = refs[0], refs[1], refs[2:5], refs[5:8]
-    refs = refs[11:]
+    factor_hbm, state_hbm, token_hbm, refs = refs[0], refs[1:4], refs[4:7], refs[10:]
     outs, gate_out, place_ref, inverse_ref, refs = refs[:3], *refs[3:6], refs[6:]
     state, tokens, refs = refs[:3], refs[3:6], refs[6:]
-    hidden_t, grad_ref, factor_ref, gate_new, before, in_sems, out_sems, sems = refs
+    hidden_t, grad_ref, factor_ref, gate_new, in_sems, out_sems, sems = refs
     part = grad_ref.shape[0]
     steps = out_sems.shape[1]
     step = part // steps
     loads = in_sems.shape[1]
     gate_load = pltpu.make_async_copy(factor_hbm, factor_ref, sems.at[0])
     gate_store = pltpu.make_async_copy(gate_new, gate_out, sems.at[1])
-    before_load = pltpu.make_async_copy(before_hbm, before, sems.at[5])
+    gate_load.start()
     token_loads = [
         pltpu.make_async_copy(source, target, sems.at[2 + i])
         for i, (source, target) in enumerate(zip(token_hbm, tokens))
@@ -641,8 +638,6 @@
     for i in range(loads):
         for copy in state_copies(i, low, state_hbm, state, in_sems, True):
             copy.start()
-    gate_load.start()
-    before_load.start()
     transpose_rows([hidden_ref], hidden_t)
     form_grad(hidden_t, [rows_ref], grad_ref)
     for copy in token_loads:
@@ -661,12 +656,9 @@
             copy.start()
 
     gate_load.wait()
-    before_load.wait()
     for s, ref in enumerate(grad_refs):
         width = ref.shape[1]
         grad = ref[...].astype(f32)
-        if s == 0:
-            grad += before[...]
         for first in unit_columns(shards, s, width):
             own = pl.ds(first, width)
             gate_new[:, own] = (grad * factor_ref[:, own]).astype(bf16)
@@ -680,7 +672,7 @@
     gate_store.wait()
 
 
-def update(low, hidden, rows, grads, before, factors, state, tokens, done):
+def update(low, hidden, rows, grads, factors, state, tokens, done):
     total, part = hidden.shape
     cols = rows.shape[1]
     step = min(part, 128)
@@ -689,22 +681,21 @@
     scratch += [pltpu.VMEM(token.shape, token.dtype) for token in tokens]
     scratch += [pltpu.VMEM((part, total), bf16), pltpu.VMEM((part, cols), f32)]
     scratch += [pltpu.VMEM(factors.shape, kind) for kind in (f32, bf16)]
-    scratch += [pltpu.VMEM(before.shape, f32)]
     steps = part // step
     scratch += [pltpu.SemaphoreType.DMA((3, count)) for count in (min(2, steps), steps)]
-    scratch += [pltpu.SemaphoreType.DMA((6,))]
+    scratch += [pltpu.SemaphoreType.DMA((5,))]
     return pl.pallas_call(
         functools.partial(update_kernel, low, shards),
-        in_specs=[VMEM] * (2 + shards) + [HBM] * 11,
+        in_specs=[VMEM] * (2 + shards) + [HBM] * 10,
         out_specs=[HBM] * 4 + [VMEM] * 2,
         out_shape=[out_hbm(array.shape, array.dtype) for array in state]
         + [out_hbm(factors.shape, bf16)]
         + [plain(tokens[0].shape, kind) for kind in (jnp.int32, f32)],
         scratch_shapes=scratch,
-        input_output_aliases={2 + shards + 8 + i: i for i in range(3)},
+        input_output_aliases={2 + shards + 7 + i: i for i in range(3)},
         compiler_params=params(12 * part * cols + 2 * total * part + 6 * factors.size),
         cost_estimate=cost(2 * total * part * cols, 16 * part * cols, part * cols),
-    )(hidden, rows, *grads, *in_hbm(factors, before, *state, *tokens, *done))
+    )(hidden, rows, *grads, *in_hbm(factors, *state, *tokens, *done))
 
 
 def close_kernel(shards, place_ref, inverse_ref, score_ref, gate_ref):
@@ -770,14 +761,14 @@
         ep_size, peers, rows, hidden, hidden_t, weight_a, held, state
     )
     projs, score = finish(
-        ep_size, arrived_b, hidden_mixed, weight_b, before, [score_own] + scores
+        ep_size, arrived_b, hidden_mixed, weight_b, [proj] + before, [score_own] + scores
     )
     grads = [projs[0]] + [shift(projs[s], rep_size - s) for s in steps]
     score = lax.all_to_all(score, ("rep", "ep"), split_axis=0, concat_axis=0, tiled=True)
 
     tokens = (ids_t, slots_t, gates_t)
     *done, grad_gate_up, place, inverse = update(
-        edges[1], hidden_mixed, arrived_b, grads, proj, factors, state, tokens, done
+        edges[1], hidden_mixed, arrived_b, grads, factors, state, tokens, done
     )
     gate_grad = close(rep_size, place, inverse, score).T
     return (grad_gate_up.reshape(saved_gate_up.shape), gate_grad) + tuple(done)

time: 82.3 us -> 82.2 us (level)
  transfers between devices with their start and end apart: 7 -> 7, of which waited for: 4 -> 4; matrix products, arithmetic and copies ran while one was open for 0% -> 0% of each run, Pallas kernels for 29% -> 30%
where the time goes in v16:
time: 82.2 us; the launch traced here: 81.3 us
  Pallas kernels  31.3 us (38%)
  waiting for transfers between devices  24.9 us (30%)
  starting transfers between devices  23.6 us (29%)
    ppermute x4, waiting for transfers between devices, shift(): return lax.ppermute(value, 'rep', perm)  24.7 us
    all_to_all x2, starting transfers between devices, exchange(): return lax.all_to_all(value, 'ep', split_axis=0, concat_axis=0, tiled=True)  13.1 us
    pallas_call x1, Pallas kernels, update(): pl.pallas_call(functools.partial(update_kernel, low, shards), in_specs=[V...  6.95 us
    pallas_call x1, Pallas kernels, settle(): pl.pallas_call(functools.partial(settle_kernel, fresh, blocks), in_specs=...  6.39 us
    ppermute x4, starting transfers between devices, shift(): return lax.ppermute(value, 'rep', perm)  5.27 us
    all_to_all x1, starting transfers between devices, per_device(): lax.all_to_all(score, ('rep', 'ep'), split_axis=0, concat_axis=0, tiled=T...  5.22 us
    pallas_call x1, Pallas kernels, load_state(): pl.pallas_call(functools.partial(load_kernel, middle), in_specs=[ANY] + [...  4.47 us
    pallas_call x1, Pallas kernels, dispatch(): pl.pallas_call(functools.partial(dispatch_kernel, edges), in_specs=[HBM]...  3.26 us
  transfers between devices with their start and end apart: 7, of which 4 were waited for; matrix products, arithmetic and copies ran while one was open for 0% of the time, Pallas kernels for 30%

profile of v16, /device:TPU:0, one launch (start us, length us, event | category | flops | bytes accessed | tf_op | source)
XLA Modules:
  0.0 81.3 jit_solution(9332573020753151744)
XLA Ops:
  0.6 3.3 %shard_map.119 = (bf16[256,1536]{1,0:T(8,128)(2,1)}, bf16[256,1152]{1,0:T(8,128)(2,1)S(1)}) custom-call(s32[8,256]{1,0:T(8,128)} %bitcast.17, s32[8,256]{1,0:T(8,128)} %bitcast.19, bf16[8,256]{1,0:T(8,128)(2,1)} %bitcast.21, bf16[256,3584]{1,0:T(8,128)(2,1)} %grad_hbm.1), custom_call_target="tpu_custom_call" | custom-call | flops 469762048 | bytes 3670016 | tf_op jit(solution)/shard_map/pallas_call | solution.py:135
  3.9 7.4 %all-to-all-start = ((bf16[16,16,1536]{2,1,0:T(8,128)(2,1)}), bf16[16,16,1536]{2,1,0:T(8,128)(2,1)S(1)}, u32[]{:S(2)}, u32[]{:S(2)}) async-start(bf16[16,16,1536]{2,1,0:T(8,128)(2,1)} %bitcast.3), calls=%async_computation | async-start | bytes 1572864 | tf_op jit(solution)/shard_map/all_to_all | solution.py:746
  11.3 1.6 %collective-permute-start.2 = (bf16[256,1152]{1,0:T(8,128)(2,1)S(1)}, bf16[256,1152]{1,0:T(8,128)(2,1)S(1)}, u32[]{:S(2)}, u32[]{:S(2)}) collective-permute-start(bf16[256,1152]{1,0:T(8,128)(2,1)S(1)} %get-tuple-element.39.after_ref.refs_0_), channel_id=1, source_target_pairs={{0,16},{16,0},{1,17},{17,1},{2,18},{18,2},{3,19},{19,3},{4,20},{20... | collective-permute-start | bytes 1769480 | tf_op jit(solution)/shard_map/ppermute | solution.py:743
  12.9 2.7 %shard_map.121 = (bf16[192,512]{1,0:T(8,128)(2,1)}, bf16[192,512]{1,0:T(8,128)(2,1)}, f32[192,2048]{1,0:T(8,128)}) custom-call(bf16[192,2048]{1,0:T(8,128)(2,1)} %bitcast.16, bf16[256,1152]{1,0:T(8,128)(2,1)S(1)} %get-tuple-element.39.after_ref.refs_0_), custom_call_target="tpu_custom_call" | custom-call | flops 3145728 | bytes 2752512 | tf_op jit(solution)/shard_map/pallas_call | solution.py:175
  15.6 0.5 collective-permute-start.1
  16.1 11.4 %collective-permute-done.2.refs_1_ = bf16[256,1152]{1,0:T(8,128)(2,1)S(1)} collective-permute-done((bf16[256,1152]{1,0:T(8,128)(2,1)S(1)}, bf16[256,1152]{1,0:T(8,128)(2,1)S(1)}, u32[]{:S(2)}, u32[]{:S(2)}) %collective-permute-start.2) | collective-permute-done | bytes 589856 | tf_op jit(solution)/shard_map/ppermute | solution.py:743
  27.5 2.2 %shard_map.122 = bf16[384,1536]{1,0:T(8,128)(2,1)} custom-call(bf16[256,1152]{1,0:T(8,128)(2,1)S(1)} %get-tuple-element.39.after_ref.refs_0_, bf16[256,1152]{1,0:T(8,128)(2,1)S(1)} %collective-permute-done.2.refs_1_), custom_call_target="tpu_custom_call" | custom-call | bytes 2949120 | tf_op jit(solution)/shard_map/pallas_call | solution.py:306
  29.7 1.4 %collective-permute-done.1.refs_1_ = bf16[192,512]{1,0:T(8,128)(2,1)S(1)} collective-permute-done((bf16[192,512]{1,0:T(8,128)(2,1)}, bf16[192,512]{1,0:T(8,128)(2,1)S(1)}, u32[]{:S(2)}, u32[]{:S(2)}) %collective-permute-start.1) | collective-permute-done | bytes 196640 | tf_op jit(solution)/shard_map/ppermute | solution.py:743
  31.1 0.0 copy-start
  31.1 0.7 copy-done
  31.8 0.0 all-to-all-done
  31.8 5.8 %all-to-all-start.1 = ((bf16[16,24,1536]{2,1,0:T(8,128)(2,1)}), bf16[16,24,1536]{2,1,0:T(8,128)(2,1)S(1)}, u32[]{:S(2)}, u32[]{:S(2)}) async-start(bf16[16,24,1536]{2,1,0:T(8,128)(2,1)} %bitcast.15), calls=%async_computation.1 | async-start | bytes 2359296 | tf_op jit(solution)/shard_map/all_to_all | solution.py:746
  37.6 0.0 copy-start.1
  37.6 1.6 %collective-permute-start = (bf16[256,1536]{1,0:T(8,128)(2,1)S(1)}, bf16[256,1536]{1,0:T(8,128)(2,1)S(1)}, u32[]{:S(2)}, u32[]{:S(2)}) collective-permute-start(bf16[256,1536]{1,0:T(8,128)(2,1)S(1)} %bitcast.12), channel_id=1, source_target_pairs={{0,16},{16,0},{1,17},{17,1},{2,18},{18,2},{3,19},{19,3},{4,20},{20... | collective-permute-start | bytes 2359304 | tf_op jit(solution)/shard_map/ppermute | solution.py:743
  39.2 4.5 %shard_map.120 = (f32[512,2048]{1,0:T(8,128)S(1)}, bf16[512,2048]{1,0:T(8,128)(2,1)S(1)}, bf16[512,2048]{1,0:T(8,128)(2,1)S(1)}, bf16[512,2048]{1,0:T(8,128)(2,1)S(1)}, bf16[512,1536]{1,0:T(8,128)(2,1)S(1)}) custom-call(bf16[256,1536]{1,0:T(8,128)(2,1)S(1)} %bitcast.13, f32[1,512,3584]{2,1,0:T(8,128)} %refs_3_.1, bf16[1,512,3584]{2,1,0:T(8,128)(2,1)} %refs_4_.1, ...), custom_call_target="tpu_custom_call" | custom-call | flops 1835008 | bytes 25690112 | tf_op jit(solution)/shard_map/pallas_call | solution.py:228
  43.6 0.0 copy-done.1
  43.7 1.9 %shard_map.123 = (bf16[192,2048]{1,0:T(8,128)(2,1)S(1)}, bf16[384,512]{1,0:T(8,128)(2,1)S(1)}, bf16[512,384]{1,0:T(8,128)(2,1)S(1)}, f32[16,1,128]{2,1,0:T(1,128)S(1)}, f32[192,512]{1,0:T(8,128)}) custom-call(bf16[256,1536]{1,0:T(8,128)(2,1)S(1)} %bitcast.14, bf16[512,2048]{1,0:T(8,128)(2,1)S(1)} %get-tuple-element.38.weight_ref.refs_4_, ...), custom_call_target="tpu_custom_call" | custom-call | flops 805306368 | bytes 2097152 | tf_op jit(solution)/shard_map/pallas_call | solution.py:393
  45.6 11.9 %collective-permute-done.refs_0_ = bf16[256,1536]{1,0:T(8,128)(2,1)S(1)} collective-permute-done((bf16[256,1536]{1,0:T(8,128)(2,1)S(1)}, bf16[256,1536]{1,0:T(8,128)(2,1)S(1)}, u32[]{:S(2)}, u32[]{:S(2)}) %collective-permute-start) | collective-permute-done | bytes 786464 | tf_op jit(solution)/shard_map/ppermute | solution.py:743
  57.5 6.4 %shard_map.124 = (f32[16,1,128]{2,1,0:T(1,128)S(1)}, bf16[384,512]{1,0:T(8,128)(2,1)S(1)}, f32[192,512]{1,0:T(8,128)}, f32[1,512,3584]{2,1,0:T(8,128)}, bf16[1,5...) custom-call(bf16[256,1536]{1,0:T(8,128)(2,1)S(1)} %collective-permute-done.refs_0_, ...), custom_call_target="tpu_custom_call" | custom-call | flops 1610612736 | bytes 16777216 | tf_op jit(solution)/shard_map/pallas_call | solution.py:606
  63.9 0.0 all-to-all-done.1
  63.9 2.4 %shard_map.125 = (bf16[192,512]{1,0:T(8,128)(2,1)S(1)}, bf16[192,512]{1,0:T(8,128)(2,1)}, f32[32,1,128]{2,1,0:T(1,128)}) custom-call(bf16[384,1536]{1,0:T(8,128)(2,1)S(1)} %bitcast.10, bf16[384,512]{1,0:T(8,128)(2,1)S(1)} %get-tuple-element.49.hidden_ref, bf16[512,1536]{1,0:T(8,128)(2,1)S(1)} %get-tuple-element.51.weight_ref, ...), custom_call_target="tpu_custom_call" | custom-call | flops 603979776 | bytes 1572864 | tf_op jit(solution)/shard_map/pallas_call | solution.py:447
  66.3 1.6 %collective-permute-start.3 = (bf16[192,512]{1,0:T(8,128)(2,1)}, bf16[192,512]{1,0:T(8,128)(2,1)S(1)}, u32[]{:S(2)}, u32[]{:S(2)}) collective-permute-start(bf16[192,512]{1,0:T(8,128)(2,1)} %get-tuple-element.57), channel_id=1, source_target_pairs={{0,16},{16,0},{1,17},{17,1},{2,18},{18,2},{3,19},{19,3},{4,20},{20... | collective-permute-start | bytes 589832 | tf_op jit(solution)/shard_map/ppermute | solution.py:743
  67.9 5.2 %all-to-all-start.2 = ((f32[32,1,128]{2,1,0:T(1,128)}), f32[32,1,128]{2,1,0:T(1,128)S(1)}, u32[]{:S(2)}, u32[]{:S(2)}) async-start(f32[32,1,128]{2,1,0:T(1,128)} %get-tuple-element.65), calls=%async_computation.2 | async-start | bytes 32768 | tf_op jit(solution)/shard_map/all_to_all | solution.py:767
  73.2 0.0 collective-permute-done.3.refs_1_
  73.2 7.0 %shard_map.126 = (f32[1,512,3584]{2,1,0:T(8,128)}, bf16[1,512,3584]{2,1,0:T(8,128)(2,1)}, bf16[1,512,3584]{2,1,0:T(8,128)(2,1)}, bf16[192,2048]{1,0:T(8,128)(2,1...) custom-call(bf16[384,512]{1,0:T(8,128)(2,1)S(1)} %get-tuple-element., ...), custom_call_target="tpu_custom_call", output_to_operand_aliasing={{0}: (11, {}), {1}: (12, {}), {2}: (13, {})} | custom-call | flops 603979776 | bytes 12582912 | tf_op jit(solution)/shard_map/pallas_call | solution.py:687
  80.1 0.2 all-to-all-done.2.score_ref
  80.3 0.9 %shard_map.127 = f32[8,256]{1,0:T(8,128)} custom-call(s32[8,256]{1,0:T(8,128)S(1)} %get-tuple-element.63.place_ref, f32[8,256]{1,0:T(8,128)S(1)} %get-tuple-element.64.inverse_ref, f32[32,1,128]{2,1,0:T(1,128)S(1)} %all-to-all-done.2.score_ref), custom_call_target="tpu_custom_call" | custom-call | flops 16777216 | bytes 65536 | tf_op jit(solution)/shard_map/pallas_call | solution.py:722
Async XLA Ops:
  3.9 27.9 %all-to-all-start = ((bf16[16,16,1536]{2,1,0:T(8,128)(2,1)}), bf16[16,16,1536]{2,1,0:T(8,128)(2,1)S(1)}, u32[]{:S(2)}, u32[]{:S(2)}) async-start(bf16[16,16,1536]{2,1,0:T(8,128)(2,1)} %bitcast.3), calls=%async_computation | async-start | bytes 1572864 | tf_op jit(solution)/shard_map/all_to_all | solution.py:746
  11.3 16.2 %collective-permute-start.2 = (bf16[256,1152]{1,0:T(8,128)(2,1)S(1)}, bf16[256,1152]{1,0:T(8,128)(2,1)S(1)}, u32[]{:S(2)}, u32[]{:S(2)}) collective-permute-start(bf16[256,1152]{1,0:T(8,128)(2,1)S(1)} %get-tuple-element.39.after_ref.refs_0_), channel_id=1, source_target_pairs={{0,16},{16,0},{1,17},{17,1},{2,18},{18,2},{3,19},{19,3},{4,20},{20... | collective-permute-start | bytes 1769480 | tf_op jit(solution)/shard_map/ppermute | solution.py:743
  15.6 15.5 %collective-permute-start.1 = (bf16[192,512]{1,0:T(8,128)(2,1)}, bf16[192,512]{1,0:T(8,128)(2,1)S(1)}, u32[]{:S(2)}, u32[]{:S(2)}) collective-permute-start(bf16[192,512]{1,0:T(8,128)(2,1)} %get-tuple-element.41), channel_id=1, source_target_pairs={{0,16},{16,0},{1,17},{17,1},{2,18},{18,2},{3,19},{19,3},{4,20},{20... | collective-permute-start | bytes 589832 | tf_op jit(solution)/shard_map/ppermute | solution.py:743
  31.1 0.7 copy-start
  31.8 32.1 %all-to-all-start.1 = ((bf16[16,24,1536]{2,1,0:T(8,128)(2,1)}), bf16[16,24,1536]{2,1,0:T(8,128)(2,1)S(1)}, u32[]{:S(2)}, u32[]{:S(2)}) async-start(bf16[16,24,1536]{2,1,0:T(8,128)(2,1)} %bitcast.15), calls=%async_computation.1 | async-start | bytes 2359296 | tf_op jit(solution)/shard_map/all_to_all | solution.py:746
  37.6 6.1 %copy-start.1 = (bf16[192,512]{1,0:T(8,128)(2,1)S(1)}, bf16[192,512]{1,0:T(8,128)(2,1)}, u32[]{:S(2)}) copy-start(bf16[192,512]{1,0:T(8,128)(2,1)} %copy-done) | copy-start | bytes 589828
  37.6 19.9 %collective-permute-start = (bf16[256,1536]{1,0:T(8,128)(2,1)S(1)}, bf16[256,1536]{1,0:T(8,128)(2,1)S(1)}, u32[]{:S(2)}, u32[]{:S(2)}) collective-permute-start(bf16[256,1536]{1,0:T(8,128)(2,1)S(1)} %bitcast.12), channel_id=1, source_target_pairs={{0,16},{16,0},{1,17},{17,1},{2,18},{18,2},{3,19},{19,3},{4,20},{20... | collective-permute-start | bytes 2359304 | tf_op jit(solution)/shard_map/ppermute | solution.py:743
  66.3 6.8 %collective-permute-start.3 = (bf16[192,512]{1,0:T(8,128)(2,1)}, bf16[192,512]{1,0:T(8,128)(2,1)S(1)}, u32[]{:S(2)}, u32[]{:S(2)}) collective-permute-start(bf16[192,512]{1,0:T(8,128)(2,1)} %get-tuple-element.57), channel_id=1, source_target_pairs={{0,16},{16,0},{1,17},{17,1},{2,18},{18,2},{3,19},{19,3},{4,20},{20... | collective-permute-start | bytes 589832 | tf_op jit(solution)/shard_map/ppermute | solution.py:743
  67.9 12.4 %all-to-all-start.2 = ((f32[32,1,128]{2,1,0:T(1,128)}), f32[32,1,128]{2,1,0:T(1,128)S(1)}, u32[]{:S(2)}, u32[]{:S(2)}) async-start(f32[32,1,128]{2,1,0:T(1,128)} %get-tuple-element.65), calls=%async_computation.2 | async-start | bytes 32768 | tf_op jit(solution)/shard_map/all_to_all | solution.py:767
